TPU v7x, 32 devices: a whole 2x2x4 slice. The times are simulated.
32 devices in a mesh: grp: 2 (over x), pool: 8 (over z, y), tp: 2 (over core).
Axes of the slice: x: 2, y: 2, z: 4, core: 2. Of those that a mesh axis runs over, the one named last changes fastest.
Arguments:
- hidden: bfloat16 [768, 8192], P(('grp', 'pool'), 'tp'), parts along dimension 0, may hold values from -6 to 6
- queries: bfloat16 [768, 4096], P(('grp', 'pool'), 'tp'), parts along dimension 0, may hold values from -8 to 8
- key_value_weight: bfloat16 [8192, 1024], P('tp'), may hold values from -0.0625 to 0.0625
- adapter_down_weight: bfloat16 [8, 8192, 128], P('pool', 'tp'), may hold values from -0.0625 to 0.0625
- adapter_up_weight: bfloat16 [8, 2, 64, 512], P('pool', None, None, 'tp'), may hold values from -0.75 to 0.75
- stored_cache_keys: bfloat16 [768, 4, 32, 128], P(('grp', 'pool'), 'tp'), parts along dimension 0, may hold values from -4 to 4
- stored_cache_values: bfloat16 [768, 4, 32, 128], P(('grp', 'pool'), 'tp'), parts along dimension 0, may hold values from -6 to 6
- row_adapter_index: int32 [768, 1], P(('grp', 'pool')), parts along dimension 0, may hold values from 0 to 7; in each aligned block of 48 rows (0 to 47, 48 to 95, ...) at most 12 rows name the same one
- stored_cache_lengths: int32 [768], P(('grp', 'pool')), parts along dimension 0, may hold values from 2 to 32, as said below
- adapter_slot_table: int32 [8], replicated, may hold values from 0 to 7, each once
Outputs:
- token_key_value: bfloat16 [768, 1024], P(('grp', 'pool'), 'tp'), parts along dimension 0
- attended: bfloat16 [768, 4096], P(('grp', 'pool'), 'tp'), parts along dimension 0
There are 2 independent parts, one for each index of `grp`. A program takes and returns all parts, laid end to end along the dimension named above; an argument that names none is the same for every part. Nothing has to cross between parts.
Inputs may be any that keep to these rules, and one draw needn't show every extreme that they name: `row_adapter_index`: among the rows of one index of pool at most 12 name the same adapter, and in some such block one adapter is named by exactly 12 rows. `stored_cache_lengths`: some row has exactly 32 valid positions. `adapter_slot_table`: each adapter has its own slot.
All inputs are finite; a program needn't handle non-finite values.
Results may differ from a plain program's by a relative error of at most 0.0061.
Values may be sent and summed in bfloat16 or wider, within the bound.
No kernel may reach another device: no remote copies, remote signals or barrier semaphores. Data moves between devices by JAX's collectives and lax.ppermute only.
A program may use at most 128 MiB of HBM per device.

v0:
```python
import jax
import jax.numpy as jnp
from jax import lax
from jax.sharding import PartitionSpec as P


def expand_rows(reduced_input, up_weight_rows):
    adapter_rank_size = up_weight_rows.shape[1]
    paired_rows = reduced_input.reshape(reduced_input.shape[:-1] + (2, adapter_rank_size))
    return jnp.einsum(
        "...ck,ckm->...cm", paired_rows, up_weight_rows, preferred_element_type=jnp.float32
    )


def shards(
    hidden,
    queries,
    key_value_weight,
    adapter_down_weight,
    adapter_up_weight,
    stored_cache_keys,
    stored_cache_values,
    row_adapter_index,
    stored_cache_lengths,
    adapter_slot_table,
):
    batch_row_count = hidden.shape[0]
    my_index = lax.axis_index("pool")
    local_key_value = stored_cache_keys.shape[1]
    head_width = stored_cache_keys.shape[3]
    local_columns = adapter_up_weight.shape[3]
    down_weight_rows = adapter_down_weight[0]
    up_weight_rows = adapter_up_weight[0]
    partial_sum = jnp.dot(hidden, key_value_weight, preferred_element_type=jnp.float32)
    projected_rows = lax.psum_scatter(partial_sum, "tp", scatter_dimension=1, tiled=True)
    all_rows, all_ids = (
        lax.all_gather(hidden, "pool", axis=0, tiled=True),
        lax.all_gather(row_adapter_index, "pool", axis=0, tiled=True),
    )
    shrink_part = jnp.dot(all_rows, down_weight_rows, preferred_element_type=jnp.float32)
    reduced_input = lax.psum(shrink_part, "tp").astype(jnp.bfloat16)
    is_mine = adapter_slot_table[all_ids[:, 0]] == my_index
    keep_rows = lax.slice_in_dim(is_mine, 0, batch_row_count * lax.axis_size("pool"), axis=0)
    row_terms = expand_rows(reduced_input, up_weight_rows)
    adapter_terms = lax.psum_scatter(
        jnp.where(keep_rows[:, None, None], row_terms, 0.0).reshape(
            batch_row_count * lax.axis_size("pool"), 2 * local_columns
        ),
        "pool",
        scatter_dimension=0,
        tiled=True,
    )
    merged_projection = projected_rows.reshape(batch_row_count, local_key_value, 2, head_width)
    merged_projection = merged_projection + adapter_terms.reshape(
        batch_row_count, 2, local_key_value, head_width
    ).transpose(0, 2, 1, 3)
    token_key_value = merged_projection.reshape(
        batch_row_count, local_key_value * 2 * head_width
    ).astype(jnp.bfloat16)
    heads_kv = token_key_value.reshape(batch_row_count, local_key_value, 2, head_width)
    group_size = queries.shape[1] // (local_key_value * head_width)
    query_heads = queries.reshape(batch_row_count, local_key_value, group_size, head_width)
    score_scale = head_width ** (-0.5)
    cache_scores = (
        jnp.einsum(
            "rgqd,rgpd->rgqp", query_heads, stored_cache_keys, preferred_element_type=jnp.float32
        )
        * score_scale
    )
    valid_mask = jnp.arange(stored_cache_keys.shape[2])[None, :] < stored_cache_lengths[:, None]
    cache_scores = jnp.where(valid_mask[:, None, None, :], cache_scores, -jnp.inf)
    own_scores = (
        jnp.einsum(
            "rgqd,rgd->rgq", query_heads, heads_kv[:, :, 0], preferred_element_type=jnp.float32
        )
        * score_scale
    )
    highest = jnp.maximum(jnp.max(cache_scores, axis=-1), own_scores)
    cache_exp = jnp.exp(cache_scores - highest[..., None])
    own_exp = jnp.exp(own_scores - highest)
    denominator = jnp.sum(cache_exp, axis=-1) + own_exp
    cache_weights = (cache_exp / denominator[..., None]).astype(jnp.bfloat16)
    own_weights = (own_exp / denominator).astype(jnp.bfloat16)
    attended = jnp.einsum(
        "rgqp,rgpd->rgqd", cache_weights, stored_cache_values, preferred_element_type=jnp.float32
    )
    attended = (
        attended
        + own_weights.astype(jnp.float32)[..., None]
        * heads_kv[:, :, 1].astype(jnp.float32)[:, :, None, :]
    )
    return (
        token_key_value,
        attended.reshape(batch_row_count, queries.shape[1]).astype(jnp.bfloat16),
    )


def solution(mesh):
    in_specs = (
        P(("grp", "pool"), "tp"),
        P(("grp", "pool"), "tp"),
        P("tp", None),
        P("pool", "tp", None),
        P("pool", None, None, "tp"),
        P(("grp", "pool"), "tp", None, None),
        P(("grp", "pool"), "tp", None, None),
        P(("grp", "pool"), None),
        P(("grp", "pool")),
        P(),
    )
    out_specs = (P(("grp", "pool"), "tp"), P(("grp", "pool"), "tp"))
    return jax.shard_map(shards, mesh=mesh, in_specs=in_specs, out_specs=out_specs, check_vma=False)
```

profile of v0, /device:TPU:0, one launch (start us, length us, event | category | flops | bytes accessed | tf_op | source)
XLA Modules:
  0.0 156.5 jit_solution(5316501462481115915)
XLA Ops:
  8.0 0.0 copy-start
  8.0 0.0 all-gather.2.cloned.1.call-start
  8.1 0.7 all-gather.2.cloned.1.call-update
  8.7 0.0 copy-start.4
  8.8 0.0 copy-start.7
  8.8 0.0 copy-start.6
  8.8 0.0 copy-start.3
  8.8 0.0 reduce-scatter.3.cloned.1.call-start
  8.8 5.8 %fusion.18 = f32[48,1024]{1,0:T(8,128)} fusion(bf16[48,4096]{1,0:T(8,128)(2,1)} %param.10, bf16[4096,1024]{1,0:T(8,128)(2,1)} %param.12), kind=kOutput, calls=%fused_computation.41 | convolution fusion | flops 402653184 | bytes 8978432 | tf_op jit(solution)/shard_map/dot_general | solution.py:34
  14.6 0.0 reduce-scatter.3.cloned.1.call-update
  14.6 0.0 reduce-scatter.5.cloned.1.call-start
  14.7 0.0 copy-done.4
  14.7 0.7 fusion.16
  15.4 0.0 copy-done.7
  15.4 0.6 dynamic-slice
  16.6 0.0 copy-done.6
  16.7 0.1 bitcast_dynamic-update-slice_fusion
  16.8 13.1 %all-reduce = s32[384]{0:T(512)S(1)} all-reduce(s32[384]{0:T(512)S(1)} %bitcast_dynamic-update-slice_fusion), channel_id=1, replica_groups=mesh['grp'=2,'pool'=8,'tp'=2] {'pool'}, use_global_device_ids=true, to_apply=%add | all-reduce | flops 384 | bytes 3072
  29.9 4.2 %fusion.15 = s32[384]{0:T(512)S(1)} fusion(s32[]{:T(128)} %bitcast.3, s32[]{:T(128)} %bitcast.4, s32[]{:T(128)} %bitcast.5, s32[]{:T(128)} %bitcast.6, s32[]{:T(128)} %bitcast.7, s32[]{:T(128)} %bitcast.9, s32[]{:T(128)} %bitcast.8, s32[384]{0:T(512)S(1)} %all-reduce), kind=kLoop, calls=%fused_computation.37 | loop fusion | flops 5760 | bytes 3100 | tf_op jit(solution)/shard_map/gather | solution.py:42
  34.1 0.7 select_compare_fusion
  34.8 39.6 %all-gather.2.cloned.1.call-done = bf16[384,4096]{1,0:T(8,128)(2,1)} async-done(((bf16[48,4096]{1,0:T(8,128)(2,1)}), bf16[384,4096]{1,0:T(8,128)(2,1)}) %all-gather.2.cloned.1.call-update) | async-done | bytes 3145744 | tf_op jit(solution)/shard_map/all_gather | solution.py:37
  74.3 0.0 copy-done
  74.4 2.9 %fusion.2 = f32[384,128]{1,0:T(8,128)S(1)} fusion(bf16[384,4096]{1,0:T(8,128)(2,1)} %all-gather.2.cloned.1.call-done, bf16[1,4096,128]{2,1,0:T(8,128)(2,1)S(1)} %copy-done), kind=kOutput, calls=%fused_computation.5 | convolution fusion | flops 402653184 | bytes 4390912 | tf_op jit(solution)/shard_map/dot_general | solution.py:40
  77.2 4.0 %all-reduce.2 = bf16[384,128]{1,0:T(8,128)(2,1)S(1)} all-reduce(f32[384,128]{1,0:T(8,128)S(1)} %fusion.2), channel_id=1, replica_groups=mesh['grp'=2,'pool'=8,'tp'=2] {'tp'}, use_global_device_ids=true, to_apply=%region_1.0 | all-reduce | flops 49152 | bytes 294912 | tf_op jit(solution)/shard_map/psum | solution.py:41
  81.2 0.1 copy.39
  81.3 0.0 copy-done.3
  81.3 0.3 convolution_select_fusion
  81.6 1.1 copy.40
  82.8 0.0 reduce-scatter.5.cloned.1.call-update
  82.8 0.0 copy-done.2
  82.9 0.0 copy-done.5
  82.9 0.1 iota_compare_fusion
  82.9 0.0 copy-done.1
  83.0 0.7 fusion.17
  83.6 0.1 copy.44
  83.7 1.0 reshape.47
  84.7 59.4 %reduce-scatter.5.cloned.1.call-done = f32[48,512]{1,0:T(8,128)} async-done(((f32[384,512]{1,0:T(8,128)}), f32[48,512]{1,0:T(8,128)}) %reduce-scatter.5.cloned.1.call-update) | async-done | bytes 98320 | tf_op jit(solution)/shard_map/reduce_scatter | solution.py:45
  144.0 1.0 reshape.50
  145.1 0.2 fusion.9
  145.3 0.1 copy.51
  145.4 0.1 copy.45
  145.5 0.4 fusion.4
  145.9 0.1 copy.46
  145.9 0.1 copy.47
  146.1 0.1 copy.48
  146.2 1.5 fusion.1
  147.7 0.7 copy.59
  148.5 0.6 convert_element_type.29
  (13 shorter events, 0.2 us)
Async XLA Ops:
  8.0 66.4 %copy-start = (bf16[1,4096,128]{2,1,0:T(8,128)(2,1)S(1)}, bf16[1,4096,128]{2,1,0:T(8,128)(2,1)}, u32[]{:S(2)}) copy-start(bf16[1,4096,128]{2,1,0:T(8,128)(2,1)} %param.13) | copy-start | bytes 3145732
  8.0 66.3 %all-gather.2.cloned.1.call-start = ((), (), s32[]{:S(2)}) async-start(), calls=%async_computation.3 | async-start | bytes 3538944 | tf_op jit(solution)/shard_map/all_gather | solution.py:37
  8.7 6.0 %copy-start.4 = (s32[8]{0:T(128)S(1)}, s32[8]{0:T(128)}, u32[]{:S(2)}) copy-start(s32[8]{0:T(128)} %param.19) | copy-start | bytes 100
  8.8 6.6 %copy-start.7 = (u32[32]{0:T(128)S(1)}, u32[32]{0:T(128)}, u32[]{:S(2)}) copy-start(u32[32]{0:T(128)} %constant.29) | copy-start | bytes 388
  8.8 7.9 %copy-start.6 = (s32[48,1]{0,1:T(1,128)S(1)}, s32[48,1]{0,1:T(1,128)}, u32[]{:S(2)}) copy-start(s32[48,1]{0,1:T(1,128)} %param.17) | copy-start | bytes 580
  8.8 72.5 %copy-start.3 = (bf16[1,2,64,256]{3,2,1,0:T(8,128)(2,1)S(1)}, bf16[1,2,64,256]{3,2,1,0:T(8,128)(2,1)}, u32[]{:S(2)}) copy-start(bf16[1,2,64,256]{3,2,1,0:T(8,128)(2,1)} %param.14) | copy-start | bytes 196612
  8.8 74.9 %reduce-scatter.3.cloned.1.call-start = ((), (), s32[]{:S(2)}) async-start(), calls=%async_computation.2 | async-start | bytes 294912 | tf_op jit(solution)/shard_map/reduce_scatter | solution.py:35
  14.6 68.2 %copy-start.2 = (bf16[48,2048]{1,0:T(8,128)(2,1)S(1)}, bf16[48,2048]{1,0:T(8,128)(2,1)}, u32[]{:S(2)}) copy-start(bf16[48,2048]{1,0:T(8,128)(2,1)} %param.11) | copy-start | bytes 589828
  14.6 68.2 %copy-start.5 = (s32[48]{0:T(128)S(1)}, s32[48]{0:T(128)}, u32[]{:S(2)}) copy-start(s32[48]{0:T(128)} %param.18) | copy-start | bytes 580
  14.6 68.3 %copy-start.1 = (bf16[48,2,32,128]{3,2,1,0:T(8,128)(2,1)S(1)}, bf16[48,2,32,128]{3,2,1,0:T(8,128)(2,1)}, u32[]{:S(2)}) copy-start(bf16[48,2,32,128]{3,2,1,0:T(8,128)(2,1)} %param.15) | copy-start | bytes 2359300
  14.6 129.4 %reduce-scatter.5.cloned.1.call-start = ((), (), s32[]{:S(2)}) async-start(), calls=%async_computation.4 | async-start | bytes 884736 | tf_op jit(solution)/shard_map/reduce_scatter | solution.py:45
Sparse Core Ops, SparseCore 0:
  11.0 63.2 all-gather.1
Sparse Core Ops, SparseCore 1:
  14.7 10.2 reduce-scatter.2
  82.9 61.1 reduce-scatter.4
where the time goes:
time: 157 us
  waiting for transfers between devices  99.6 us (63%)
  blocking collectives  17.1 us (11%)
  between operations  16.4 us (10%)
  matrix products  11.4 us (7%)
  local copies, waits for them, and re-layouts  6.58 us (4%)
  other arithmetic  5.4 us (3%)
    reduce_scatter x1, waiting for transfers between devices, shards(): lax.psum_scatter(jnp.where(keep_rows[:, None, None], row_terms, 0.0).resh...  59.4 us
    all_gather x1, waiting for transfers between devices, shards(): lax.all_gather(hidden, 'pool', axis=0, tiled=True)  39.6 us
    unnamed x1, blocking collectives  13.1 us
    dot_general x1, matrix products, shards(): jnp.dot(hidden, key_value_weight, preferred_element_type=jnp.float32)  5.78 us
    gather x2, other arithmetic, shards(): is_mine = adapter_slot_table[all_ids[:, 0]] == my_index  4.25 us
    psum x1, blocking collectives, shards(): reduced_input = lax.psum(shrink_part, 'tp').astype(jnp.bfloat16)  3.97 us
  transfers between devices with their start and end apart: 3, of which 2 were waited for; matrix products, arithmetic and copies ran while one was open for 12% of the time, Pallas kernels for 0%

commit v1 on v0

v1 whole, which is shorter than its diff:
```python
import functools

import jax
import jax.numpy as jnp
from jax import lax
from jax.experimental import pallas as pl
from jax.experimental.pallas import tpu as pltpu
from jax.sharding import PartitionSpec as P

BF16 = jnp.bfloat16
F32 = jnp.float32
I32 = jnp.int32
VMEM_LIMIT = 48 * 1024 * 1024


def iota(shape, dim):
    return lax.broadcasted_iota(I32, shape, dim)


def split_count(cap):
    pieces = 4
    while cap * pieces % 16:
        pieces *= 2
    return pieces


def dot(a, b):
    return jnp.dot(a, b, preferred_element_type=F32)


def dot_first(a, b):
    return lax.dot_general(a, b, (((0,), (0,)), ((), ())), preferred_element_type=F32)


def exact_select(one_hot, x):
    high = x.astype(BF16)
    rest = x - high.astype(F32)
    middle = rest.astype(BF16)
    low = (rest - middle.astype(F32)).astype(BF16)
    return dot(one_hot, high) + (dot(one_hot, middle) + dot(one_hot, low))


def placement(rel, rank, cap, pieces):
    rows = rel.shape[1]
    code = rel * (pieces * cap) + rank
    codes = jnp.concatenate([code + piece * cap for piece in range(pieces)], axis=1)
    return codes


def pack_kernel(n, cap, pieces, me_ref, idx_ref, table_ref, hidden_ref, *out_refs):
    code_refs, chunk_refs = out_refs[:2], out_refs[2:]
    rows = hidden_ref.shape[0]
    width = hidden_ref.shape[1] // pieces
    me = me_ref[0]
    named = (iota((n, rows), 0) == idx_ref[...]).astype(F32).astype(BF16)
    table = jnp.broadcast_to(table_ref[...].astype(F32).astype(BF16), (16, n))
    slot = dot(table, named)[0:1, :].astype(I32)
    rel = lax.bitwise_xor(slot, me)
    member = (iota((n, rows), 0) == rel).astype(F32)
    before = (iota((rows, rows), 0) < iota((rows, rows), 1)).astype(F32).astype(BF16)
    count = dot(member.astype(BF16), before)
    rank = jnp.sum(member * count, axis=0, keepdims=True).astype(I32)
    code_refs[0][...] = rel
    code_refs[1][...] = rank
    codes = placement(rel, rank, cap, pieces)
    total = n * pieces * cap
    one_hot = (iota((total, pieces * rows), 0) == codes).astype(F32).astype(BF16)
    stacked = jnp.concatenate(
        [hidden_ref[:, piece * width : (piece + 1) * width] for piece in range(pieces)], axis=0
    )
    packed = dot(one_hot, stacked).astype(BF16)
    for s in range(n):
        chunk_refs[s][...] = packed[s * pieces * cap : (s + 1) * pieces * cap]


def shrink_kernel(n, cap, pieces, *refs):
    chunk_refs, down_ref, out_ref = refs[:n], refs[n], refs[n + 1]
    per = pieces * cap
    width = chunk_refs[0].shape[1]
    rank2 = down_ref.shape[2]
    received = jnp.concatenate([ref[...] for ref in chunk_refs], axis=0)
    total = jnp.zeros((n * per, rank2), F32)
    piece_of = (iota((n * per, rank2), 0) // cap) % pieces
    for piece in range(pieces):
        part = dot(received, down_ref[0, piece * width : (piece + 1) * width, :])
        total = total + jnp.where(piece_of == piece, part, 0.0)
    out_row, in_row = iota((n * cap, n * per), 0), iota((n * cap, n * per), 1)
    same = (out_row // cap == in_row // per) & (out_row % cap == in_row % cap)
    out_ref[...] = exact_select(same.astype(F32).astype(BF16), total)


def expand_kernel(n, cap, mine_ref, other_ref, up_ref, *out_refs):
    rank = up_ref.shape[2]
    head = 128
    blocks = up_ref.shape[3] // head
    reduced = (mine_ref[...] + other_ref[...]).astype(BF16)
    terms = []
    for c in range(2):
        kept = reduced[:, c * rank : (c + 1) * rank]
        wide = dot(kept, up_ref[0, c]).astype(BF16)
        terms += [wide[:, g * head : (g + 1) * head] for g in range(blocks)]
    stacked = jnp.concatenate(terms, axis=0)
    pieces = 2 * blocks
    per = pieces * cap
    size = n * per
    out_row, in_row = iota((size, size), 0), iota((size, size), 1)
    source = (out_row // cap % pieces) * (n * cap) + (out_row // per) * cap + out_row % cap
    moved = dot((source == in_row).astype(F32).astype(BF16), stacked).astype(BF16)
    for s in range(n):
        out_refs[s][...] = moved[s * per : (s + 1) * per]


def combine_kernel(n, cap, *refs):
    delta_refs = refs[:n]
    rel_ref, rank_ref, base_ref, other_ref, query_ref, max_ref, sum_ref, acc_ref, token_ref, out_ref = refs[n:]
    rows = base_ref.shape[0]
    head = 128
    groups = base_ref.shape[1] // (2 * head)
    pieces = 2 * groups
    total = n * pieces * cap
    codes = placement(rel_ref[...], rank_ref[...], cap, pieces)
    one_hot = (iota((total, pieces * rows), 0) == codes).astype(F32).astype(BF16)
    received = jnp.concatenate([ref[...] for ref in delta_refs], axis=0)
    delta = dot_first(one_hot, received)
    heads = query_ref.shape[1] // head
    per_group = heads // groups
    scale = head ** (-0.5)
    for g in range(groups):
        made = []
        for c in range(2):
            at = (g * 2 + c) * head
            piece = c * groups + g
            value = base_ref[:, at : at + head] + other_ref[:, at : at + head]
            value = (value + delta[piece * rows : (piece + 1) * rows]).astype(BF16)
            token_ref[:, at : at + head] = value
            made.append(value.astype(F32))
        key, value = made
        for h in range(g * per_group, (g + 1) * per_group):
            lanes = slice(h * head, (h + 1) * head)
            own = jnp.sum(query_ref[:, lanes].astype(F32) * key, axis=1, keepdims=True) * scale
            cache_max = max_ref[:, h : h + 1]
            highest = jnp.maximum(own, cache_max)
            cache_factor = jnp.exp(cache_max - highest)
            own_factor = jnp.exp(own - highest)
            inverse = 1.0 / (sum_ref[:, h : h + 1] * cache_factor + own_factor)
            out = acc_ref[:, lanes] * (cache_factor * inverse) + value * (own_factor * inverse)
            out_ref[:, lanes] = out.astype(BF16)


def call(kernel, outs, flops, bytes_accessed, smem_first=False, inputs=0):
    vmem = pl.BlockSpec(memory_space=pltpu.VMEM)
    specs = [vmem] * inputs
    if smem_first:
        specs[0] = pl.BlockSpec(memory_space=pltpu.SMEM)
    return pl.pallas_call(
        kernel,
        out_shape=outs,
        in_specs=specs,
        out_specs=[vmem] * len(outs),
        compiler_params=pltpu.CompilerParams(vmem_limit_bytes=VMEM_LIMIT),
        cost_estimate=pl.CostEstimate(flops=flops, bytes_accessed=bytes_accessed, transcendentals=0),
    )


def shards(
    hidden,
    queries,
    key_value_weight,
    adapter_down_weight,
    adapter_up_weight,
    stored_cache_keys,
    stored_cache_values,
    row_adapter_index,
    stored_cache_lengths,
    adapter_slot_table,
):
    n = lax.axis_size("pool")
    rows, width = hidden.shape
    cap = -(-2 * rows // n)
    pieces = split_count(cap)
    me = lax.axis_index("pool")
    groups = stored_cache_keys.shape[1]
    head = stored_cache_keys.shape[3]
    columns = key_value_weight.shape[1] // 2
    out_pieces = 2 * groups
    rank2 = adapter_down_weight.shape[2]

    def exchange(chunks):
        return [chunks[0]] + [
            lax.ppermute(chunks[s], "pool", [(i, i ^ s) for i in range(n)]) for s in range(1, n)
        ]

    swap = functools.partial(lax.ppermute, axis_name="tp", perm=[(0, 1), (1, 0)])

    packed = call(
        functools.partial(pack_kernel, n, cap, pieces),
        [jax.ShapeDtypeStruct((1, rows), I32)] * 2
        + [jax.ShapeDtypeStruct((pieces * cap, width // pieces), BF16)] * n,
        2 * n * cap * width * 64,
        3 * rows * width * 2,
        True,
        4,
    )(me.reshape(1), row_adapter_index.reshape(1, rows), adapter_slot_table.reshape(1, n), hidden)
    rel, rank = packed[:2]
    arrived = exchange(packed[2:])

    half = lax.axis_index("tp")
    partial_sum = jnp.dot(hidden, key_value_weight, preferred_element_type=F32)
    base_mine = lax.dynamic_slice_in_dim(partial_sum, half * columns, columns, axis=1)
    base_other = swap(lax.dynamic_slice_in_dim(partial_sum, (1 - half) * columns, columns, axis=1))

    query_heads = queries.reshape(rows, groups, -1, head)
    scores = jnp.einsum("rgqd,rgpd->rgqp", query_heads, stored_cache_keys, preferred_element_type=F32)
    scores = scores * (head ** (-0.5))
    valid = jnp.arange(stored_cache_keys.shape[2])[None, :] < stored_cache_lengths[:, None]
    scores = jnp.where(valid[:, None, None, :], scores, -jnp.inf)
    cache_max = jnp.max(scores, axis=-1)
    weights = jnp.exp(scores - cache_max[..., None])
    cache_sum = jnp.sum(weights, axis=-1).reshape(rows, -1)
    attended = jnp.einsum(
        "rgqp,rgpd->rgqd", weights.astype(BF16), stored_cache_values, preferred_element_type=F32
    ).reshape(rows, -1)
    cache_max = cache_max.reshape(rows, -1)

    (reduced,) = call(
        functools.partial(shrink_kernel, n, cap, pieces),
        [jax.ShapeDtypeStruct((n * cap, rank2), F32)],
        2 * n * cap * width * rank2,
        n * cap * width * 2 + width * rank2 * 2,
        False,
        n + 1,
    )(*arrived, adapter_down_weight)
    reduced_other = swap(reduced)
    terms = call(
        functools.partial(expand_kernel, n, cap),
        [jax.ShapeDtypeStruct((out_pieces * cap, head), BF16)] * n,
        2 * n * cap * rank2 * columns,
        n * cap * columns * 4,
        False,
        3,
    )(reduced, reduced_other, adapter_up_weight)
    deltas = exchange(terms)
    token, out = call(
        functools.partial(combine_kernel, n, cap),
        [jax.ShapeDtypeStruct((rows, columns), BF16), jax.ShapeDtypeStruct(queries.shape, BF16)],
        2 * n * cap * columns * rows,
        rows * 2048 * 8,
        False,
        n + 8,
    )(*deltas, rel, rank, base_mine, base_other, queries, cache_max, cache_sum, attended)
    return token, out


def solution(mesh):
    in_specs = (
        P(("grp", "pool"), "tp"),
        P(("grp", "pool"), "tp"),
        P("tp", None),
        P("pool", "tp", None),
        P("pool", None, None, "tp"),
        P(("grp", "pool"), "tp", None, None),
        P(("grp", "pool"), "tp", None, None),
        P(("grp", "pool"), None),
        P(("grp", "pool")),
        P(),
    )
    out_specs = (P(("grp", "pool"), "tp"), P(("grp", "pool"), "tp"))
    return jax.shard_map(shards, mesh=mesh, in_specs=in_specs, out_specs=out_specs, check_vma=False)
```

time: 157 us -> 51.2 us (0.33)
  waiting for transfers between devices: 99.6 us -> 8.56 us
  starting transfers between devices: 0.13 us -> 24 us
  blocking collectives: 17.1 us -> 0 us
  between operations: 16.4 us -> 0.81 us
  other arithmetic: 5.4 us -> 0.42 us
  Pallas kernels: 0 us -> 4.81 us
  matrix products: 11.4 us -> 7.9 us
  local copies, waits for them, and re-layouts: 6.58 us -> 4.49 us
    reduce_scatter x2 -> x0, waiting for transfers between devices: 59.4 us -> none  [the longest x1 59.4 us: shards(): lax.psum_scatter(jnp.where(keep_rows[:, None, None], row_terms, 0.0).resh...]
    all_gather x1 -> x0, waiting for transfers between devices: 39.6 us -> none  [shards(): lax.all_gather(hidden, 'pool', axis=0, tiled=True)]
    ppermute x0 -> x16, starting transfers between devices: none -> 24 us  [the longest x14 23.8 us: exchange(): lax.ppermute(chunks[s], 'pool', [(i, i ^ s) for i in range(n)])]
    unnamed x1 -> x0, blocking collectives: 13.1 us -> none
    ppermute x0 -> x16, waiting for transfers between devices: none -> 8.56 us  [the longest x14 8.56 us: exchange(): lax.ppermute(chunks[s], 'pool', [(i, i ^ s) for i in range(n)])]
    pallas_call x0 -> x4, Pallas kernels: none -> 4.81 us  [the longest x1 2.52 us: shards(): call(functools.partial(combine_kernel, n, cap), [jax.ShapeDtypeStruct((ro...]
    dot_general x5 -> x2, matrix products: 10.7 us -> 6.03 us  [the longest x1 5.64 us: shards(): partial_sum = jnp.dot(hidden, key_value_weight, preferred_element_type=F32)]
    gather x2 -> x0, other arithmetic: 4.25 us -> none  [shards(): is_mine = adapter_slot_table[all_ids[:, 0]] == my_index]
  transfers between devices with their start and end apart: 3 -> 16, of which waited for: 2 -> 3; matrix products, arithmetic and copies ran while one was open for 12% -> 20% of each run, Pallas kernels for 0% -> 3%
where the time goes in v1:
time: 51.2 us; the launch traced here: 51 us
  starting transfers between devices  24 us (47%)
  waiting for transfers between devices  8.56 us (17%)
  matrix products  7.9 us (15%)
  Pallas kernels  4.81 us (9%)
  local copies, waits for them, and re-layouts  4.49 us (9%)
  between operations  0.81 us (2%)
    ppermute x14, starting transfers between devices, exchange(): lax.ppermute(chunks[s], 'pool', [(i, i ^ s) for i in range(n)])  23.8 us
    ppermute x14, waiting for transfers between devices, exchange(): lax.ppermute(chunks[s], 'pool', [(i, i ^ s) for i in range(n)])  8.56 us
    dot_general x1, matrix products, shards(): partial_sum = jnp.dot(hidden, key_value_weight, preferred_element_type=F32)  5.64 us
    unnamed x18, local copies, waits for them, and re-layouts  3.23 us
    pallas_call x1, Pallas kernels, shards(): call(functools.partial(combine_kernel, n, cap), [jax.ShapeDtypeStruct((ro...  2.52 us
    dot_general x1, matrix products, shards(): jnp.einsum('rgqd,rgpd->rgqp', query_heads, stored_cache_keys, preferred_e...  1.87 us
    pallas_call x1, Pallas kernels, shards(): call(functools.partial(shrink_kernel, n, cap, pieces), [jax.ShapeDtypeStr...  1.18 us
  transfers between devices with their start and end apart: 16, of which 3 were waited for; matrix products, arithmetic and copies ran while one was open for 20% of the time, Pallas kernels for 3%

profile of v1, /device:TPU:0, one launch (start us, length us, event | category | flops | bytes accessed | tf_op | source)
XLA Modules:
  0.0 51.0 jit_solution(12333003004581450560)
XLA Ops:
  0.6 0.0 copy-start
  0.7 1.1 %copy-done.1 = bf16[48,4096]{1,0:T(8,128)(2,1)S(1)} copy-done((bf16[48,4096]{1,0:T(8,128)(2,1)S(1)}, bf16[48,4096]{1,0:T(8,128)(2,1)}, u32[]{:S(2)}) %copy-start.1) | copy-done | bytes 393240
  1.7 0.7 %copy-done.5 = s32[48,1]{0,1:T(1,128)S(1)} copy-done((s32[48,1]{0,1:T(1,128)S(1)}, s32[48,1]{0,1:T(1,128)}, u32[]{:S(2)}) %copy-start.5) | copy-done | bytes 216
  2.4 0.7 %copy-done.6 = s32[8]{0:T(128)S(1)} copy-done((s32[8]{0:T(128)S(1)}, s32[8]{0:T(128)}, u32[]{:S(2)}) %copy-start.6) | copy-done | bytes 56
  3.0 0.6 %shard_map.113 = (s32[1,48]{1,0:T(1,128)S(1)}, s32[1,48]{1,0:T(1,128)S(1)}, bf16[48,1024]{1,0:T(8,128)(2,1)S(1)}, bf16[48,1024]{1,0:T(8,128)(2,1)S(1)}, bf16[48,...) custom-call(s32[1]{0:T(128)} %bitcast.me_ref, ...), custom_call_target="tpu_custom_call" | custom-call | flops 50331648 | bytes 1179648 | tf_op jit(solution)/shard_map/pallas_call | solution.py:195
  3.7 3.0 %collective-permute-start = (bf16[48,1024]{1,0:T(8,128)(2,1)S(1)}, bf16[48,1024]{1,0:T(8,128)(2,1)S(1)}, u32[]{:S(2)}, u32[]{:S(2)}) collective-permute-start(bf16[48,1024]{1,0:T(8,128)(2,1)S(1)} %get-tuple-element.21), channel_id=1, source_target_pairs={{0,2},{2,0},{4,6},{6,4},{8,10},{10,8},{12,14},{14,12},{1,3},{3,1},... | collective-permute-start | bytes 294920 | tf_op jit(solution)/shard_map/ppermute | solution.py:190
  6.7 1.6 %collective-permute-start.1 = (bf16[48,1024]{1,0:T(8,128)(2,1)S(1)}, bf16[48,1024]{1,0:T(8,128)(2,1)S(1)}, u32[]{:S(2)}, u32[]{:S(2)}) collective-permute-start(bf16[48,1024]{1,0:T(8,128)(2,1)S(1)} %get-tuple-element.22), channel_id=1, source_target_pairs={{0,4},{2,6},{4,0},{6,2},{8,12},{10,14},{12,8},{14,10},{1,5},{3,7},... | collective-permute-start | bytes 294920 | tf_op jit(solution)/shard_map/ppermute | solution.py:190
  8.3 0.0 collective-permute-start.2
  8.3 3.0 %collective-permute-start.3 = (bf16[48,1024]{1,0:T(8,128)(2,1)S(1)}, bf16[48,1024]{1,0:T(8,128)(2,1)S(1)}, u32[]{:S(2)}, u32[]{:S(2)}) collective-permute-start(bf16[48,1024]{1,0:T(8,128)(2,1)S(1)} %get-tuple-element.24), channel_id=1, source_target_pairs={{0,8},{2,10},{4,12},{6,14},{8,0},{10,2},{12,4},{14,6},{1,9},{3,11}... | collective-permute-start | bytes 294920 | tf_op jit(solution)/shard_map/ppermute | solution.py:190
  11.3 1.4 %collective-permute-start.4 = (bf16[48,1024]{1,0:T(8,128)(2,1)S(1)}, bf16[48,1024]{1,0:T(8,128)(2,1)S(1)}, u32[]{:S(2)}, u32[]{:S(2)}) collective-permute-start(bf16[48,1024]{1,0:T(8,128)(2,1)S(1)} %get-tuple-element.25), channel_id=1, source_target_pairs={{0,10},{2,8},{4,14},{6,12},{8,2},{10,0},{12,6},{14,4},{1,11},{3,9}... | collective-permute-start | bytes 294920 | tf_op jit(solution)/shard_map/ppermute | solution.py:190
  12.6 5.6 %fusion.7 = f32[48,1024]{1,0:T(8,128)} fusion(bf16[48,4096]{1,0:T(8,128)(2,1)S(1)} %copy-done.1, bf16[4096,1024]{1,0:T(8,128)(2,1)} %param.12), kind=kOutput, calls=%fused_computation.12 | convolution fusion | flops 402653184 | bytes 8978432 | tf_op jit(solution)/shard_map/dot_general | solution.py:208
  18.3 0.1 iota_compare_fusion
  18.4 0.7 %copy.19 = bf16[6,8,16,128]{3,2,1,0:T(8,128)(2,1)} copy(bf16[6,8,16,128]{3,1,2,0:T(8,128)(2,1)S(1)} %bitcast.19) | data formatting | bytes 393216
  19.1 0.0 collective-permute-done.refs_1_
  19.1 3.6 %collective-permute-start.5 = (bf16[48,1024]{1,0:T(8,128)(2,1)S(1)}, bf16[48,1024]{1,0:T(8,128)(2,1)S(1)}, u32[]{:S(2)}, u32[]{:S(2)}) collective-permute-start(bf16[48,1024]{1,0:T(8,128)(2,1)S(1)} %get-tuple-element.26), channel_id=1, source_target_pairs={{0,12},{2,14},{4,8},{6,10},{8,4},{10,6},{12,0},{14,2},{1,13},{3,15... | collective-permute-start | bytes 294920 | tf_op jit(solution)/shard_map/ppermute | solution.py:190
  22.7 0.0 collective-permute-done.1.refs_2_
  22.7 0.0 collective-permute-start.6
  22.7 1.0 %constant_dynamic-slice_fusion = (f32[48,512]{1,0:T(8,128)S(1)}, f32[48,512]{1,0:T(8,128)S(1)}) fusion(f32[48,1024]{1,0:T(8,128)} %fusion.7, s32[]{:T(128)S(6)} %select_n.11, s32[]{:T(128)S(6)} %select_n.10), kind=kLoop, calls=%fused_computation.9 | loop fusion | bytes 393224 | tf_op jit(solution)/shard_map/dynamic_slice | solution.py:210
  23.7 0.0 collective-permute-done.2.refs_3_
  23.7 0.1 collective-permute-start.15
  23.8 0.0 collective-permute-done.3.refs_4_
  23.8 0.0 collective-permute-done.4.refs_5_
  23.8 2.2 %collective-permute-done.5.refs_6_ = bf16[48,1024]{1,0:T(8,128)(2,1)S(1)} collective-permute-done((bf16[48,1024]{1,0:T(8,128)(2,1)S(1)}, bf16[48,1024]{1,0:T(8,128)(2,1)S(1)}, u32[]{:S(2)}, u32[]{:S(2)}) %collective-permute-start.5) | collective-permute-done | bytes 98336 | tf_op jit(solution)/shard_map/ppermute | solution.py:190
  26.0 4.1 %collective-permute-done.6.refs_7_ = bf16[48,1024]{1,0:T(8,128)(2,1)S(1)} collective-permute-done((bf16[48,1024]{1,0:T(8,128)(2,1)S(1)}, bf16[48,1024]{1,0:T(8,128)(2,1)S(1)}, u32[]{:S(2)}, u32[]{:S(2)}) %collective-permute-start.6) | collective-permute-done | bytes 98336 | tf_op jit(solution)/shard_map/ppermute | solution.py:190
  30.0 1.2 %shard_map.114.mine_ref = f32[96,128]{1,0:T(8,128)S(1)} custom-call(bf16[48,1024]{1,0:T(8,128)(2,1)S(1)} %get-tuple-element.20.refs_0_, bf16[48,1024]{1,0:T(8,128)(2,1)S(1)} %collective-permute-done.refs_1_, bf16[48,1024]{1,0:T(8,128)(2,1)S(1)} %collective-permute-done.1.refs_2_, bf16[48,1024]{1,0:T(8,128)(2,1)S(1)} %collective-permute-done.2.refs_3_, ...), custom_call_target="tpu_custom_call" | custom-call | flops 100663296 | bytes 1835008 | tf_op jit(solution)/shard_map/pallas_call | solution.py:225
  31.2 0.1 collective-permute-start.7
  31.3 1.9 %fusion.6 = (f32[48,2,8]{2,1,0:T(2,128)S(1)}, f32[48,2,8,32]{3,2,1,0:T(8,128)S(1)}) fusion(bf16[48,2,8,128]{3,2,1,0:T(8,128)(2,1)} %bitcast.22, bf16[48,2,32,128]{3,2,1,0:T(8,128)(2,1)} %param.15, pred[48,32]{1,0:T(8,128)(4,1)S(1)} %iota_compare_fusion), kind=kOutput, calls=%fused_computation.11 | convolution fusion | flops 6364416 | bytes 1085952 | tf_op jit(solution)/shard_map/rgqd,rgpd->rgqp/dot_general | solution.py:213
  33.2 0.0 collective-permute-done.7.other_ref
  33.2 0.5 shard_map.115
  33.7 0.7 %collective-permute-start.8 = (bf16[48,128]{1,0:T(8,128)(2,1)S(1)}, bf16[48,128]{1,0:T(8,128)(2,1)S(1)}, u32[]{:S(2)}, u32[]{:S(2)}) collective-permute-start(bf16[48,128]{1,0:T(8,128)(2,1)S(1)} %get-tuple-element.29), channel_id=1, source_target_pairs={{0,2},{2,0},{4,6},{6,4},{8,10},{10,8},{12,14},{14,12},{1,3},{3,1},... | collective-permute-start | bytes 36872 | tf_op jit(solution)/shard_map/ppermute | solution.py:190
  34.3 1.0 %collective-permute-start.9 = (bf16[48,128]{1,0:T(8,128)(2,1)S(1)}, bf16[48,128]{1,0:T(8,128)(2,1)S(1)}, u32[]{:S(2)}, u32[]{:S(2)}) collective-permute-start(bf16[48,128]{1,0:T(8,128)(2,1)S(1)} %get-tuple-element.30), channel_id=1, source_target_pairs={{0,4},{2,6},{4,0},{6,2},{8,12},{10,14},{12,8},{14,10},{1,5},{3,7},... | collective-permute-start | bytes 36872 | tf_op jit(solution)/shard_map/ppermute | solution.py:190
  35.3 0.4 fusion.3
  35.7 2.0 %collective-permute-start.10 = (bf16[48,128]{1,0:T(8,128)(2,1)S(1)}, bf16[48,128]{1,0:T(8,128)(2,1)S(1)}, u32[]{:S(2)}, u32[]{:S(2)}) collective-permute-start(bf16[48,128]{1,0:T(8,128)(2,1)S(1)} %get-tuple-element.31), channel_id=1, source_target_pairs={{0,6},{2,4},{4,2},{6,0},{8,14},{10,12},{12,10},{14,8},{1,7},{3,5},... | collective-permute-start | bytes 36872 | tf_op jit(solution)/shard_map/ppermute | solution.py:190
  37.7 1.7 %collective-permute-start.11 = (bf16[48,128]{1,0:T(8,128)(2,1)S(1)}, bf16[48,128]{1,0:T(8,128)(2,1)S(1)}, u32[]{:S(2)}, u32[]{:S(2)}) collective-permute-start(bf16[48,128]{1,0:T(8,128)(2,1)S(1)} %get-tuple-element.32), channel_id=1, source_target_pairs={{0,8},{2,10},{4,12},{6,14},{8,0},{10,2},{12,4},{14,6},{1,9},{3,11}... | collective-permute-start | bytes 36872 | tf_op jit(solution)/shard_map/ppermute | solution.py:190
  39.3 1.3 %collective-permute-start.12 = (bf16[48,128]{1,0:T(8,128)(2,1)S(1)}, bf16[48,128]{1,0:T(8,128)(2,1)S(1)}, u32[]{:S(2)}, u32[]{:S(2)}) collective-permute-start(bf16[48,128]{1,0:T(8,128)(2,1)S(1)} %get-tuple-element.33), channel_id=1, source_target_pairs={{0,10},{2,8},{4,14},{6,12},{8,2},{10,0},{12,6},{14,4},{1,11},{3,9}... | collective-permute-start | bytes 36872 | tf_op jit(solution)/shard_map/ppermute | solution.py:190
  40.6 0.0 collective-permute-done.8.refs_1_
  40.6 1.4 %collective-permute-start.13 = (bf16[48,128]{1,0:T(8,128)(2,1)S(1)}, bf16[48,128]{1,0:T(8,128)(2,1)S(1)}, u32[]{:S(2)}, u32[]{:S(2)}) collective-permute-start(bf16[48,128]{1,0:T(8,128)(2,1)S(1)} %get-tuple-element.34), channel_id=1, source_target_pairs={{0,12},{2,14},{4,8},{6,10},{8,4},{10,6},{12,0},{14,2},{1,13},{3,15... | collective-permute-start | bytes 36872 | tf_op jit(solution)/shard_map/ppermute | solution.py:190
  42.1 3.3 %collective-permute-start.14 = (bf16[48,128]{1,0:T(8,128)(2,1)S(1)}, bf16[48,128]{1,0:T(8,128)(2,1)S(1)}, u32[]{:S(2)}, u32[]{:S(2)}) collective-permute-start(bf16[48,128]{1,0:T(8,128)(2,1)S(1)} %get-tuple-element.35), channel_id=1, source_target_pairs={{0,14},{2,12},{4,10},{6,8},{8,6},{10,4},{12,2},{14,0},{1,15},{3,13... | collective-permute-start | bytes 36872 | tf_op jit(solution)/shard_map/ppermute | solution.py:190
  45.3 0.3 fusion.2
  45.7 0.1 copy.15
  45.7 0.1 copy.17.refs_13_
  45.8 0.1 copy.16
  45.9 0.1 copy.18.refs_14_
  46.0 0.1 copy.22
  46.1 0.0 collective-permute-done.12.refs_5_
  46.2 0.0 collective-permute-done.13.refs_6_
  46.2 2.3 %collective-permute-done.14.refs_7_ = bf16[48,128]{1,0:T(8,128)(2,1)S(1)} collective-permute-done((bf16[48,128]{1,0:T(8,128)(2,1)S(1)}, bf16[48,128]{1,0:T(8,128)(2,1)S(1)}, u32[]{:S(2)}, u32[]{:S(2)}) %collective-permute-start.14) | collective-permute-done | bytes 12320 | tf_op jit(solution)/shard_map/ppermute | solution.py:190
  48.5 2.5 %shard_map.116 = (bf16[48,512]{1,0:T(8,128)(2,1)}, bf16[48,2048]{1,0:T(8,128)(2,1)}) custom-call(bf16[48,128]{1,0:T(8,128)(2,1)S(1)} %get-tuple-element.28.refs_0_, bf16[48,128]{1,0:T(8,128)(2,1)S(1)} %collective-permute-done.8.refs_1_, bf16[48,128]{1,0:T(8,128)(2,1)S(1)} %collective-permute-done.9.refs_2_, ...), custom_call_target="tpu_custom_call" | custom-call | flops 4718592 | bytes 786432 | tf_op jit(solution)/shard_map/pallas_call | solution.py:243
  (16 shorter events, 0.0 us)
Async XLA Ops:
  0.6 34.7 %copy-start = (bf16[48,2,32,128]{3,2,1,0:T(8,128)(2,1)S(1)}, bf16[48,2,32,128]{3,2,1,0:T(8,128)(2,1)}, u32[]{:S(2)}) copy-start(bf16[48,2,32,128]{3,2,1,0:T(8,128)(2,1)} %param.16) | copy-start | bytes 2359300
  0.7 1.1 %copy-start.1 = (bf16[48,4096]{1,0:T(8,128)(2,1)S(1)}, bf16[48,4096]{1,0:T(8,128)(2,1)}, u32[]{:S(2)}) copy-start(bf16[48,4096]{1,0:T(8,128)(2,1)} %hidden_ref.1) | copy-start | bytes 1179652
  1.7 0.7 %copy-start.5 = (s32[48,1]{0,1:T(1,128)S(1)}, s32[48,1]{0,1:T(1,128)}, u32[]{:S(2)}) copy-start(s32[48,1]{0,1:T(1,128)} %param.17) | copy-start | bytes 580
  2.4 0.7 %copy-start.6 = (s32[8]{0:T(128)S(1)}, s32[8]{0:T(128)}, u32[]{:S(2)}) copy-start(s32[8]{0:T(128)} %param.19) | copy-start | bytes 100
  3.7 15.4 %collective-permute-start = (bf16[48,1024]{1,0:T(8,128)(2,1)S(1)}, bf16[48,1024]{1,0:T(8,128)(2,1)S(1)}, u32[]{:S(2)}, u32[]{:S(2)}) collective-permute-start(bf16[48,1024]{1,0:T(8,128)(2,1)S(1)} %get-tuple-element.21), channel_id=1, source_target_pairs={{0,2},{2,0},{4,6},{6,4},{8,10},{10,8},{12,14},{14,12},{1,3},{3,1},... | collective-permute-start | bytes 294920 | tf_op jit(solution)/shard_map/ppermute | solution.py:190
  6.7 16.0 %collective-permute-start.1 = (bf16[48,1024]{1,0:T(8,128)(2,1)S(1)}, bf16[48,1024]{1,0:T(8,128)(2,1)S(1)}, u32[]{:S(2)}, u32[]{:S(2)}) collective-permute-start(bf16[48,1024]{1,0:T(8,128)(2,1)S(1)} %get-tuple-element.22), channel_id=1, source_target_pairs={{0,4},{2,6},{4,0},{6,2},{8,12},{10,14},{12,8},{14,10},{1,5},{3,7},... | collective-permute-start | bytes 294920 | tf_op jit(solution)/shard_map/ppermute | solution.py:190
  8.3 15.4 %collective-permute-start.2 = (bf16[48,1024]{1,0:T(8,128)(2,1)S(1)}, bf16[48,1024]{1,0:T(8,128)(2,1)S(1)}, u32[]{:S(2)}, u32[]{:S(2)}) collective-permute-start(bf16[48,1024]{1,0:T(8,128)(2,1)S(1)} %get-tuple-element.23), channel_id=1, source_target_pairs={{0,6},{2,4},{4,2},{6,0},{8,14},{10,12},{12,10},{14,8},{1,7},{3,5},... | collective-permute-start | bytes 294920 | tf_op jit(solution)/shard_map/ppermute | solution.py:190
  8.3 15.5 %collective-permute-start.3 = (bf16[48,1024]{1,0:T(8,128)(2,1)S(1)}, bf16[48,1024]{1,0:T(8,128)(2,1)S(1)}, u32[]{:S(2)}, u32[]{:S(2)}) collective-permute-start(bf16[48,1024]{1,0:T(8,128)(2,1)S(1)} %get-tuple-element.24), channel_id=1, source_target_pairs={{0,8},{2,10},{4,12},{6,14},{8,0},{10,2},{12,4},{14,6},{1,9},{3,11}... | collective-permute-start | bytes 294920 | tf_op jit(solution)/shard_map/ppermute | solution.py:190
  11.3 7.0 %copy-start.7 = (s32[48]{0:T(128)S(1)}, s32[48]{0:T(128)}, u32[]{:S(2)}) copy-start(s32[48]{0:T(128)} %param.18) | copy-start | bytes 580
  11.3 7.1 %copy-start.3 = (bf16[48,2048]{1,0:T(8,128)(2,1)S(1)}, bf16[48,2048]{1,0:T(8,128)(2,1)}, u32[]{:S(2)}) copy-start(bf16[48,2048]{1,0:T(8,128)(2,1)} %refs_12_.1) | copy-start | bytes 589828
  11.3 18.7 %copy-start.2 = (bf16[1,4096,128]{2,1,0:T(8,128)(2,1)S(1)}, bf16[1,4096,128]{2,1,0:T(8,128)(2,1)}, u32[]{:S(2)}) copy-start(bf16[1,4096,128]{2,1,0:T(8,128)(2,1)} %refs_8_.1) | copy-start | bytes 3145732
  11.3 21.9 %copy-start.4 = (bf16[1,2,64,256]{3,2,1,0:T(8,128)(2,1)S(1)}, bf16[1,2,64,256]{3,2,1,0:T(8,128)(2,1)}, u32[]{:S(2)}) copy-start(bf16[1,2,64,256]{3,2,1,0:T(8,128)(2,1)} %up_ref.1) | copy-start | bytes 196612
  11.3 12.5 %collective-permute-start.4 = (bf16[48,1024]{1,0:T(8,128)(2,1)S(1)}, bf16[48,1024]{1,0:T(8,128)(2,1)S(1)}, u32[]{:S(2)}, u32[]{:S(2)}) collective-permute-start(bf16[48,1024]{1,0:T(8,128)(2,1)S(1)} %get-tuple-element.25), channel_id=1, source_target_pairs={{0,10},{2,8},{4,14},{6,12},{8,2},{10,0},{12,6},{14,4},{1,11},{3,9}... | collective-permute-start | bytes 294920 | tf_op jit(solution)/shard_map/ppermute | solution.py:190
  19.1 6.9 %collective-permute-start.5 = (bf16[48,1024]{1,0:T(8,128)(2,1)S(1)}, bf16[48,1024]{1,0:T(8,128)(2,1)S(1)}, u32[]{:S(2)}, u32[]{:S(2)}) collective-permute-start(bf16[48,1024]{1,0:T(8,128)(2,1)S(1)} %get-tuple-element.26), channel_id=1, source_target_pairs={{0,12},{2,14},{4,8},{6,10},{8,4},{10,6},{12,0},{14,2},{1,13},{3,15... | collective-permute-start | bytes 294920 | tf_op jit(solution)/shard_map/ppermute | solution.py:190
  22.7 7.3 %collective-permute-start.6 = (bf16[48,1024]{1,0:T(8,128)(2,1)S(1)}, bf16[48,1024]{1,0:T(8,128)(2,1)S(1)}, u32[]{:S(2)}, u32[]{:S(2)}) collective-permute-start(bf16[48,1024]{1,0:T(8,128)(2,1)S(1)} %get-tuple-element.27), channel_id=1, source_target_pairs={{0,14},{2,12},{4,10},{6,8},{8,6},{10,4},{12,2},{14,0},{1,15},{3,13... | collective-permute-start | bytes 294920 | tf_op jit(solution)/shard_map/ppermute | solution.py:190
  23.7 15.7 %collective-permute-start.15 = (f32[48,512]{1,0:T(8,128)S(1)}, f32[48,512]{1,0:T(8,128)S(1)}, u32[]{:S(2)}, u32[]{:S(2)}) collective-permute-start(f32[48,512]{1,0:T(8,128)S(1)} %get-tuple-element.38), channel_id=1, source_target_pairs={{0,1},{1,0},{2,3},{3,2},{4,5},{5,4},{6,7},{7,6},{8,9},{9,8},{10,11... | collective-permute-start | bytes 294920 | tf_op jit(solution)/shard_map/ppermute | solution.py:210
  31.2 2.0 %collective-permute-start.7 = (f32[96,128]{1,0:T(8,128)S(1)}, f32[96,128]{1,0:T(8,128)S(1)}, u32[]{:S(2)}, u32[]{:S(2)}) collective-permute-start(f32[96,128]{1,0:T(8,128)S(1)} %shard_map.114.mine_ref), channel_id=1, source_target_pairs={{0,1},{1,0},{2,3},{3,2},{4,5},{5,4},{6,7},{7,6},{8,9},{9,8},{10,11... | collective-permute-start | bytes 147464 | tf_op jit(solution)/shard_map/ppermute | solution.py:233
  33.7 7.0 %collective-permute-start.8 = (bf16[48,128]{1,0:T(8,128)(2,1)S(1)}, bf16[48,128]{1,0:T(8,128)(2,1)S(1)}, u32[]{:S(2)}, u32[]{:S(2)}) collective-permute-start(bf16[48,128]{1,0:T(8,128)(2,1)S(1)} %get-tuple-element.29), channel_id=1, source_target_pairs={{0,2},{2,0},{4,6},{6,4},{8,10},{10,8},{12,14},{14,12},{1,3},{3,1},... | collective-permute-start | bytes 36872 | tf_op jit(solution)/shard_map/ppermute | solution.py:190
  34.3 7.7 %collective-permute-start.9 = (bf16[48,128]{1,0:T(8,128)(2,1)S(1)}, bf16[48,128]{1,0:T(8,128)(2,1)S(1)}, u32[]{:S(2)}, u32[]{:S(2)}) collective-permute-start(bf16[48,128]{1,0:T(8,128)(2,1)S(1)} %get-tuple-element.30), channel_id=1, source_target_pairs={{0,4},{2,6},{4,0},{6,2},{8,12},{10,14},{12,8},{14,10},{1,5},{3,7},... | collective-permute-start | bytes 36872 | tf_op jit(solution)/shard_map/ppermute | solution.py:190
  35.7 10.4 %collective-permute-start.10 = (bf16[48,128]{1,0:T(8,128)(2,1)S(1)}, bf16[48,128]{1,0:T(8,128)(2,1)S(1)}, u32[]{:S(2)}, u32[]{:S(2)}) collective-permute-start(bf16[48,128]{1,0:T(8,128)(2,1)S(1)} %get-tuple-element.31), channel_id=1, source_target_pairs={{0,6},{2,4},{4,2},{6,0},{8,14},{10,12},{12,10},{14,8},{1,7},{3,5},... | collective-permute-start | bytes 36872 | tf_op jit(solution)/shard_map/ppermute | solution.py:190
  37.7 8.5 %collective-permute-start.11 = (bf16[48,128]{1,0:T(8,128)(2,1)S(1)}, bf16[48,128]{1,0:T(8,128)(2,1)S(1)}, u32[]{:S(2)}, u32[]{:S(2)}) collective-permute-start(bf16[48,128]{1,0:T(8,128)(2,1)S(1)} %get-tuple-element.32), channel_id=1, source_target_pairs={{0,8},{2,10},{4,12},{6,14},{8,0},{10,2},{12,4},{14,6},{1,9},{3,11}... | collective-permute-start | bytes 36872 | tf_op jit(solution)/shard_map/ppermute | solution.py:190
  39.3 6.8 %collective-permute-start.12 = (bf16[48,128]{1,0:T(8,128)(2,1)S(1)}, bf16[48,128]{1,0:T(8,128)(2,1)S(1)}, u32[]{:S(2)}, u32[]{:S(2)}) collective-permute-start(bf16[48,128]{1,0:T(8,128)(2,1)S(1)} %get-tuple-element.33), channel_id=1, source_target_pairs={{0,10},{2,8},{4,14},{6,12},{8,2},{10,0},{12,6},{14,4},{1,11},{3,9}... | collective-permute-start | bytes 36872 | tf_op jit(solution)/shard_map/ppermute | solution.py:190
  40.6 5.5 %collective-permute-start.13 = (bf16[48,128]{1,0:T(8,128)(2,1)S(1)}, bf16[48,128]{1,0:T(8,128)(2,1)S(1)}, u32[]{:S(2)}, u32[]{:S(2)}) collective-permute-start(bf16[48,128]{1,0:T(8,128)(2,1)S(1)} %get-tuple-element.34), channel_id=1, source_target_pairs={{0,12},{2,14},{4,8},{6,10},{8,4},{10,6},{12,0},{14,2},{1,13},{3,15... | collective-permute-start | bytes 36872 | tf_op jit(solution)/shard_map/ppermute | solution.py:190
  42.1 6.4 %collective-permute-start.14 = (bf16[48,128]{1,0:T(8,128)(2,1)S(1)}, bf16[48,128]{1,0:T(8,128)(2,1)S(1)}, u32[]{:S(2)}, u32[]{:S(2)}) collective-permute-start(bf16[48,128]{1,0:T(8,128)(2,1)S(1)} %get-tuple-element.35), channel_id=1, source_target_pairs={{0,14},{2,12},{4,10},{6,8},{8,6},{10,4},{12,2},{14,0},{1,15},{3,13... | collective-permute-start | bytes 36872 | tf_op jit(solution)/shard_map/ppermute | solution.py:190

commit v2 on v1

--- a/solution.py
+++ b/solution.py
@@ -40,45 +40,38 @@
     return dot(one_hot, high) + (dot(one_hot, middle) + dot(one_hot, low))
 
 
-def placement(rel, rank, cap, pieces):
-    rows = rel.shape[1]
-    code = rel * (pieces * cap) + rank
+def placement(slot, rank, cap, pieces):
+    code = slot * (pieces * cap) + rank
     codes = jnp.concatenate([code + piece * cap for piece in range(pieces)], axis=1)
     return codes
 
 
-def pack_kernel(n, cap, pieces, me_ref, idx_ref, table_ref, hidden_ref, *out_refs):
-    code_refs, chunk_refs = out_refs[:2], out_refs[2:]
+def pack_kernel(n, cap, pieces, idx_ref, table_ref, hidden_ref, slot_ref, rank_ref, packed_ref):
     rows = hidden_ref.shape[0]
     width = hidden_ref.shape[1] // pieces
-    me = me_ref[0]
     named = (iota((n, rows), 0) == idx_ref[...]).astype(F32).astype(BF16)
     table = jnp.broadcast_to(table_ref[...].astype(F32).astype(BF16), (16, n))
     slot = dot(table, named)[0:1, :].astype(I32)
-    rel = lax.bitwise_xor(slot, me)
-    member = (iota((n, rows), 0) == rel).astype(F32)
+    member = (iota((n, rows), 0) == slot).astype(F32)
     before = (iota((rows, rows), 0) < iota((rows, rows), 1)).astype(F32).astype(BF16)
     count = dot(member.astype(BF16), before)
     rank = jnp.sum(member * count, axis=0, keepdims=True).astype(I32)
-    code_refs[0][...] = rel
-    code_refs[1][...] = rank
-    codes = placement(rel, rank, cap, pieces)
+    slot_ref[...] = slot
+    rank_ref[...] = rank
+    codes = placement(slot, rank, cap, pieces)
     total = n * pieces * cap
     one_hot = (iota((total, pieces * rows), 0) == codes).astype(F32).astype(BF16)
     stacked = jnp.concatenate(
         [hidden_ref[:, piece * width : (piece + 1) * width] for piece in range(pieces)], axis=0
     )
-    packed = dot(one_hot, stacked).astype(BF16)
-    for s in range(n):
-        chunk_refs[s][...] = packed[s * pieces * cap : (s + 1) * pieces * cap]
-
-
-def shrink_kernel(n, cap, pieces, *refs):
-    chunk_refs, down_ref, out_ref = refs[:n], refs[n], refs[n + 1]
+    packed_ref[...] = dot(one_hot, stacked).astype(BF16)
+
+
+def shrink_kernel(n, cap, pieces, received_ref, down_ref, out_ref):
     per = pieces * cap
-    width = chunk_refs[0].shape[1]
+    width = received_ref.shape[1]
     rank2 = down_ref.shape[2]
-    received = jnp.concatenate([ref[...] for ref in chunk_refs], axis=0)
+    received = received_ref[...]
     total = jnp.zeros((n * per, rank2), F32)
     piece_of = (iota((n * per, rank2), 0) // cap) % pieces
     for piece in range(pieces):
@@ -89,7 +82,7 @@
     out_ref[...] = exact_select(same.astype(F32).astype(BF16), total)
 
 
-def expand_kernel(n, cap, mine_ref, other_ref, up_ref, *out_refs):
+def expand_kernel(n, cap, mine_ref, other_ref, up_ref, out_ref):
     rank = up_ref.shape[2]
     head = 128
     blocks = up_ref.shape[3] // head
@@ -105,23 +98,32 @@
     size = n * per
     out_row, in_row = iota((size, size), 0), iota((size, size), 1)
     source = (out_row // cap % pieces) * (n * cap) + (out_row // per) * cap + out_row % cap
-    moved = dot((source == in_row).astype(F32).astype(BF16), stacked).astype(BF16)
-    for s in range(n):
-        out_refs[s][...] = moved[s * per : (s + 1) * per]
-
-
-def combine_kernel(n, cap, *refs):
-    delta_refs = refs[:n]
-    rel_ref, rank_ref, base_ref, other_ref, query_ref, max_ref, sum_ref, acc_ref, token_ref, out_ref = refs[n:]
+    out_ref[...] = dot((source == in_row).astype(F32).astype(BF16), stacked).astype(BF16)
+
+
+def combine_kernel(
+    n,
+    cap,
+    delta_ref,
+    slot_ref,
+    rank_ref,
+    base_ref,
+    other_ref,
+    query_ref,
+    max_ref,
+    sum_ref,
+    acc_ref,
+    token_ref,
+    out_ref,
+):
     rows = base_ref.shape[0]
     head = 128
     groups = base_ref.shape[1] // (2 * head)
     pieces = 2 * groups
     total = n * pieces * cap
-    codes = placement(rel_ref[...], rank_ref[...], cap, pieces)
+    codes = placement(slot_ref[...], rank_ref[...], cap, pieces)
     one_hot = (iota((total, pieces * rows), 0) == codes).astype(F32).astype(BF16)
-    received = jnp.concatenate([ref[...] for ref in delta_refs], axis=0)
-    delta = dot_first(one_hot, received)
+    delta = dot_first(one_hot, delta_ref[...])
     heads = query_ref.shape[1] // head
     per_group = heads // groups
     scale = head ** (-0.5)
@@ -147,15 +149,12 @@
             out_ref[:, lanes] = out.astype(BF16)
 
 
-def call(kernel, outs, flops, bytes_accessed, smem_first=False, inputs=0):
+def call(kernel, outs, flops, bytes_accessed, inputs):
     vmem = pl.BlockSpec(memory_space=pltpu.VMEM)
-    specs = [vmem] * inputs
-    if smem_first:
-        specs[0] = pl.BlockSpec(memory_space=pltpu.SMEM)
     return pl.pallas_call(
         kernel,
         out_shape=outs,
-        in_specs=specs,
+        in_specs=[vmem] * inputs,
         out_specs=[vmem] * len(outs),
         compiler_params=pltpu.CompilerParams(vmem_limit_bytes=VMEM_LIMIT),
         cost_estimate=pl.CostEstimate(flops=flops, bytes_accessed=bytes_accessed, transcendentals=0),
@@ -178,7 +177,6 @@
     rows, width = hidden.shape
     cap = -(-2 * rows // n)
     pieces = split_count(cap)
-    me = lax.axis_index("pool")
     groups = stored_cache_keys.shape[1]
     head = stored_cache_keys.shape[3]
     columns = key_value_weight.shape[1] // 2
@@ -186,23 +184,19 @@
     rank2 = adapter_down_weight.shape[2]
 
     def exchange(chunks):
-        return [chunks[0]] + [
-            lax.ppermute(chunks[s], "pool", [(i, i ^ s) for i in range(n)]) for s in range(1, n)
-        ]
+        return lax.all_to_all(chunks, "pool", split_axis=0, concat_axis=0, tiled=True)
 
     swap = functools.partial(lax.ppermute, axis_name="tp", perm=[(0, 1), (1, 0)])
 
-    packed = call(
+    slot, rank, packed = call(
         functools.partial(pack_kernel, n, cap, pieces),
         [jax.ShapeDtypeStruct((1, rows), I32)] * 2
-        + [jax.ShapeDtypeStruct((pieces * cap, width // pieces), BF16)] * n,
+        + [jax.ShapeDtypeStruct((n * pieces * cap, width // pieces), BF16)],
         2 * n * cap * width * 64,
         3 * rows * width * 2,
-        True,
-        4,
-    )(me.reshape(1), row_adapter_index.reshape(1, rows), adapter_slot_table.reshape(1, n), hidden)
-    rel, rank = packed[:2]
-    arrived = exchange(packed[2:])
+        3,
+    )(row_adapter_index.reshape(1, rows), adapter_slot_table.reshape(1, n), hidden)
+    arrived = exchange(packed)
 
     half = lax.axis_index("tp")
     partial_sum = jnp.dot(hidden, key_value_weight, preferred_element_type=F32)
@@ -227,16 +221,14 @@
         [jax.ShapeDtypeStruct((n * cap, rank2), F32)],
         2 * n * cap * width * rank2,
         n * cap * width * 2 + width * rank2 * 2,
-        False,
-        n + 1,
-    )(*arrived, adapter_down_weight)
+        2,
+    )(arrived, adapter_down_weight)
     reduced_other = swap(reduced)
-    terms = call(
+    (terms,) = call(
         functools.partial(expand_kernel, n, cap),
-        [jax.ShapeDtypeStruct((out_pieces * cap, head), BF16)] * n,
+        [jax.ShapeDtypeStruct((n * out_pieces * cap, head), BF16)],
         2 * n * cap * rank2 * columns,
         n * cap * columns * 4,
-        False,
         3,
     )(reduced, reduced_other, adapter_up_weight)
     deltas = exchange(terms)
@@ -245,9 +237,8 @@
         [jax.ShapeDtypeStruct((rows, columns), BF16), jax.ShapeDtypeStruct(queries.shape, BF16)],
         2 * n * cap * columns * rows,
         rows * 2048 * 8,
-        False,
-        n + 8,
-    )(*deltas, rel, rank, base_mine, base_other, queries, cache_max, cache_sum, attended)
+        9,
+    )(deltas, slot, rank, base_mine, base_other, queries, cache_max, cache_sum, attended)
     return token, out
 
 

time: 51.2 us -> 49.1 us (0.959)
  starting transfers between devices: 24 us -> 10.9 us
  waiting for transfers between devices: 8.56 us -> 20.6 us
  matrix products: 7.9 us -> 6.24 us
  Pallas kernels: 4.81 us -> 6.35 us
  local copies, waits for them, and re-layouts: 4.49 us -> 3.54 us
    ppermute x14 -> x0, starting transfers between devices: 23.8 us -> none  [exchange(): lax.ppermute(chunks[s], 'pool', [(i, i ^ s) for i in range(n)])]
    all_to_all x0 -> x2, waiting for transfers between devices: none -> 19.8 us  [exchange(): lax.all_to_all(chunks, 'pool', split_axis=0, concat_axis=0, tiled=True)]
    all_to_all x0 -> x2, starting transfers between devices: none -> 10.8 us  [exchange(): lax.all_to_all(chunks, 'pool', split_axis=0, concat_axis=0, tiled=True)]
    ppermute x14 -> x0, waiting for transfers between devices: 8.56 us -> none  [exchange(): lax.ppermute(chunks[s], 'pool', [(i, i ^ s) for i in range(n)])]
    dot_general x1, matrix products: 1.87 us -> 0.65 us  [shards(): jnp.einsum('rgqd,rgpd->rgqp', query_heads, stored_cache_keys, preferred_e...]
    pallas_call x1, Pallas kernels: 0.65 us -> 1.55 us  [shards(): call(functools.partial(pack_kernel, n, cap, pieces), [jax.ShapeDtypeStruc...]
    ppermute x1, waiting for transfers between devices: 0.01 us -> 0.82 us  [shards(): reduced_other = swap(reduced)]
    unnamed x18 -> x20, local copies, waits for them, and re-layouts: 3.23 us -> 2.57 us
  transfers between devices with their start and end apart: 16 -> 4, of which waited for: 3 -> 3; matrix products, arithmetic and copies ran while one was open for 20% -> 16% of each run, Pallas kernels for 3% -> 5%
where the time goes in v2:
time: 49.1 us; the launch traced here: 48.8 us
  waiting for transfers between devices  20.6 us (42%)
  starting transfers between devices  10.9 us (22%)
  Pallas kernels  6.35 us (13%)
  matrix products  6.24 us (13%)
  local copies, waits for them, and re-layouts  3.54 us (7%)
  between operations  0.77 us (2%)
    all_to_all x2, waiting for transfers between devices, exchange(): lax.all_to_all(chunks, 'pool', split_axis=0, concat_axis=0, tiled=True)  19.8 us
    all_to_all x2, starting transfers between devices, exchange(): lax.all_to_all(chunks, 'pool', split_axis=0, concat_axis=0, tiled=True)  10.8 us
    dot_general x1, matrix products, shards(): partial_sum = jnp.dot(hidden, key_value_weight, preferred_element_type=F32)  5.21 us
    unnamed x20, local copies, waits for them, and re-layouts  2.57 us
    pallas_call x1, Pallas kernels, shards(): call(functools.partial(combine_kernel, n, cap), [jax.ShapeDtypeStruct((ro...  2.52 us
    pallas_call x1, Pallas kernels, shards(): call(functools.partial(pack_kernel, n, cap, pieces), [jax.ShapeDtypeStruc...  1.55 us
    pallas_call x1, Pallas kernels, shards(): call(functools.partial(shrink_kernel, n, cap, pieces), [jax.ShapeDtypeStr...  1.18 us
    pallas_call x1, Pallas kernels, shards(): call(functools.partial(expand_kernel, n, cap), [jax.ShapeDtypeStruct((n *...  1.11 us
  transfers between devices with their start and end apart: 4, of which 3 were waited for; matrix products, arithmetic and copies ran while one was open for 16% of the time, Pallas kernels for 5%

profile of v2, /device:TPU:0, one launch (start us, length us, event | category | flops | bytes accessed | tf_op | source)
XLA Modules:
  0.0 48.8 jit_solution(1446823793948731358)
XLA Ops:
  0.6 0.0 copy-start
  0.6 0.0 copy-start.1
  0.7 1.1 %copy-done.1 = bf16[48,4096]{1,0:T(8,128)(2,1)S(1)} copy-done((bf16[48,4096]{1,0:T(8,128)(2,1)S(1)}, bf16[48,4096]{1,0:T(8,128)(2,1)}, u32[]{:S(2)}) %copy-start.1) | copy-done | bytes 393240
  1.7 0.0 copy-start.5
  1.7 0.7 %copy-done.5 = s32[48,1]{0,1:T(1,128)S(1)} copy-done((s32[48,1]{0,1:T(1,128)S(1)}, s32[48,1]{0,1:T(1,128)}, u32[]{:S(2)}) %copy-start.5) | copy-done | bytes 216
  2.4 0.0 copy-start.6
  2.4 0.7 %copy-done.6 = s32[8]{0:T(128)S(1)} copy-done((s32[8]{0:T(128)S(1)}, s32[8]{0:T(128)}, u32[]{:S(2)}) %copy-start.6) | copy-done | bytes 56
  3.0 1.5 %shard_map.113 = (s32[1,48]{1,0:T(1,128)S(1)}, s32[1,48]{1,0:T(1,128)S(1)}, bf16[384,1024]{1,0:T(8,128)(2,1)}) custom-call(s32[1,48]{1,0:T(1,128)S(1)} %bitcast.25, s32[1,8]{1,0:T(1,128)S(1)} %bitcast.26, bf16[48,4096]{1,0:T(8,128)(2,1)S(1)} %copy-done.1), custom_call_target="tpu_custom_call" | custom-call | flops 50331648 | bytes 1179648 | tf_op jit(solution)/shard_map/pallas_call | solution.py:191
  4.6 7.3 %all-to-all-start = ((bf16[8,48,1024]{2,1,0:T(8,128)(2,1)}), bf16[8,48,1024]{2,1,0:T(8,128)(2,1)S(1)}, u32[]{:S(2)}, u32[]{:S(2)}) async-start(bf16[8,48,1024]{2,1,0:T(8,128)(2,1)} %bitcast.2), calls=%async_computation | async-start | bytes 1572864 | tf_op jit(solution)/shard_map/all_to_all | solution.py:187
  11.8 0.0 copy-start.3
  11.9 0.0 copy-start.8
  11.9 0.0 copy-start.7
  11.9 0.0 copy-start.2
  11.9 0.0 copy-start.4
  11.9 5.2 %fusion.7 = f32[48,1024]{1,0:T(8,128)S(1)} fusion(bf16[48,4096]{1,0:T(8,128)(2,1)} %hidden_ref.1, bf16[4096,1024]{1,0:T(8,128)(2,1)} %param.12), kind=kOutput, calls=%fused_computation.12 | convolution fusion | flops 402653184 | bytes 8978432 | tf_op jit(solution)/shard_map/dot_general | solution.py:202
  17.1 0.7 %constant_dynamic-slice_fusion = (f32[48,512]{1,0:T(8,128)}, f32[48,512]{1,0:T(8,128)S(1)}) fusion(f32[48,1024]{1,0:T(8,128)S(1)} %fusion.7, s32[]{:T(128)S(6)} %select_n.11, s32[]{:T(128)S(6)} %select_n.10), kind=kLoop, calls=%fused_computation.9 | loop fusion | bytes 393224 | tf_op jit(solution)/shard_map/dynamic_slice | solution.py:204
  17.8 0.0 collective-permute-start.1
  17.8 0.0 copy-done.3
  17.8 0.0 copy-done.8
  17.8 0.1 iota_compare_fusion
  17.9 0.0 copy-done.7
  17.9 0.7 %fusion.6 = (f32[48,2,8]{2,1,0:T(2,128)S(1)}, f32[48,2,8,32]{3,2,1,0:T(8,128)S(1)}) fusion(bf16[48,2,8,128]{3,2,1,0:T(8,128)(2,1)S(1)} %bitcast.27, bf16[48,2,32,128]{3,2,1,0:T(8,128)(2,1)S(1)} %copy-done.7, pred[48,32]{1,0:T(8,128)(4,1)S(1)} %iota_compare_fusion), kind=kOutput, calls=%fused_computation.11 | convolution fusion | flops 6364416 | bytes 1085952 | tf_op jit(solution)/shard_map/rgqd,rgpd->rgqp/dot_general | solution.py:207
  18.6 13.5 %all-to-all-done = bf16[8,48,1024]{2,1,0:T(8,128)(2,1)S(1)} async-done(((bf16[8,48,1024]{2,1,0:T(8,128)(2,1)}), bf16[8,48,1024]{2,1,0:T(8,128)(2,1)S(1)}, u32[]{:S(2)}, u32[]{:S(2)}) %all-to-all-start) | async-done | bytes 786464 | tf_op jit(solution)/shard_map/all_to_all | solution.py:187
  32.0 0.0 copy-done.2
  32.0 1.2 %shard_map.114.mine_ref = f32[96,128]{1,0:T(8,128)S(1)} custom-call(bf16[384,1024]{1,0:T(8,128)(2,1)S(1)} %bitcast.21, bf16[1,4096,128]{2,1,0:T(8,128)(2,1)S(1)} %copy-done.2), custom_call_target="tpu_custom_call" | custom-call | flops 100663296 | bytes 1835008 | tf_op jit(solution)/shard_map/pallas_call | solution.py:219
  33.2 0.1 collective-permute-start
  33.3 0.0 copy-done
  33.3 0.4 fusion.3
  33.7 0.8 %collective-permute-done.other_ref = f32[96,128]{1,0:T(8,128)S(1)} collective-permute-done((f32[96,128]{1,0:T(8,128)S(1)}, f32[96,128]{1,0:T(8,128)S(1)}, u32[]{:S(2)}, u32[]{:S(2)}) %collective-permute-start) | collective-permute-done | bytes 49184 | tf_op jit(solution)/shard_map/ppermute | solution.py:226
  34.5 0.0 copy-done.4
  34.5 1.1 %shard_map.115 = bf16[384,128]{1,0:T(8,128)(2,1)} custom-call(f32[96,128]{1,0:T(8,128)S(1)} %shard_map.114.mine_ref, f32[96,128]{1,0:T(8,128)S(1)} %collective-permute-done.other_ref, bf16[1,2,64,256]{3,2,1,0:T(8,128)(2,1)S(1)} %copy-done.4), custom_call_target="tpu_custom_call" | custom-call | flops 12582912 | bytes 196608 | tf_op jit(solution)/shard_map/pallas_call | solution.py:227
  35.6 3.6 %all-to-all-start.1 = ((bf16[8,48,128]{2,1,0:T(8,128)(2,1)}), bf16[8,48,128]{2,1,0:T(8,128)(2,1)S(1)}, u32[]{:S(2)}, u32[]{:S(2)}) async-start(bf16[8,48,128]{2,1,0:T(8,128)(2,1)} %bitcast.4), calls=%async_computation.1 | async-start | bytes 196608 | tf_op jit(solution)/shard_map/all_to_all | solution.py:187
  39.2 0.3 fusion.2
  39.5 0.1 copy.15
  39.6 0.1 copy.17.max_ref
  39.7 0.1 copy.16
  39.8 0.1 copy.18.sum_ref
  39.8 0.1 copy.22
  40.0 0.0 collective-permute-done.1.other_ref
  40.0 6.3 %all-to-all-done.1 = bf16[8,48,128]{2,1,0:T(8,128)(2,1)S(1)} async-done(((bf16[8,48,128]{2,1,0:T(8,128)(2,1)}), bf16[8,48,128]{2,1,0:T(8,128)(2,1)S(1)}, u32[]{:S(2)}, u32[]{:S(2)}) %all-to-all-start.1) | async-done | bytes 98336 | tf_op jit(solution)/shard_map/all_to_all | solution.py:187
  46.3 2.5 %shard_map.116 = (bf16[48,512]{1,0:T(8,128)(2,1)}, bf16[48,2048]{1,0:T(8,128)(2,1)}) custom-call(bf16[384,128]{1,0:T(8,128)(2,1)S(1)} %bitcast.24, s32[1,48]{1,0:T(1,128)S(1)} %get-tuple-element.6.slot_ref, s32[1,48]{1,0:T(1,128)S(1)} %get-tuple-element.7.rank_ref, f32[48,512]{1,0:T(8,128)S(1)} %get-tuple-element.9.base_ref, ...), custom_call_target="tpu_custom_call" | custom-call | flops 4718592 | bytes 786432 | tf_op jit(solution)/shard_map/pallas_call | solution.py:235
  (1 shorter events, 0.0 us)
Async XLA Ops:
  0.6 32.7 %copy-start = (bf16[48,2,32,128]{3,2,1,0:T(8,128)(2,1)S(1)}, bf16[48,2,32,128]{3,2,1,0:T(8,128)(2,1)}, u32[]{:S(2)}) copy-start(bf16[48,2,32,128]{3,2,1,0:T(8,128)(2,1)} %param.16) | copy-start | bytes 2359300
  0.6 1.1 %copy-start.1 = (bf16[48,4096]{1,0:T(8,128)(2,1)S(1)}, bf16[48,4096]{1,0:T(8,128)(2,1)}, u32[]{:S(2)}) copy-start(bf16[48,4096]{1,0:T(8,128)(2,1)} %hidden_ref.1) | copy-start | bytes 1179652
  1.7 0.7 %copy-start.5 = (s32[48,1]{0,1:T(1,128)S(1)}, s32[48,1]{0,1:T(1,128)}, u32[]{:S(2)}) copy-start(s32[48,1]{0,1:T(1,128)} %param.17) | copy-start | bytes 580
  2.4 0.7 %copy-start.6 = (s32[8]{0:T(128)S(1)}, s32[8]{0:T(128)}, u32[]{:S(2)}) copy-start(s32[8]{0:T(128)} %param.19) | copy-start | bytes 100
  4.6 27.5 %all-to-all-start = ((bf16[8,48,1024]{2,1,0:T(8,128)(2,1)}), bf16[8,48,1024]{2,1,0:T(8,128)(2,1)S(1)}, u32[]{:S(2)}, u32[]{:S(2)}) async-start(bf16[8,48,1024]{2,1,0:T(8,128)(2,1)} %bitcast.2), calls=%async_computation | async-start | bytes 1572864 | tf_op jit(solution)/shard_map/all_to_all | solution.py:187
  11.8 5.9 %copy-start.3 = (bf16[48,2048]{1,0:T(8,128)(2,1)S(1)}, bf16[48,2048]{1,0:T(8,128)(2,1)}, u32[]{:S(2)}) copy-start(bf16[48,2048]{1,0:T(8,128)(2,1)} %query_ref.1) | copy-start | bytes 589828
  11.9 6.0 %copy-start.8 = (s32[48]{0:T(128)S(1)}, s32[48]{0:T(128)}, u32[]{:S(2)}) copy-start(s32[48]{0:T(128)} %param.18) | copy-start | bytes 580
  11.9 6.0 %copy-start.7 = (bf16[48,2,32,128]{3,2,1,0:T(8,128)(2,1)S(1)}, bf16[48,2,32,128]{3,2,1,0:T(8,128)(2,1)}, u32[]{:S(2)}) copy-start(bf16[48,2,32,128]{3,2,1,0:T(8,128)(2,1)} %param.15) | copy-start | bytes 2359300
  11.9 20.2 %copy-start.2 = (bf16[1,4096,128]{2,1,0:T(8,128)(2,1)S(1)}, bf16[1,4096,128]{2,1,0:T(8,128)(2,1)}, u32[]{:S(2)}) copy-start(bf16[1,4096,128]{2,1,0:T(8,128)(2,1)} %down_ref.1) | copy-start | bytes 3145732
  11.9 22.6 %copy-start.4 = (bf16[1,2,64,256]{3,2,1,0:T(8,128)(2,1)S(1)}, bf16[1,2,64,256]{3,2,1,0:T(8,128)(2,1)}, u32[]{:S(2)}) copy-start(bf16[1,2,64,256]{3,2,1,0:T(8,128)(2,1)} %up_ref.1) | copy-start | bytes 196612
  17.8 22.2 %collective-permute-start.1 = (f32[48,512]{1,0:T(8,128)}, f32[48,512]{1,0:T(8,128)S(1)}, u32[]{:S(2)}, u32[]{:S(2)}) collective-permute-start(f32[48,512]{1,0:T(8,128)} %get-tuple-element.8), channel_id=1, source_target_pairs={{0,1},{1,0},{2,3},{3,2},{4,5},{5,4},{6,7},{7,6},{8,9},{9,8},{10,11... | collective-permute-start | bytes 294920 | tf_op jit(solution)/shard_map/ppermute | solution.py:204
  33.2 1.3 %collective-permute-start = (f32[96,128]{1,0:T(8,128)S(1)}, f32[96,128]{1,0:T(8,128)S(1)}, u32[]{:S(2)}, u32[]{:S(2)}) collective-permute-start(f32[96,128]{1,0:T(8,128)S(1)} %shard_map.114.mine_ref), channel_id=1, source_target_pairs={{0,1},{1,0},{2,3},{3,2},{4,5},{5,4},{6,7},{7,6},{8,9},{9,8},{10,11... | collective-permute-start | bytes 147464 | tf_op jit(solution)/shard_map/ppermute | solution.py:226
  35.6 10.7 %all-to-all-start.1 = ((bf16[8,48,128]{2,1,0:T(8,128)(2,1)}), bf16[8,48,128]{2,1,0:T(8,128)(2,1)S(1)}, u32[]{:S(2)}, u32[]{:S(2)}) async-start(bf16[8,48,128]{2,1,0:T(8,128)(2,1)} %bitcast.4), calls=%async_computation.1 | async-start | bytes 196608 | tf_op jit(solution)/shard_map/all_to_all | solution.py:187

commit v3 on v2

--- a/solution.py
+++ b/solution.py
@@ -46,9 +46,23 @@
     return codes
 
 
-def pack_kernel(n, cap, pieces, idx_ref, table_ref, hidden_ref, slot_ref, rank_ref, packed_ref):
+def pack_kernel(n, cap, pieces, me_ref, idx_hbm, table_hbm, hidden_hbm, slot_ref, rank_ref, near_ref, *refs):
+    far_refs, (idx_ref, table_ref, hidden_ref, sems) = refs[:-4], refs[-4:]
+    copies = [
+        pltpu.make_async_copy(source, target, sems.at[i])
+        for i, (source, target) in enumerate(
+            [(idx_hbm, idx_ref), (table_hbm, table_ref), (hidden_hbm, hidden_ref)]
+        )
+    ]
+    for copy in copies:
+        copy.start()
     rows = hidden_ref.shape[0]
     width = hidden_ref.shape[1] // pieces
+    per = pieces * cap
+    me = me_ref[0]
+    half = n // 2
+    copies[0].wait()
+    copies[1].wait()
     named = (iota((n, rows), 0) == idx_ref[...]).astype(F32).astype(BF16)
     table = jnp.broadcast_to(table_ref[...].astype(F32).astype(BF16), (16, n))
     slot = dot(table, named)[0:1, :].astype(I32)
@@ -58,20 +72,26 @@
     rank = jnp.sum(member * count, axis=0, keepdims=True).astype(I32)
     slot_ref[...] = slot
     rank_ref[...] = rank
-    codes = placement(slot, rank, cap, pieces)
-    total = n * pieces * cap
-    one_hot = (iota((total, pieces * rows), 0) == codes).astype(F32).astype(BF16)
+    apart = lax.bitwise_xor(slot, me)
+    place = jnp.where(apart < half, lax.bitwise_and(slot, half - 1), apart)
+    codes = placement(place, rank, cap, pieces)
+    one_hot = (iota((n * per, pieces * rows), 0) == codes).astype(F32).astype(BF16)
+    copies[2].wait()
     stacked = jnp.concatenate(
         [hidden_ref[:, piece * width : (piece + 1) * width] for piece in range(pieces)], axis=0
     )
-    packed_ref[...] = dot(one_hot, stacked).astype(BF16)
-
-
-def shrink_kernel(n, cap, pieces, received_ref, down_ref, out_ref):
+    packed = dot(one_hot, stacked).astype(BF16)
+    near_ref[...] = packed[: half * per]
+    for s in range(half, n):
+        far_refs[s - half][...] = packed[s * per : (s + 1) * per]
+
+
+def shrink_kernel(n, cap, pieces, *refs):
+    received_refs, down_ref, out_ref = refs[:-2], refs[-2], refs[-1]
     per = pieces * cap
-    width = received_ref.shape[1]
+    width = received_refs[0].shape[1]
     rank2 = down_ref.shape[2]
-    received = received_ref[...]
+    received = jnp.concatenate([ref[...] for ref in received_refs], axis=0)
     total = jnp.zeros((n * per, rank2), F32)
     piece_of = (iota((n * per, rank2), 0) // cap) % pieces
     for piece in range(pieces):
@@ -82,7 +102,7 @@
     out_ref[...] = exact_select(same.astype(F32).astype(BF16), total)
 
 
-def expand_kernel(n, cap, mine_ref, other_ref, up_ref, out_ref):
+def expand_kernel(n, cap, me_ref, mine_ref, other_ref, up_ref, out_ref):
     rank = up_ref.shape[2]
     head = 128
     blocks = up_ref.shape[3] // head
@@ -97,7 +117,9 @@
     per = pieces * cap
     size = n * per
     out_row, in_row = iota((size, size), 0), iota((size, size), 1)
-    source = (out_row // cap % pieces) * (n * cap) + (out_row // per) * cap + out_row % cap
+    apart = lax.bitwise_xor(out_row // per, me_ref[0])
+    place = jnp.where(apart < n // 2, lax.bitwise_and(out_row // per, n // 2 - 1), apart)
+    source = (out_row // cap % pieces) * (n * cap) + place * cap + out_row % cap
     out_ref[...] = dot((source == in_row).astype(F32).astype(BF16), stacked).astype(BF16)
 
 
@@ -149,13 +171,18 @@
             out_ref[:, lanes] = out.astype(BF16)
 
 
-def call(kernel, outs, flops, bytes_accessed, inputs):
-    vmem = pl.BlockSpec(memory_space=pltpu.VMEM)
+VMEM = pl.BlockSpec(memory_space=pltpu.VMEM)
+SMEM = pl.BlockSpec(memory_space=pltpu.SMEM)
+ANY = pl.BlockSpec(memory_space=pl.ANY)
+
+
+def call(kernel, outs, flops, bytes_accessed, specs, scratch=()):
     return pl.pallas_call(
         kernel,
         out_shape=outs,
-        in_specs=[vmem] * inputs,
-        out_specs=[vmem] * len(outs),
+        in_specs=specs,
+        out_specs=[VMEM] * len(outs),
+        scratch_shapes=scratch,
         compiler_params=pltpu.CompilerParams(vmem_limit_bytes=VMEM_LIMIT),
         cost_estimate=pl.CostEstimate(flops=flops, bytes_accessed=bytes_accessed, transcendentals=0),
     )
@@ -183,25 +210,42 @@
     out_pieces = 2 * groups
     rank2 = adapter_down_weight.shape[2]
 
-    def exchange(chunks):
-        return lax.all_to_all(chunks, "pool", split_axis=0, concat_axis=0, tiled=True)
-
     swap = functools.partial(lax.ppermute, axis_name="tp", perm=[(0, 1), (1, 0)])
 
-    slot, rank, packed = call(
+    half = n // 2
+    per = pieces * cap
+    me = lax.axis_index("pool").reshape(1)
+    slot, rank, near, *far = call(
         functools.partial(pack_kernel, n, cap, pieces),
         [jax.ShapeDtypeStruct((1, rows), I32)] * 2
-        + [jax.ShapeDtypeStruct((n * pieces * cap, width // pieces), BF16)],
+        + [jax.ShapeDtypeStruct((half * per, width // pieces), BF16)]
+        + [jax.ShapeDtypeStruct((per, width // pieces), BF16)] * half,
         2 * n * cap * width * 64,
         3 * rows * width * 2,
-        3,
-    )(row_adapter_index.reshape(1, rows), adapter_slot_table.reshape(1, n), hidden)
-    arrived = exchange(packed)
-
-    half = lax.axis_index("tp")
+        [SMEM, ANY, ANY, ANY],
+        [
+            pltpu.VMEM((1, rows), I32),
+            pltpu.VMEM((1, n), I32),
+            pltpu.VMEM((rows, width), BF16),
+            pltpu.SemaphoreType.DMA((3,)),
+        ],
+    )(me, row_adapter_index.reshape(1, rows), adapter_slot_table.reshape(1, n), hidden)
+    far = [
+        lax.ppermute(chunk, "pool", [(i, i ^ s) for i in range(n)]) for s, chunk in enumerate(far, half)
+    ]
+    near = lax.all_to_all(
+        near,
+        "pool",
+        split_axis=0,
+        concat_axis=0,
+        tiled=True,
+        axis_index_groups=[list(range(half)), list(range(half, n))],
+    )
+
+    core = lax.axis_index("tp")
     partial_sum = jnp.dot(hidden, key_value_weight, preferred_element_type=F32)
-    base_mine = lax.dynamic_slice_in_dim(partial_sum, half * columns, columns, axis=1)
-    base_other = swap(lax.dynamic_slice_in_dim(partial_sum, (1 - half) * columns, columns, axis=1))
+    base_mine = lax.dynamic_slice_in_dim(partial_sum, core * columns, columns, axis=1)
+    base_other = swap(lax.dynamic_slice_in_dim(partial_sum, (1 - core) * columns, columns, axis=1))
 
     query_heads = queries.reshape(rows, groups, -1, head)
     scores = jnp.einsum("rgqd,rgpd->rgqp", query_heads, stored_cache_keys, preferred_element_type=F32)
@@ -221,23 +265,23 @@
         [jax.ShapeDtypeStruct((n * cap, rank2), F32)],
         2 * n * cap * width * rank2,
         n * cap * width * 2 + width * rank2 * 2,
-        2,
-    )(arrived, adapter_down_weight)
+        [VMEM] * (half + 2),
+    )(near, *far, adapter_down_weight)
     reduced_other = swap(reduced)
     (terms,) = call(
         functools.partial(expand_kernel, n, cap),
         [jax.ShapeDtypeStruct((n * out_pieces * cap, head), BF16)],
         2 * n * cap * rank2 * columns,
         n * cap * columns * 4,
-        3,
-    )(reduced, reduced_other, adapter_up_weight)
-    deltas = exchange(terms)
+        [SMEM, VMEM, VMEM, VMEM],
+    )(me, reduced, reduced_other, adapter_up_weight)
+    deltas = lax.all_to_all(terms, "pool", split_axis=0, concat_axis=0, tiled=True)
     token, out = call(
         functools.partial(combine_kernel, n, cap),
         [jax.ShapeDtypeStruct((rows, columns), BF16), jax.ShapeDtypeStruct(queries.shape, BF16)],
         2 * n * cap * columns * rows,
         rows * 2048 * 8,
-        9,
+        [VMEM] * 9,
     )(deltas, slot, rank, base_mine, base_other, queries, cache_max, cache_sum, attended)
     return token, out
 

time: 49.1 us -> 48.8 us (level)
  waiting for transfers between devices: 20.6 us -> 5.99 us
  starting transfers between devices: 10.9 us -> 19.6 us
  matrix products: 6.24 us -> 9.68 us
  other arithmetic: 0.42 us -> 1.4 us
  local copies, waits for them, and re-layouts: 3.54 us -> 4.46 us
    all_to_all x2, waiting for transfers between devices: 19.8 us -> 5.37 us  [the longest x1 5.36 us: shards(): lax.all_to_all(terms, 'pool', split_axis=0, concat_axis=0, tiled=True)]
    ppermute x1 -> x5, starting transfers between devices: 0.01 us -> 7.88 us  [the longest x4 7.88 us: shards(): lax.ppermute(chunk, 'pool', [(i, i ^ s) for i in range(n)])]
    dot_general x1, matrix products: 0.65 us -> 2.45 us  [shards(): jnp.einsum('rgqd,rgpd->rgqp', query_heads, stored_cache_keys, preferred_e...]
    dot_general x1, matrix products: 0.38 us -> 1.38 us  [shards(): jnp.einsum('rgqp,rgpd->rgqd', weights.astype(BF16), stored_cache_values,...]
    reduce_sum x1, other arithmetic: 0.35 us -> 1.32 us  [shards(): cache_sum = jnp.sum(weights, axis=-1).reshape(rows, -1)]
    dynamic_slice x1, local copies, waits for them, and re-layouts: 0.66 us -> 1.6 us  [shards(): lax.dynamic_slice_in_dim(partial_sum, (1 - core) * columns, columns, axis=1)]
    ppermute x1, waiting for transfers between devices: 0.82 us -> 0.01 us  [shards(): reduced_other = swap(reduced)]
    all_to_all x2, starting transfers between devices: 10.8 us -> 11.6 us  [the longest x1 6.38 us: shards(): lax.all_to_all(terms, 'pool', split_axis=0, concat_axis=0, tiled=True)]
  transfers between devices with their start and end apart: 4 -> 8, of which waited for: 3 -> 2; matrix products, arithmetic and copies ran while one was open for 16% -> 27% of each run, Pallas kernels for 5% -> 5%
where the time goes in v3:
time: 48.8 us; the launch traced here: 48.4 us
  starting transfers between devices  19.6 us (40%)
  matrix products  9.68 us (20%)
  Pallas kernels  6.46 us (13%)
  waiting for transfers between devices  5.99 us (12%)
  local copies, waits for them, and re-layouts  4.46 us (9%)
  other arithmetic  1.4 us (3%)
  between operations  0.79 us (2%)
    ppermute x4, starting transfers between devices, shards(): lax.ppermute(chunk, 'pool', [(i, i ^ s) for i in range(n)])  7.88 us
    all_to_all x1, starting transfers between devices, shards(): lax.all_to_all(terms, 'pool', split_axis=0, concat_axis=0, tiled=True)  6.38 us
    dot_general x1, matrix products, shards(): partial_sum = jnp.dot(hidden, key_value_weight, preferred_element_type=F32)  5.85 us
    all_to_all x1, waiting for transfers between devices, shards(): lax.all_to_all(terms, 'pool', split_axis=0, concat_axis=0, tiled=True)  5.36 us
    all_to_all x1, starting transfers between devices, shards(): lax.all_to_all(near, 'pool', split_axis=0, concat_axis=0, tiled=True, axi...  5.26 us
    unnamed x18, local copies, waits for them, and re-layouts  2.56 us
    pallas_call x1, Pallas kernels, shards(): call(functools.partial(combine_kernel, n, cap), [jax.ShapeDtypeStruct((ro...  2.52 us
    dot_general x1, matrix products, shards(): jnp.einsum('rgqd,rgpd->rgqp', query_heads, stored_cache_keys, preferred_e...  2.45 us
  transfers between devices with their start and end apart: 8, of which 2 were waited for; matrix products, arithmetic and copies ran while one was open for 27% of the time, Pallas kernels for 5%

profile of v3, /device:TPU:0, one launch (start us, length us, event | category | flops | bytes accessed | tf_op | source)
XLA Modules:
  0.0 48.4 jit_solution(7219679062018068850)
XLA Ops:
  0.6 0.0 copy-start
  0.7 0.0 copy-start.1
  0.7 1.1 %copy-done.1 = bf16[48,4096]{1,0:T(8,128)(2,1)S(1)} copy-done((bf16[48,4096]{1,0:T(8,128)(2,1)S(1)}, bf16[48,4096]{1,0:T(8,128)(2,1)}, u32[]{:S(2)}) %copy-start.1) | copy-done | bytes 393240
  1.7 0.0 copy-start.5
  1.7 0.7 %copy-done.5 = s32[48,1]{0,1:T(1,128)S(1)} copy-done((s32[48,1]{0,1:T(1,128)S(1)}, s32[48,1]{0,1:T(1,128)}, u32[]{:S(2)}) %copy-start.5) | copy-done | bytes 216
  2.4 0.0 copy-start.6
  2.4 0.7 %copy-done.6 = s32[8]{0:T(128)S(1)} copy-done((s32[8]{0:T(128)S(1)}, s32[8]{0:T(128)}, u32[]{:S(2)}) %copy-start.6) | copy-done | bytes 56
  3.0 1.6 %shard_map.113 = (s32[1,48]{1,0:T(1,128)S(1)}, s32[1,48]{1,0:T(1,128)S(1)}, bf16[192,1024]{1,0:T(8,128)(2,1)}, bf16[48,1024]{1,0:T(8,128)(2,1)S(1)}, bf16[48,102...) custom-call(s32[1]{0:T(128)} %bitcast.me_ref, s32[1,48]{1,0:T(1,128)S(1)} %bitcast.26, ...), custom_call_target="tpu_custom_call" | custom-call | flops 50331648 | bytes 1179648 | tf_op jit(solution)/shard_map/pallas_call | solution.py:218
  4.7 5.3 %all-to-all-start = ((bf16[4,48,1024]{2,1,0:T(8,128)(2,1)}), bf16[4,48,1024]{2,1,0:T(8,128)(2,1)S(1)}, u32[]{:S(2)}, u32[]{:S(2)}) async-start(bf16[4,48,1024]{2,1,0:T(8,128)(2,1)} %bitcast.3), calls=%async_computation | async-start | bytes 786432 | tf_op jit(solution)/shard_map/all_to_all | solution.py:236
  9.9 2.6 %collective-permute-start = (bf16[48,1024]{1,0:T(8,128)(2,1)S(1)}, bf16[48,1024]{1,0:T(8,128)(2,1)S(1)}, u32[]{:S(2)}, u32[]{:S(2)}) collective-permute-start(bf16[48,1024]{1,0:T(8,128)(2,1)S(1)} %get-tuple-element.10), channel_id=1, source_target_pairs={{0,8},{2,10},{4,12},{6,14},{8,0},{10,2},{12,4},{14,6},{1,9},{3,11}... | collective-permute-start | bytes 294920 | tf_op jit(solution)/shard_map/ppermute | solution.py:234
  12.5 1.8 %collective-permute-start.1 = (bf16[48,1024]{1,0:T(8,128)(2,1)S(1)}, bf16[48,1024]{1,0:T(8,128)(2,1)S(1)}, u32[]{:S(2)}, u32[]{:S(2)}) collective-permute-start(bf16[48,1024]{1,0:T(8,128)(2,1)S(1)} %get-tuple-element.11), channel_id=1, source_target_pairs={{0,10},{2,8},{4,14},{6,12},{8,2},{10,0},{12,6},{14,4},{1,11},{3,9}... | collective-permute-start | bytes 294920 | tf_op jit(solution)/shard_map/ppermute | solution.py:234
  14.3 3.5 %collective-permute-start.2 = (bf16[48,1024]{1,0:T(8,128)(2,1)S(1)}, bf16[48,1024]{1,0:T(8,128)(2,1)S(1)}, u32[]{:S(2)}, u32[]{:S(2)}) collective-permute-start(bf16[48,1024]{1,0:T(8,128)(2,1)S(1)} %get-tuple-element.12), channel_id=1, source_target_pairs={{0,12},{2,14},{4,8},{6,10},{8,4},{10,6},{12,0},{14,2},{1,13},{3,15... | collective-permute-start | bytes 294920 | tf_op jit(solution)/shard_map/ppermute | solution.py:234
  17.8 0.0 collective-permute-start.3
  17.8 0.0 copy-start.3
  17.8 0.0 copy-start.7
  17.8 0.0 copy-start.2
  17.8 0.0 copy-start.4
  17.8 5.9 %fusion.7 = f32[48,1024]{1,0:T(8,128)} fusion(bf16[48,4096]{1,0:T(8,128)(2,1)} %hidden_hbm.1, bf16[4096,1024]{1,0:T(8,128)(2,1)} %param.12), kind=kOutput, calls=%fused_computation.12 | convolution fusion | flops 402653184 | bytes 8978432 | tf_op jit(solution)/shard_map/dot_general | solution.py:246
  23.7 1.6 %constant_dynamic-slice_fusion = (f32[48,512]{1,0:T(8,128)}, f32[48,512]{1,0:T(8,128)S(1)}) fusion(f32[48,1024]{1,0:T(8,128)} %fusion.7, s32[]{:T(128)S(6)} %select_n.11, s32[]{:T(128)S(6)} %select_n.10), kind=kLoop, calls=%fused_computation.9 | loop fusion | bytes 393224 | tf_op jit(solution)/shard_map/dynamic_slice | solution.py:248
  25.3 0.0 collective-permute-start.5
  25.3 0.0 copy-done.3
  25.3 0.0 copy-done.7
  25.3 0.1 iota_compare_fusion
  25.4 2.5 %fusion.6 = (f32[48,2,8]{2,1,0:T(2,128)S(1)}, f32[48,2,8,32]{3,2,1,0:T(8,128)}) fusion(bf16[48,2,8,128]{3,2,1,0:T(8,128)(2,1)S(1)} %bitcast.28, bf16[48,2,32,128]{3,2,1,0:T(8,128)(2,1)} %param.15, pred[48,32]{1,0:T(8,128)(4,1)S(1)} %iota_compare_fusion), kind=kOutput, calls=%fused_computation.11 | convolution fusion | flops 6364416 | bytes 1085952 | tf_op jit(solution)/shard_map/rgqd,rgpd->rgqp/dot_general | solution.py:251
  27.9 0.0 collective-permute-done.refs_1_
  27.9 0.6 %collective-permute-done.1.refs_2_ = bf16[48,1024]{1,0:T(8,128)(2,1)S(1)} collective-permute-done((bf16[48,1024]{1,0:T(8,128)(2,1)S(1)}, bf16[48,1024]{1,0:T(8,128)(2,1)S(1)}, u32[]{:S(2)}, u32[]{:S(2)}) %collective-permute-start.1) | collective-permute-done | bytes 98336 | tf_op jit(solution)/shard_map/ppermute | solution.py:234
  28.5 0.0 collective-permute-done.2.refs_3_
  28.5 0.0 collective-permute-done.3.refs_4_
  28.5 0.0 all-to-all-done
  28.5 0.0 copy-done.2
  28.5 1.2 %shard_map.114.mine_ref = f32[96,128]{1,0:T(8,128)S(1)} custom-call(bf16[192,1024]{1,0:T(8,128)(2,1)S(1)} %bitcast.22, bf16[48,1024]{1,0:T(8,128)(2,1)S(1)} %collective-permute-done.refs_1_, bf16[48,1024]{1,0:T(8,128)(2,1)S(1)} %collective-permute-done.1.refs_2_, bf16[48,1024]{1,0:T(8,128)(2,1)S(1)} %collective-permute-done.2.refs_3_, ...), custom_call_target="tpu_custom_call" | custom-call | flops 100663296 | bytes 1835008 | tf_op jit(solution)/shard_map/pallas_call | solution.py:263
  29.7 0.1 collective-permute-start.4
  29.8 0.0 copy-done
  29.8 1.4 %fusion.3 = f32[48,2,8,128]{3,2,1,0:T(8,128)S(1)} fusion(bf16[48,2,32,128]{3,2,1,0:T(8,128)(2,1)S(1)} %copy-done, f32[48,2,8,32]{3,2,1,0:T(8,128)} %get-tuple-element.19, f32[48,2,8]{2,1,0:T(2,128)S(1)} %get-tuple-element.18), kind=kOutput, calls=%fused_computation.6 | convolution fusion | flops 6340608 | bytes 1281024 | tf_op jit(solution)/shard_map/rgqp,rgpd->rgqd/dot_general | solution.py:258
  31.2 0.0 collective-permute-done.4.other_ref
  31.2 0.0 copy-done.4
  31.2 1.1 %shard_map.115 = bf16[384,128]{1,0:T(8,128)(2,1)} custom-call(s32[1]{0:T(128)} %bitcast.me_ref, f32[96,128]{1,0:T(8,128)S(1)} %shard_map.114.mine_ref, f32[96,128]{1,0:T(8,128)S(1)} %collective-permute-done.4.other_ref, bf16[1,2,64,256]{3,2,1,0:T(8,128)(2,1)S(1)} %copy-done.4), custom_call_target="tpu_custom_call" | custom-call | flops 12582912 | bytes 196608 | tf_op jit(solution)/shard_map/pallas_call | solution.py:271
  32.3 6.4 %all-to-all-start.1 = ((bf16[8,48,128]{2,1,0:T(8,128)(2,1)}), bf16[8,48,128]{2,1,0:T(8,128)(2,1)S(1)}, u32[]{:S(2)}, u32[]{:S(2)}) async-start(bf16[8,48,128]{2,1,0:T(8,128)(2,1)} %bitcast.5), calls=%async_computation.1 | async-start | bytes 196608 | tf_op jit(solution)/shard_map/all_to_all | solution.py:278
  38.7 1.3 %fusion.2 = f32[48,2,8]{2,1,0:T(2,128)S(1)} fusion(f32[48,2,8,32]{3,2,1,0:T(8,128)} %get-tuple-element.19, f32[48,2,8]{2,1,0:T(2,128)S(1)} %get-tuple-element.18), kind=kLoop, calls=%fused_computation.5 | loop fusion | flops 48384 | bytes 104448 | tf_op jit(solution)/shard_map/reduce_sum | solution.py:257
  40.0 0.1 copy.15
  40.1 0.1 copy.17.max_ref
  40.2 0.1 copy.16
  40.3 0.1 copy.18.sum_ref
  40.3 0.1 copy.22
  40.5 0.0 collective-permute-done.5.other_ref
  40.5 5.4 %all-to-all-done.1 = bf16[8,48,128]{2,1,0:T(8,128)(2,1)S(1)} async-done(((bf16[8,48,128]{2,1,0:T(8,128)(2,1)}), bf16[8,48,128]{2,1,0:T(8,128)(2,1)S(1)}, u32[]{:S(2)}, u32[]{:S(2)}) %all-to-all-start.1) | async-done | bytes 98336 | tf_op jit(solution)/shard_map/all_to_all | solution.py:278
  45.9 2.5 %shard_map.116 = (bf16[48,512]{1,0:T(8,128)(2,1)}, bf16[48,2048]{1,0:T(8,128)(2,1)}) custom-call(bf16[384,128]{1,0:T(8,128)(2,1)S(1)} %bitcast.25, s32[1,48]{1,0:T(1,128)S(1)} %get-tuple-element.14.slot_ref, s32[1,48]{1,0:T(1,128)S(1)} %get-tuple-element.15.rank_ref, f32[48,512]{1,0:T(8,128)S(1)} %get-tuple-element.17.base_ref, ...), custom_call_target="tpu_custom_call" | custom-call | flops 4718592 | bytes 786432 | tf_op jit(solution)/shard_map/pallas_call | solution.py:279
  (1 shorter events, 0.0 us)
Async XLA Ops:
  0.6 29.2 %copy-start = (bf16[48,2,32,128]{3,2,1,0:T(8,128)(2,1)S(1)}, bf16[48,2,32,128]{3,2,1,0:T(8,128)(2,1)}, u32[]{:S(2)}) copy-start(bf16[48,2,32,128]{3,2,1,0:T(8,128)(2,1)} %param.16) | copy-start | bytes 2359300
  0.7 1.1 %copy-start.1 = (bf16[48,4096]{1,0:T(8,128)(2,1)S(1)}, bf16[48,4096]{1,0:T(8,128)(2,1)}, u32[]{:S(2)}) copy-start(bf16[48,4096]{1,0:T(8,128)(2,1)} %hidden_hbm.1) | copy-start | bytes 1179652
  1.7 0.7 %copy-start.5 = (s32[48,1]{0,1:T(1,128)S(1)}, s32[48,1]{0,1:T(1,128)}, u32[]{:S(2)}) copy-start(s32[48,1]{0,1:T(1,128)} %param.17) | copy-start | bytes 580
  2.4 0.7 %copy-start.6 = (s32[8]{0:T(128)S(1)}, s32[8]{0:T(128)}, u32[]{:S(2)}) copy-start(s32[8]{0:T(128)} %param.19) | copy-start | bytes 100
  4.7 23.8 %all-to-all-start = ((bf16[4,48,1024]{2,1,0:T(8,128)(2,1)}), bf16[4,48,1024]{2,1,0:T(8,128)(2,1)S(1)}, u32[]{:S(2)}, u32[]{:S(2)}) async-start(bf16[4,48,1024]{2,1,0:T(8,128)(2,1)} %bitcast.3), calls=%async_computation | async-start | bytes 786432 | tf_op jit(solution)/shard_map/all_to_all | solution.py:236
  9.9 17.9 %collective-permute-start = (bf16[48,1024]{1,0:T(8,128)(2,1)S(1)}, bf16[48,1024]{1,0:T(8,128)(2,1)S(1)}, u32[]{:S(2)}, u32[]{:S(2)}) collective-permute-start(bf16[48,1024]{1,0:T(8,128)(2,1)S(1)} %get-tuple-element.10), channel_id=1, source_target_pairs={{0,8},{2,10},{4,12},{6,14},{8,0},{10,2},{12,4},{14,6},{1,9},{3,11}... | collective-permute-start | bytes 294920 | tf_op jit(solution)/shard_map/ppermute | solution.py:234
  12.5 16.0 %collective-permute-start.1 = (bf16[48,1024]{1,0:T(8,128)(2,1)S(1)}, bf16[48,1024]{1,0:T(8,128)(2,1)S(1)}, u32[]{:S(2)}, u32[]{:S(2)}) collective-permute-start(bf16[48,1024]{1,0:T(8,128)(2,1)S(1)} %get-tuple-element.11), channel_id=1, source_target_pairs={{0,10},{2,8},{4,14},{6,12},{8,2},{10,0},{12,6},{14,4},{1,11},{3,9}... | collective-permute-start | bytes 294920 | tf_op jit(solution)/shard_map/ppermute | solution.py:234
  14.3 14.2 %collective-permute-start.2 = (bf16[48,1024]{1,0:T(8,128)(2,1)S(1)}, bf16[48,1024]{1,0:T(8,128)(2,1)S(1)}, u32[]{:S(2)}, u32[]{:S(2)}) collective-permute-start(bf16[48,1024]{1,0:T(8,128)(2,1)S(1)} %get-tuple-element.12), channel_id=1, source_target_pairs={{0,12},{2,14},{4,8},{6,10},{8,4},{10,6},{12,0},{14,2},{1,13},{3,15... | collective-permute-start | bytes 294920 | tf_op jit(solution)/shard_map/ppermute | solution.py:234
  17.8 10.7 %collective-permute-start.3 = (bf16[48,1024]{1,0:T(8,128)(2,1)S(1)}, bf16[48,1024]{1,0:T(8,128)(2,1)S(1)}, u32[]{:S(2)}, u32[]{:S(2)}) collective-permute-start(bf16[48,1024]{1,0:T(8,128)(2,1)S(1)} %get-tuple-element.13), channel_id=1, source_target_pairs={{0,14},{2,12},{4,10},{6,8},{8,6},{10,4},{12,2},{14,0},{1,15},{3,13... | collective-permute-start | bytes 294920 | tf_op jit(solution)/shard_map/ppermute | solution.py:234
  17.8 7.5 %copy-start.3 = (bf16[48,2048]{1,0:T(8,128)(2,1)S(1)}, bf16[48,2048]{1,0:T(8,128)(2,1)}, u32[]{:S(2)}) copy-start(bf16[48,2048]{1,0:T(8,128)(2,1)} %query_ref.1) | copy-start | bytes 589828
  17.8 7.5 %copy-start.7 = (s32[48]{0:T(128)S(1)}, s32[48]{0:T(128)}, u32[]{:S(2)}) copy-start(s32[48]{0:T(128)} %param.18) | copy-start | bytes 580
  17.8 10.7 %copy-start.2 = (bf16[1,4096,128]{2,1,0:T(8,128)(2,1)S(1)}, bf16[1,4096,128]{2,1,0:T(8,128)(2,1)}, u32[]{:S(2)}) copy-start(bf16[1,4096,128]{2,1,0:T(8,128)(2,1)} %refs_5_.1) | copy-start | bytes 3145732
  17.8 13.4 %copy-start.4 = (bf16[1,2,64,256]{3,2,1,0:T(8,128)(2,1)S(1)}, bf16[1,2,64,256]{3,2,1,0:T(8,128)(2,1)}, u32[]{:S(2)}) copy-start(bf16[1,2,64,256]{3,2,1,0:T(8,128)(2,1)} %up_ref.1) | copy-start | bytes 196612
  25.3 15.2 %collective-permute-start.5 = (f32[48,512]{1,0:T(8,128)}, f32[48,512]{1,0:T(8,128)S(1)}, u32[]{:S(2)}, u32[]{:S(2)}) collective-permute-start(f32[48,512]{1,0:T(8,128)} %get-tuple-element.16), channel_id=1, source_target_pairs={{0,1},{1,0},{2,3},{3,2},{4,5},{5,4},{6,7},{7,6},{8,9},{9,8},{10,11... | collective-permute-start | bytes 294920 | tf_op jit(solution)/shard_map/ppermute | solution.py:248
  29.7 1.5 %collective-permute-start.4 = (f32[96,128]{1,0:T(8,128)S(1)}, f32[96,128]{1,0:T(8,128)S(1)}, u32[]{:S(2)}, u32[]{:S(2)}) collective-permute-start(f32[96,128]{1,0:T(8,128)S(1)} %shard_map.114.mine_ref), channel_id=1, source_target_pairs={{0,1},{1,0},{2,3},{3,2},{4,5},{5,4},{6,7},{7,6},{8,9},{9,8},{10,11... | collective-permute-start | bytes 147464 | tf_op jit(solution)/shard_map/ppermute | solution.py:270
  32.3 13.5 %all-to-all-start.1 = ((bf16[8,48,128]{2,1,0:T(8,128)(2,1)}), bf16[8,48,128]{2,1,0:T(8,128)(2,1)S(1)}, u32[]{:S(2)}, u32[]{:S(2)}) async-start(bf16[8,48,128]{2,1,0:T(8,128)(2,1)} %bitcast.5), calls=%async_computation.1 | async-start | bytes 196608 | tf_op jit(solution)/shard_map/all_to_all | solution.py:278

commit v4 on v3

v4 whole, which is shorter than its diff:
```python
import functools

import jax
import jax.numpy as jnp
from jax import lax
from jax.experimental import pallas as pl
from jax.experimental.pallas import tpu as pltpu
from jax.sharding import PartitionSpec as P

BF16 = jnp.bfloat16
F32 = jnp.float32
I32 = jnp.int32
VMEM_LIMIT = 48 * 1024 * 1024


def iota(shape, dim):
    return lax.broadcasted_iota(I32, shape, dim)


def split_count(cap):
    pieces = 4
    while cap * pieces % 16:
        pieces *= 2
    return pieces


def dot(a, b):
    return jnp.dot(a, b, preferred_element_type=F32)


def dot_first(a, b):
    return lax.dot_general(a, b, (((0,), (0,)), ((), ())), preferred_element_type=F32)


def exact_select(one_hot, x):
    high = x.astype(BF16)
    rest = x - high.astype(F32)
    middle = rest.astype(BF16)
    low = (rest - middle.astype(F32)).astype(BF16)
    return dot(one_hot, high) + (dot(one_hot, middle) + dot(one_hot, low))


def codes_of(place, rank, cap, pieces):
    code = place * (pieces * cap) + rank
    return jnp.concatenate([code + piece * cap for piece in range(pieces)], axis=1)


def one_hot_of(codes, first, count):
    return ((iota((count, codes.shape[1]), 0) + first) == codes).astype(F32).astype(BF16)


def stack_pieces(hidden, pieces):
    width = hidden.shape[1] // pieces
    return jnp.concatenate(
        [hidden[:, piece * width : (piece + 1) * width] for piece in range(pieces)], axis=0
    )


def pack_far_kernel(n, cap, pieces, me_ref, idx_hbm, table_hbm, hidden_hbm, place_ref, rank_ref, *refs):
    far_refs, (idx_ref, table_ref, hidden_ref, sems) = refs[:-4], refs[-4:]
    copies = [
        pltpu.make_async_copy(source, target, sems.at[i])
        for i, (source, target) in enumerate(
            [(idx_hbm, idx_ref), (table_hbm, table_ref), (hidden_hbm, hidden_ref)]
        )
    ]
    for copy in copies:
        copy.start()
    rows = hidden_ref.shape[0]
    per = pieces * cap
    half = n // 2
    copies[0].wait()
    copies[1].wait()
    named = (iota((n, rows), 0) == idx_ref[...]).astype(F32).astype(BF16)
    table = jnp.broadcast_to(table_ref[...].astype(F32).astype(BF16), (16, n))
    slot = dot(table, named)[0:1, :].astype(I32)
    member = (iota((n, rows), 0) == slot).astype(F32)
    before = (iota((rows, rows), 0) < iota((rows, rows), 1)).astype(F32).astype(BF16)
    count = dot(member.astype(BF16), before)
    rank = jnp.sum(member * count, axis=0, keepdims=True).astype(I32)
    apart = lax.bitwise_xor(slot, me_ref[0])
    place = jnp.where(apart < half, lax.bitwise_and(slot, half - 1), apart)
    place_ref[...] = place
    rank_ref[...] = rank
    one_hot = one_hot_of(codes_of(place, rank, cap, pieces), half * per, half * per)
    copies[2].wait()
    packed = dot(one_hot, stack_pieces(hidden_ref[...], pieces)).astype(BF16)
    for s in range(half):
        far_refs[s][...] = packed[s * per : (s + 1) * per]


def pack_near_kernel(cap, pieces, place_ref, rank_ref, hidden_ref, near_ref):
    one_hot = one_hot_of(codes_of(place_ref[...], rank_ref[...], cap, pieces), 0, near_ref.shape[0])
    near_ref[...] = dot(one_hot, stack_pieces(hidden_ref[...], pieces)).astype(BF16)


def shrink_kernel(cap, pieces, count, *refs):
    received_refs, down_ref, out_ref = refs[:count], refs[count], refs[-1]
    per = pieces * cap
    width = received_refs[0].shape[1]
    rank2 = down_ref.shape[2]
    received = jnp.concatenate([ref[...] for ref in received_refs], axis=0)
    size = received.shape[0]
    total = jnp.zeros((size, rank2), F32)
    piece_of = (iota((size, rank2), 0) // cap) % pieces
    for piece in range(pieces):
        part = dot(received, down_ref[0, piece * width : (piece + 1) * width, :])
        total = total + jnp.where(piece_of == piece, part, 0.0)
    out_row, in_row = iota((size // pieces, size), 0), iota((size // pieces, size), 1)
    same = (out_row // cap == in_row // per) & (out_row % cap == in_row % cap)
    out_ref[...] = exact_select(same.astype(F32).astype(BF16), total)


def expand_kernel(cap, mine_ref, other_ref, up_ref, *out_refs):
    rank = up_ref.shape[2]
    head = 128
    blocks = up_ref.shape[3] // head
    reduced = (mine_ref[...] + other_ref[...]).astype(BF16)
    terms = []
    for c in range(2):
        kept = reduced[:, c * rank : (c + 1) * rank]
        wide = dot(kept, up_ref[0, c]).astype(BF16)
        terms += [wide[:, g * head : (g + 1) * head] for g in range(blocks)]
    stacked = jnp.concatenate(terms, axis=0)
    pieces = 2 * blocks
    per = pieces * cap
    size = stacked.shape[0]
    out_row, in_row = iota((size, size), 0), iota((size, size), 1)
    source = (out_row // cap % pieces) * (size // pieces) + (out_row // per) * cap + out_row % cap
    moved = dot((source == in_row).astype(F32).astype(BF16), stacked).astype(BF16)
    each = size // len(out_refs)
    for s, out_ref in enumerate(out_refs):
        out_ref[...] = moved[s * each : (s + 1) * each]


def precombine_kernel(cap, near_ref, place_ref, rank_ref, mine_ref, other_ref, base_ref, far_ref):
    rows = base_ref.shape[0]
    head = 128
    groups = base_ref.shape[1] // (2 * head)
    pieces = 2 * groups
    size = near_ref.shape[0]
    codes = codes_of(place_ref[...], rank_ref[...], cap, pieces)
    delta = dot_first(one_hot_of(codes, 0, size), near_ref[...])
    for g in range(groups):
        for c in range(2):
            at = (g * 2 + c) * head
            piece = c * groups + g
            value = mine_ref[:, at : at + head] + other_ref[:, at : at + head]
            base_ref[:, at : at + head] = value + delta[piece * rows : (piece + 1) * rows]
    same = (iota((size, size), 0) == iota((size, size), 1)).astype(F32).astype(BF16)
    far_ref[...] = dot_first(one_hot_of(codes, size, size), same).astype(BF16)


def combine_kernel(*refs):
    delta_refs = refs[:-8]
    one_hot_ref, base_ref, query_ref, max_ref, sum_ref, acc_ref, token_ref, out_ref = refs[-8:]
    rows = base_ref.shape[0]
    head = 128
    groups = base_ref.shape[1] // (2 * head)
    received = jnp.concatenate([ref[...] for ref in delta_refs], axis=0)
    delta = dot(one_hot_ref[...], received)
    heads = query_ref.shape[1] // head
    per_group = heads // groups
    scale = head ** (-0.5)
    lane = iota((rows, head), 1)
    own = jnp.zeros((rows, head), F32)
    values = []
    for g in range(groups):
        made = []
        for c in range(2):
            at = (g * 2 + c) * head
            piece = c * groups + g
            made.append((base_ref[:, at : at + head] + delta[piece * rows : (piece + 1) * rows]).astype(BF16))
            token_ref[:, at : at + head] = made[-1]
        key = made[0].astype(F32)
        values.append(made[1].astype(F32))
        for h in range(g * per_group, (g + 1) * per_group):
            query = query_ref[:, h * head : (h + 1) * head].astype(F32)
            own = jnp.where(lane == h, jnp.sum(query * key, axis=1, keepdims=True), own)
    own = own[:, :heads] * scale
    cache_max = max_ref[...]
    highest = jnp.maximum(own, cache_max)
    cache_factor = jnp.exp(cache_max - highest)
    own_factor = jnp.exp(own - highest)
    inverse = 1.0 / (sum_ref[...] * cache_factor + own_factor)
    cache_factor = cache_factor * inverse
    own_factor = own_factor * inverse
    for h in range(heads):
        lanes = slice(h * head, (h + 1) * head)
        out = acc_ref[:, lanes] * cache_factor[:, h : h + 1]
        out = out + values[h // per_group] * own_factor[:, h : h + 1]
        out_ref[:, lanes] = out.astype(BF16)


VMEM = pl.BlockSpec(memory_space=pltpu.VMEM)
SMEM = pl.BlockSpec(memory_space=pltpu.SMEM)
HBM = pl.BlockSpec(memory_space=pltpu.HBM)
ANY = pl.BlockSpec(memory_space=pl.ANY)


def call(kernel, outs, flops, bytes_accessed, specs, scratch=()):
    return pl.pallas_call(
        kernel,
        out_shape=outs,
        in_specs=specs,
        out_specs=[VMEM] * len(outs),
        scratch_shapes=scratch,
        compiler_params=pltpu.CompilerParams(vmem_limit_bytes=VMEM_LIMIT),
        cost_estimate=pl.CostEstimate(flops=flops, bytes_accessed=bytes_accessed, transcendentals=0),
    )


def shards(
    hidden,
    queries,
    key_value_weight,
    adapter_down_weight,
    adapter_up_weight,
    stored_cache_keys,
    stored_cache_values,
    row_adapter_index,
    stored_cache_lengths,
    adapter_slot_table,
):
    n = lax.axis_size("pool")
    rows, width = hidden.shape
    cap = -(-2 * rows // n)
    pieces = split_count(cap)
    groups = stored_cache_keys.shape[1]
    head = stored_cache_keys.shape[3]
    columns = key_value_weight.shape[1] // 2
    out_pieces = 2 * groups
    rank2 = adapter_down_weight.shape[2]

    swap = functools.partial(lax.ppermute, axis_name="tp", perm=[(0, 1), (1, 0)])

    half = n // 2
    per = pieces * cap
    me = lax.axis_index("pool").reshape(1)
    place, rank, *far = call(
        functools.partial(pack_far_kernel, n, cap, pieces),
        [jax.ShapeDtypeStruct((1, rows), I32)] * 2
        + [jax.ShapeDtypeStruct((per, width // pieces), BF16)] * half,
        n * cap * width * 64,
        2 * rows * width * 2,
        [SMEM, HBM, HBM, HBM],
        [
            pltpu.VMEM((1, rows), I32),
            pltpu.VMEM((1, n), I32),
            pltpu.VMEM((rows, width), BF16),
            pltpu.SemaphoreType.DMA((3,)),
        ],
    )(me, row_adapter_index.reshape(1, rows), adapter_slot_table.reshape(1, n), hidden)

    def far_exchange(chunks):
        return [
            lax.ppermute(chunk, "pool", [(i, i ^ s) for i in range(n)])
            for s, chunk in enumerate(chunks, half)
        ]

    near_exchange = functools.partial(
        lax.all_to_all,
        axis_name="pool",
        split_axis=0,
        concat_axis=0,
        tiled=True,
        axis_index_groups=[list(range(half)), list(range(half, n))],
    )
    far = far_exchange(far)
    (near,) = call(
        functools.partial(pack_near_kernel, cap, pieces),
        [jax.ShapeDtypeStruct((half * per, width // pieces), BF16)],
        n * cap * width * 64,
        2 * rows * width * 2,
        [VMEM] * 3,
    )(place, rank, hidden)
    near = near_exchange(near)

    core = lax.axis_index("tp")
    partial_sum = jnp.dot(hidden, key_value_weight, preferred_element_type=F32)
    base_mine = lax.dynamic_slice_in_dim(partial_sum, core * columns, columns, axis=1)
    base_other = swap(lax.dynamic_slice_in_dim(partial_sum, (1 - core) * columns, columns, axis=1))

    query_heads = queries.reshape(rows, groups, -1, head)
    scores = jnp.einsum("rgqd,rgpd->rgqp", query_heads, stored_cache_keys, preferred_element_type=F32)
    scores = scores * (head ** (-0.5))
    valid = jnp.arange(stored_cache_keys.shape[2])[None, :] < stored_cache_lengths[:, None]
    scores = jnp.where(valid[:, None, None, :], scores, -jnp.inf)
    cache_max = jnp.max(scores, axis=-1)
    weights = jnp.exp(scores - cache_max[..., None])
    cache_sum = jnp.sum(weights, axis=-1).reshape(rows, -1)
    attended = jnp.einsum(
        "rgqp,rgpd->rgqd", weights.astype(BF16), stored_cache_values, preferred_element_type=F32
    ).reshape(rows, -1)
    cache_max = cache_max.reshape(rows, -1)

    def correct(chunks, outs, *after):
        count = len(chunks)
        (reduced,) = call(
            functools.partial(shrink_kernel, cap, pieces, count),
            [jax.ShapeDtypeStruct((half * cap, rank2), F32)],
            n * cap * width * rank2,
            half * cap * width * 2 + width * rank2 * 2,
            [VMEM] * (count + 1) + [ANY] * len(after),
        )(*chunks, adapter_down_weight, *after)
        return call(
            functools.partial(expand_kernel, cap),
            [jax.ShapeDtypeStruct((half * out_pieces * cap // outs, head), BF16)] * outs,
            n * cap * rank2 * columns,
            half * cap * columns * 4,
            [VMEM] * 3,
        )(reduced, swap(reduced), adapter_up_weight)

    size = half * out_pieces * cap
    base, far_one_hot = call(
        functools.partial(precombine_kernel, cap),
        [
            jax.ShapeDtypeStruct((rows, columns), F32),
            jax.ShapeDtypeStruct((out_pieces * rows, size), BF16),
        ],
        4 * size * columns * rows,
        rows * columns * 12,
        [VMEM] * 5,
    )(near_exchange(correct([near], 1)[0]), place, rank, base_mine, base_other)
    token, out = call(
        combine_kernel,
        [jax.ShapeDtypeStruct((rows, columns), BF16), jax.ShapeDtypeStruct(queries.shape, BF16)],
        2 * size * columns * rows,
        rows * 2048 * 8,
        [VMEM] * (half + 6),
    )(
        *far_exchange(correct(far, half, base, attended)),
        far_one_hot,
        base,
        queries,
        cache_max,
        cache_sum,
        attended,
    )
    return token, out


def solution(mesh):
    in_specs = (
        P(("grp", "pool"), "tp"),
        P(("grp", "pool"), "tp"),
        P("tp", None),
        P("pool", "tp", None),
        P("pool", None, None, "tp"),
        P(("grp", "pool"), "tp", None, None),
        P(("grp", "pool"), "tp", None, None),
        P(("grp", "pool"), None),
        P(("grp", "pool")),
        P(),
    )
    out_specs = (P(("grp", "pool"), "tp"), P(("grp", "pool"), "tp"))
    return jax.shard_map(shards, mesh=mesh, in_specs=in_specs, out_specs=out_specs, check_vma=False)
```

time: 48.8 us -> 59.1 us (1.21)
  starting transfers between devices: 19.6 us -> 25.1 us
  local copies, waits for them, and re-layouts: 4.46 us -> 7.17 us
  waiting for transfers between devices: 5.99 us -> 6.69 us
  other arithmetic: 1.4 us -> 2.05 us
    ppermute x5 -> x10, starting transfers between devices: 7.95 us -> 17 us  [the longest x8 17 us: far_exchange(): lax.ppermute(chunk, 'pool', [(i, i ^ s) for i in range(n)])]
    all_to_all x2, starting transfers between devices: 11.6 us -> 7.62 us  [the longest x1 4.16 us: shards(): near_exchange(correct([near], 1)[0])]
    ppermute x5 -> x10, waiting for transfers between devices: 0.62 us -> 3.42 us  [the longest x8 2.21 us: far_exchange(): lax.ppermute(chunk, 'pool', [(i, i ^ s) for i in range(n)])]
    all_to_all x2, waiting for transfers between devices: 5.37 us -> 3.27 us  [the longest x1 3.27 us: shards(): near_exchange(correct([near], 1)[0])]
    unnamed x18 -> x20, local copies, waits for them, and re-layouts: 2.56 us -> 4.48 us
    reduce_max x1, local copies, waits for them, and re-layouts: 0.07 us -> 0.86 us  [shards(): cache_max = jnp.max(scores, axis=-1)]
    lt x1, other arithmetic: 0.07 us -> 0.73 us  [shards(): jnp.arange(stored_cache_keys.shape[2])[None, :]]
    pallas_call x4 -> x8, Pallas kernels: 6.46 us -> 6.95 us  [the longest x2 1.53 us: correct(): call(functools.partial(shrink_kernel, cap, pieces, count), [jax.ShapeDtyp...]
  transfers between devices with their start and end apart: 8 -> 13, of which waited for: 2 -> 3; matrix products, arithmetic and copies ran while one was open for 27% -> 26% of each run, Pallas kernels for 5% -> 5%
where the time goes in v4:
time: 59.1 us; the launch traced here: 58.5 us
  starting transfers between devices  25.1 us (42%)
  matrix products  9.66 us (16%)
  local copies, waits for them, and re-layouts  7.17 us (12%)
  Pallas kernels  6.95 us (12%)
  waiting for transfers between devices  6.69 us (11%)
  other arithmetic  2.05 us (3%)
  between operations  0.84 us (1%)
    ppermute x8, starting transfers between devices, far_exchange(): lax.ppermute(chunk, 'pool', [(i, i ^ s) for i in range(n)])  17 us
    dot_general x1, matrix products, shards(): partial_sum = jnp.dot(hidden, key_value_weight, preferred_element_type=F32)  5.85 us
    unnamed x20, local copies, waits for them, and re-layouts  4.48 us
    all_to_all x1, starting transfers between devices, shards(): near_exchange(correct([near], 1)[0])  4.16 us
    all_to_all x1, starting transfers between devices, shards(): near = near_exchange(near)  3.46 us
    all_to_all x1, waiting for transfers between devices, shards(): near_exchange(correct([near], 1)[0])  3.27 us
    dot_general x1, matrix products, shards(): jnp.einsum('rgqd,rgpd->rgqp', query_heads, stored_cache_keys, preferred_e...  2.44 us
    ppermute x8, waiting for transfers between devices, far_exchange(): lax.ppermute(chunk, 'pool', [(i, i ^ s) for i in range(n)])  2.21 us
  transfers between devices with their start and end apart: 13, of which 3 were waited for; matrix products, arithmetic and copies ran while one was open for 26% of the time, Pallas kernels for 5%

profile of v4, /device:TPU:0, one launch (start us, length us, event | category | flops | bytes accessed | tf_op | source)
XLA Modules:
  0.0 58.5 jit_solution(15715048036756118093)
XLA Ops:
  0.6 0.0 copy-start
  0.7 0.0 copy-start.1
  0.7 1.1 %copy-done.1 = bf16[48,4096]{1,0:T(8,128)(2,1)S(1)} copy-done((bf16[48,4096]{1,0:T(8,128)(2,1)S(1)}, bf16[48,4096]{1,0:T(8,128)(2,1)}, u32[]{:S(2)}) %copy-start.1) | copy-done | bytes 393240
  1.7 0.7 %copy-done.6 = s32[48,1]{0,1:T(1,128)S(1)} copy-done((s32[48,1]{0,1:T(1,128)S(1)}, s32[48,1]{0,1:T(1,128)}, u32[]{:S(2)}) %copy-start.6) | copy-done | bytes 216
  2.4 0.7 %copy-done.7 = s32[8]{0:T(128)S(1)} copy-done((s32[8]{0:T(128)S(1)}, s32[8]{0:T(128)}, u32[]{:S(2)}) %copy-start.7) | copy-done | bytes 56
  3.0 1.4 %shard_map.113 = (s32[1,48]{1,0:T(1,128)S(1)}, s32[1,48]{1,0:T(1,128)S(1)}, bf16[48,1024]{1,0:T(8,128)(2,1)}, bf16[48,1024]{1,0:T(8,128)(2,1)}, bf16[48,1024]{1,...) custom-call(s32[1]{0:T(128)} %bitcast.me_ref, s32[1,48]{1,0:T(1,128)S(1)} %bitcast.27, s32[1,8]{1,0:T(1,128)S(1)} %bitcast.28, ...), custom_call_target="tpu_custom_call" | custom-call | flops 25165824 | bytes 786432 | tf_op jit(solution)/shard_map/pallas_call | solution.py:240
  4.5 4.1 %collective-permute-start = (bf16[48,1024]{1,0:T(8,128)(2,1)}, bf16[48,1024]{1,0:T(8,128)(2,1)S(1)}, u32[]{:S(2)}, u32[]{:S(2)}) collective-permute-start(bf16[48,1024]{1,0:T(8,128)(2,1)} %get-tuple-element.14), channel_id=1, source_target_pairs={{0,8},{2,10},{4,12},{6,14},{8,0},{10,2},{12,4},{14,6},{1,9},{3,11}... | collective-permute-start | bytes 294920 | tf_op jit(solution)/shard_map/ppermute | solution.py:257
  8.6 1.3 %collective-permute-start.1 = (bf16[48,1024]{1,0:T(8,128)(2,1)}, bf16[48,1024]{1,0:T(8,128)(2,1)S(1)}, u32[]{:S(2)}, u32[]{:S(2)}) collective-permute-start(bf16[48,1024]{1,0:T(8,128)(2,1)} %get-tuple-element.15), channel_id=1, source_target_pairs={{0,10},{2,8},{4,14},{6,12},{8,2},{10,0},{12,6},{14,4},{1,11},{3,9}... | collective-permute-start | bytes 294920 | tf_op jit(solution)/shard_map/ppermute | solution.py:257
  9.9 3.6 %collective-permute-start.2 = (bf16[48,1024]{1,0:T(8,128)(2,1)S(1)}, bf16[48,1024]{1,0:T(8,128)(2,1)S(1)}, u32[]{:S(2)}, u32[]{:S(2)}) collective-permute-start(bf16[48,1024]{1,0:T(8,128)(2,1)S(1)} %get-tuple-element.16), channel_id=1, source_target_pairs={{0,12},{2,14},{4,8},{6,10},{8,4},{10,6},{12,0},{14,2},{1,13},{3,15... | collective-permute-start | bytes 294920 | tf_op jit(solution)/shard_map/ppermute | solution.py:257
  13.5 0.0 collective-permute-start.3
  13.5 1.0 %copy-done.2 = bf16[48,4096]{1,0:T(8,128)(2,1)S(1)} copy-done((bf16[48,4096]{1,0:T(8,128)(2,1)S(1)}, bf16[48,4096]{1,0:T(8,128)(2,1)}, u32[]{:S(2)}) %copy-start.2) | copy-done | bytes 393240
  14.5 1.1 %shard_map.114 = bf16[192,1024]{1,0:T(8,128)(2,1)} custom-call(s32[1,48]{1,0:T(1,128)S(1)} %get-tuple-element.18.place_ref, s32[1,48]{1,0:T(1,128)S(1)} %get-tuple-element.19.rank_ref, bf16[48,4096]{1,0:T(8,128)(2,1)S(1)} %copy-done.2), custom_call_target="tpu_custom_call" | custom-call | flops 25165824 | bytes 786432 | tf_op jit(solution)/shard_map/pallas_call | solution.py:270
  15.5 3.5 %all-to-all-start = ((bf16[4,48,1024]{2,1,0:T(8,128)(2,1)}), bf16[4,48,1024]{2,1,0:T(8,128)(2,1)S(1)}, u32[]{:S(2)}, u32[]{:S(2)}) async-start(bf16[4,48,1024]{2,1,0:T(8,128)(2,1)} %bitcast.3), calls=%async_computation | async-start | bytes 786432 | tf_op jit(solution)/shard_map/all_to_all | solution.py:277
  19.0 1.0 %copy.19 = bf16[6,8,16,128]{3,2,1,0:T(8,128)(2,1)S(1)} copy(bf16[6,8,16,128]{3,1,2,0:T(8,128)(2,1)} %bitcast.25) | data formatting | bytes 393216
  20.0 0.7 %iota_compare_fusion = pred[48,32]{1,0:T(8,128)(4,1)S(1)} fusion(s32[48]{0:T(128)} %param.18), kind=kLoop, calls=%fused_computation.8 | loop fusion | flops 1536 | bytes 1728 | tf_op jit(solution)/shard_map/lt | solution.py:287
  20.7 2.4 %fusion.6 = (f32[48,2,8]{2,1,0:T(2,128)S(1)}, f32[48,2,8,32]{3,2,1,0:T(8,128)}) fusion(bf16[48,2,8,128]{3,2,1,0:T(8,128)(2,1)S(1)} %bitcast.29, bf16[48,2,32,128]{3,2,1,0:T(8,128)(2,1)} %param.15, pred[48,32]{1,0:T(8,128)(4,1)S(1)} %iota_compare_fusion), kind=kOutput, calls=%fused_computation.11 | convolution fusion | flops 6364416 | bytes 1085952 | tf_op jit(solution)/shard_map/rgqd,rgpd->rgqp/dot_general | solution.py:285
  23.1 0.0 copy-start.3
  23.2 0.0 copy-start.5
  23.2 5.8 %fusion.7 = f32[48,1024]{1,0:T(8,128)} fusion(bf16[48,4096]{1,0:T(8,128)(2,1)} %hidden_ref.1, bf16[4096,1024]{1,0:T(8,128)(2,1)} %param.12), kind=kOutput, calls=%fused_computation.12 | convolution fusion | flops 402653184 | bytes 8978432 | tf_op jit(solution)/shard_map/dot_general | solution.py:280
  29.0 0.8 %shard_map.115.mine_ref = f32[48,128]{1,0:T(8,128)S(1)} custom-call(bf16[192,1024]{1,0:T(8,128)(2,1)S(1)} %bitcast.24, bf16[1,4096,128]{2,1,0:T(8,128)(2,1)S(1)} %copy-done.3), custom_call_target="tpu_custom_call" | custom-call | flops 50331648 | bytes 1441792 | tf_op jit(solution)/shard_map/pallas_call | solution.py:299
  29.8 0.0 collective-permute-start.4
  29.8 1.6 %constant_dynamic-slice_fusion = (f32[48,512]{1,0:T(8,128)}, f32[48,512]{1,0:T(8,128)S(1)}) fusion(f32[48,1024]{1,0:T(8,128)} %fusion.7, s32[]{:T(128)S(6)} %select_n.11, s32[]{:T(128)S(6)} %select_n.10), kind=kLoop, calls=%fused_computation.9 | loop fusion | bytes 393224 | tf_op jit(solution)/shard_map/dynamic_slice | solution.py:282
  31.4 0.5 collective-permute-start.5
  31.9 1.0 %shard_map.116 = bf16[192,128]{1,0:T(8,128)(2,1)} custom-call(f32[48,128]{1,0:T(8,128)S(1)} %shard_map.115.mine_ref, f32[48,128]{1,0:T(8,128)S(1)} %collective-permute-done.4.other_ref, bf16[1,2,64,256]{3,2,1,0:T(8,128)(2,1)S(1)} %copy-done.5), custom_call_target="tpu_custom_call" | custom-call | flops 6291456 | bytes 98304 | tf_op jit(solution)/shard_map/pallas_call | solution.py:306
  32.9 4.2 %all-to-all-start.1 = ((bf16[4,48,128]{2,1,0:T(8,128)(2,1)}), bf16[4,48,128]{2,1,0:T(8,128)(2,1)S(1)}, u32[]{:S(2)}, u32[]{:S(2)}) async-start(bf16[4,48,128]{2,1,0:T(8,128)(2,1)} %bitcast.5), calls=%async_computation.1 | async-start | bytes 98304 | tf_op jit(solution)/shard_map/all_to_all | solution.py:324
  37.0 1.4 %fusion.3 = f32[48,2,8,128]{3,2,1,0:T(8,128)S(1)} fusion(bf16[48,2,32,128]{3,2,1,0:T(8,128)(2,1)S(1)} %copy-done, f32[48,2,8,32]{3,2,1,0:T(8,128)} %get-tuple-element.29, f32[48,2,8]{2,1,0:T(2,128)S(1)} %get-tuple-element.28), kind=kOutput, calls=%fused_computation.6 | convolution fusion | flops 6340608 | bytes 1281024 | tf_op jit(solution)/shard_map/rgqp,rgpd->rgqd/dot_general | solution.py:292
  38.4 0.1 copy.22
  38.6 0.0 collective-permute-done.5.other_ref
  38.6 3.3 %all-to-all-done.1 = bf16[4,48,128]{2,1,0:T(8,128)(2,1)S(1)} async-done(((bf16[4,48,128]{2,1,0:T(8,128)(2,1)}), bf16[4,48,128]{2,1,0:T(8,128)(2,1)S(1)}, u32[]{:S(2)}, u32[]{:S(2)}) %all-to-all-start.1) | async-done | bytes 49184 | tf_op jit(solution)/shard_map/all_to_all | solution.py:324
  41.8 0.3 shard_map.117
  42.2 0.0 collective-permute-done.2.refs_2_
  42.2 0.8 %shard_map.118.mine_ref = f32[48,128]{1,0:T(8,128)S(1)} custom-call(bf16[48,1024]{1,0:T(8,128)(2,1)S(1)} %collective-permute-done.refs_0_, bf16[48,1024]{1,0:T(8,128)(2,1)S(1)} %collective-permute-done.1.refs_1_, bf16[48,1024]{1,0:T(8,128)(2,1)S(1)} %collective-permute-done.2.refs_2_, bf16[48,1024]{1,0:T(8,128)(2,1)S(1)} %collective-permute-done.3.refs_3_, ...), custom_call_target="tpu_custom_call" | custom-call | flops 50331648 | bytes 1441792 | tf_op jit(solution)/shard_map/pallas_call | solution.py:299
  43.0 0.0 collective-permute-start.6
  43.0 1.2 %collective-permute-done.6.other_ref = f32[48,128]{1,0:T(8,128)S(1)} collective-permute-done((f32[48,128]{1,0:T(8,128)S(1)}, f32[48,128]{1,0:T(8,128)S(1)}, u32[]{:S(2)}, u32[]{:S(2)}) %collective-permute-start.6) | collective-permute-done | bytes 24608 | tf_op jit(solution)/shard_map/ppermute | solution.py:312
  44.2 0.3 shard_map.119
  44.5 3.2 %collective-permute-start.7 = (bf16[48,128]{1,0:T(8,128)(2,1)S(1)}, bf16[48,128]{1,0:T(8,128)(2,1)S(1)}, u32[]{:S(2)}, u32[]{:S(2)}) collective-permute-start(bf16[48,128]{1,0:T(8,128)(2,1)S(1)} %get-tuple-element.21), channel_id=1, source_target_pairs={{0,8},{2,10},{4,12},{6,14},{8,0},{10,2},{12,4},{14,6},{1,9},{3,11}... | collective-permute-start | bytes 36872 | tf_op jit(solution)/shard_map/ppermute | solution.py:257
  47.7 0.2 collective-permute-start.8
  47.9 2.8 %collective-permute-start.9 = (bf16[48,128]{1,0:T(8,128)(2,1)S(1)}, bf16[48,128]{1,0:T(8,128)(2,1)S(1)}, u32[]{:S(2)}, u32[]{:S(2)}) collective-permute-start(bf16[48,128]{1,0:T(8,128)(2,1)S(1)} %get-tuple-element.23), channel_id=1, source_target_pairs={{0,12},{2,14},{4,8},{6,10},{8,4},{10,6},{12,0},{14,2},{1,13},{3,15... | collective-permute-start | bytes 36872 | tf_op jit(solution)/shard_map/ppermute | solution.py:257
  50.8 1.7 %collective-permute-start.10 = (bf16[48,128]{1,0:T(8,128)(2,1)S(1)}, bf16[48,128]{1,0:T(8,128)(2,1)S(1)}, u32[]{:S(2)}, u32[]{:S(2)}) collective-permute-start(bf16[48,128]{1,0:T(8,128)(2,1)S(1)} %get-tuple-element.24), channel_id=1, source_target_pairs={{0,14},{2,12},{4,10},{6,8},{8,6},{10,4},{12,2},{14,0},{1,15},{3,13... | collective-permute-start | bytes 36872 | tf_op jit(solution)/shard_map/ppermute | solution.py:257
  52.5 1.3 %fusion.1 = f32[48,2,8]{2,1,0:T(2,128)S(1)} fusion(f32[48,2,8,32]{3,2,1,0:T(8,128)} %get-tuple-element.29, f32[48,2,8]{2,1,0:T(2,128)} %copy-done.8), kind=kLoop, calls=%fused_computation.4 | loop fusion | flops 48384 | bytes 104448 | tf_op jit(solution)/shard_map/reduce_sum | solution.py:291
  53.9 0.9 %copy.15 = f32[48,2,8]{0,2,1:T(8,128)S(1)} copy(f32[48,2,8]{2,1,0:T(2,128)} %copy-done.8) | data formatting | bytes 6144 | tf_op jit(solution)/shard_map/reduce_max | solution.py:289
  54.7 0.1 copy.17.refs_7_
  54.8 0.1 copy.16
  54.9 0.1 copy.18.refs_8_
  55.0 0.0 collective-permute-done.7.refs_0_
  55.0 0.0 collective-permute-done.8.refs_1_
  55.0 2.2 %collective-permute-done.10.refs_3_ = bf16[48,128]{1,0:T(8,128)(2,1)S(1)} collective-permute-done((bf16[48,128]{1,0:T(8,128)(2,1)S(1)}, bf16[48,128]{1,0:T(8,128)(2,1)S(1)}, u32[]{:S(2)}, u32[]{:S(2)}) %collective-permute-start.10) | collective-permute-done | bytes 12320 | tf_op jit(solution)/shard_map/ppermute | solution.py:257
  57.2 1.3 %shard_map.120 = (bf16[48,512]{1,0:T(8,128)(2,1)}, bf16[48,2048]{1,0:T(8,128)(2,1)}) custom-call(bf16[48,128]{1,0:T(8,128)(2,1)S(1)} %collective-permute-done.7.refs_0_, bf16[48,128]{1,0:T(8,128)(2,1)S(1)} %collective-permute-done.8.refs_1_, bf16[48,128]{1,0:T(8,128)(2,1)S(1)} %collective-permute-done.9.refs_2_, ...), custom_call_target="tpu_custom_call" | custom-call | flops 9437184 | bytes 786432 | tf_op jit(solution)/shard_map/pallas_call | solution.py:325
  (16 shorter events, 0.0 us)
Async XLA Ops:
  0.6 36.4 %copy-start = (bf16[48,2,32,128]{3,2,1,0:T(8,128)(2,1)S(1)}, bf16[48,2,32,128]{3,2,1,0:T(8,128)(2,1)}, u32[]{:S(2)}) copy-start(bf16[48,2,32,128]{3,2,1,0:T(8,128)(2,1)} %param.16) | copy-start | bytes 2359300
  0.7 1.1 %copy-start.1 = (bf16[48,4096]{1,0:T(8,128)(2,1)S(1)}, bf16[48,4096]{1,0:T(8,128)(2,1)}, u32[]{:S(2)}) copy-start(bf16[48,4096]{1,0:T(8,128)(2,1)} %hidden_ref.1) | copy-start | bytes 1179652
  1.7 0.7 %copy-start.6 = (s32[48,1]{0,1:T(1,128)S(1)}, s32[48,1]{0,1:T(1,128)}, u32[]{:S(2)}) copy-start(s32[48,1]{0,1:T(1,128)} %param.17) | copy-start | bytes 580
  2.4 0.7 %copy-start.7 = (s32[8]{0:T(128)S(1)}, s32[8]{0:T(128)}, u32[]{:S(2)}) copy-start(s32[8]{0:T(128)} %param.19) | copy-start | bytes 100
  4.5 37.7 %collective-permute-start = (bf16[48,1024]{1,0:T(8,128)(2,1)}, bf16[48,1024]{1,0:T(8,128)(2,1)S(1)}, u32[]{:S(2)}, u32[]{:S(2)}) collective-permute-start(bf16[48,1024]{1,0:T(8,128)(2,1)} %get-tuple-element.14), channel_id=1, source_target_pairs={{0,8},{2,10},{4,12},{6,14},{8,0},{10,2},{12,4},{14,6},{1,9},{3,11}... | collective-permute-start | bytes 294920 | tf_op jit(solution)/shard_map/ppermute | solution.py:257
  8.6 33.6 %collective-permute-start.1 = (bf16[48,1024]{1,0:T(8,128)(2,1)}, bf16[48,1024]{1,0:T(8,128)(2,1)S(1)}, u32[]{:S(2)}, u32[]{:S(2)}) collective-permute-start(bf16[48,1024]{1,0:T(8,128)(2,1)} %get-tuple-element.15), channel_id=1, source_target_pairs={{0,10},{2,8},{4,14},{6,12},{8,2},{10,0},{12,6},{14,4},{1,11},{3,9}... | collective-permute-start | bytes 294920 | tf_op jit(solution)/shard_map/ppermute | solution.py:257
  9.9 32.3 %collective-permute-start.2 = (bf16[48,1024]{1,0:T(8,128)(2,1)S(1)}, bf16[48,1024]{1,0:T(8,128)(2,1)S(1)}, u32[]{:S(2)}, u32[]{:S(2)}) collective-permute-start(bf16[48,1024]{1,0:T(8,128)(2,1)S(1)} %get-tuple-element.16), channel_id=1, source_target_pairs={{0,12},{2,14},{4,8},{6,10},{8,4},{10,6},{12,0},{14,2},{1,13},{3,15... | collective-permute-start | bytes 294920 | tf_op jit(solution)/shard_map/ppermute | solution.py:257
  13.5 28.7 %collective-permute-start.3 = (bf16[48,1024]{1,0:T(8,128)(2,1)S(1)}, bf16[48,1024]{1,0:T(8,128)(2,1)S(1)}, u32[]{:S(2)}, u32[]{:S(2)}) collective-permute-start(bf16[48,1024]{1,0:T(8,128)(2,1)S(1)} %get-tuple-element.17), channel_id=1, source_target_pairs={{0,14},{2,12},{4,10},{6,8},{8,6},{10,4},{12,2},{14,0},{1,15},{3,13... | collective-permute-start | bytes 294920 | tf_op jit(solution)/shard_map/ppermute | solution.py:257
  13.5 1.0 %copy-start.2 = (bf16[48,4096]{1,0:T(8,128)(2,1)S(1)}, bf16[48,4096]{1,0:T(8,128)(2,1)}, u32[]{:S(2)}) copy-start(bf16[48,4096]{1,0:T(8,128)(2,1)} %hidden_ref.1) | copy-start | bytes 1179652
  15.5 13.5 %all-to-all-start = ((bf16[4,48,1024]{2,1,0:T(8,128)(2,1)}), bf16[4,48,1024]{2,1,0:T(8,128)(2,1)S(1)}, u32[]{:S(2)}, u32[]{:S(2)}) async-start(bf16[4,48,1024]{2,1,0:T(8,128)(2,1)} %bitcast.3), calls=%async_computation | async-start | bytes 786432 | tf_op jit(solution)/shard_map/all_to_all | solution.py:277
  23.1 13.9 %copy-start.8 = (f32[48,2,8]{2,1,0:T(2,128)}, f32[48,2,8]{2,1,0:T(2,128)S(1)}, u32[]{:S(2)}) copy-start(f32[48,2,8]{2,1,0:T(2,128)S(1)} %get-tuple-element.28) | copy-start | bytes 9220
  23.1 5.9 %copy-start.3 = (bf16[1,4096,128]{2,1,0:T(8,128)(2,1)S(1)}, bf16[1,4096,128]{2,1,0:T(8,128)(2,1)}, u32[]{:S(2)}) copy-start(bf16[1,4096,128]{2,1,0:T(8,128)(2,1)} %refs_4_.1) | copy-start | bytes 3145732
  23.2 8.8 %copy-start.5 = (bf16[1,2,64,256]{3,2,1,0:T(8,128)(2,1)S(1)}, bf16[1,2,64,256]{3,2,1,0:T(8,128)(2,1)}, u32[]{:S(2)}) copy-start(bf16[1,2,64,256]{3,2,1,0:T(8,128)(2,1)} %up_ref.3) | copy-start | bytes 196612
  29.0 28.2 %copy-start.4 = (bf16[48,2048]{1,0:T(8,128)(2,1)S(1)}, bf16[48,2048]{1,0:T(8,128)(2,1)}, u32[]{:S(2)}) copy-start(bf16[48,2048]{1,0:T(8,128)(2,1)} %refs_6_.1) | copy-start | bytes 589828
  29.8 1.6 %collective-permute-start.4 = (f32[48,128]{1,0:T(8,128)S(1)}, f32[48,128]{1,0:T(8,128)S(1)}, u32[]{:S(2)}, u32[]{:S(2)}) collective-permute-start(f32[48,128]{1,0:T(8,128)S(1)} %shard_map.115.mine_ref), channel_id=1, source_target_pairs={{0,1},{1,0},{2,3},{3,2},{4,5},{5,4},{6,7},{7,6},{8,9},{9,8},{10,11... | collective-permute-start | bytes 73736 | tf_op jit(solution)/shard_map/ppermute | solution.py:312
  31.4 7.2 %collective-permute-start.5 = (f32[48,512]{1,0:T(8,128)}, f32[48,512]{1,0:T(8,128)S(1)}, u32[]{:S(2)}, u32[]{:S(2)}) collective-permute-start(f32[48,512]{1,0:T(8,128)} %get-tuple-element.26), channel_id=1, source_target_pairs={{0,1},{1,0},{2,3},{3,2},{4,5},{5,4},{6,7},{7,6},{8,9},{9,8},{10,11... | collective-permute-start | bytes 294920 | tf_op jit(solution)/shard_map/ppermute | solution.py:282
  32.9 9.0 %all-to-all-start.1 = ((bf16[4,48,128]{2,1,0:T(8,128)(2,1)}), bf16[4,48,128]{2,1,0:T(8,128)(2,1)S(1)}, u32[]{:S(2)}, u32[]{:S(2)}) async-start(bf16[4,48,128]{2,1,0:T(8,128)(2,1)} %bitcast.5), calls=%async_computation.1 | async-start | bytes 98304 | tf_op jit(solution)/shard_map/all_to_all | solution.py:324
  43.0 1.2 %collective-permute-start.6 = (f32[48,128]{1,0:T(8,128)S(1)}, f32[48,128]{1,0:T(8,128)S(1)}, u32[]{:S(2)}, u32[]{:S(2)}) collective-permute-start(f32[48,128]{1,0:T(8,128)S(1)} %shard_map.118.mine_ref), channel_id=1, source_target_pairs={{0,1},{1,0},{2,3},{3,2},{4,5},{5,4},{6,7},{7,6},{8,9},{9,8},{10,11... | collective-permute-start | bytes 73736 | tf_op jit(solution)/shard_map/ppermute | solution.py:312
  44.5 10.4 %collective-permute-start.7 = (bf16[48,128]{1,0:T(8,128)(2,1)S(1)}, bf16[48,128]{1,0:T(8,128)(2,1)S(1)}, u32[]{:S(2)}, u32[]{:S(2)}) collective-permute-start(bf16[48,128]{1,0:T(8,128)(2,1)S(1)} %get-tuple-element.21), channel_id=1, source_target_pairs={{0,8},{2,10},{4,12},{6,14},{8,0},{10,2},{12,4},{14,6},{1,9},{3,11}... | collective-permute-start | bytes 36872 | tf_op jit(solution)/shard_map/ppermute | solution.py:257
  47.7 7.2 %collective-permute-start.8 = (bf16[48,128]{1,0:T(8,128)(2,1)S(1)}, bf16[48,128]{1,0:T(8,128)(2,1)S(1)}, u32[]{:S(2)}, u32[]{:S(2)}) collective-permute-start(bf16[48,128]{1,0:T(8,128)(2,1)S(1)} %get-tuple-element.22), channel_id=1, source_target_pairs={{0,10},{2,8},{4,14},{6,12},{8,2},{10,0},{12,6},{14,4},{1,11},{3,9}... | collective-permute-start | bytes 36872 | tf_op jit(solution)/shard_map/ppermute | solution.py:257
  47.9 7.0 %collective-permute-start.9 = (bf16[48,128]{1,0:T(8,128)(2,1)S(1)}, bf16[48,128]{1,0:T(8,128)(2,1)S(1)}, u32[]{:S(2)}, u32[]{:S(2)}) collective-permute-start(bf16[48,128]{1,0:T(8,128)(2,1)S(1)} %get-tuple-element.23), channel_id=1, source_target_pairs={{0,12},{2,14},{4,8},{6,10},{8,4},{10,6},{12,0},{14,2},{1,13},{3,15... | collective-permute-start | bytes 36872 | tf_op jit(solution)/shard_map/ppermute | solution.py:257
  50.8 6.4 %collective-permute-start.10 = (bf16[48,128]{1,0:T(8,128)(2,1)S(1)}, bf16[48,128]{1,0:T(8,128)(2,1)S(1)}, u32[]{:S(2)}, u32[]{:S(2)}) collective-permute-start(bf16[48,128]{1,0:T(8,128)(2,1)S(1)} %get-tuple-element.24), channel_id=1, source_target_pairs={{0,14},{2,12},{4,10},{6,8},{8,6},{10,4},{12,2},{14,0},{1,15},{3,13... | collective-permute-start | bytes 36872 | tf_op jit(solution)/shard_map/ppermute | solution.py:257

commit v5 on v4

--- a/solution.py
+++ b/solution.py
@@ -56,7 +56,7 @@
     )
 
 
-def pack_far_kernel(n, cap, pieces, me_ref, idx_hbm, table_hbm, hidden_hbm, place_ref, rank_ref, *refs):
+def pack_far_kernel(n, cap, pieces, me_ref, idx_hbm, table_hbm, hidden_hbm, slot_ref, place_ref, rank_ref, *refs):
     far_refs, (idx_ref, table_ref, hidden_ref, sems) = refs[:-4], refs[-4:]
     copies = [
         pltpu.make_async_copy(source, target, sems.at[i])
@@ -80,6 +80,7 @@
     rank = jnp.sum(member * count, axis=0, keepdims=True).astype(I32)
     apart = lax.bitwise_xor(slot, me_ref[0])
     place = jnp.where(apart < half, lax.bitwise_and(slot, half - 1), apart)
+    slot_ref[...] = slot
     place_ref[...] = place
     rank_ref[...] = rank
     one_hot = one_hot_of(codes_of(place, rank, cap, pieces), half * per, half * per)
@@ -111,11 +112,13 @@
     out_ref[...] = exact_select(same.astype(F32).astype(BF16), total)
 
 
-def expand_kernel(cap, mine_ref, other_ref, up_ref, *out_refs):
+def expand_kernel(n, cap, me_ref, near_ref, near_other_ref, far_ref, far_other_ref, up_ref, out_ref):
     rank = up_ref.shape[2]
     head = 128
     blocks = up_ref.shape[3] // head
-    reduced = (mine_ref[...] + other_ref[...]).astype(BF16)
+    reduced = jnp.concatenate(
+        [near_ref[...] + near_other_ref[...], far_ref[...] + far_other_ref[...]], axis=0
+    ).astype(BF16)
     terms = []
     for c in range(2):
         kept = reduced[:, c * rank : (c + 1) * rank]
@@ -124,41 +127,31 @@
     stacked = jnp.concatenate(terms, axis=0)
     pieces = 2 * blocks
     per = pieces * cap
-    size = stacked.shape[0]
+    size = n * per
+    half = n // 2
     out_row, in_row = iota((size, size), 0), iota((size, size), 1)
-    source = (out_row // cap % pieces) * (size // pieces) + (out_row // per) * cap + out_row % cap
-    moved = dot((source == in_row).astype(F32).astype(BF16), stacked).astype(BF16)
-    each = size // len(out_refs)
-    for s, out_ref in enumerate(out_refs):
-        out_ref[...] = moved[s * each : (s + 1) * each]
-
-
-def precombine_kernel(cap, near_ref, place_ref, rank_ref, mine_ref, other_ref, base_ref, far_ref):
+    apart = lax.bitwise_xor(out_row // per, me_ref[0])
+    place = jnp.where(apart < half, lax.bitwise_and(out_row // per, half - 1), apart)
+    source = (out_row // cap % pieces) * (n * cap) + place * cap + out_row % cap
+    out_ref[...] = dot((source == in_row).astype(F32).astype(BF16), stacked).astype(BF16)
+
+
+def prepare_kernel(cap, slot_ref, rank_ref, mine_ref, other_ref, base_ref, one_hot_ref):
+    pieces = one_hot_ref.shape[0] // slot_ref.shape[1]
+    size = one_hot_ref.shape[1]
+    base_ref[...] = mine_ref[...] + other_ref[...]
+    one_hot = one_hot_of(codes_of(slot_ref[...], rank_ref[...], cap, pieces), 0, size)
+    same = (iota((size, size), 0) == iota((size, size), 1)).astype(F32).astype(BF16)
+    one_hot_ref[...] = dot_first(one_hot, same).astype(BF16)
+
+
+def combine_kernel(
+    delta_ref, one_hot_ref, base_ref, query_ref, max_ref, sum_ref, acc_ref, token_ref, out_ref
+):
     rows = base_ref.shape[0]
     head = 128
     groups = base_ref.shape[1] // (2 * head)
-    pieces = 2 * groups
-    size = near_ref.shape[0]
-    codes = codes_of(place_ref[...], rank_ref[...], cap, pieces)
-    delta = dot_first(one_hot_of(codes, 0, size), near_ref[...])
-    for g in range(groups):
-        for c in range(2):
-            at = (g * 2 + c) * head
-            piece = c * groups + g
-            value = mine_ref[:, at : at + head] + other_ref[:, at : at + head]
-            base_ref[:, at : at + head] = value + delta[piece * rows : (piece + 1) * rows]
-    same = (iota((size, size), 0) == iota((size, size), 1)).astype(F32).astype(BF16)
-    far_ref[...] = dot_first(one_hot_of(codes, size, size), same).astype(BF16)
-
-
-def combine_kernel(*refs):
-    delta_refs = refs[:-8]
-    one_hot_ref, base_ref, query_ref, max_ref, sum_ref, acc_ref, token_ref, out_ref = refs[-8:]
-    rows = base_ref.shape[0]
-    head = 128
-    groups = base_ref.shape[1] // (2 * head)
-    received = jnp.concatenate([ref[...] for ref in delta_refs], axis=0)
-    delta = dot(one_hot_ref[...], received)
+    delta = dot(one_hot_ref[...], delta_ref[...])
     heads = query_ref.shape[1] // head
     per_group = heads // groups
     scale = head ** (-0.5)
@@ -237,9 +230,9 @@
     half = n // 2
     per = pieces * cap
     me = lax.axis_index("pool").reshape(1)
-    place, rank, *far = call(
+    slot, place, rank, *far = call(
         functools.partial(pack_far_kernel, n, cap, pieces),
-        [jax.ShapeDtypeStruct((1, rows), I32)] * 2
+        [jax.ShapeDtypeStruct((1, rows), I32)] * 3
         + [jax.ShapeDtypeStruct((per, width // pieces), BF16)] * half,
         n * cap * width * 64,
         2 * rows * width * 2,
@@ -252,21 +245,9 @@
         ],
     )(me, row_adapter_index.reshape(1, rows), adapter_slot_table.reshape(1, n), hidden)
 
-    def far_exchange(chunks):
-        return [
-            lax.ppermute(chunk, "pool", [(i, i ^ s) for i in range(n)])
-            for s, chunk in enumerate(chunks, half)
-        ]
-
-    near_exchange = functools.partial(
-        lax.all_to_all,
-        axis_name="pool",
-        split_axis=0,
-        concat_axis=0,
-        tiled=True,
-        axis_index_groups=[list(range(half)), list(range(half, n))],
-    )
-    far = far_exchange(far)
+    far = [
+        lax.ppermute(chunk, "pool", [(i, i ^ s) for i in range(n)]) for s, chunk in enumerate(far, half)
+    ]
     (near,) = call(
         functools.partial(pack_near_kernel, cap, pieces),
         [jax.ShapeDtypeStruct((half * per, width // pieces), BF16)],
@@ -274,7 +255,14 @@
         2 * rows * width * 2,
         [VMEM] * 3,
     )(place, rank, hidden)
-    near = near_exchange(near)
+    near = lax.all_to_all(
+        near,
+        "pool",
+        split_axis=0,
+        concat_axis=0,
+        tiled=True,
+        axis_index_groups=[list(range(half)), list(range(half, n))],
+    )
 
     core = lax.axis_index("tp")
     partial_sum = jnp.dot(hidden, key_value_weight, preferred_element_type=F32)
@@ -294,49 +282,44 @@
     ).reshape(rows, -1)
     cache_max = cache_max.reshape(rows, -1)
 
-    def correct(chunks, outs, *after):
-        count = len(chunks)
-        (reduced,) = call(
-            functools.partial(shrink_kernel, cap, pieces, count),
+    def shrink(chunks, *after):
+        return call(
+            functools.partial(shrink_kernel, cap, pieces, len(chunks)),
             [jax.ShapeDtypeStruct((half * cap, rank2), F32)],
             n * cap * width * rank2,
             half * cap * width * 2 + width * rank2 * 2,
-            [VMEM] * (count + 1) + [ANY] * len(after),
-        )(*chunks, adapter_down_weight, *after)
-        return call(
-            functools.partial(expand_kernel, cap),
-            [jax.ShapeDtypeStruct((half * out_pieces * cap // outs, head), BF16)] * outs,
-            n * cap * rank2 * columns,
-            half * cap * columns * 4,
-            [VMEM] * 3,
-        )(reduced, swap(reduced), adapter_up_weight)
-
-    size = half * out_pieces * cap
-    base, far_one_hot = call(
-        functools.partial(precombine_kernel, cap),
+            [VMEM] * (len(chunks) + 1) + [ANY] * len(after),
+        )(*chunks, adapter_down_weight, *after)[0]
+
+    size = n * out_pieces * cap
+    base, one_hot = call(
+        functools.partial(prepare_kernel, cap),
         [
             jax.ShapeDtypeStruct((rows, columns), F32),
             jax.ShapeDtypeStruct((out_pieces * rows, size), BF16),
         ],
-        4 * size * columns * rows,
+        2 * size * size * rows,
         rows * columns * 12,
-        [VMEM] * 5,
-    )(near_exchange(correct([near], 1)[0]), place, rank, base_mine, base_other)
+        [VMEM] * 4,
+    )(slot, rank, base_mine, base_other)
+    near_sum = shrink([near])
+    near_other = swap(near_sum)
+    far_sum = shrink(far, base, near_sum)
+    (terms,) = call(
+        functools.partial(expand_kernel, n, cap),
+        [jax.ShapeDtypeStruct((size, head), BF16)],
+        2 * n * cap * rank2 * columns,
+        n * cap * columns * 4,
+        [SMEM] + [VMEM] * 5,
+    )(me, near_sum, near_other, far_sum, swap(far_sum), adapter_up_weight)
+    deltas = lax.all_to_all(terms, "pool", split_axis=0, concat_axis=0, tiled=True)
     token, out = call(
         combine_kernel,
         [jax.ShapeDtypeStruct((rows, columns), BF16), jax.ShapeDtypeStruct(queries.shape, BF16)],
         2 * size * columns * rows,
         rows * 2048 * 8,
-        [VMEM] * (half + 6),
-    )(
-        *far_exchange(correct(far, half, base, attended)),
-        far_one_hot,
-        base,
-        queries,
-        cache_max,
-        cache_sum,
-        attended,
-    )
+        [VMEM] * 7,
+    )(deltas, one_hot, base, queries, cache_max, cache_sum, attended)
     return token, out
 
 

time: 59.1 us -> 49.5 us (0.84)
  starting transfers between devices: 25.1 us -> 20.1 us
  local copies, waits for them, and re-layouts: 7.17 us -> 4.66 us
  Pallas kernels: 6.95 us -> 6.2 us
  other arithmetic: 2.05 us -> 1.41 us
    ppermute x10 -> x6, starting transfers between devices: 17 us -> 8.39 us  [the longest x4 7.88 us: shards(): lax.ppermute(chunk, 'pool', [(i, i ^ s) for i in range(n)])]
    all_to_all x2, starting transfers between devices: 7.62 us -> 11.6 us  [the longest x1 6.39 us: shards(): lax.all_to_all(terms, 'pool', split_axis=0, concat_axis=0, tiled=True)]
    ppermute x10 -> x6, waiting for transfers between devices: 3.42 us -> 0.51 us  [the longest x4 0.51 us: shards(): lax.ppermute(chunk, 'pool', [(i, i ^ s) for i in range(n)])]
    all_to_all x2, waiting for transfers between devices: 3.27 us -> 5.65 us  [the longest x1 5.65 us: shards(): lax.all_to_all(terms, 'pool', split_axis=0, concat_axis=0, tiled=True)]
    dynamic_slice x1, local copies, waits for them, and re-layouts: 1.6 us -> 0.02 us  [shards(): lax.dynamic_slice_in_dim(partial_sum, (1 - core) * columns, columns, axis=1)]
    unnamed x20, local copies, waits for them, and re-layouts: 4.48 us -> 3.54 us
    dot_general x1, matrix products: 5.85 us -> 5.17 us  [shards(): partial_sum = jnp.dot(hidden, key_value_weight, preferred_element_type=F32)]
    lt x1, other arithmetic: 0.73 us -> 0.07 us  [shards(): jnp.arange(stored_cache_keys.shape[2])[None, :]]
  transfers between devices with their start and end apart: 13 -> 9, of which waited for: 3 -> 2; matrix products, arithmetic and copies ran while one was open for 26% -> 25% of each run, Pallas kernels for 5% -> 4%
where the time goes in v5:
time: 49.5 us; the launch traced here: 49 us
  starting transfers between devices  20.1 us (41%)
  matrix products  9.61 us (19%)
  Pallas kernels  6.2 us (13%)
  waiting for transfers between devices  6.16 us (12%)
  local copies, waits for them, and re-layouts  4.66 us (9%)
  other arithmetic  1.41 us (3%)
  between operations  0.83 us (2%)
    ppermute x4, starting transfers between devices, shards(): lax.ppermute(chunk, 'pool', [(i, i ^ s) for i in range(n)])  7.88 us
    all_to_all x1, starting transfers between devices, shards(): lax.all_to_all(terms, 'pool', split_axis=0, concat_axis=0, tiled=True)  6.39 us
    all_to_all x1, waiting for transfers between devices, shards(): lax.all_to_all(terms, 'pool', split_axis=0, concat_axis=0, tiled=True)  5.65 us
    all_to_all x1, starting transfers between devices, shards(): lax.all_to_all(near, 'pool', split_axis=0, concat_axis=0, tiled=True, axi...  5.25 us
    dot_general x1, matrix products, shards(): partial_sum = jnp.dot(hidden, key_value_weight, preferred_element_type=F32)  5.17 us
    unnamed x20, local copies, waits for them, and re-layouts  3.54 us
    dot_general x1, matrix products, shards(): jnp.einsum('rgqd,rgpd->rgqp', query_heads, stored_cache_keys, preferred_e...  3.06 us
    pallas_call x2, Pallas kernels, shrink(): call(functools.partial(shrink_kernel, cap, pieces, len(chunks)), [jax.Sha...  1.53 us
  transfers between devices with their start and end apart: 9, of which 2 were waited for; matrix products, arithmetic and copies ran while one was open for 25% of the time, Pallas kernels for 4%

profile of v5, /device:TPU:0, one launch (start us, length us, event | category | flops | bytes accessed | tf_op | source)
XLA Modules:
  0.0 49.0 jit_solution(13368310315135124757)
XLA Ops:
  0.6 0.0 copy-start
  0.7 0.0 copy-start.1
  0.7 1.1 %copy-done.1 = bf16[48,4096]{1,0:T(8,128)(2,1)S(1)} copy-done((bf16[48,4096]{1,0:T(8,128)(2,1)S(1)}, bf16[48,4096]{1,0:T(8,128)(2,1)}, u32[]{:S(2)}) %copy-start.1) | copy-done | bytes 393240
  1.7 0.7 %copy-done.6 = s32[48,1]{0,1:T(1,128)S(1)} copy-done((s32[48,1]{0,1:T(1,128)S(1)}, s32[48,1]{0,1:T(1,128)}, u32[]{:S(2)}) %copy-start.6) | copy-done | bytes 216
  2.4 0.7 %copy-done.7 = s32[8]{0:T(128)S(1)} copy-done((s32[8]{0:T(128)S(1)}, s32[8]{0:T(128)}, u32[]{:S(2)}) %copy-start.7) | copy-done | bytes 56
  3.0 0.8 %shard_map.113 = (s32[1,48]{1,0:T(1,128)S(1)}, s32[1,48]{1,0:T(1,128)S(1)}, s32[1,48]{1,0:T(1,128)S(1)}, bf16[48,1024]{1,0:T(8,128)(2,1)S(1)}, bf16[48,1024]{1,0...) custom-call(s32[1]{0:T(128)} %bitcast.me_ref, s32[1,48]{1,0:T(1,128)S(1)} %bitcast.26, ...), custom_call_target="tpu_custom_call" | custom-call | flops 25165824 | bytes 786432 | tf_op jit(solution)/shard_map/pallas_call | solution.py:233
  3.8 0.0 copy-start.2
  3.9 1.0 %copy-done.2 = bf16[48,4096]{1,0:T(8,128)(2,1)S(1)} copy-done((bf16[48,4096]{1,0:T(8,128)(2,1)S(1)}, bf16[48,4096]{1,0:T(8,128)(2,1)}, u32[]{:S(2)}) %copy-start.2) | copy-done | bytes 393240
  4.8 1.1 %shard_map.114 = bf16[192,1024]{1,0:T(8,128)(2,1)} custom-call(s32[1,48]{1,0:T(1,128)S(1)} %get-tuple-element.11.place_ref, s32[1,48]{1,0:T(1,128)S(1)} %get-tuple-element.12.rank_ref, bf16[48,4096]{1,0:T(8,128)(2,1)S(1)} %copy-done.2), custom_call_target="tpu_custom_call" | custom-call | flops 25165824 | bytes 786432 | tf_op jit(solution)/shard_map/pallas_call | solution.py:251
  5.9 5.2 %all-to-all-start = ((bf16[4,48,1024]{2,1,0:T(8,128)(2,1)}), bf16[4,48,1024]{2,1,0:T(8,128)(2,1)S(1)}, u32[]{:S(2)}, u32[]{:S(2)}) async-start(bf16[4,48,1024]{2,1,0:T(8,128)(2,1)} %bitcast.3), calls=%async_computation | async-start | bytes 786432 | tf_op jit(solution)/shard_map/all_to_all | solution.py:258
  11.1 2.6 %collective-permute-start.1 = (bf16[48,1024]{1,0:T(8,128)(2,1)S(1)}, bf16[48,1024]{1,0:T(8,128)(2,1)S(1)}, u32[]{:S(2)}, u32[]{:S(2)}) collective-permute-start(bf16[48,1024]{1,0:T(8,128)(2,1)S(1)} %get-tuple-element.13), channel_id=1, source_target_pairs={{0,8},{2,10},{4,12},{6,14},{8,0},{10,2},{12,4},{14,6},{1,9},{3,11}... | collective-permute-start | bytes 294920 | tf_op jit(solution)/shard_map/ppermute | solution.py:249
  13.7 1.8 %collective-permute-start.2 = (bf16[48,1024]{1,0:T(8,128)(2,1)S(1)}, bf16[48,1024]{1,0:T(8,128)(2,1)S(1)}, u32[]{:S(2)}, u32[]{:S(2)}) collective-permute-start(bf16[48,1024]{1,0:T(8,128)(2,1)S(1)} %get-tuple-element.14), channel_id=1, source_target_pairs={{0,10},{2,8},{4,14},{6,12},{8,2},{10,0},{12,6},{14,4},{1,11},{3,9}... | collective-permute-start | bytes 294920 | tf_op jit(solution)/shard_map/ppermute | solution.py:249
  15.5 3.5 %collective-permute-start.3 = (bf16[48,1024]{1,0:T(8,128)(2,1)S(1)}, bf16[48,1024]{1,0:T(8,128)(2,1)S(1)}, u32[]{:S(2)}, u32[]{:S(2)}) collective-permute-start(bf16[48,1024]{1,0:T(8,128)(2,1)S(1)} %get-tuple-element.15), channel_id=1, source_target_pairs={{0,12},{2,14},{4,8},{6,10},{8,4},{10,6},{12,0},{14,2},{1,13},{3,15... | collective-permute-start | bytes 294920 | tf_op jit(solution)/shard_map/ppermute | solution.py:249
  19.0 0.0 collective-permute-start.4
  19.0 0.0 copy-start.5
  19.0 5.2 %fusion.7 = f32[48,1024]{1,0:T(8,128)S(1)} fusion(bf16[48,4096]{1,0:T(8,128)(2,1)} %hidden_ref.1, bf16[4096,1024]{1,0:T(8,128)(2,1)} %param.12), kind=kOutput, calls=%fused_computation.12 | convolution fusion | flops 402653184 | bytes 8978432 | tf_op jit(solution)/shard_map/dot_general | solution.py:268
  24.2 0.1 collective-permute-start.5
  24.3 0.0 copy-done.4
  24.4 0.0 copy-done.8
  24.4 0.1 iota_compare_fusion
  24.5 3.1 %fusion.6 = (f32[48,2,8]{2,1,0:T(2,128)}, f32[48,2,8,32]{3,2,1,0:T(8,128)}) fusion(bf16[48,2,8,128]{3,2,1,0:T(8,128)(2,1)S(1)} %bitcast.28, bf16[48,2,32,128]{3,2,1,0:T(8,128)(2,1)} %param.15, pred[48,32]{1,0:T(8,128)(4,1)S(1)} %iota_compare_fusion), kind=kOutput, calls=%fused_computation.11 | convolution fusion | flops 6364416 | bytes 1085952 | tf_op jit(solution)/shard_map/rgqd,rgpd->rgqp/dot_general | solution.py:273
  27.5 0.0 collective-permute-done.5.other_ref
  27.5 0.4 shard_map.116
  27.9 0.0 all-to-all-done
  27.9 0.0 copy-done.3
  27.9 0.8 %shard_map.115.refs_6_.near_ref = f32[48,128]{1,0:T(8,128)S(1)} custom-call(bf16[192,1024]{1,0:T(8,128)(2,1)S(1)} %bitcast.22, bf16[1,4096,128]{2,1,0:T(8,128)(2,1)S(1)} %copy-done.3), custom_call_target="tpu_custom_call" | custom-call | flops 50331648 | bytes 1441792 | tf_op jit(solution)/shard_map/pallas_call | solution.py:286
  28.7 0.5 %collective-permute-start = (f32[48,128]{1,0:T(8,128)S(1)}, f32[48,128]{1,0:T(8,128)S(1)}, u32[]{:S(2)}, u32[]{:S(2)}) collective-permute-start(f32[48,128]{1,0:T(8,128)S(1)} %shard_map.115.refs_6_.near_ref), channel_id=1, source_target_pairs={{0,1},{1,0},{2,3},{3,2},{4,5},{5,4},{6,7},{7,6},{8,9},{9,8},{10,11... | collective-permute-start | bytes 73736 | tf_op jit(solution)/shard_map/ppermute | solution.py:306
  29.2 0.0 collective-permute-done.1.refs_0_
  29.2 0.5 %collective-permute-done.2.refs_1_ = bf16[48,1024]{1,0:T(8,128)(2,1)S(1)} collective-permute-done((bf16[48,1024]{1,0:T(8,128)(2,1)S(1)}, bf16[48,1024]{1,0:T(8,128)(2,1)S(1)}, u32[]{:S(2)}, u32[]{:S(2)}) %collective-permute-start.2) | collective-permute-done | bytes 98336 | tf_op jit(solution)/shard_map/ppermute | solution.py:249
  29.7 0.0 collective-permute-done.3.refs_2_
  29.7 0.0 collective-permute-done.4.refs_3_
  29.7 0.8 %shard_map.117.far_ref = f32[48,128]{1,0:T(8,128)S(1)} custom-call(bf16[48,1024]{1,0:T(8,128)(2,1)S(1)} %collective-permute-done.1.refs_0_, bf16[48,1024]{1,0:T(8,128)(2,1)S(1)} %collective-permute-done.2.refs_1_, bf16[48,1024]{1,0:T(8,128)(2,1)S(1)} %collective-permute-done.3.refs_2_, bf16[48,1024]{1,0:T(8,128)(2,1)S(1)} %collective-permute-done.4.refs_3_, ...), custom_call_target="tpu_custom_call" | custom-call | flops 50331648 | bytes 1441792 | tf_op jit(solution)/shard_map/pallas_call | solution.py:286
  30.5 0.0 collective-permute-start.6
  30.5 1.3 %fusion.2 = f32[48,2,8]{2,1,0:T(2,128)S(1)} fusion(f32[48,2,8,32]{3,2,1,0:T(8,128)} %get-tuple-element.23, f32[48,2,8]{2,1,0:T(2,128)} %get-tuple-element.22), kind=kLoop, calls=%fused_computation.5 | loop fusion | flops 48384 | bytes 104448 | tf_op jit(solution)/shard_map/reduce_sum | solution.py:279
  31.8 0.9 %copy.15 = f32[48,2,8]{0,2,1:T(8,128)S(1)} copy(f32[48,2,8]{2,1,0:T(2,128)} %get-tuple-element.22) | data formatting | bytes 6144 | tf_op jit(solution)/shard_map/reduce_max | solution.py:277
  32.7 0.1 copy.17.max_ref
  32.8 0.1 copy.16
  32.8 0.1 copy.18.sum_ref
  32.9 0.0 collective-permute-done.near_other_ref
  32.9 0.0 collective-permute-done.6.far_other_ref
  32.9 0.0 copy-done.5
  32.9 1.1 %shard_map.118 = bf16[384,128]{1,0:T(8,128)(2,1)} custom-call(s32[1]{0:T(128)} %bitcast.me_ref, f32[48,128]{1,0:T(8,128)S(1)} %shard_map.115.refs_6_.near_ref, f32[48,128]{1,0:T(8,128)S(1)} %collective-permute-done.near_other_ref, f32[48,128]{1,0:T(8,128)S(1)} %shard_map.117.far_ref, f32[48,128]{1,0:T(8,128)S(1)} %collective-permute-done.6.far_other_ref, ...), custom_call_target="tpu_custom_call" | custom-call | flops 12582912 | bytes 196608 | tf_op jit(solution)/shard_map/pallas_call | solution.py:308
  34.1 6.4 %all-to-all-start.1 = ((bf16[8,48,128]{2,1,0:T(8,128)(2,1)}), bf16[8,48,128]{2,1,0:T(8,128)(2,1)S(1)}, u32[]{:S(2)}, u32[]{:S(2)}) async-start(bf16[8,48,128]{2,1,0:T(8,128)(2,1)} %bitcast.5), calls=%async_computation.1 | async-start | bytes 196608 | tf_op jit(solution)/shard_map/all_to_all | solution.py:315
  40.5 0.0 copy-done
  40.5 1.4 %fusion.3 = f32[48,2,8,128]{3,2,1,0:T(8,128)S(1)} fusion(bf16[48,2,32,128]{3,2,1,0:T(8,128)(2,1)S(1)} %copy-done, f32[48,2,8,32]{3,2,1,0:T(8,128)} %get-tuple-element.23, f32[48,2,8]{2,1,0:T(2,128)} %get-tuple-element.22), kind=kOutput, calls=%fused_computation.6 | convolution fusion | flops 6340608 | bytes 1281024 | tf_op jit(solution)/shard_map/rgqp,rgpd->rgqd/dot_general | solution.py:280
  41.9 0.1 copy.22
  42.0 5.6 %all-to-all-done.1 = bf16[8,48,128]{2,1,0:T(8,128)(2,1)S(1)} async-done(((bf16[8,48,128]{2,1,0:T(8,128)(2,1)}), bf16[8,48,128]{2,1,0:T(8,128)(2,1)S(1)}, u32[]{:S(2)}, u32[]{:S(2)}) %all-to-all-start.1) | async-done | bytes 98336 | tf_op jit(solution)/shard_map/all_to_all | solution.py:315
  47.6 1.3 %shard_map.119 = (bf16[48,512]{1,0:T(8,128)(2,1)}, bf16[48,2048]{1,0:T(8,128)(2,1)}) custom-call(bf16[384,128]{1,0:T(8,128)(2,1)S(1)} %bitcast.25, bf16[192,384]{1,0:T(8,128)(2,1)S(1)} %get-tuple-element.19.one_hot_ref, f32[48,512]{1,0:T(8,128)S(1)} %get-tuple-element.18.refs_5_.base_ref, bf16[48,2048]{1,0:T(8,128)(2,1)S(1)} %copy-done.4, ...), custom_call_target="tpu_custom_call" | custom-call | flops 18874368 | bytes 786432 | tf_op jit(solution)/shard_map/pallas_call | solution.py:316
  (7 shorter events, 0.1 us)
Async XLA Ops:
  0.6 39.8 %copy-start = (bf16[48,2,32,128]{3,2,1,0:T(8,128)(2,1)S(1)}, bf16[48,2,32,128]{3,2,1,0:T(8,128)(2,1)}, u32[]{:S(2)}) copy-start(bf16[48,2,32,128]{3,2,1,0:T(8,128)(2,1)} %param.16) | copy-start | bytes 2359300
  0.7 1.1 %copy-start.1 = (bf16[48,4096]{1,0:T(8,128)(2,1)S(1)}, bf16[48,4096]{1,0:T(8,128)(2,1)}, u32[]{:S(2)}) copy-start(bf16[48,4096]{1,0:T(8,128)(2,1)} %hidden_ref.1) | copy-start | bytes 1179652
  1.7 0.7 %copy-start.6 = (s32[48,1]{0,1:T(1,128)S(1)}, s32[48,1]{0,1:T(1,128)}, u32[]{:S(2)}) copy-start(s32[48,1]{0,1:T(1,128)} %param.17) | copy-start | bytes 580
  2.4 0.7 %copy-start.7 = (s32[8]{0:T(128)S(1)}, s32[8]{0:T(128)}, u32[]{:S(2)}) copy-start(s32[8]{0:T(128)} %param.19) | copy-start | bytes 100
  3.8 1.0 %copy-start.2 = (bf16[48,4096]{1,0:T(8,128)(2,1)S(1)}, bf16[48,4096]{1,0:T(8,128)(2,1)}, u32[]{:S(2)}) copy-start(bf16[48,4096]{1,0:T(8,128)(2,1)} %hidden_ref.1) | copy-start | bytes 1179652
  5.9 22.0 %all-to-all-start = ((bf16[4,48,1024]{2,1,0:T(8,128)(2,1)}), bf16[4,48,1024]{2,1,0:T(8,128)(2,1)S(1)}, u32[]{:S(2)}, u32[]{:S(2)}) async-start(bf16[4,48,1024]{2,1,0:T(8,128)(2,1)} %bitcast.3), calls=%async_computation | async-start | bytes 786432 | tf_op jit(solution)/shard_map/all_to_all | solution.py:258
  11.1 18.1 %collective-permute-start.1 = (bf16[48,1024]{1,0:T(8,128)(2,1)S(1)}, bf16[48,1024]{1,0:T(8,128)(2,1)S(1)}, u32[]{:S(2)}, u32[]{:S(2)}) collective-permute-start(bf16[48,1024]{1,0:T(8,128)(2,1)S(1)} %get-tuple-element.13), channel_id=1, source_target_pairs={{0,8},{2,10},{4,12},{6,14},{8,0},{10,2},{12,4},{14,6},{1,9},{3,11}... | collective-permute-start | bytes 294920 | tf_op jit(solution)/shard_map/ppermute | solution.py:249
  13.7 16.0 %collective-permute-start.2 = (bf16[48,1024]{1,0:T(8,128)(2,1)S(1)}, bf16[48,1024]{1,0:T(8,128)(2,1)S(1)}, u32[]{:S(2)}, u32[]{:S(2)}) collective-permute-start(bf16[48,1024]{1,0:T(8,128)(2,1)S(1)} %get-tuple-element.14), channel_id=1, source_target_pairs={{0,10},{2,8},{4,14},{6,12},{8,2},{10,0},{12,6},{14,4},{1,11},{3,9}... | collective-permute-start | bytes 294920 | tf_op jit(solution)/shard_map/ppermute | solution.py:249
  15.5 14.2 %collective-permute-start.3 = (bf16[48,1024]{1,0:T(8,128)(2,1)S(1)}, bf16[48,1024]{1,0:T(8,128)(2,1)S(1)}, u32[]{:S(2)}, u32[]{:S(2)}) collective-permute-start(bf16[48,1024]{1,0:T(8,128)(2,1)S(1)} %get-tuple-element.15), channel_id=1, source_target_pairs={{0,12},{2,14},{4,8},{6,10},{8,4},{10,6},{12,0},{14,2},{1,13},{3,15... | collective-permute-start | bytes 294920 | tf_op jit(solution)/shard_map/ppermute | solution.py:249
  19.0 10.7 %collective-permute-start.4 = (bf16[48,1024]{1,0:T(8,128)(2,1)S(1)}, bf16[48,1024]{1,0:T(8,128)(2,1)S(1)}, u32[]{:S(2)}, u32[]{:S(2)}) collective-permute-start(bf16[48,1024]{1,0:T(8,128)(2,1)S(1)} %get-tuple-element.16), channel_id=1, source_target_pairs={{0,14},{2,12},{4,10},{6,8},{8,6},{10,4},{12,2},{14,0},{1,15},{3,13... | collective-permute-start | bytes 294920 | tf_op jit(solution)/shard_map/ppermute | solution.py:249
  19.0 5.3 %copy-start.4 = (bf16[48,2048]{1,0:T(8,128)(2,1)S(1)}, bf16[48,2048]{1,0:T(8,128)(2,1)}, u32[]{:S(2)}) copy-start(bf16[48,2048]{1,0:T(8,128)(2,1)} %query_ref.1) | copy-start | bytes 589828
  19.0 5.4 %copy-start.8 = (s32[48]{0:T(128)S(1)}, s32[48]{0:T(128)}, u32[]{:S(2)}) copy-start(s32[48]{0:T(128)} %param.18) | copy-start | bytes 580
  19.0 8.9 %copy-start.3 = (bf16[1,4096,128]{2,1,0:T(8,128)(2,1)S(1)}, bf16[1,4096,128]{2,1,0:T(8,128)(2,1)}, u32[]{:S(2)}) copy-start(bf16[1,4096,128]{2,1,0:T(8,128)(2,1)} %refs_4_.1) | copy-start | bytes 3145732
  19.0 13.9 %copy-start.5 = (bf16[1,2,64,256]{3,2,1,0:T(8,128)(2,1)S(1)}, bf16[1,2,64,256]{3,2,1,0:T(8,128)(2,1)}, u32[]{:S(2)}) copy-start(bf16[1,2,64,256]{3,2,1,0:T(8,128)(2,1)} %up_ref.1) | copy-start | bytes 196612
  24.2 3.3 %collective-permute-start.5 = (f32[48,512]{1,0:T(8,128)S(1)}, f32[48,512]{1,0:T(8,128)S(1)}, u32[]{:S(2)}, u32[]{:S(2)}) collective-permute-start(f32[48,512]{1,0:T(8,128)S(1)} %get-tuple-element.20), channel_id=1, source_target_pairs={{0,1},{1,0},{2,3},{3,2},{4,5},{5,4},{6,7},{7,6},{8,9},{9,8},{10,11... | collective-permute-start | bytes 294920 | tf_op jit(solution)/shard_map/ppermute | solution.py:270
  28.7 4.2 %collective-permute-start = (f32[48,128]{1,0:T(8,128)S(1)}, f32[48,128]{1,0:T(8,128)S(1)}, u32[]{:S(2)}, u32[]{:S(2)}) collective-permute-start(f32[48,128]{1,0:T(8,128)S(1)} %shard_map.115.refs_6_.near_ref), channel_id=1, source_target_pairs={{0,1},{1,0},{2,3},{3,2},{4,5},{5,4},{6,7},{7,6},{8,9},{9,8},{10,11... | collective-permute-start | bytes 73736 | tf_op jit(solution)/shard_map/ppermute | solution.py:306
  30.5 2.5 %collective-permute-start.6 = (f32[48,128]{1,0:T(8,128)S(1)}, f32[48,128]{1,0:T(8,128)S(1)}, u32[]{:S(2)}, u32[]{:S(2)}) collective-permute-start(f32[48,128]{1,0:T(8,128)S(1)} %shard_map.117.far_ref), channel_id=1, source_target_pairs={{0,1},{1,0},{2,3},{3,2},{4,5},{5,4},{6,7},{7,6},{8,9},{9,8},{10,11... | collective-permute-start | bytes 73736 | tf_op jit(solution)/shard_map/ppermute | solution.py:314
  34.1 13.6 %all-to-all-start.1 = ((bf16[8,48,128]{2,1,0:T(8,128)(2,1)}), bf16[8,48,128]{2,1,0:T(8,128)(2,1)S(1)}, u32[]{:S(2)}, u32[]{:S(2)}) async-start(bf16[8,48,128]{2,1,0:T(8,128)(2,1)} %bitcast.5), calls=%async_computation.1 | async-start | bytes 196608 | tf_op jit(solution)/shard_map/all_to_all | solution.py:315

commit v6 on v5

--- a/solution.py
+++ b/solution.py
@@ -56,24 +56,16 @@
     )
 
 
-def pack_far_kernel(n, cap, pieces, me_ref, idx_hbm, table_hbm, hidden_hbm, slot_ref, place_ref, rank_ref, *refs):
-    far_refs, (idx_ref, table_ref, hidden_ref, sems) = refs[:-4], refs[-4:]
-    copies = [
-        pltpu.make_async_copy(source, target, sems.at[i])
-        for i, (source, target) in enumerate(
-            [(idx_hbm, idx_ref), (table_hbm, table_ref), (hidden_hbm, hidden_ref)]
-        )
-    ]
-    for copy in copies:
-        copy.start()
+def pack_far_kernel(
+    n, cap, pieces, me_ref, idx_ref, table_ref, hidden_ref, slot_ref, place_ref, rank_ref, *far_refs
+):
     rows = hidden_ref.shape[0]
     per = pieces * cap
     half = n // 2
-    copies[0].wait()
-    copies[1].wait()
-    named = (iota((n, rows), 0) == idx_ref[...]).astype(F32).astype(BF16)
-    table = jnp.broadcast_to(table_ref[...].astype(F32).astype(BF16), (16, n))
-    slot = dot(table, named)[0:1, :].astype(I32)
+    lane = iota((1, rows), 1)
+    slot = jnp.zeros((1, rows), I32)
+    for r in range(rows):
+        slot = jnp.where(lane == r, table_ref[idx_ref[r]], slot)
     member = (iota((n, rows), 0) == slot).astype(F32)
     before = (iota((rows, rows), 0) < iota((rows, rows), 1)).astype(F32).astype(BF16)
     count = dot(member.astype(BF16), before)
@@ -84,13 +76,12 @@
     place_ref[...] = place
     rank_ref[...] = rank
     one_hot = one_hot_of(codes_of(place, rank, cap, pieces), half * per, half * per)
-    copies[2].wait()
     packed = dot(one_hot, stack_pieces(hidden_ref[...], pieces)).astype(BF16)
     for s in range(half):
         far_refs[s][...] = packed[s * per : (s + 1) * per]
 
 
-def pack_near_kernel(cap, pieces, place_ref, rank_ref, hidden_ref, near_ref):
+def pack_near_kernel(cap, pieces, place_ref, rank_ref, hidden_ref, _, near_ref):
     one_hot = one_hot_of(codes_of(place_ref[...], rank_ref[...], cap, pieces), 0, near_ref.shape[0])
     near_ref[...] = dot(one_hot, stack_pieces(hidden_ref[...], pieces)).astype(BF16)
 
@@ -187,7 +178,6 @@
 
 VMEM = pl.BlockSpec(memory_space=pltpu.VMEM)
 SMEM = pl.BlockSpec(memory_space=pltpu.SMEM)
-HBM = pl.BlockSpec(memory_space=pltpu.HBM)
 ANY = pl.BlockSpec(memory_space=pl.ANY)
 
 
@@ -236,25 +226,29 @@
         + [jax.ShapeDtypeStruct((per, width // pieces), BF16)] * half,
         n * cap * width * 64,
         2 * rows * width * 2,
-        [SMEM, HBM, HBM, HBM],
-        [
-            pltpu.VMEM((1, rows), I32),
-            pltpu.VMEM((1, n), I32),
-            pltpu.VMEM((rows, width), BF16),
-            pltpu.SemaphoreType.DMA((3,)),
-        ],
-    )(me, row_adapter_index.reshape(1, rows), adapter_slot_table.reshape(1, n), hidden)
-
+        [SMEM, SMEM, SMEM, VMEM],
+    )(me, row_adapter_index.reshape(rows), adapter_slot_table, hidden)
     far = [
         lax.ppermute(chunk, "pool", [(i, i ^ s) for i in range(n)]) for s, chunk in enumerate(far, half)
     ]
+    core = lax.axis_index("tp")
+    partial_sum = jnp.dot(hidden, key_value_weight, preferred_element_type=F32)
+    base_mine = lax.dynamic_slice_in_dim(partial_sum, core * columns, columns, axis=1)
+    base_other = swap(lax.dynamic_slice_in_dim(partial_sum, (1 - core) * columns, columns, axis=1))
+
+    query_heads = queries.reshape(rows, groups, -1, head)
+    scores = jnp.einsum("rgqd,rgpd->rgqp", query_heads, stored_cache_keys, preferred_element_type=F32)
+    scores = scores * (head ** (-0.5))
+    valid = jnp.arange(stored_cache_keys.shape[2])[None, :] < stored_cache_lengths[:, None]
+    scores = jnp.where(valid[:, None, None, :], scores, -jnp.inf)
+    cache_max = jnp.max(scores, axis=-1)
     (near,) = call(
         functools.partial(pack_near_kernel, cap, pieces),
         [jax.ShapeDtypeStruct((half * per, width // pieces), BF16)],
         n * cap * width * 64,
         2 * rows * width * 2,
-        [VMEM] * 3,
-    )(place, rank, hidden)
+        [VMEM] * 3 + [ANY],
+    )(place, rank, hidden, cache_max)
     near = lax.all_to_all(
         near,
         "pool",
@@ -264,17 +258,6 @@
         axis_index_groups=[list(range(half)), list(range(half, n))],
     )
 
-    core = lax.axis_index("tp")
-    partial_sum = jnp.dot(hidden, key_value_weight, preferred_element_type=F32)
-    base_mine = lax.dynamic_slice_in_dim(partial_sum, core * columns, columns, axis=1)
-    base_other = swap(lax.dynamic_slice_in_dim(partial_sum, (1 - core) * columns, columns, axis=1))
-
-    query_heads = queries.reshape(rows, groups, -1, head)
-    scores = jnp.einsum("rgqd,rgpd->rgqp", query_heads, stored_cache_keys, preferred_element_type=F32)
-    scores = scores * (head ** (-0.5))
-    valid = jnp.arange(stored_cache_keys.shape[2])[None, :] < stored_cache_lengths[:, None]
-    scores = jnp.where(valid[:, None, None, :], scores, -jnp.inf)
-    cache_max = jnp.max(scores, axis=-1)
     weights = jnp.exp(scores - cache_max[..., None])
     cache_sum = jnp.sum(weights, axis=-1).reshape(rows, -1)
     attended = jnp.einsum(

time: 49.5 us -> 60.4 us (1.22)
  waiting for transfers between devices: 6.16 us -> 15.3 us
  starting transfers between devices: 20.1 us -> 21 us
  Pallas kernels: 6.2 us -> 7.03 us
  other arithmetic: 1.41 us -> 2.06 us
  matrix products: 9.61 us -> 8.97 us
    ppermute x4, waiting for transfers between devices: 0.51 us -> 9.65 us  [shards(): lax.ppermute(chunk, 'pool', [(i, i ^ s) for i in range(n)])]
    all_to_all x1, starting transfers between devices: 6.39 us -> 7.68 us  [shards(): lax.all_to_all(terms, 'pool', split_axis=0, concat_axis=0, tiled=True)]
    unnamed x20 -> x18, local copies, waits for them, and re-layouts: 3.54 us -> 4.47 us
    pallas_call x1, Pallas kernels: 0.8 us -> 1.62 us  [shards(): call(functools.partial(pack_far_kernel, n, cap, pieces), [jax.ShapeDtypeS...]
    reduce_max x1, local copies, waits for them, and re-layouts: 0.86 us -> 0.07 us  [shards(): cache_max = jnp.max(scores, axis=-1)]
    lt x1, other arithmetic: 0.07 us -> 0.73 us  [shards(): jnp.arange(stored_cache_keys.shape[2])[None, :]]
    dot_general x1, matrix products: 3.06 us -> 2.44 us  [shards(): jnp.einsum('rgqd,rgpd->rgqp', query_heads, stored_cache_keys, preferred_e...]
  transfers between devices with their start and end apart: 9 -> 9, of which waited for: 2 -> 3; matrix products, arithmetic and copies ran while one was open for 25% -> 14% of each run, Pallas kernels for 4% -> 3%
where the time goes in v6:
time: 60.4 us; the launch traced here: 59.9 us
  starting transfers between devices  21 us (35%)
  waiting for transfers between devices  15.3 us (25%)
  matrix products  8.97 us (15%)
  Pallas kernels  7.03 us (12%)
  local copies, waits for them, and re-layouts  4.8 us (8%)
  other arithmetic  2.06 us (3%)
  between operations  0.8 us (1%)
    ppermute x4, waiting for transfers between devices, shards(): lax.ppermute(chunk, 'pool', [(i, i ^ s) for i in range(n)])  9.65 us
    ppermute x4, starting transfers between devices, shards(): lax.ppermute(chunk, 'pool', [(i, i ^ s) for i in range(n)])  7.94 us
    all_to_all x1, starting transfers between devices, shards(): lax.all_to_all(terms, 'pool', split_axis=0, concat_axis=0, tiled=True)  7.68 us
    all_to_all x1, waiting for transfers between devices, shards(): lax.all_to_all(terms, 'pool', split_axis=0, concat_axis=0, tiled=True)  5.6 us
    all_to_all x1, starting transfers between devices, shards(): lax.all_to_all(near, 'pool', split_axis=0, concat_axis=0, tiled=True, axi...  5.25 us
    dot_general x1, matrix products, shards(): partial_sum = jnp.dot(hidden, key_value_weight, preferred_element_type=F32)  5.16 us
    unnamed x18, local copies, waits for them, and re-layouts  4.47 us
    dot_general x1, matrix products, shards(): jnp.einsum('rgqd,rgpd->rgqp', query_heads, stored_cache_keys, preferred_e...  2.44 us
  transfers between devices with their start and end apart: 9, of which 3 were waited for; matrix products, arithmetic and copies ran while one was open for 14% of the time, Pallas kernels for 3%

profile of v6, /device:TPU:0, one launch (start us, length us, event | category | flops | bytes accessed | tf_op | source)
XLA Modules:
  0.0 59.9 jit_solution(12388155613391046384)
XLA Ops:
  0.6 0.0 copy-start
  0.7 1.0 %copy.19 = bf16[6,8,16,128]{3,2,1,0:T(8,128)(2,1)S(1)} copy(bf16[6,8,16,128]{3,1,2,0:T(8,128)(2,1)} %bitcast.23) | data formatting | bytes 393216
  1.7 0.7 %iota_compare_fusion = pred[48,32]{1,0:T(8,128)(4,1)S(1)} fusion(s32[48]{0:T(128)} %param.18), kind=kLoop, calls=%fused_computation.8 | loop fusion | flops 1536 | bytes 1728 | tf_op jit(solution)/shard_map/lt | solution.py:242
  2.4 2.4 %fusion.6 = (f32[48,2,8]{2,1,0:T(2,128)S(1)}, f32[48,2,8,32]{3,2,1,0:T(8,128)}) fusion(bf16[48,2,8,128]{3,2,1,0:T(8,128)(2,1)S(1)} %bitcast.26, bf16[48,2,32,128]{3,2,1,0:T(8,128)(2,1)} %param.15, pred[48,32]{1,0:T(8,128)(4,1)S(1)} %iota_compare_fusion), kind=kOutput, calls=%fused_computation.11 | convolution fusion | flops 6364416 | bytes 1085952 | tf_op jit(solution)/shard_map/rgqd,rgpd->rgqp/dot_general | solution.py:240
  4.9 0.0 copy-start.1
  4.9 1.0 %copy-done.1 = bf16[48,4096]{1,0:T(8,128)(2,1)S(1)} copy-done((bf16[48,4096]{1,0:T(8,128)(2,1)S(1)}, bf16[48,4096]{1,0:T(8,128)(2,1)}, u32[]{:S(2)}) %copy-start.1) | copy-done | bytes 393240
  5.9 0.0 copy-start.6
  5.9 0.7 %copy-done.6 = s32[48,1]{0,1:T(1,128)S(1)} copy-done((s32[48,1]{0,1:T(1,128)S(1)}, s32[48,1]{0,1:T(1,128)}, u32[]{:S(2)}) %copy-start.6) | copy-done | bytes 216
  6.5 0.7 %copy-done.7 = s32[8]{0:T(128)S(1)} copy-done((s32[8]{0:T(128)S(1)}, s32[8]{0:T(128)}, u32[]{:S(2)}) %copy-start.7) | copy-done | bytes 56
  7.2 1.6 %shard_map.113 = (s32[1,48]{1,0:T(1,128)S(1)}, s32[1,48]{1,0:T(1,128)S(1)}, s32[1,48]{1,0:T(1,128)S(1)}, bf16[48,1024]{1,0:T(8,128)(2,1)}, bf16[48,1024]{1,0:T(8...) custom-call(s32[1]{0:T(128)} %bitcast.me_ref, s32[48]{0:T(128)S(1)} %bitcast.25, ...), custom_call_target="tpu_custom_call" | custom-call | flops 25165824 | bytes 786432 | tf_op jit(solution)/shard_map/pallas_call | solution.py:223
  8.8 1.0 %copy-done.2 = bf16[48,4096]{1,0:T(8,128)(2,1)S(1)} copy-done((bf16[48,4096]{1,0:T(8,128)(2,1)S(1)}, bf16[48,4096]{1,0:T(8,128)(2,1)}, u32[]{:S(2)}) %copy-start.2) | copy-done | bytes 393240
  9.8 1.1 %shard_map.114 = bf16[192,1024]{1,0:T(8,128)(2,1)} custom-call(s32[1,48]{1,0:T(1,128)S(1)} %get-tuple-element.11.place_ref, s32[1,48]{1,0:T(1,128)S(1)} %get-tuple-element.12.rank_ref, bf16[48,4096]{1,0:T(8,128)(2,1)S(1)} %copy-done.2, f32[48,2,8]{2,1,0:T(2,128)S(1)} %get-tuple-element.22._), custom_call_target="tpu_custom_call" | custom-call | flops 25165824 | bytes 786432 | tf_op jit(solution)/shard_map/pallas_call | solution.py:245
  10.8 5.2 %all-to-all-start = ((bf16[4,48,1024]{2,1,0:T(8,128)(2,1)}), bf16[4,48,1024]{2,1,0:T(8,128)(2,1)S(1)}, u32[]{:S(2)}, u32[]{:S(2)}) async-start(bf16[4,48,1024]{2,1,0:T(8,128)(2,1)} %bitcast.2), calls=%async_computation | async-start | bytes 786432 | tf_op jit(solution)/shard_map/all_to_all | solution.py:252
  16.1 5.2 %fusion.7 = f32[48,1024]{1,0:T(8,128)S(1)} fusion(bf16[48,4096]{1,0:T(8,128)(2,1)} %hidden_ref.3, bf16[4096,1024]{1,0:T(8,128)(2,1)} %param.12), kind=kOutput, calls=%fused_computation.12 | convolution fusion | flops 402653184 | bytes 8978432 | tf_op jit(solution)/shard_map/dot_general | solution.py:235
  21.3 0.0 copy-start.4
  21.3 0.1 collective-permute-start.5
  21.4 2.7 %collective-permute-start.1 = (bf16[48,1024]{1,0:T(8,128)(2,1)}, bf16[48,1024]{1,0:T(8,128)(2,1)S(1)}, u32[]{:S(2)}, u32[]{:S(2)}) collective-permute-start(bf16[48,1024]{1,0:T(8,128)(2,1)} %get-tuple-element.13), channel_id=1, source_target_pairs={{0,8},{2,10},{4,12},{6,14},{8,0},{10,2},{12,4},{14,6},{1,9},{3,11}... | collective-permute-start | bytes 294920 | tf_op jit(solution)/shard_map/ppermute | solution.py:232
  24.0 1.8 %collective-permute-start.2 = (bf16[48,1024]{1,0:T(8,128)(2,1)S(1)}, bf16[48,1024]{1,0:T(8,128)(2,1)S(1)}, u32[]{:S(2)}, u32[]{:S(2)}) collective-permute-start(bf16[48,1024]{1,0:T(8,128)(2,1)S(1)} %get-tuple-element.14), channel_id=1, source_target_pairs={{0,10},{2,8},{4,14},{6,12},{8,2},{10,0},{12,6},{14,4},{1,11},{3,9}... | collective-permute-start | bytes 294920 | tf_op jit(solution)/shard_map/ppermute | solution.py:232
  25.8 3.5 %collective-permute-start.3 = (bf16[48,1024]{1,0:T(8,128)(2,1)S(1)}, bf16[48,1024]{1,0:T(8,128)(2,1)S(1)}, u32[]{:S(2)}, u32[]{:S(2)}) collective-permute-start(bf16[48,1024]{1,0:T(8,128)(2,1)S(1)} %get-tuple-element.15), channel_id=1, source_target_pairs={{0,12},{2,14},{4,8},{6,10},{8,4},{10,6},{12,0},{14,2},{1,13},{3,15... | collective-permute-start | bytes 294920 | tf_op jit(solution)/shard_map/ppermute | solution.py:232
  29.3 0.0 collective-permute-start.4
  29.3 0.0 collective-permute-done.5.other_ref
  29.3 0.4 shard_map.116
  29.7 0.0 all-to-all-done
  29.7 0.0 copy-done.3
  29.7 0.8 %shard_map.115.refs_6_.near_ref = f32[48,128]{1,0:T(8,128)S(1)} custom-call(bf16[192,1024]{1,0:T(8,128)(2,1)S(1)} %bitcast.21, bf16[1,4096,128]{2,1,0:T(8,128)(2,1)S(1)} %copy-done.3), custom_call_target="tpu_custom_call" | custom-call | flops 50331648 | bytes 1441792 | tf_op jit(solution)/shard_map/pallas_call | solution.py:269
  30.5 0.0 collective-permute-start
  30.5 6.1 %collective-permute-done.1.refs_0_ = bf16[48,1024]{1,0:T(8,128)(2,1)S(1)} collective-permute-done((bf16[48,1024]{1,0:T(8,128)(2,1)}, bf16[48,1024]{1,0:T(8,128)(2,1)S(1)}, u32[]{:S(2)}, u32[]{:S(2)}) %collective-permute-start.1) | collective-permute-done | bytes 98336 | tf_op jit(solution)/shard_map/ppermute | solution.py:232
  36.6 3.6 %collective-permute-done.2.refs_1_ = bf16[48,1024]{1,0:T(8,128)(2,1)S(1)} collective-permute-done((bf16[48,1024]{1,0:T(8,128)(2,1)S(1)}, bf16[48,1024]{1,0:T(8,128)(2,1)S(1)}, u32[]{:S(2)}, u32[]{:S(2)}) %collective-permute-start.2) | collective-permute-done | bytes 98336 | tf_op jit(solution)/shard_map/ppermute | solution.py:232
  40.1 0.0 collective-permute-done.3.refs_2_
  40.1 0.0 collective-permute-done.4.refs_3_
  40.1 0.8 %shard_map.117.far_ref = f32[48,128]{1,0:T(8,128)S(1)} custom-call(bf16[48,1024]{1,0:T(8,128)(2,1)S(1)} %collective-permute-done.1.refs_0_, bf16[48,1024]{1,0:T(8,128)(2,1)S(1)} %collective-permute-done.2.refs_1_, bf16[48,1024]{1,0:T(8,128)(2,1)S(1)} %collective-permute-done.3.refs_2_, bf16[48,1024]{1,0:T(8,128)(2,1)S(1)} %collective-permute-done.4.refs_3_, ...), custom_call_target="tpu_custom_call" | custom-call | flops 50331648 | bytes 1441792 | tf_op jit(solution)/shard_map/pallas_call | solution.py:269
  40.9 0.0 collective-permute-start.6
  40.9 1.3 %fusion.2 = f32[48,2,8]{2,1,0:T(2,128)S(1)} fusion(f32[48,2,8,32]{3,2,1,0:T(8,128)} %get-tuple-element.23, f32[48,2,8]{2,1,0:T(2,128)S(1)} %get-tuple-element.22._), kind=kLoop, calls=%fused_computation.5 | loop fusion | flops 48384 | bytes 104448 | tf_op jit(solution)/shard_map/reduce_sum | solution.py:262
  42.3 0.1 copy.15
  42.3 0.1 copy.17.max_ref
  42.4 0.1 copy.16
  42.5 0.1 copy.18.sum_ref
  42.6 0.0 collective-permute-done.near_other_ref
  42.6 0.0 collective-permute-done.6.far_other_ref
  42.6 0.0 copy-done.5
  42.6 1.1 %shard_map.118 = bf16[384,128]{1,0:T(8,128)(2,1)} custom-call(s32[1]{0:T(128)} %bitcast.me_ref, f32[48,128]{1,0:T(8,128)S(1)} %shard_map.115.refs_6_.near_ref, f32[48,128]{1,0:T(8,128)S(1)} %collective-permute-done.near_other_ref, f32[48,128]{1,0:T(8,128)S(1)} %shard_map.117.far_ref, f32[48,128]{1,0:T(8,128)S(1)} %collective-permute-done.6.far_other_ref, ...), custom_call_target="tpu_custom_call" | custom-call | flops 12582912 | bytes 196608 | tf_op jit(solution)/shard_map/pallas_call | solution.py:291
  43.7 7.7 %all-to-all-start.1 = ((bf16[8,48,128]{2,1,0:T(8,128)(2,1)}), bf16[8,48,128]{2,1,0:T(8,128)(2,1)S(1)}, u32[]{:S(2)}, u32[]{:S(2)}) async-start(bf16[8,48,128]{2,1,0:T(8,128)(2,1)} %bitcast.4), calls=%async_computation.1 | async-start | bytes 196608 | tf_op jit(solution)/shard_map/all_to_all | solution.py:298
  51.4 0.0 copy-done
  51.4 1.4 %fusion.3 = f32[48,2,8,128]{3,2,1,0:T(8,128)S(1)} fusion(bf16[48,2,32,128]{3,2,1,0:T(8,128)(2,1)S(1)} %copy-done, f32[48,2,8,32]{3,2,1,0:T(8,128)} %get-tuple-element.23, f32[48,2,8]{2,1,0:T(2,128)S(1)} %get-tuple-element.22._), kind=kOutput, calls=%fused_computation.6 | convolution fusion | flops 6340608 | bytes 1281024 | tf_op jit(solution)/shard_map/rgqp,rgpd->rgqd/dot_general | solution.py:263
  52.8 0.1 copy.22
  53.0 5.6 %all-to-all-done.1 = bf16[8,48,128]{2,1,0:T(8,128)(2,1)S(1)} async-done(((bf16[8,48,128]{2,1,0:T(8,128)(2,1)}), bf16[8,48,128]{2,1,0:T(8,128)(2,1)S(1)}, u32[]{:S(2)}, u32[]{:S(2)}) %all-to-all-start.1) | async-done | bytes 98336 | tf_op jit(solution)/shard_map/all_to_all | solution.py:298
  58.6 0.0 copy-done.4
  58.6 1.3 %shard_map.119 = (bf16[48,512]{1,0:T(8,128)(2,1)}, bf16[48,2048]{1,0:T(8,128)(2,1)}) custom-call(bf16[384,128]{1,0:T(8,128)(2,1)S(1)} %bitcast.24, bf16[192,384]{1,0:T(8,128)(2,1)S(1)} %get-tuple-element.19.one_hot_ref, f32[48,512]{1,0:T(8,128)S(1)} %get-tuple-element.18.refs_5_.base_ref, bf16[48,2048]{1,0:T(8,128)(2,1)S(1)} %copy-done.4, ...), custom_call_target="tpu_custom_call" | custom-call | flops 18874368 | bytes 786432 | tf_op jit(solution)/shard_map/pallas_call | solution.py:299
  (5 shorter events, 0.0 us)
Async XLA Ops:
  0.6 50.8 %copy-start = (bf16[48,2,32,128]{3,2,1,0:T(8,128)(2,1)S(1)}, bf16[48,2,32,128]{3,2,1,0:T(8,128)(2,1)}, u32[]{:S(2)}) copy-start(bf16[48,2,32,128]{3,2,1,0:T(8,128)(2,1)} %param.16) | copy-start | bytes 2359300
  4.9 1.0 %copy-start.1 = (bf16[48,4096]{1,0:T(8,128)(2,1)S(1)}, bf16[48,4096]{1,0:T(8,128)(2,1)}, u32[]{:S(2)}) copy-start(bf16[48,4096]{1,0:T(8,128)(2,1)} %hidden_ref.3) | copy-start | bytes 1179652
  5.9 0.7 %copy-start.6 = (s32[48,1]{0,1:T(1,128)S(1)}, s32[48,1]{0,1:T(1,128)}, u32[]{:S(2)}) copy-start(s32[48,1]{0,1:T(1,128)} %param.17) | copy-start | bytes 580
  6.5 0.7 %copy-start.7 = (s32[8]{0:T(128)S(1)}, s32[8]{0:T(128)}, u32[]{:S(2)}) copy-start(s32[8]{0:T(128)} %table_ref.1) | copy-start | bytes 100
  8.8 1.0 %copy-start.2 = (bf16[48,4096]{1,0:T(8,128)(2,1)S(1)}, bf16[48,4096]{1,0:T(8,128)(2,1)}, u32[]{:S(2)}) copy-start(bf16[48,4096]{1,0:T(8,128)(2,1)} %hidden_ref.3) | copy-start | bytes 1179652
  10.8 18.9 %all-to-all-start = ((bf16[4,48,1024]{2,1,0:T(8,128)(2,1)}), bf16[4,48,1024]{2,1,0:T(8,128)(2,1)S(1)}, u32[]{:S(2)}, u32[]{:S(2)}) async-start(bf16[4,48,1024]{2,1,0:T(8,128)(2,1)} %bitcast.2), calls=%async_computation | async-start | bytes 786432 | tf_op jit(solution)/shard_map/all_to_all | solution.py:252
  16.1 13.6 %copy-start.3 = (bf16[1,4096,128]{2,1,0:T(8,128)(2,1)S(1)}, bf16[1,4096,128]{2,1,0:T(8,128)(2,1)}, u32[]{:S(2)}) copy-start(bf16[1,4096,128]{2,1,0:T(8,128)(2,1)} %refs_4_.1) | copy-start | bytes 3145732
  16.1 26.5 %copy-start.5 = (bf16[1,2,64,256]{3,2,1,0:T(8,128)(2,1)S(1)}, bf16[1,2,64,256]{3,2,1,0:T(8,128)(2,1)}, u32[]{:S(2)}) copy-start(bf16[1,2,64,256]{3,2,1,0:T(8,128)(2,1)} %up_ref.1) | copy-start | bytes 196612
  21.3 37.3 %copy-start.4 = (bf16[48,2048]{1,0:T(8,128)(2,1)S(1)}, bf16[48,2048]{1,0:T(8,128)(2,1)}, u32[]{:S(2)}) copy-start(bf16[48,2048]{1,0:T(8,128)(2,1)} %query_ref.1) | copy-start | bytes 589828
  21.3 8.0 %collective-permute-start.5 = (f32[48,512]{1,0:T(8,128)S(1)}, f32[48,512]{1,0:T(8,128)S(1)}, u32[]{:S(2)}, u32[]{:S(2)}) collective-permute-start(f32[48,512]{1,0:T(8,128)S(1)} %get-tuple-element.20), channel_id=1, source_target_pairs={{0,1},{1,0},{2,3},{3,2},{4,5},{5,4},{6,7},{7,6},{8,9},{9,8},{10,11... | collective-permute-start | bytes 294920 | tf_op jit(solution)/shard_map/ppermute | solution.py:237
  21.4 15.2 %collective-permute-start.1 = (bf16[48,1024]{1,0:T(8,128)(2,1)}, bf16[48,1024]{1,0:T(8,128)(2,1)S(1)}, u32[]{:S(2)}, u32[]{:S(2)}) collective-permute-start(bf16[48,1024]{1,0:T(8,128)(2,1)} %get-tuple-element.13), channel_id=1, source_target_pairs={{0,8},{2,10},{4,12},{6,14},{8,0},{10,2},{12,4},{14,6},{1,9},{3,11}... | collective-permute-start | bytes 294920 | tf_op jit(solution)/shard_map/ppermute | solution.py:232
  24.0 16.1 %collective-permute-start.2 = (bf16[48,1024]{1,0:T(8,128)(2,1)S(1)}, bf16[48,1024]{1,0:T(8,128)(2,1)S(1)}, u32[]{:S(2)}, u32[]{:S(2)}) collective-permute-start(bf16[48,1024]{1,0:T(8,128)(2,1)S(1)} %get-tuple-element.14), channel_id=1, source_target_pairs={{0,10},{2,8},{4,14},{6,12},{8,2},{10,0},{12,6},{14,4},{1,11},{3,9}... | collective-permute-start | bytes 294920 | tf_op jit(solution)/shard_map/ppermute | solution.py:232
  25.8 14.3 %collective-permute-start.3 = (bf16[48,1024]{1,0:T(8,128)(2,1)S(1)}, bf16[48,1024]{1,0:T(8,128)(2,1)S(1)}, u32[]{:S(2)}, u32[]{:S(2)}) collective-permute-start(bf16[48,1024]{1,0:T(8,128)(2,1)S(1)} %get-tuple-element.15), channel_id=1, source_target_pairs={{0,12},{2,14},{4,8},{6,10},{8,4},{10,6},{12,0},{14,2},{1,13},{3,15... | collective-permute-start | bytes 294920 | tf_op jit(solution)/shard_map/ppermute | solution.py:232
  29.3 10.8 %collective-permute-start.4 = (bf16[48,1024]{1,0:T(8,128)(2,1)S(1)}, bf16[48,1024]{1,0:T(8,128)(2,1)S(1)}, u32[]{:S(2)}, u32[]{:S(2)}) collective-permute-start(bf16[48,1024]{1,0:T(8,128)(2,1)S(1)} %get-tuple-element.16), channel_id=1, source_target_pairs={{0,14},{2,12},{4,10},{6,8},{8,6},{10,4},{12,2},{14,0},{1,15},{3,13... | collective-permute-start | bytes 294920 | tf_op jit(solution)/shard_map/ppermute | solution.py:232
  30.5 12.1 %collective-permute-start = (f32[48,128]{1,0:T(8,128)S(1)}, f32[48,128]{1,0:T(8,128)S(1)}, u32[]{:S(2)}, u32[]{:S(2)}) collective-permute-start(f32[48,128]{1,0:T(8,128)S(1)} %shard_map.115.refs_6_.near_ref), channel_id=1, source_target_pairs={{0,1},{1,0},{2,3},{3,2},{4,5},{5,4},{6,7},{7,6},{8,9},{9,8},{10,11... | collective-permute-start | bytes 73736 | tf_op jit(solution)/shard_map/ppermute | solution.py:289
  40.9 1.7 %collective-permute-start.6 = (f32[48,128]{1,0:T(8,128)S(1)}, f32[48,128]{1,0:T(8,128)S(1)}, u32[]{:S(2)}, u32[]{:S(2)}) collective-permute-start(f32[48,128]{1,0:T(8,128)S(1)} %shard_map.117.far_ref), channel_id=1, source_target_pairs={{0,1},{1,0},{2,3},{3,2},{4,5},{5,4},{6,7},{7,6},{8,9},{9,8},{10,11... | collective-permute-start | bytes 73736 | tf_op jit(solution)/shard_map/ppermute | solution.py:297
  43.7 14.8 %all-to-all-start.1 = ((bf16[8,48,128]{2,1,0:T(8,128)(2,1)}), bf16[8,48,128]{2,1,0:T(8,128)(2,1)S(1)}, u32[]{:S(2)}, u32[]{:S(2)}) async-start(bf16[8,48,128]{2,1,0:T(8,128)(2,1)} %bitcast.4), calls=%async_computation.1 | async-start | bytes 196608 | tf_op jit(solution)/shard_map/all_to_all | solution.py:298

commit v7 on v6

v7 whole, which is shorter than its diff:
```python
import functools

import jax
import jax.numpy as jnp
from jax import lax
from jax.experimental import pallas as pl
from jax.experimental.pallas import tpu as pltpu
from jax.sharding import PartitionSpec as P

BF16 = jnp.bfloat16
F32 = jnp.float32
I32 = jnp.int32
VMEM_LIMIT = 48 * 1024 * 1024


def iota(shape, dim):
    return lax.broadcasted_iota(I32, shape, dim)


def split_count(cap):
    pieces = 4
    while cap * pieces % 16:
        pieces *= 2
    return pieces


def dot(a, b):
    return jnp.dot(a, b, preferred_element_type=F32)


def dot_first(a, b):
    return lax.dot_general(a, b, (((0,), (0,)), ((), ())), preferred_element_type=F32)


def exact_select(one_hot, x):
    high = x.astype(BF16)
    rest = x - high.astype(F32)
    middle = rest.astype(BF16)
    low = (rest - middle.astype(F32)).astype(BF16)
    return dot(one_hot, high) + (dot(one_hot, middle) + dot(one_hot, low))


def codes_of(place, rank, cap, pieces):
    code = place * (pieces * cap) + rank
    return jnp.concatenate([code + piece * cap for piece in range(pieces)], axis=1)


def one_hot_of(codes, first, count):
    return ((iota((count, codes.shape[1]), 0) + first) == codes).astype(F32).astype(BF16)


def stack_pieces(hidden, pieces):
    width = hidden.shape[1] // pieces
    return jnp.concatenate(
        [hidden[:, piece * width : (piece + 1) * width] for piece in range(pieces)], axis=0
    )


def pack_kernel(n, cap, pieces, me_ref, idx_ref, table_ref, hidden_ref, slot_ref, rank_ref, *out_refs):
    rows = hidden_ref.shape[0]
    named = (iota((n, rows), 0) == idx_ref[...]).astype(F32).astype(BF16)
    table = jnp.broadcast_to(table_ref[...].astype(F32).astype(BF16), (16, n))
    slot = dot(table, named)[0:1, :].astype(I32)
    member = (iota((n, rows), 0) == slot).astype(F32)
    before = (iota((rows, rows), 0) < iota((rows, rows), 1)).astype(F32).astype(BF16)
    count = dot(member.astype(BF16), before)
    rank = jnp.sum(member * count, axis=0, keepdims=True).astype(I32)
    slot_ref[...] = slot
    rank_ref[...] = rank
    per = pieces * cap
    apart = lax.bitwise_xor(slot, me_ref[0])
    one_hot = one_hot_of(codes_of(apart, rank, cap, pieces), 0, n * per)
    packed = dot(one_hot, stack_pieces(hidden_ref[...], pieces)).astype(BF16)
    for s, out_ref in enumerate(out_refs):
        out_ref[...] = packed[s * per : (s + 1) * per]


def shrink_kernel(n, cap, pieces, order, *refs):
    received_refs, (down_ref, base_ref, out_ref) = dict(zip(order, refs[:n])), refs[n:]
    per = pieces * cap
    width = refs[0].shape[1]
    rank2 = down_ref.shape[2]
    received = jnp.concatenate([received_refs[s][...] for s in range(n)], axis=0)
    size = received.shape[0]
    total = jnp.zeros((size, rank2), F32)
    piece_of = (iota((size, rank2), 0) // cap) % pieces
    for piece in range(pieces):
        part = dot(received, down_ref[0, piece * width : (piece + 1) * width, :])
        total = total + jnp.where(piece_of == piece, part, 0.0)
    out_row, in_row = iota((size // pieces, size), 0), iota((size // pieces, size), 1)
    same = (out_row // cap == in_row // per) & (out_row % cap == in_row % cap)
    reduced = exact_select(same.astype(F32).astype(BF16), total)
    size = reduced.shape[0]
    out_ref[:size, :] = reduced
    rows = base_ref.shape[0]
    for i in range(base_ref.shape[1] // rank2):
        first = size + i * rows
        out_ref[first : first + rows, :] = base_ref[:, i * rank2 : (i + 1) * rank2]


def expand_kernel(n, cap, me_ref, mine_ref, other_ref, up_ref, out_ref):
    rank = up_ref.shape[2]
    head = 128
    blocks = up_ref.shape[3] // head
    reduced = (mine_ref[: n * cap, :] + other_ref[: n * cap, :]).astype(BF16)
    terms = []
    for c in range(2):
        kept = reduced[:, c * rank : (c + 1) * rank]
        wide = dot(kept, up_ref[0, c]).astype(BF16)
        terms += [wide[:, g * head : (g + 1) * head] for g in range(blocks)]
    stacked = jnp.concatenate(terms, axis=0)
    pieces = 2 * blocks
    per = pieces * cap
    size = n * per
    out_row, in_row = iota((size, size), 0), iota((size, size), 1)
    apart = lax.bitwise_xor(out_row // per, me_ref[0])
    source = (out_row // cap % pieces) * (n * cap) + apart * cap + out_row % cap
    out_ref[...] = dot((source == in_row).astype(F32).astype(BF16), stacked).astype(BF16)


def prepare_kernel(n, cap, slot_ref, rank_ref, mine_ref, other_ref, _, base_ref, one_hot_ref):
    pieces = one_hot_ref.shape[0] // slot_ref.shape[1]
    size = one_hot_ref.shape[1]
    rows = mine_ref.shape[0]
    width = other_ref.shape[1]
    for i in range(mine_ref.shape[1] // width):
        lanes, first = slice(i * width, (i + 1) * width), n * cap + i * rows
        base_ref[:, lanes] = mine_ref[:, lanes] + other_ref[first : first + rows, :]
    one_hot = one_hot_of(codes_of(slot_ref[...], rank_ref[...], cap, pieces), 0, size)
    same = (iota((size, size), 0) == iota((size, size), 1)).astype(F32).astype(BF16)
    one_hot_ref[...] = dot_first(one_hot, same).astype(BF16)


def base_kernel(core_ref, hidden_ref, weight_ref, first_ref, second_ref, mine_ref, other_ref, total_ref):
    step = pl.program_id(0)
    part = dot(hidden_ref[...], weight_ref[...])

    @pl.when(step == 0)
    def _():
        total_ref[...] = part

    @pl.when(step > 0)
    def _():
        total_ref[...] += part

    @pl.when(step == pl.num_programs(0) - 1)
    def _():
        columns = mine_ref.shape[1]
        first, second = total_ref[:, :columns], total_ref[:, columns:]
        mine_ref[...] = jnp.where(core_ref[0] == 0, first, second)
        other_ref[...] = jnp.where(core_ref[0] == 0, second, first)


def cache_kernel(query_ref, key_ref, value_ref, length_ref, _, acc_ref, max_ref, sum_ref):
    rows, groups, positions, head = key_ref.shape
    per_group = query_ref.shape[1] // (groups * head)
    tile = 16
    wide, deep = tile * positions, tile * per_group
    scale = head ** (-0.5)
    row_of = iota((deep, wide), 0) % tile
    own_row = row_of == iota((deep, wide), 1) // positions
    position = iota((deep, wide), 1) % positions
    lane = iota((tile, head), 1)
    for first in range(0, rows, tile):
        at = slice(first, first + tile)
        length = jnp.concatenate([length_ref[at, :]] * per_group, axis=0)
        valid = own_row & (position < length)
        tops = jnp.zeros((tile, head), F32)
        sums = jnp.zeros((tile, head), F32)
        for g in range(groups):
            query = jnp.concatenate(
                [query_ref[at, h * head : (h + 1) * head] for h in range(g * per_group, (g + 1) * per_group)],
                axis=0,
            )
            key = key_ref[at, g].reshape(wide, head)
            value = value_ref[at, g].reshape(wide, head)
            scores = lax.dot_general(query, key, (((1,), (1,)), ((), ())), preferred_element_type=F32)
            scores = jnp.where(valid, scores * scale, -jnp.inf)
            top = jnp.max(scores, axis=1, keepdims=True)
            weight = jnp.exp(scores - top)
            total = jnp.sum(weight, axis=1, keepdims=True)
            mixed = dot(weight.astype(BF16), value)
            for i in range(per_group):
                h = g * per_group + i
                part = slice(i * tile, (i + 1) * tile)
                acc_ref[at, h * head : (h + 1) * head] = mixed[part]
                tops = jnp.where(lane == h, top[part], tops)
                sums = jnp.where(lane == h, total[part], sums)
        max_ref[at, :] = tops
        sum_ref[at, :] = sums


def combine_kernel(
    delta_ref, one_hot_ref, base_ref, query_ref, max_ref, sum_ref, acc_ref, token_ref, out_ref
):
    rows = base_ref.shape[0]
    head = 128
    groups = base_ref.shape[1] // (2 * head)
    delta = dot(one_hot_ref[...], delta_ref[...])
    heads = query_ref.shape[1] // head
    per_group = heads // groups
    scale = head ** (-0.5)
    lane = iota((rows, head), 1)
    own = jnp.zeros((rows, head), F32)
    values = []
    for g in range(groups):
        made = []
        for c in range(2):
            at = (g * 2 + c) * head
            piece = c * groups + g
            made.append((base_ref[:, at : at + head] + delta[piece * rows : (piece + 1) * rows]).astype(BF16))
            token_ref[:, at : at + head] = made[-1]
        key = made[0].astype(F32)
        values.append(made[1].astype(F32))
        for h in range(g * per_group, (g + 1) * per_group):
            query = query_ref[:, h * head : (h + 1) * head].astype(F32)
            own = jnp.where(lane == h, jnp.sum(query * key, axis=1, keepdims=True), own)
    own = own[:, :heads] * scale
    cache_max = max_ref[:, :heads]
    highest = jnp.maximum(own, cache_max)
    cache_factor = jnp.exp(cache_max - highest)
    own_factor = jnp.exp(own - highest)
    inverse = 1.0 / (sum_ref[:, :heads] * cache_factor + own_factor)
    cache_factor = cache_factor * inverse
    own_factor = own_factor * inverse
    for h in range(heads):
        lanes = slice(h * head, (h + 1) * head)
        out = acc_ref[:, lanes] * cache_factor[:, h : h + 1]
        out = out + values[h // per_group] * own_factor[:, h : h + 1]
        out_ref[:, lanes] = out.astype(BF16)


VMEM = pl.BlockSpec(memory_space=pltpu.VMEM)
SMEM = pl.BlockSpec(memory_space=pltpu.SMEM)
HBM = pl.BlockSpec(memory_space=pltpu.HBM)
ANY = pl.BlockSpec(memory_space=pl.ANY)
NO_COST = pl.CostEstimate(flops=0, bytes_accessed=0, transcendentals=0)


def call(kernel, outs, specs):
    return pl.pallas_call(
        kernel,
        out_shape=outs,
        in_specs=specs,
        out_specs=[VMEM] * len(outs),
        compiler_params=pltpu.CompilerParams(vmem_limit_bytes=VMEM_LIMIT),
        cost_estimate=NO_COST,
    )


def shards(
    hidden,
    queries,
    key_value_weight,
    adapter_down_weight,
    adapter_up_weight,
    stored_cache_keys,
    stored_cache_values,
    row_adapter_index,
    stored_cache_lengths,
    adapter_slot_table,
):
    n = lax.axis_size("pool")
    rows, width = hidden.shape
    cap = -(-2 * rows // n)
    pieces = split_count(cap)
    groups = stored_cache_keys.shape[1]
    head = stored_cache_keys.shape[3]
    columns = key_value_weight.shape[1] // 2
    out_pieces = 2 * groups
    rank2 = adapter_down_weight.shape[2]

    swap = functools.partial(lax.ppermute, axis_name="tp", perm=[(0, 1), (1, 0)])

    me = lax.axis_index("pool").reshape(1)
    slot, rank, *packed = call(
        functools.partial(pack_kernel, n, cap, pieces),
        [jax.ShapeDtypeStruct((1, rows), I32)] * 2
        + [jax.ShapeDtypeStruct((pieces * cap, width // pieces), BF16)] * n,
        [SMEM, VMEM, VMEM, VMEM],
    )(me, row_adapter_index.reshape(1, rows), adapter_slot_table.reshape(1, n), hidden)
    order = [0, 1, 2, *range(n // 2, n), *range(3, n // 2)]
    arrived = {0: packed[0]}
    for s in order[1:]:
        arrived[s] = lax.ppermute(packed[s], "pool", [(i, i ^ s) for i in range(n)])

    depth = 512
    base_mine, base_other = pl.pallas_call(
        base_kernel,
        grid=(width // depth,),
        in_specs=[
            SMEM,
            pl.BlockSpec((rows, depth), lambda k: (0, k)),
            pl.BlockSpec((depth, 2 * columns), lambda k: (k, 0)),
            ANY,
            ANY,
        ],
        out_specs=[pl.BlockSpec((rows, columns), lambda k: (0, 0))] * 2,
        out_shape=[jax.ShapeDtypeStruct((rows, columns), F32)] * 2,
        scratch_shapes=[pltpu.VMEM((rows, 2 * columns), F32)],
        compiler_params=pltpu.CompilerParams(vmem_limit_bytes=VMEM_LIMIT),
        cost_estimate=pl.CostEstimate(
            flops=4 * rows * width * columns, bytes_accessed=16 * width * columns, transcendentals=0
        ),
    )(lax.axis_index("tp").reshape(1), hidden, key_value_weight, arrived[1], arrived[2])

    size = n * out_pieces * cap
    (sums,) = call(
        functools.partial(shrink_kernel, n, cap, pieces, order),
        [jax.ShapeDtypeStruct((n * cap + rows * columns // rank2, rank2), F32)],
        [VMEM] * (n + 2),
    )(*[arrived[s] for s in order], adapter_down_weight, base_other)
    other_sums = swap(sums)
    (terms,) = call(
        functools.partial(expand_kernel, n, cap),
        [jax.ShapeDtypeStruct((size, head), BF16)],
        [SMEM] + [VMEM] * 3,
    )(me, sums, other_sums, adapter_up_weight)
    base, one_hot = call(
        functools.partial(prepare_kernel, n, cap),
        [
            jax.ShapeDtypeStruct((rows, columns), F32),
            jax.ShapeDtypeStruct((out_pieces * rows, size), BF16),
        ],
        [VMEM] * 4 + [ANY],
    )(slot, rank, base_mine, other_sums, terms)
    deltas = lax.all_to_all(terms, "pool", split_axis=0, concat_axis=0, tiled=True)
    attended, cache_max, cache_sum = call(
        cache_kernel,
        [jax.ShapeDtypeStruct(queries.shape, F32)] + [jax.ShapeDtypeStruct((rows, head), F32)] * 2,
        [VMEM] * 4 + [ANY],
    )(queries, stored_cache_keys, stored_cache_values, stored_cache_lengths.reshape(rows, 1), terms)
    token, out = call(
        combine_kernel,
        [jax.ShapeDtypeStruct((rows, columns), BF16), jax.ShapeDtypeStruct(queries.shape, BF16)],
        [VMEM] * 7,
    )(deltas, one_hot, base, queries, cache_max, cache_sum, attended)
    return token, out


def solution(mesh):
    in_specs = (
        P(("grp", "pool"), "tp"),
        P(("grp", "pool"), "tp"),
        P("tp", None),
        P("pool", "tp", None),
        P("pool", None, None, "tp"),
        P(("grp", "pool"), "tp", None, None),
        P(("grp", "pool"), "tp", None, None),
        P(("grp", "pool"), None),
        P(("grp", "pool")),
        P(),
    )
    out_specs = (P(("grp", "pool"), "tp"), P(("grp", "pool"), "tp"))
    return jax.shard_map(shards, mesh=mesh, in_specs=in_specs, out_specs=out_specs, check_vma=False)
```

time: 60.4 us -> 44.2 us (0.73)
  matrix products: 8.97 us -> 0 us
  waiting for transfers between devices: 15.3 us -> 7.78 us
  Pallas kernels: 7.03 us -> 13.3 us
  starting transfers between devices: 21 us -> 18.6 us
  other arithmetic: 2.06 us -> 0 us
  local copies, waits for them, and re-layouts: 4.8 us -> 3.41 us
    dot_general x3 -> x0, matrix products: 8.97 us -> none  [the longest x1 5.16 us: shards(): partial_sum = jnp.dot(hidden, key_value_weight, preferred_element_type=F32)]
    ppermute x7 -> x8, waiting for transfers between devices: 9.66 us -> 2.86 us  [the longest x7 1.5 us: shards(): arrived[s] = lax.ppermute(packed[s], 'pool', [(i, i ^ s) for i in range(n)])]
    pallas_call x5, Pallas kernels: 4.57 us -> 10.8 us  [the longest x1 6.93 us: shards(): pl.pallas_call(base_kernel, grid=(width // depth,), in_specs=[SMEM, pl.Bl...]
    all_to_all x1 -> x0, starting transfers between devices: 5.25 us -> none  [shards(): lax.all_to_all(near, 'pool', split_axis=0, concat_axis=0, tiled=True, axi...]
    ppermute x7 -> x8, starting transfers between devices: 8.02 us -> 12.3 us  [the longest x7 12.3 us: shards(): arrived[s] = lax.ppermute(packed[s], 'pool', [(i, i ^ s) for i in range(n)])]
    all_to_all x1, starting transfers between devices: 7.68 us -> 6.29 us  [shards(): lax.all_to_all(terms, 'pool', split_axis=0, concat_axis=0, tiled=True)]
    reduce_sum x1 -> x0, other arithmetic: 1.33 us -> none  [shards(): cache_sum = jnp.sum(weights, axis=-1).reshape(rows, -1)]
    unnamed x18 -> x20, local copies, waits for them, and re-layouts: 4.47 us -> 3.32 us
  transfers between devices with their start and end apart: 9 -> 9, of which waited for: 3 -> 3; matrix products, arithmetic and copies ran while one was open for 14% -> 0% of each run, Pallas kernels for 3% -> 21%
where the time goes in v7:
time: 44.2 us; the launch traced here: 43.8 us
  starting transfers between devices  18.6 us (42%)
  Pallas kernels  13.3 us (30%)
  waiting for transfers between devices  7.78 us (18%)
  local copies, waits for them, and re-layouts  3.41 us (8%)
  between operations  0.76 us (2%)
    ppermute x7, starting transfers between devices, shards(): arrived[s] = lax.ppermute(packed[s], 'pool', [(i, i ^ s) for i in range(n)])  12.3 us
    pallas_call x1, Pallas kernels, shards(): pl.pallas_call(base_kernel, grid=(width // depth,), in_specs=[SMEM, pl.Bl...  6.93 us
    all_to_all x1, starting transfers between devices, shards(): lax.all_to_all(terms, 'pool', split_axis=0, concat_axis=0, tiled=True)  6.29 us
    all_to_all x1, waiting for transfers between devices, shards(): lax.all_to_all(terms, 'pool', split_axis=0, concat_axis=0, tiled=True)  4.92 us
    unnamed x20, local copies, waits for them, and re-layouts  3.32 us
    pallas_call x1, Pallas kernels, shards(): call(cache_kernel, [jax.ShapeDtypeStruct(queries.shape, F32)] + [jax.Shap...  1.71 us
    ppermute x7, waiting for transfers between devices, shards(): arrived[s] = lax.ppermute(packed[s], 'pool', [(i, i ^ s) for i in range(n)])  1.5 us
    ppermute x1, waiting for transfers between devices, shards(): other_sums = swap(sums)  1.36 us
  transfers between devices with their start and end apart: 9, of which 3 were waited for; matrix products, arithmetic and copies ran while one was open for 0% of the time, Pallas kernels for 21%

profile of v7, /device:TPU:0, one launch (start us, length us, event | category | flops | bytes accessed | tf_op | source)
XLA Modules:
  0.0 43.8 jit_solution(15744685008646528107)
XLA Ops:
  0.6 0.0 copy-start.9
  0.6 0.0 copy-start
  0.7 1.0 %copy-done = bf16[48,4096]{1,0:T(8,128)(2,1)S(1)} copy-done((bf16[48,4096]{1,0:T(8,128)(2,1)S(1)}, bf16[48,4096]{1,0:T(8,128)(2,1)}, u32[]{:S(2)}) %copy-start) | copy-done | bytes 393240
  1.6 0.0 copy-start.7
  1.6 0.7 %copy-done.7 = s32[48,1]{0,1:T(1,128)S(1)} copy-done((s32[48,1]{0,1:T(1,128)S(1)}, s32[48,1]{0,1:T(1,128)}, u32[]{:S(2)}) %copy-start.7) | copy-done | bytes 216
  2.3 0.0 copy-start.8
  2.3 0.7 %copy-done.8 = s32[8]{0:T(128)S(1)} copy-done((s32[8]{0:T(128)S(1)}, s32[8]{0:T(128)}, u32[]{:S(2)}) %copy-start.8) | copy-done | bytes 56
  3.0 0.0 copy-start.6
  3.0 0.0 copy-start.5
  3.0 0.7 %shard_map.113 = (s32[1,48]{1,0:T(1,128)S(1)}, s32[1,48]{1,0:T(1,128)S(1)}, bf16[48,1024]{1,0:T(8,128)(2,1)S(1)}, bf16[48,1024]{1,0:T(8,128)(2,1)S(1)}, bf16[48,...) custom-call(s32[1]{0:T(128)} %bitcast.me_ref, ...), custom_call_target="tpu_custom_call" | custom-call | tf_op jit(solution)/shard_map/pallas_call | solution.py:276
  3.6 3.0 %collective-permute-start = (bf16[48,1024]{1,0:T(8,128)(2,1)S(1)}, bf16[48,1024]{1,0:T(8,128)(2,1)S(1)}, u32[]{:S(2)}, u32[]{:S(2)}) collective-permute-start(bf16[48,1024]{1,0:T(8,128)(2,1)S(1)} %get-tuple-element.20), channel_id=1, source_target_pairs={{0,2},{2,0},{4,6},{6,4},{8,10},{10,8},{12,14},{14,12},{1,3},{3,1},... | collective-permute-start | bytes 294920 | tf_op jit(solution)/shard_map/ppermute | solution.py:285
  6.7 1.6 %collective-permute-start.1 = (bf16[48,1024]{1,0:T(8,128)(2,1)S(1)}, bf16[48,1024]{1,0:T(8,128)(2,1)S(1)}, u32[]{:S(2)}, u32[]{:S(2)}) collective-permute-start(bf16[48,1024]{1,0:T(8,128)(2,1)S(1)} %get-tuple-element.21), channel_id=1, source_target_pairs={{0,4},{2,6},{4,0},{6,2},{8,12},{10,14},{12,8},{14,10},{1,5},{3,7},... | collective-permute-start | bytes 294920 | tf_op jit(solution)/shard_map/ppermute | solution.py:285
  8.2 2.6 %collective-permute-start.2 = (bf16[48,1024]{1,0:T(8,128)(2,1)S(1)}, bf16[48,1024]{1,0:T(8,128)(2,1)S(1)}, u32[]{:S(2)}, u32[]{:S(2)}) collective-permute-start(bf16[48,1024]{1,0:T(8,128)(2,1)S(1)} %get-tuple-element.22), channel_id=1, source_target_pairs={{0,8},{2,10},{4,12},{6,14},{8,0},{10,2},{12,4},{14,6},{1,9},{3,11}... | collective-permute-start | bytes 294920 | tf_op jit(solution)/shard_map/ppermute | solution.py:285
  10.8 0.3 collective-permute-start.3
  11.1 2.5 %collective-permute-start.4 = (bf16[48,1024]{1,0:T(8,128)(2,1)S(1)}, bf16[48,1024]{1,0:T(8,128)(2,1)S(1)}, u32[]{:S(2)}, u32[]{:S(2)}) collective-permute-start(bf16[48,1024]{1,0:T(8,128)(2,1)S(1)} %get-tuple-element.24), channel_id=1, source_target_pairs={{0,12},{2,14},{4,8},{6,10},{8,4},{10,6},{12,0},{14,2},{1,13},{3,15... | collective-permute-start | bytes 294920 | tf_op jit(solution)/shard_map/ppermute | solution.py:285
  13.6 0.0 collective-permute-done.first_ref.refs_1_
  13.6 2.3 %collective-permute-start.5 = (bf16[48,1024]{1,0:T(8,128)(2,1)S(1)}, bf16[48,1024]{1,0:T(8,128)(2,1)S(1)}, u32[]{:S(2)}, u32[]{:S(2)}) collective-permute-start(bf16[48,1024]{1,0:T(8,128)(2,1)S(1)} %get-tuple-element.25), channel_id=1, source_target_pairs={{0,14},{2,12},{4,10},{6,8},{8,6},{10,4},{12,2},{14,0},{1,15},{3,13... | collective-permute-start | bytes 294920 | tf_op jit(solution)/shard_map/ppermute | solution.py:285
  15.9 0.0 collective-permute-done.1.second_ref.refs_2_
  15.9 0.0 collective-permute-start.6
  15.9 0.0 copy-start.1
  15.9 1.0 %copy-done.1 = bf16[48,4096]{1,0:T(8,128)(2,1)S(1)} copy-done((bf16[48,4096]{1,0:T(8,128)(2,1)S(1)}, bf16[48,4096]{1,0:T(8,128)(2,1)}, u32[]{:S(2)}) %copy-start.1) | copy-done | bytes 393240
  16.9 0.0 copy-start.2
  16.9 0.0 copy-start.3
  16.9 0.0 copy-start.4
  16.9 6.9 %shard_map.114 = (f32[48,512]{1,0:T(8,128)S(1)}, f32[48,512]{1,0:T(8,128)S(1)}) custom-call(s32[1]{0:T(128)} %bitcast.3.core_ref, bf16[48,4096]{1,0:T(8,128)(2,1)S(1)} %copy-done.1, bf16[4096,1024]{1,0:T(8,128)(2,1)} %weight_ref.1, bf16[48,1024]{1,0:T(8,128)(2,1)S(1)} %collective-permute-done.first_ref.refs_1_, ...), custom_call_target="tpu_custom_call" | custom-call | flops 402653184 | bytes 33554432 | tf_op jit(solution)/shard_map/pallas_call | solution.py:288
  23.8 0.0 collective-permute-done.2.refs_3_
  23.8 0.0 collective-permute-done.3.refs_4_
  23.9 0.0 collective-permute-done.4.refs_5_
  23.9 0.0 collective-permute-done.5.refs_6_
  23.9 1.5 %collective-permute-done.6.refs_7_ = bf16[48,1024]{1,0:T(8,128)(2,1)S(1)} collective-permute-done((bf16[48,1024]{1,0:T(8,128)(2,1)S(1)}, bf16[48,1024]{1,0:T(8,128)(2,1)S(1)}, u32[]{:S(2)}, u32[]{:S(2)}) %collective-permute-start.6) | collective-permute-done | bytes 98336 | tf_op jit(solution)/shard_map/ppermute | solution.py:285
  25.4 0.0 copy-done.2
  25.4 1.2 %shard_map.115.mine_ref = f32[288,128]{1,0:T(8,128)S(1)} custom-call(bf16[48,1024]{1,0:T(8,128)(2,1)S(1)} %get-tuple-element.19.refs_0_, bf16[48,1024]{1,0:T(8,128)(2,1)S(1)} %collective-permute-done.first_ref.refs_1_, bf16[48,1024]{1,0:T(8,128)(2,1)S(1)} %collective-permute-done.1.second_ref.refs_2_, bf16[48,1024]{1,0:T(8,128)(2,1)S(1)} %collective-permute-done.2.refs_3_, ...), custom_call_target="tpu_custom_call" | custom-call | tf_op jit(solution)/shard_map/pallas_call | solution.py:308
  26.5 0.1 collective-permute-start.7
  26.6 1.4 %collective-permute-done.7.other_ref = f32[288,128]{1,0:T(8,128)S(1)} collective-permute-done((f32[288,128]{1,0:T(8,128)S(1)}, f32[288,128]{1,0:T(8,128)S(1)}, u32[]{:S(2)}, u32[]{:S(2)}) %collective-permute-start.7) | collective-permute-done | bytes 147488 | tf_op jit(solution)/shard_map/ppermute | solution.py:313
  28.0 0.0 copy-done.6
  28.0 1.1 %shard_map.116._ = bf16[384,128]{1,0:T(8,128)(2,1)} custom-call(s32[1]{0:T(128)} %bitcast.me_ref, f32[288,128]{1,0:T(8,128)S(1)} %shard_map.115.mine_ref, f32[288,128]{1,0:T(8,128)S(1)} %collective-permute-done.7.other_ref, bf16[1,2,64,256]{3,2,1,0:T(8,128)(2,1)S(1)} %copy-done.6), custom_call_target="tpu_custom_call" | custom-call | tf_op jit(solution)/shard_map/pallas_call | solution.py:314
  29.1 6.3 %all-to-all-start = ((bf16[8,48,128]{2,1,0:T(8,128)(2,1)}), bf16[8,48,128]{2,1,0:T(8,128)(2,1)S(1)}, u32[]{:S(2)}, u32[]{:S(2)}) async-start(bf16[8,48,128]{2,1,0:T(8,128)(2,1)} %bitcast.4), calls=%async_computation | async-start | bytes 196608 | tf_op jit(solution)/shard_map/all_to_all | solution.py:327
  35.4 0.0 copy-done.9
  35.4 0.1 copy.12.length_ref
  35.5 0.0 copy-done.5
  35.5 0.0 copy-done.3
  35.5 0.0 copy-done.4
  35.5 1.7 %shard_map.118 = (f32[48,2048]{1,0:T(8,128)S(1)}, f32[48,128]{1,0:T(8,128)S(1)}, f32[48,128]{1,0:T(8,128)S(1)}) custom-call(bf16[48,2048]{1,0:T(8,128)(2,1)S(1)} %copy-done.5, bf16[48,2,32,128]{3,2,1,0:T(8,128)(2,1)S(1)} %copy-done.3, bf16[48,2,32,128]{3,2,1,0:T(8,128)(2,1)S(1)} %copy-done.4, s32[48,1]{1,0:T(8,128)S(1)} %copy.12.length_ref, ...), custom_call_target="tpu_custom_call" | custom-call | tf_op jit(solution)/shard_map/pallas_call | solution.py:328
  37.2 0.4 shard_map.117
  37.6 4.9 %all-to-all-done = bf16[8,48,128]{2,1,0:T(8,128)(2,1)S(1)} async-done(((bf16[8,48,128]{2,1,0:T(8,128)(2,1)}), bf16[8,48,128]{2,1,0:T(8,128)(2,1)S(1)}, u32[]{:S(2)}, u32[]{:S(2)}) %all-to-all-start) | async-done | bytes 98336 | tf_op jit(solution)/shard_map/all_to_all | solution.py:327
  42.5 1.3 %shard_map.119 = (bf16[48,512]{1,0:T(8,128)(2,1)}, bf16[48,2048]{1,0:T(8,128)(2,1)}) custom-call(bf16[384,128]{1,0:T(8,128)(2,1)S(1)} %bitcast.7, bf16[192,384]{1,0:T(8,128)(2,1)S(1)} %get-tuple-element.31.one_hot_ref, f32[48,512]{1,0:T(8,128)S(1)} %get-tuple-element.32.base_ref, bf16[48,2048]{1,0:T(8,128)(2,1)S(1)} %copy-done.5, ...), custom_call_target="tpu_custom_call" | custom-call | tf_op jit(solution)/shard_map/pallas_call | solution.py:333
Async XLA Ops:
  0.6 34.8 %copy-start.9 = (s32[48]{0:T(128)S(1)}, s32[48]{0:T(128)}, u32[]{:S(2)}) copy-start(s32[48]{0:T(128)} %param.18) | copy-start | bytes 580
  0.6 1.0 %copy-start = (bf16[48,4096]{1,0:T(8,128)(2,1)S(1)}, bf16[48,4096]{1,0:T(8,128)(2,1)}, u32[]{:S(2)}) copy-start(bf16[48,4096]{1,0:T(8,128)(2,1)} %hidden_ref.3) | copy-start | bytes 1179652
  1.6 0.7 %copy-start.7 = (s32[48,1]{0,1:T(1,128)S(1)}, s32[48,1]{0,1:T(1,128)}, u32[]{:S(2)}) copy-start(s32[48,1]{0,1:T(1,128)} %param.17) | copy-start | bytes 580
  2.3 0.7 %copy-start.8 = (s32[8]{0:T(128)S(1)}, s32[8]{0:T(128)}, u32[]{:S(2)}) copy-start(s32[8]{0:T(128)} %param.19) | copy-start | bytes 100
  3.0 25.0 %copy-start.6 = (bf16[1,2,64,256]{3,2,1,0:T(8,128)(2,1)S(1)}, bf16[1,2,64,256]{3,2,1,0:T(8,128)(2,1)}, u32[]{:S(2)}) copy-start(bf16[1,2,64,256]{3,2,1,0:T(8,128)(2,1)} %up_ref.1) | copy-start | bytes 196612
  3.0 32.5 %copy-start.5 = (bf16[48,2048]{1,0:T(8,128)(2,1)S(1)}, bf16[48,2048]{1,0:T(8,128)(2,1)}, u32[]{:S(2)}) copy-start(bf16[48,2048]{1,0:T(8,128)(2,1)} %query_ref.3) | copy-start | bytes 589828
  3.6 10.0 %collective-permute-start = (bf16[48,1024]{1,0:T(8,128)(2,1)S(1)}, bf16[48,1024]{1,0:T(8,128)(2,1)S(1)}, u32[]{:S(2)}, u32[]{:S(2)}) collective-permute-start(bf16[48,1024]{1,0:T(8,128)(2,1)S(1)} %get-tuple-element.20), channel_id=1, source_target_pairs={{0,2},{2,0},{4,6},{6,4},{8,10},{10,8},{12,14},{14,12},{1,3},{3,1},... | collective-permute-start | bytes 294920 | tf_op jit(solution)/shard_map/ppermute | solution.py:285
  6.7 9.2 %collective-permute-start.1 = (bf16[48,1024]{1,0:T(8,128)(2,1)S(1)}, bf16[48,1024]{1,0:T(8,128)(2,1)S(1)}, u32[]{:S(2)}, u32[]{:S(2)}) collective-permute-start(bf16[48,1024]{1,0:T(8,128)(2,1)S(1)} %get-tuple-element.21), channel_id=1, source_target_pairs={{0,4},{2,6},{4,0},{6,2},{8,12},{10,14},{12,8},{14,10},{1,5},{3,7},... | collective-permute-start | bytes 294920 | tf_op jit(solution)/shard_map/ppermute | solution.py:285
  8.2 15.6 %collective-permute-start.2 = (bf16[48,1024]{1,0:T(8,128)(2,1)S(1)}, bf16[48,1024]{1,0:T(8,128)(2,1)S(1)}, u32[]{:S(2)}, u32[]{:S(2)}) collective-permute-start(bf16[48,1024]{1,0:T(8,128)(2,1)S(1)} %get-tuple-element.22), channel_id=1, source_target_pairs={{0,8},{2,10},{4,12},{6,14},{8,0},{10,2},{12,4},{14,6},{1,9},{3,11}... | collective-permute-start | bytes 294920 | tf_op jit(solution)/shard_map/ppermute | solution.py:285
  10.8 13.0 %collective-permute-start.3 = (bf16[48,1024]{1,0:T(8,128)(2,1)S(1)}, bf16[48,1024]{1,0:T(8,128)(2,1)S(1)}, u32[]{:S(2)}, u32[]{:S(2)}) collective-permute-start(bf16[48,1024]{1,0:T(8,128)(2,1)S(1)} %get-tuple-element.23), channel_id=1, source_target_pairs={{0,10},{2,8},{4,14},{6,12},{8,2},{10,0},{12,6},{14,4},{1,11},{3,9}... | collective-permute-start | bytes 294920 | tf_op jit(solution)/shard_map/ppermute | solution.py:285
  11.1 12.8 %collective-permute-start.4 = (bf16[48,1024]{1,0:T(8,128)(2,1)S(1)}, bf16[48,1024]{1,0:T(8,128)(2,1)S(1)}, u32[]{:S(2)}, u32[]{:S(2)}) collective-permute-start(bf16[48,1024]{1,0:T(8,128)(2,1)S(1)} %get-tuple-element.24), channel_id=1, source_target_pairs={{0,12},{2,14},{4,8},{6,10},{8,4},{10,6},{12,0},{14,2},{1,13},{3,15... | collective-permute-start | bytes 294920 | tf_op jit(solution)/shard_map/ppermute | solution.py:285
  13.6 10.3 %collective-permute-start.5 = (bf16[48,1024]{1,0:T(8,128)(2,1)S(1)}, bf16[48,1024]{1,0:T(8,128)(2,1)S(1)}, u32[]{:S(2)}, u32[]{:S(2)}) collective-permute-start(bf16[48,1024]{1,0:T(8,128)(2,1)S(1)} %get-tuple-element.25), channel_id=1, source_target_pairs={{0,14},{2,12},{4,10},{6,8},{8,6},{10,4},{12,2},{14,0},{1,15},{3,13... | collective-permute-start | bytes 294920 | tf_op jit(solution)/shard_map/ppermute | solution.py:285
  15.9 9.5 %collective-permute-start.6 = (bf16[48,1024]{1,0:T(8,128)(2,1)S(1)}, bf16[48,1024]{1,0:T(8,128)(2,1)S(1)}, u32[]{:S(2)}, u32[]{:S(2)}) collective-permute-start(bf16[48,1024]{1,0:T(8,128)(2,1)S(1)} %get-tuple-element.26), channel_id=1, source_target_pairs={{0,6},{2,4},{4,2},{6,0},{8,14},{10,12},{12,10},{14,8},{1,7},{3,5},... | collective-permute-start | bytes 294920 | tf_op jit(solution)/shard_map/ppermute | solution.py:285
  15.9 1.0 %copy-start.1 = (bf16[48,4096]{1,0:T(8,128)(2,1)S(1)}, bf16[48,4096]{1,0:T(8,128)(2,1)}, u32[]{:S(2)}) copy-start(bf16[48,4096]{1,0:T(8,128)(2,1)} %hidden_ref.3) | copy-start | bytes 1179652
  16.9 8.5 %copy-start.2 = (bf16[1,4096,128]{2,1,0:T(8,128)(2,1)S(1)}, bf16[1,4096,128]{2,1,0:T(8,128)(2,1)}, u32[]{:S(2)}) copy-start(bf16[1,4096,128]{2,1,0:T(8,128)(2,1)} %refs_8_.1) | copy-start | bytes 3145732
  16.9 18.6 %copy-start.3 = (bf16[48,2,32,128]{3,2,1,0:T(8,128)(2,1)S(1)}, bf16[48,2,32,128]{3,2,1,0:T(8,128)(2,1)}, u32[]{:S(2)}) copy-start(bf16[48,2,32,128]{3,2,1,0:T(8,128)(2,1)} %key_ref.1) | copy-start | bytes 2359300
  16.9 18.6 %copy-start.4 = (bf16[48,2,32,128]{3,2,1,0:T(8,128)(2,1)S(1)}, bf16[48,2,32,128]{3,2,1,0:T(8,128)(2,1)}, u32[]{:S(2)}) copy-start(bf16[48,2,32,128]{3,2,1,0:T(8,128)(2,1)} %value_ref.1) | copy-start | bytes 2359300
  26.5 1.4 %collective-permute-start.7 = (f32[288,128]{1,0:T(8,128)S(1)}, f32[288,128]{1,0:T(8,128)S(1)}, u32[]{:S(2)}, u32[]{:S(2)}) collective-permute-start(f32[288,128]{1,0:T(8,128)S(1)} %shard_map.115.mine_ref), channel_id=1, source_target_pairs={{0,1},{1,0},{2,3},{3,2},{4,5},{5,4},{6,7},{7,6},{8,9},{9,8},{10,11... | collective-permute-start | bytes 442376 | tf_op jit(solution)/shard_map/ppermute | solution.py:313
  29.1 13.4 %all-to-all-start = ((bf16[8,48,128]{2,1,0:T(8,128)(2,1)}), bf16[8,48,128]{2,1,0:T(8,128)(2,1)S(1)}, u32[]{:S(2)}, u32[]{:S(2)}) async-start(bf16[8,48,128]{2,1,0:T(8,128)(2,1)} %bitcast.4), calls=%async_computation | async-start | bytes 196608 | tf_op jit(solution)/shard_map/all_to_all | solution.py:327

commit v8 on v7

--- a/solution.py
+++ b/solution.py
@@ -32,12 +32,11 @@
     return lax.dot_general(a, b, (((0,), (0,)), ((), ())), preferred_element_type=F32)
 
 
-def exact_select(one_hot, x):
+def select_sum(one_hot, x):
     high = x.astype(BF16)
-    rest = x - high.astype(F32)
-    middle = rest.astype(BF16)
-    low = (rest - middle.astype(F32)).astype(BF16)
-    return dot(one_hot, high) + (dot(one_hot, middle) + dot(one_hot, low))
+    low = (x - high.astype(F32)).astype(BF16)
+    both = dot(one_hot, jnp.concatenate([high, low], axis=1))
+    return both[:, : x.shape[1]] + both[:, x.shape[1] :]
 
 
 def codes_of(place, rank, cap, pieces):
@@ -56,40 +55,55 @@
     )
 
 
-def pack_kernel(n, cap, pieces, me_ref, idx_ref, table_ref, hidden_ref, slot_ref, rank_ref, *out_refs):
-    rows = hidden_ref.shape[0]
+def route_kernel(n, idx_ref, table_ref, slot_ref, rank_ref):
+    rows = idx_ref.shape[1]
     named = (iota((n, rows), 0) == idx_ref[...]).astype(F32).astype(BF16)
     table = jnp.broadcast_to(table_ref[...].astype(F32).astype(BF16), (16, n))
     slot = dot(table, named)[0:1, :].astype(I32)
     member = (iota((n, rows), 0) == slot).astype(F32)
     before = (iota((rows, rows), 0) < iota((rows, rows), 1)).astype(F32).astype(BF16)
     count = dot(member.astype(BF16), before)
-    rank = jnp.sum(member * count, axis=0, keepdims=True).astype(I32)
     slot_ref[...] = slot
-    rank_ref[...] = rank
+    rank_ref[...] = jnp.sum(member * count, axis=0, keepdims=True).astype(I32)
+
+
+def pack_kernel(n, cap, pieces, me_ref, slot_ref, rank_ref, hidden_ref, stacked_ref, *out_refs):
     per = pieces * cap
-    apart = lax.bitwise_xor(slot, me_ref[0])
-    one_hot = one_hot_of(codes_of(apart, rank, cap, pieces), 0, n * per)
-    packed = dot(one_hot, stack_pieces(hidden_ref[...], pieces)).astype(BF16)
+    apart = lax.bitwise_xor(slot_ref[...], me_ref[0])
+    one_hot = one_hot_of(codes_of(apart, rank_ref[...], cap, pieces), 0, n * per)
+    stacked = stack_pieces(hidden_ref[...], pieces)
+    stacked_ref[...] = stacked
+    packed = dot(one_hot, stacked).astype(BF16)
     for s, out_ref in enumerate(out_refs):
         out_ref[...] = packed[s * per : (s + 1) * per]
 
 
+def tables_kernel(n, cap, pieces, out_pieces, me_ref, _, shrink_ref, expand_ref):
+    per = pieces * cap
+    out_row, in_row = iota(shrink_ref.shape, 0), iota(shrink_ref.shape, 1)
+    same = (out_row // cap == in_row // per) & (out_row % cap == in_row % cap)
+    shrink_ref[...] = same.astype(F32).astype(BF16)
+    per = out_pieces * cap
+    out_row, in_row = iota(expand_ref.shape, 0), iota(expand_ref.shape, 1)
+    apart = lax.bitwise_xor(out_row // per, me_ref[0])
+    source = (out_row // cap % out_pieces) * (n * cap) + apart * cap + out_row % cap
+    expand_ref[...] = (source == in_row).astype(F32).astype(BF16)
+
+
 def shrink_kernel(n, cap, pieces, order, *refs):
-    received_refs, (down_ref, base_ref, out_ref) = dict(zip(order, refs[:n])), refs[n:]
-    per = pieces * cap
+    received_refs, (down_ref, table_ref, base_ref, out_ref) = dict(zip(order, refs[:n])), refs[n:]
     width = refs[0].shape[1]
     rank2 = down_ref.shape[2]
     received = jnp.concatenate([received_refs[s][...] for s in range(n)], axis=0)
     size = received.shape[0]
     total = jnp.zeros((size, rank2), F32)
     piece_of = (iota((size, rank2), 0) // cap) % pieces
-    for piece in range(pieces):
-        part = dot(received, down_ref[0, piece * width : (piece + 1) * width, :])
-        total = total + jnp.where(piece_of == piece, part, 0.0)
-    out_row, in_row = iota((size // pieces, size), 0), iota((size // pieces, size), 1)
-    same = (out_row // cap == in_row // per) & (out_row % cap == in_row % cap)
-    reduced = exact_select(same.astype(F32).astype(BF16), total)
+    for piece in range(0, pieces, 2):
+        pair = [down_ref[0, i * width : (i + 1) * width, :] for i in (piece, piece + 1)]
+        part = dot(received, jnp.concatenate(pair, axis=1))
+        total = total + jnp.where(piece_of == piece, part[:, :rank2], 0.0)
+        total = total + jnp.where(piece_of == piece + 1, part[:, rank2:], 0.0)
+    reduced = select_sum(table_ref[...], total)
     size = reduced.shape[0]
     out_ref[:size, :] = reduced
     rows = base_ref.shape[0]
@@ -98,7 +112,7 @@
         out_ref[first : first + rows, :] = base_ref[:, i * rank2 : (i + 1) * rank2]
 
 
-def expand_kernel(n, cap, me_ref, mine_ref, other_ref, up_ref, out_ref):
+def expand_kernel(n, cap, mine_ref, other_ref, up_ref, table_ref, out_ref):
     rank = up_ref.shape[2]
     head = 128
     blocks = up_ref.shape[3] // head
@@ -108,14 +122,7 @@
         kept = reduced[:, c * rank : (c + 1) * rank]
         wide = dot(kept, up_ref[0, c]).astype(BF16)
         terms += [wide[:, g * head : (g + 1) * head] for g in range(blocks)]
-    stacked = jnp.concatenate(terms, axis=0)
-    pieces = 2 * blocks
-    per = pieces * cap
-    size = n * per
-    out_row, in_row = iota((size, size), 0), iota((size, size), 1)
-    apart = lax.bitwise_xor(out_row // per, me_ref[0])
-    source = (out_row // cap % pieces) * (n * cap) + apart * cap + out_row % cap
-    out_ref[...] = dot((source == in_row).astype(F32).astype(BF16), stacked).astype(BF16)
+    out_ref[...] = dot(table_ref[...], jnp.concatenate(terms, axis=0)).astype(BF16)
 
 
 def prepare_kernel(n, cap, slot_ref, rank_ref, mine_ref, other_ref, _, base_ref, one_hot_ref):
@@ -131,24 +138,23 @@
     one_hot_ref[...] = dot_first(one_hot, same).astype(BF16)
 
 
-def base_kernel(core_ref, hidden_ref, weight_ref, first_ref, second_ref, mine_ref, other_ref, total_ref):
-    step = pl.program_id(0)
-    part = dot(hidden_ref[...], weight_ref[...])
-
-    @pl.when(step == 0)
-    def _():
-        total_ref[...] = part
-
-    @pl.when(step > 0)
-    def _():
-        total_ref[...] += part
-
-    @pl.when(step == pl.num_programs(0) - 1)
-    def _():
-        columns = mine_ref.shape[1]
-        first, second = total_ref[:, :columns], total_ref[:, columns:]
-        mine_ref[...] = jnp.where(core_ref[0] == 0, first, second)
-        other_ref[...] = jnp.where(core_ref[0] == 0, second, first)
+def base_kernel(
+    pieces, core_ref, stacked_ref, weight_hbm, first_ref, second_ref, mine_ref, other_ref, weight_ref, sems
+):
+    depth = weight_ref.shape[0] // pieces
+    copies = []
+    for k in range(pieces):
+        part = pl.ds(k * depth, depth)
+        copies.append(pltpu.make_async_copy(weight_hbm.at[part, :], weight_ref.at[part, :], sems.at[k]))
+        copies[k].start()
+    rows, columns = mine_ref.shape
+    total = jnp.zeros((rows, 2 * columns), F32)
+    for k in range(pieces):
+        copies[k].wait()
+        total = total + dot(stacked_ref[k * rows : (k + 1) * rows, :], weight_ref[k * depth : (k + 1) * depth, :])
+    first, second = total[:, :columns], total[:, columns:]
+    mine_ref[...] = jnp.where(core_ref[0] == 0, first, second)
+    other_ref[...] = jnp.where(core_ref[0] == 0, second, first)
 
 
 def cache_kernel(query_ref, key_ref, value_ref, length_ref, _, acc_ref, max_ref, sum_ref):
@@ -237,14 +243,15 @@
 NO_COST = pl.CostEstimate(flops=0, bytes_accessed=0, transcendentals=0)
 
 
-def call(kernel, outs, specs):
+def call(kernel, outs, specs, scratch=(), cost=NO_COST):
     return pl.pallas_call(
         kernel,
         out_shape=outs,
         in_specs=specs,
         out_specs=[VMEM] * len(outs),
+        scratch_shapes=scratch,
         compiler_params=pltpu.CompilerParams(vmem_limit_bytes=VMEM_LIMIT),
-        cost_estimate=NO_COST,
+        cost_estimate=cost,
     )
 
 
@@ -273,49 +280,51 @@
     swap = functools.partial(lax.ppermute, axis_name="tp", perm=[(0, 1), (1, 0)])
 
     me = lax.axis_index("pool").reshape(1)
-    slot, rank, *packed = call(
+    slot, rank = call(
+        functools.partial(route_kernel, n), [jax.ShapeDtypeStruct((1, rows), I32)] * 2, [VMEM] * 2
+    )(row_adapter_index.reshape(1, rows), adapter_slot_table.reshape(1, n))
+    stacked, *packed = call(
         functools.partial(pack_kernel, n, cap, pieces),
-        [jax.ShapeDtypeStruct((1, rows), I32)] * 2
+        [jax.ShapeDtypeStruct((pieces * rows, width // pieces), BF16)]
         + [jax.ShapeDtypeStruct((pieces * cap, width // pieces), BF16)] * n,
         [SMEM, VMEM, VMEM, VMEM],
-    )(me, row_adapter_index.reshape(1, rows), adapter_slot_table.reshape(1, n), hidden)
-    order = [0, 1, 2, *range(n // 2, n), *range(3, n // 2)]
+    )(me, slot, rank, hidden)
+    half = n // 2
+    order = [0, half, 1, half + 1, 2, *range(half + 2, n), *range(3, half)]
     arrived = {0: packed[0]}
     for s in order[1:]:
         arrived[s] = lax.ppermute(packed[s], "pool", [(i, i ^ s) for i in range(n)])
 
-    depth = 512
-    base_mine, base_other = pl.pallas_call(
-        base_kernel,
-        grid=(width // depth,),
-        in_specs=[
-            SMEM,
-            pl.BlockSpec((rows, depth), lambda k: (0, k)),
-            pl.BlockSpec((depth, 2 * columns), lambda k: (k, 0)),
-            ANY,
-            ANY,
-        ],
-        out_specs=[pl.BlockSpec((rows, columns), lambda k: (0, 0))] * 2,
-        out_shape=[jax.ShapeDtypeStruct((rows, columns), F32)] * 2,
-        scratch_shapes=[pltpu.VMEM((rows, 2 * columns), F32)],
-        compiler_params=pltpu.CompilerParams(vmem_limit_bytes=VMEM_LIMIT),
-        cost_estimate=pl.CostEstimate(
+    base_mine, base_other = call(
+        functools.partial(base_kernel, pieces),
+        [jax.ShapeDtypeStruct((rows, columns), F32)] * 2,
+        [SMEM, VMEM, ANY, ANY, ANY],
+        [pltpu.VMEM((width, 2 * columns), BF16), pltpu.SemaphoreType.DMA((pieces,))],
+        pl.CostEstimate(
             flops=4 * rows * width * columns, bytes_accessed=16 * width * columns, transcendentals=0
         ),
-    )(lax.axis_index("tp").reshape(1), hidden, key_value_weight, arrived[1], arrived[2])
+    )(lax.axis_index("tp").reshape(1), stacked, key_value_weight, arrived[1], arrived[2])
 
     size = n * out_pieces * cap
+    shrink_table, expand_table = call(
+        functools.partial(tables_kernel, n, cap, pieces, out_pieces),
+        [
+            jax.ShapeDtypeStruct((n * cap, n * pieces * cap), BF16),
+            jax.ShapeDtypeStruct((size, size), BF16),
+        ],
+        [SMEM, ANY],
+    )(me, base_mine)
     (sums,) = call(
         functools.partial(shrink_kernel, n, cap, pieces, order),
         [jax.ShapeDtypeStruct((n * cap + rows * columns // rank2, rank2), F32)],
-        [VMEM] * (n + 2),
-    )(*[arrived[s] for s in order], adapter_down_weight, base_other)
+        [VMEM] * (n + 3),
+    )(*[arrived[s] for s in order], adapter_down_weight, shrink_table, base_other)
     other_sums = swap(sums)
     (terms,) = call(
         functools.partial(expand_kernel, n, cap),
         [jax.ShapeDtypeStruct((size, head), BF16)],
-        [SMEM] + [VMEM] * 3,
-    )(me, sums, other_sums, adapter_up_weight)
+        [VMEM] * 4,
+    )(sums, other_sums, adapter_up_weight, expand_table)
     base, one_hot = call(
         functools.partial(prepare_kernel, n, cap),
         [

time: 44.2 us -> 46.6 us (1.054)
  waiting for transfers between devices: 7.78 us -> 11.7 us
  Pallas kernels: 13.3 us -> 11.9 us
    ppermute x7, waiting for transfers between devices: 1.5 us -> 5.46 us  [shards(): arrived[s] = lax.ppermute(packed[s], 'pool', [(i, i ^ s) for i in range(n)])]
    pallas_call x1 -> x3, Pallas kernels: 6.93 us -> 4.52 us  [the longest x1 4.01 us: shards(): call(functools.partial(base_kernel, pieces), [jax.ShapeDtypeStruct((rows,...]
    pallas_call x1, Pallas kernels: 1.18 us -> 1.84 us  [shards(): call(functools.partial(shrink_kernel, n, cap, pieces, order), [jax.ShapeD...]
    pallas_call x1, Pallas kernels: 0.65 us -> 1.12 us  [shards(): call(functools.partial(pack_kernel, n, cap, pieces), [jax.ShapeDtypeStruc...]
    unnamed x20 -> x22, local copies, waits for them, and re-layouts: 3.32 us -> 3.14 us
  transfers between devices with their start and end apart: 9 -> 9, of which waited for: 3 -> 5; matrix products, arithmetic and copies ran while one was open for 0% -> 0% of each run, Pallas kernels for 21% -> 14%
where the time goes in v8:
time: 46.6 us; the launch traced here: 46.2 us
  starting transfers between devices  18.6 us (40%)
  Pallas kernels  11.9 us (26%)
  waiting for transfers between devices  11.7 us (25%)
  local copies, waits for them, and re-layouts  3.23 us (7%)
  between operations  0.75 us (2%)
    ppermute x7, starting transfers between devices, shards(): arrived[s] = lax.ppermute(packed[s], 'pool', [(i, i ^ s) for i in range(n)])  12.2 us
    all_to_all x1, starting transfers between devices, shards(): lax.all_to_all(terms, 'pool', split_axis=0, concat_axis=0, tiled=True)  6.32 us
    ppermute x7, waiting for transfers between devices, shards(): arrived[s] = lax.ppermute(packed[s], 'pool', [(i, i ^ s) for i in range(n)])  5.46 us
    all_to_all x1, waiting for transfers between devices, shards(): lax.all_to_all(terms, 'pool', split_axis=0, concat_axis=0, tiled=True)  4.92 us
    pallas_call x1, Pallas kernels, shards(): call(functools.partial(base_kernel, pieces), [jax.ShapeDtypeStruct((rows,...  4.01 us
    unnamed x22, local copies, waits for them, and re-layouts  3.14 us
    pallas_call x1, Pallas kernels, shards(): call(functools.partial(shrink_kernel, n, cap, pieces, order), [jax.ShapeD...  1.84 us
    pallas_call x1, Pallas kernels, shards(): call(cache_kernel, [jax.ShapeDtypeStruct(queries.shape, F32)] + [jax.Shap...  1.71 us
  transfers between devices with their start and end apart: 9, of which 5 were waited for; matrix products, arithmetic and copies ran while one was open for 0% of the time, Pallas kernels for 14%

profile of v8, /device:TPU:0, one launch (start us, length us, event | category | flops | bytes accessed | tf_op | source)
XLA Modules:
  0.0 46.2 jit_solution(8175742703222798951)
XLA Ops:
  0.6 0.0 copy-start
  0.6 0.0 copy-start.3
  0.7 0.0 copy-start.1
  0.7 0.0 copy-start.2
  0.7 0.0 copy-start.8
  0.7 0.8 %copy-done.8 = s32[48,1]{0,1:T(1,128)S(1)} copy-done((s32[48,1]{0,1:T(1,128)S(1)}, s32[48,1]{0,1:T(1,128)}, u32[]{:S(2)}) %copy-start.8) | copy-done | bytes 216
  1.5 0.0 copy-start.9
  1.5 0.7 %copy-done.9 = s32[8]{0:T(128)S(1)} copy-done((s32[8]{0:T(128)S(1)}, s32[8]{0:T(128)}, u32[]{:S(2)}) %copy-start.9) | copy-done | bytes 56
  2.2 0.2 shard_map.113
  2.4 0.0 copy-start.4
  2.4 1.0 %copy-done.4 = bf16[48,4096]{1,0:T(8,128)(2,1)S(1)} copy-done((bf16[48,4096]{1,0:T(8,128)(2,1)S(1)}, bf16[48,4096]{1,0:T(8,128)(2,1)}, u32[]{:S(2)}) %copy-start.4) | copy-done | bytes 393240
  3.4 0.0 copy-start.10
  3.4 1.1 %shard_map.114 = (bf16[192,1024]{1,0:T(8,128)(2,1)S(1)}, bf16[48,1024]{1,0:T(8,128)(2,1)S(1)}, bf16[48,1024]{1,0:T(8,128)(2,1)S(1)}, bf16[48,1024]{1,0:T(8,128)(...) custom-call(s32[1]{0:T(128)} %bitcast.me_ref, ...), custom_call_target="tpu_custom_call" | custom-call | tf_op jit(solution)/shard_map/pallas_call | solution.py:286
  4.5 0.6 %copy-done.5 = bf16[48,1024]{1,0:T(8,128)(2,1)} copy-done((bf16[48,1024]{1,0:T(8,128)(2,1)}, bf16[48,1024]{1,0:T(8,128)(2,1)S(1)}, u32[]{:S(2)}) %copy-start.5) | copy-done | bytes 98328
  5.2 3.0 %collective-permute-start.1 = (bf16[48,1024]{1,0:T(8,128)(2,1)S(1)}, bf16[48,1024]{1,0:T(8,128)(2,1)S(1)}, u32[]{:S(2)}, u32[]{:S(2)}) collective-permute-start(bf16[48,1024]{1,0:T(8,128)(2,1)S(1)} %get-tuple-element.26), channel_id=1, source_target_pairs={{0,2},{2,0},{4,6},{6,4},{8,10},{10,8},{12,14},{14,12},{1,3},{3,1},... | collective-permute-start | bytes 294920 | tf_op jit(solution)/shard_map/ppermute | solution.py:296
  8.1 1.6 %collective-permute-start.3 = (bf16[48,1024]{1,0:T(8,128)(2,1)S(1)}, bf16[48,1024]{1,0:T(8,128)(2,1)S(1)}, u32[]{:S(2)}, u32[]{:S(2)}) collective-permute-start(bf16[48,1024]{1,0:T(8,128)(2,1)S(1)} %get-tuple-element.28), channel_id=1, source_target_pairs={{0,4},{2,6},{4,0},{6,2},{8,12},{10,14},{12,8},{14,10},{1,5},{3,7},... | collective-permute-start | bytes 294920 | tf_op jit(solution)/shard_map/ppermute | solution.py:296
  9.7 2.6 %collective-permute-start = (bf16[48,1024]{1,0:T(8,128)(2,1)}, bf16[48,1024]{1,0:T(8,128)(2,1)}, u32[]{:S(2)}, u32[]{:S(2)}) collective-permute-start(bf16[48,1024]{1,0:T(8,128)(2,1)} %get-tuple-element.25), channel_id=1, source_target_pairs={{0,8},{2,10},{4,12},{6,14},{8,0},{10,2},{12,4},{14,6},{1,9},{3,11}... | collective-permute-start | bytes 294920 | tf_op jit(solution)/shard_map/ppermute | solution.py:296
  12.3 0.3 collective-permute-start.2
  12.6 2.5 %collective-permute-start.4 = (bf16[48,1024]{1,0:T(8,128)(2,1)}, bf16[48,1024]{1,0:T(8,128)(2,1)}, u32[]{:S(2)}, u32[]{:S(2)}) collective-permute-start(bf16[48,1024]{1,0:T(8,128)(2,1)} %get-tuple-element.29), channel_id=1, source_target_pairs={{0,12},{2,14},{4,8},{6,10},{8,4},{10,6},{12,0},{14,2},{1,13},{3,15... | collective-permute-start | bytes 294920 | tf_op jit(solution)/shard_map/ppermute | solution.py:296
  15.1 0.0 collective-permute-done.1.first_ref.refs_2_
  15.1 2.3 %collective-permute-start.5 = (bf16[48,1024]{1,0:T(8,128)(2,1)}, bf16[48,1024]{1,0:T(8,128)(2,1)}, u32[]{:S(2)}, u32[]{:S(2)}) collective-permute-start(bf16[48,1024]{1,0:T(8,128)(2,1)} %get-tuple-element.30), channel_id=1, source_target_pairs={{0,14},{2,12},{4,10},{6,8},{8,6},{10,4},{12,2},{14,0},{1,15},{3,13... | collective-permute-start | bytes 294920 | tf_op jit(solution)/shard_map/ppermute | solution.py:296
  17.4 0.0 collective-permute-done.3.second_ref.refs_4_
  17.4 0.0 collective-permute-start.6
  17.4 0.0 copy-start.7
  17.4 4.0 %shard_map.115 = (f32[48,512]{1,0:T(8,128)S(1)}, f32[48,512]{1,0:T(8,128)S(1)}) custom-call(s32[1]{0:T(128)} %bitcast.3.core_ref, bf16[192,1024]{1,0:T(8,128)(2,1)S(1)} %get-tuple-element.32.stacked_ref, bf16[4096,1024]{1,0:T(8,128)(2,1)} %weight_hbm.1, bf16[48,1024]{1,0:T(8,128)(2,1)S(1)} %collective-permute-done.1.first_ref.refs_2_, ...), custom_call_target="tpu_custom_call" | custom-call | flops 402653184 | bytes 33554432 | tf_op jit(solution)/shard_map/pallas_call | solution.py:298
  21.4 0.3 shard_map.116
  21.7 2.6 %collective-permute-done.refs_1_ = bf16[48,1024]{1,0:T(8,128)(2,1)} collective-permute-done((bf16[48,1024]{1,0:T(8,128)(2,1)}, bf16[48,1024]{1,0:T(8,128)(2,1)}, u32[]{:S(2)}, u32[]{:S(2)}) %collective-permute-start) | collective-permute-done | bytes 98336 | tf_op jit(solution)/shard_map/ppermute | solution.py:296
  24.3 1.5 %collective-permute-done.2.refs_3_ = bf16[48,1024]{1,0:T(8,128)(2,1)} collective-permute-done((bf16[48,1024]{1,0:T(8,128)(2,1)}, bf16[48,1024]{1,0:T(8,128)(2,1)}, u32[]{:S(2)}, u32[]{:S(2)}) %collective-permute-start.2) | collective-permute-done | bytes 98336 | tf_op jit(solution)/shard_map/ppermute | solution.py:296
  25.7 0.0 collective-permute-done.4.refs_5_
  25.7 0.0 collective-permute-done.5.refs_6_
  25.8 1.4 %collective-permute-done.6.refs_7_ = bf16[48,1024]{1,0:T(8,128)(2,1)} collective-permute-done((bf16[48,1024]{1,0:T(8,128)(2,1)}, bf16[48,1024]{1,0:T(8,128)(2,1)}, u32[]{:S(2)}, u32[]{:S(2)}) %collective-permute-start.6) | collective-permute-done | bytes 98336 | tf_op jit(solution)/shard_map/ppermute | solution.py:296
  27.1 0.0 copy-done
  27.1 0.0 copy-done.6
  27.1 1.8 %shard_map.117.mine_ref = f32[288,128]{1,0:T(8,128)S(1)} custom-call(bf16[48,1024]{1,0:T(8,128)(2,1)S(1)} %copy-done.6, bf16[48,1024]{1,0:T(8,128)(2,1)} %collective-permute-done.refs_1_, bf16[48,1024]{1,0:T(8,128)(2,1)S(1)} %collective-permute-done.1.first_ref.refs_2_, bf16[48,1024]{1,0:T(8,128)(2,1)} %collective-permute-done.2.refs_3_, ...), custom_call_target="tpu_custom_call" | custom-call | tf_op jit(solution)/shard_map/pallas_call | solution.py:317
  29.0 0.1 collective-permute-start.7
  29.1 1.4 %collective-permute-done.7.other_ref = f32[288,128]{1,0:T(8,128)S(1)} collective-permute-done((f32[288,128]{1,0:T(8,128)S(1)}, f32[288,128]{1,0:T(8,128)S(1)}, u32[]{:S(2)}, u32[]{:S(2)}) %collective-permute-start.7) | collective-permute-done | bytes 147488 | tf_op jit(solution)/shard_map/ppermute | solution.py:322
  30.4 0.0 copy-done.7
  30.4 1.0 %shard_map.118._ = bf16[384,128]{1,0:T(8,128)(2,1)} custom-call(f32[288,128]{1,0:T(8,128)S(1)} %shard_map.117.mine_ref, f32[288,128]{1,0:T(8,128)S(1)} %collective-permute-done.7.other_ref, bf16[1,2,64,256]{3,2,1,0:T(8,128)(2,1)S(1)} %copy-done.7, bf16[384,384]{1,0:T(8,128)(2,1)S(1)} %get-tuple-element.36.table_ref), custom_call_target="tpu_custom_call" | custom-call | tf_op jit(solution)/shard_map/pallas_call | solution.py:323
  31.5 6.3 %all-to-all-start = ((bf16[8,48,128]{2,1,0:T(8,128)(2,1)}), bf16[8,48,128]{2,1,0:T(8,128)(2,1)S(1)}, u32[]{:S(2)}, u32[]{:S(2)}) async-start(bf16[8,48,128]{2,1,0:T(8,128)(2,1)} %bitcast.4), calls=%async_computation | async-start | bytes 196608 | tf_op jit(solution)/shard_map/all_to_all | solution.py:336
  37.8 0.0 copy-done.10
  37.8 0.1 copy.12.length_ref
  37.9 0.0 copy-done.3
  37.9 0.0 copy-done.1
  37.9 0.0 copy-done.2
  37.9 1.7 %shard_map.120 = (f32[48,2048]{1,0:T(8,128)S(1)}, f32[48,128]{1,0:T(8,128)S(1)}, f32[48,128]{1,0:T(8,128)S(1)}) custom-call(bf16[48,2048]{1,0:T(8,128)(2,1)S(1)} %copy-done.3, bf16[48,2,32,128]{3,2,1,0:T(8,128)(2,1)S(1)} %copy-done.1, bf16[48,2,32,128]{3,2,1,0:T(8,128)(2,1)S(1)} %copy-done.2, s32[48,1]{1,0:T(8,128)S(1)} %copy.12.length_ref, ...), custom_call_target="tpu_custom_call" | custom-call | tf_op jit(solution)/shard_map/pallas_call | solution.py:337
  39.6 0.4 shard_map.119
  40.0 4.9 %all-to-all-done = bf16[8,48,128]{2,1,0:T(8,128)(2,1)S(1)} async-done(((bf16[8,48,128]{2,1,0:T(8,128)(2,1)}), bf16[8,48,128]{2,1,0:T(8,128)(2,1)S(1)}, u32[]{:S(2)}, u32[]{:S(2)}) %all-to-all-start) | async-done | bytes 98336 | tf_op jit(solution)/shard_map/all_to_all | solution.py:336
  44.9 1.3 %shard_map.121 = (bf16[48,512]{1,0:T(8,128)(2,1)}, bf16[48,2048]{1,0:T(8,128)(2,1)}) custom-call(bf16[384,128]{1,0:T(8,128)(2,1)S(1)} %bitcast.7, bf16[192,384]{1,0:T(8,128)(2,1)S(1)} %get-tuple-element.37.one_hot_ref, f32[48,512]{1,0:T(8,128)S(1)} %get-tuple-element.38.base_ref, bf16[48,2048]{1,0:T(8,128)(2,1)S(1)} %copy-done.3, ...), custom_call_target="tpu_custom_call" | custom-call | tf_op jit(solution)/shard_map/pallas_call | solution.py:342
  (2 shorter events, 0.0 us)
Async XLA Ops:
  0.6 26.5 %copy-start = (bf16[1,4096,128]{2,1,0:T(8,128)(2,1)S(1)}, bf16[1,4096,128]{2,1,0:T(8,128)(2,1)}, u32[]{:S(2)}) copy-start(bf16[1,4096,128]{2,1,0:T(8,128)(2,1)} %refs_8_.1) | copy-start | bytes 3145732
  0.6 37.3 %copy-start.3 = (bf16[48,2048]{1,0:T(8,128)(2,1)S(1)}, bf16[48,2048]{1,0:T(8,128)(2,1)}, u32[]{:S(2)}) copy-start(bf16[48,2048]{1,0:T(8,128)(2,1)} %query_ref.3) | copy-start | bytes 589828
  0.7 37.2 %copy-start.1 = (bf16[48,2,32,128]{3,2,1,0:T(8,128)(2,1)S(1)}, bf16[48,2,32,128]{3,2,1,0:T(8,128)(2,1)}, u32[]{:S(2)}) copy-start(bf16[48,2,32,128]{3,2,1,0:T(8,128)(2,1)} %key_ref.1) | copy-start | bytes 2359300
  0.7 37.2 %copy-start.2 = (bf16[48,2,32,128]{3,2,1,0:T(8,128)(2,1)S(1)}, bf16[48,2,32,128]{3,2,1,0:T(8,128)(2,1)}, u32[]{:S(2)}) copy-start(bf16[48,2,32,128]{3,2,1,0:T(8,128)(2,1)} %value_ref.1) | copy-start | bytes 2359300
  0.7 0.8 %copy-start.8 = (s32[48,1]{0,1:T(1,128)S(1)}, s32[48,1]{0,1:T(1,128)}, u32[]{:S(2)}) copy-start(s32[48,1]{0,1:T(1,128)} %param.17) | copy-start | bytes 580
  1.5 0.7 %copy-start.9 = (s32[8]{0:T(128)S(1)}, s32[8]{0:T(128)}, u32[]{:S(2)}) copy-start(s32[8]{0:T(128)} %param.19) | copy-start | bytes 100
  2.4 1.0 %copy-start.4 = (bf16[48,4096]{1,0:T(8,128)(2,1)S(1)}, bf16[48,4096]{1,0:T(8,128)(2,1)}, u32[]{:S(2)}) copy-start(bf16[48,4096]{1,0:T(8,128)(2,1)} %hidden_ref.1) | copy-start | bytes 1179652
  3.4 34.4 %copy-start.10 = (s32[48]{0:T(128)S(1)}, s32[48]{0:T(128)}, u32[]{:S(2)}) copy-start(s32[48]{0:T(128)} %param.18) | copy-start | bytes 580
  4.5 0.6 %copy-start.5 = (bf16[48,1024]{1,0:T(8,128)(2,1)}, bf16[48,1024]{1,0:T(8,128)(2,1)S(1)}, u32[]{:S(2)}) copy-start(bf16[48,1024]{1,0:T(8,128)(2,1)S(1)} %get-tuple-element.24.refs_0_) | copy-start | bytes 294916
  5.2 9.9 %collective-permute-start.1 = (bf16[48,1024]{1,0:T(8,128)(2,1)S(1)}, bf16[48,1024]{1,0:T(8,128)(2,1)S(1)}, u32[]{:S(2)}, u32[]{:S(2)}) collective-permute-start(bf16[48,1024]{1,0:T(8,128)(2,1)S(1)} %get-tuple-element.26), channel_id=1, source_target_pairs={{0,2},{2,0},{4,6},{6,4},{8,10},{10,8},{12,14},{14,12},{1,3},{3,1},... | collective-permute-start | bytes 294920 | tf_op jit(solution)/shard_map/ppermute | solution.py:296
  8.1 9.2 %collective-permute-start.3 = (bf16[48,1024]{1,0:T(8,128)(2,1)S(1)}, bf16[48,1024]{1,0:T(8,128)(2,1)S(1)}, u32[]{:S(2)}, u32[]{:S(2)}) collective-permute-start(bf16[48,1024]{1,0:T(8,128)(2,1)S(1)} %get-tuple-element.28), channel_id=1, source_target_pairs={{0,4},{2,6},{4,0},{6,2},{8,12},{10,14},{12,8},{14,10},{1,5},{3,7},... | collective-permute-start | bytes 294920 | tf_op jit(solution)/shard_map/ppermute | solution.py:296
  9.7 14.6 %collective-permute-start = (bf16[48,1024]{1,0:T(8,128)(2,1)}, bf16[48,1024]{1,0:T(8,128)(2,1)}, u32[]{:S(2)}, u32[]{:S(2)}) collective-permute-start(bf16[48,1024]{1,0:T(8,128)(2,1)} %get-tuple-element.25), channel_id=1, source_target_pairs={{0,8},{2,10},{4,12},{6,14},{8,0},{10,2},{12,4},{14,6},{1,9},{3,11}... | collective-permute-start | bytes 294920 | tf_op jit(solution)/shard_map/ppermute | solution.py:296
  12.3 13.4 %collective-permute-start.2 = (bf16[48,1024]{1,0:T(8,128)(2,1)}, bf16[48,1024]{1,0:T(8,128)(2,1)}, u32[]{:S(2)}, u32[]{:S(2)}) collective-permute-start(bf16[48,1024]{1,0:T(8,128)(2,1)} %get-tuple-element.27), channel_id=1, source_target_pairs={{0,10},{2,8},{4,14},{6,12},{8,2},{10,0},{12,6},{14,4},{1,11},{3,9}... | collective-permute-start | bytes 294920 | tf_op jit(solution)/shard_map/ppermute | solution.py:296
  12.6 13.2 %collective-permute-start.4 = (bf16[48,1024]{1,0:T(8,128)(2,1)}, bf16[48,1024]{1,0:T(8,128)(2,1)}, u32[]{:S(2)}, u32[]{:S(2)}) collective-permute-start(bf16[48,1024]{1,0:T(8,128)(2,1)} %get-tuple-element.29), channel_id=1, source_target_pairs={{0,12},{2,14},{4,8},{6,10},{8,4},{10,6},{12,0},{14,2},{1,13},{3,15... | collective-permute-start | bytes 294920 | tf_op jit(solution)/shard_map/ppermute | solution.py:296
  15.1 10.7 %collective-permute-start.5 = (bf16[48,1024]{1,0:T(8,128)(2,1)}, bf16[48,1024]{1,0:T(8,128)(2,1)}, u32[]{:S(2)}, u32[]{:S(2)}) collective-permute-start(bf16[48,1024]{1,0:T(8,128)(2,1)} %get-tuple-element.30), channel_id=1, source_target_pairs={{0,14},{2,12},{4,10},{6,8},{8,6},{10,4},{12,2},{14,0},{1,15},{3,13... | collective-permute-start | bytes 294920 | tf_op jit(solution)/shard_map/ppermute | solution.py:296
  17.4 9.8 %collective-permute-start.6 = (bf16[48,1024]{1,0:T(8,128)(2,1)}, bf16[48,1024]{1,0:T(8,128)(2,1)}, u32[]{:S(2)}, u32[]{:S(2)}) collective-permute-start(bf16[48,1024]{1,0:T(8,128)(2,1)} %get-tuple-element.31), channel_id=1, source_target_pairs={{0,6},{2,4},{4,2},{6,0},{8,14},{10,12},{12,10},{14,8},{1,7},{3,5},... | collective-permute-start | bytes 294920 | tf_op jit(solution)/shard_map/ppermute | solution.py:296
  17.4 9.8 %copy-start.6 = (bf16[48,1024]{1,0:T(8,128)(2,1)S(1)}, bf16[48,1024]{1,0:T(8,128)(2,1)}, u32[]{:S(2)}) copy-start(bf16[48,1024]{1,0:T(8,128)(2,1)} %copy-done.5) | copy-start | bytes 294916
  17.4 13.1 %copy-start.7 = (bf16[1,2,64,256]{3,2,1,0:T(8,128)(2,1)S(1)}, bf16[1,2,64,256]{3,2,1,0:T(8,128)(2,1)}, u32[]{:S(2)}) copy-start(bf16[1,2,64,256]{3,2,1,0:T(8,128)(2,1)} %up_ref.1) | copy-start | bytes 196612
  29.0 1.4 %collective-permute-start.7 = (f32[288,128]{1,0:T(8,128)S(1)}, f32[288,128]{1,0:T(8,128)S(1)}, u32[]{:S(2)}, u32[]{:S(2)}) collective-permute-start(f32[288,128]{1,0:T(8,128)S(1)} %shard_map.117.mine_ref), channel_id=1, source_target_pairs={{0,1},{1,0},{2,3},{3,2},{4,5},{5,4},{6,7},{7,6},{8,9},{9,8},{10,11... | collective-permute-start | bytes 442376 | tf_op jit(solution)/shard_map/ppermute | solution.py:322
  31.5 13.4 %all-to-all-start = ((bf16[8,48,128]{2,1,0:T(8,128)(2,1)}), bf16[8,48,128]{2,1,0:T(8,128)(2,1)S(1)}, u32[]{:S(2)}, u32[]{:S(2)}) async-start(bf16[8,48,128]{2,1,0:T(8,128)(2,1)} %bitcast.4), calls=%async_computation | async-start | bytes 196608 | tf_op jit(solution)/shard_map/all_to_all | solution.py:336

commit v9 on v8

--- a/solution.py
+++ b/solution.py
@@ -55,25 +55,21 @@
     )
 
 
-def route_kernel(n, idx_ref, table_ref, slot_ref, rank_ref):
-    rows = idx_ref.shape[1]
+def pack_kernel(n, cap, pieces, me_ref, idx_ref, table_ref, hidden_ref, slot_ref, rank_ref, *out_refs):
+    rows = hidden_ref.shape[0]
     named = (iota((n, rows), 0) == idx_ref[...]).astype(F32).astype(BF16)
     table = jnp.broadcast_to(table_ref[...].astype(F32).astype(BF16), (16, n))
     slot = dot(table, named)[0:1, :].astype(I32)
     member = (iota((n, rows), 0) == slot).astype(F32)
     before = (iota((rows, rows), 0) < iota((rows, rows), 1)).astype(F32).astype(BF16)
     count = dot(member.astype(BF16), before)
+    rank = jnp.sum(member * count, axis=0, keepdims=True).astype(I32)
     slot_ref[...] = slot
-    rank_ref[...] = jnp.sum(member * count, axis=0, keepdims=True).astype(I32)
-
-
-def pack_kernel(n, cap, pieces, me_ref, slot_ref, rank_ref, hidden_ref, stacked_ref, *out_refs):
+    rank_ref[...] = rank
     per = pieces * cap
-    apart = lax.bitwise_xor(slot_ref[...], me_ref[0])
-    one_hot = one_hot_of(codes_of(apart, rank_ref[...], cap, pieces), 0, n * per)
-    stacked = stack_pieces(hidden_ref[...], pieces)
-    stacked_ref[...] = stacked
-    packed = dot(one_hot, stacked).astype(BF16)
+    apart = lax.bitwise_xor(slot, me_ref[0])
+    one_hot = one_hot_of(codes_of(apart, rank, cap, pieces), 0, n * per)
+    packed = dot(one_hot, stack_pieces(hidden_ref[...], pieces)).astype(BF16)
     for s, out_ref in enumerate(out_refs):
         out_ref[...] = packed[s * per : (s + 1) * per]
 
@@ -90,26 +86,33 @@
     expand_ref[...] = (source == in_row).astype(F32).astype(BF16)
 
 
-def shrink_kernel(n, cap, pieces, order, *refs):
-    received_refs, (down_ref, table_ref, base_ref, out_ref) = dict(zip(order, refs[:n])), refs[n:]
-    width = refs[0].shape[1]
+def shrink(cap, pieces, received_refs, down_ref, table_ref):
+    width = received_refs[0].shape[1]
     rank2 = down_ref.shape[2]
-    received = jnp.concatenate([received_refs[s][...] for s in range(n)], axis=0)
+    received = jnp.concatenate([ref[...] for ref in received_refs], axis=0)
     size = received.shape[0]
     total = jnp.zeros((size, rank2), F32)
     piece_of = (iota((size, rank2), 0) // cap) % pieces
-    for piece in range(0, pieces, 2):
-        pair = [down_ref[0, i * width : (i + 1) * width, :] for i in (piece, piece + 1)]
-        part = dot(received, jnp.concatenate(pair, axis=1))
-        total = total + jnp.where(piece_of == piece, part[:, :rank2], 0.0)
-        total = total + jnp.where(piece_of == piece + 1, part[:, rank2:], 0.0)
-    reduced = select_sum(table_ref[...], total)
-    size = reduced.shape[0]
-    out_ref[:size, :] = reduced
+    for piece in range(pieces):
+        part = dot(received, down_ref[0, piece * width : (piece + 1) * width, :])
+        total = total + jnp.where(piece_of == piece, part, 0.0)
+    return select_sum(table_ref[...], total)
+
+
+def shrink_near_kernel(cap, pieces, *refs):
+    refs[-1][...] = shrink(cap, pieces, refs[:-3], *refs[-3:-1])
+
+
+def shrink_far_kernel(cap, pieces, *refs):
+    near_ref, base_ref, out_ref = refs[-3:]
+    half = near_ref.shape[0]
+    out_ref[:half, :] = near_ref[...]
+    out_ref[half : 2 * half, :] = shrink(cap, pieces, refs[:-5], *refs[-5:-3])
     rows = base_ref.shape[0]
-    for i in range(base_ref.shape[1] // rank2):
-        first = size + i * rows
-        out_ref[first : first + rows, :] = base_ref[:, i * rank2 : (i + 1) * rank2]
+    lanes = out_ref.shape[1]
+    for i in range(base_ref.shape[1] // lanes):
+        first = 2 * half + i * rows
+        out_ref[first : first + rows, :] = base_ref[:, i * lanes : (i + 1) * lanes]
 
 
 def expand_kernel(n, cap, mine_ref, other_ref, up_ref, table_ref, out_ref):
@@ -139,19 +142,19 @@
 
 
 def base_kernel(
-    pieces, core_ref, stacked_ref, weight_hbm, first_ref, second_ref, mine_ref, other_ref, weight_ref, sems
+    core_ref, hidden_ref, weight_hbm, first_ref, second_ref, mine_ref, other_ref, weight_ref, sems
 ):
-    depth = weight_ref.shape[0] // pieces
+    blocks, depth = weight_ref.shape[:2]
     copies = []
-    for k in range(pieces):
-        part = pl.ds(k * depth, depth)
-        copies.append(pltpu.make_async_copy(weight_hbm.at[part, :], weight_ref.at[part, :], sems.at[k]))
+    for k in range(blocks):
+        part = weight_hbm.at[pl.ds(k * depth, depth), :]
+        copies.append(pltpu.make_async_copy(part, weight_ref.at[k], sems.at[k]))
         copies[k].start()
     rows, columns = mine_ref.shape
     total = jnp.zeros((rows, 2 * columns), F32)
-    for k in range(pieces):
+    for k in range(blocks):
         copies[k].wait()
-        total = total + dot(stacked_ref[k * rows : (k + 1) * rows, :], weight_ref[k * depth : (k + 1) * depth, :])
+        total = total + dot(hidden_ref[:, k * depth : (k + 1) * depth], weight_ref[k])
     first, second = total[:, :columns], total[:, columns:]
     mine_ref[...] = jnp.where(core_ref[0] == 0, first, second)
     other_ref[...] = jnp.where(core_ref[0] == 0, second, first)
@@ -280,45 +283,51 @@
     swap = functools.partial(lax.ppermute, axis_name="tp", perm=[(0, 1), (1, 0)])
 
     me = lax.axis_index("pool").reshape(1)
-    slot, rank = call(
-        functools.partial(route_kernel, n), [jax.ShapeDtypeStruct((1, rows), I32)] * 2, [VMEM] * 2
-    )(row_adapter_index.reshape(1, rows), adapter_slot_table.reshape(1, n))
-    stacked, *packed = call(
+    slot, rank, *packed = call(
         functools.partial(pack_kernel, n, cap, pieces),
-        [jax.ShapeDtypeStruct((pieces * rows, width // pieces), BF16)]
+        [jax.ShapeDtypeStruct((1, rows), I32)] * 2
         + [jax.ShapeDtypeStruct((pieces * cap, width // pieces), BF16)] * n,
         [SMEM, VMEM, VMEM, VMEM],
-    )(me, slot, rank, hidden)
+    )(me, row_adapter_index.reshape(1, rows), adapter_slot_table.reshape(1, n), hidden)
     half = n // 2
-    order = [0, half, 1, half + 1, 2, *range(half + 2, n), *range(3, half)]
+    order = [0, 1, 2, *range(half, n), *range(3, half)]
     arrived = {0: packed[0]}
     for s in order[1:]:
         arrived[s] = lax.ppermute(packed[s], "pool", [(i, i ^ s) for i in range(n)])
 
+    blocks = 4
     base_mine, base_other = call(
-        functools.partial(base_kernel, pieces),
+        base_kernel,
         [jax.ShapeDtypeStruct((rows, columns), F32)] * 2,
         [SMEM, VMEM, ANY, ANY, ANY],
-        [pltpu.VMEM((width, 2 * columns), BF16), pltpu.SemaphoreType.DMA((pieces,))],
+        [
+            pltpu.VMEM((blocks, width // blocks, 2 * columns), BF16),
+            pltpu.SemaphoreType.DMA((blocks,)),
+        ],
         pl.CostEstimate(
             flops=4 * rows * width * columns, bytes_accessed=16 * width * columns, transcendentals=0
         ),
-    )(lax.axis_index("tp").reshape(1), stacked, key_value_weight, arrived[1], arrived[2])
+    )(lax.axis_index("tp").reshape(1), hidden, key_value_weight, arrived[1], arrived[2])
 
     size = n * out_pieces * cap
     shrink_table, expand_table = call(
         functools.partial(tables_kernel, n, cap, pieces, out_pieces),
         [
-            jax.ShapeDtypeStruct((n * cap, n * pieces * cap), BF16),
+            jax.ShapeDtypeStruct((half * cap, half * pieces * cap), BF16),
             jax.ShapeDtypeStruct((size, size), BF16),
         ],
         [SMEM, ANY],
     )(me, base_mine)
+    (near_sum,) = call(
+        functools.partial(shrink_near_kernel, cap, pieces),
+        [jax.ShapeDtypeStruct((half * cap, rank2), F32)],
+        [VMEM] * (half + 2),
+    )(*[arrived[s] for s in range(half)], adapter_down_weight, shrink_table)
     (sums,) = call(
-        functools.partial(shrink_kernel, n, cap, pieces, order),
+        functools.partial(shrink_far_kernel, cap, pieces),
         [jax.ShapeDtypeStruct((n * cap + rows * columns // rank2, rank2), F32)],
-        [VMEM] * (n + 3),
-    )(*[arrived[s] for s in order], adapter_down_weight, shrink_table, base_other)
+        [VMEM] * (half + 4),
+    )(*[arrived[s] for s in range(half, n)], adapter_down_weight, shrink_table, near_sum, base_other)
     other_sums = swap(sums)
     (terms,) = call(
         functools.partial(expand_kernel, n, cap),

time: 46.6 us -> 45.5 us (0.976)
  waiting for transfers between devices: 11.7 us -> 7.04 us
  starting transfers between devices: 18.6 us -> 21.4 us
  Pallas kernels: 11.9 us -> 12.5 us
    ppermute x7, waiting for transfers between devices: 5.46 us -> 0.74 us  [shards(): arrived[s] = lax.ppermute(packed[s], 'pool', [(i, i ^ s) for i in range(n)])]
    ppermute x7, starting transfers between devices: 12.2 us -> 14.2 us  [shards(): arrived[s] = lax.ppermute(packed[s], 'pool', [(i, i ^ s) for i in range(n)])]
    all_to_all x1, starting transfers between devices: 6.32 us -> 7.26 us  [shards(): lax.all_to_all(terms, 'pool', split_axis=0, concat_axis=0, tiled=True)]
    unnamed x22 -> x20, local copies, waits for them, and re-layouts: 3.14 us -> 3.41 us
  transfers between devices with their start and end apart: 9 -> 9, of which waited for: 5 -> 3; matrix products, arithmetic and copies ran while one was open for 0% -> 0% of each run, Pallas kernels for 14% -> 16%
where the time goes in v9:
time: 45.5 us; the launch traced here: 45.2 us
  starting transfers between devices  21.4 us (47%)
  Pallas kernels  12.5 us (27%)
  waiting for transfers between devices  7.04 us (15%)
  local copies, waits for them, and re-layouts  3.5 us (8%)
  between operations  0.74 us (2%)
    ppermute x7, starting transfers between devices, shards(): arrived[s] = lax.ppermute(packed[s], 'pool', [(i, i ^ s) for i in range(n)])  14.2 us
    all_to_all x1, starting transfers between devices, shards(): lax.all_to_all(terms, 'pool', split_axis=0, concat_axis=0, tiled=True)  7.26 us
    all_to_all x1, waiting for transfers between devices, shards(): lax.all_to_all(terms, 'pool', split_axis=0, concat_axis=0, tiled=True)  4.93 us
    pallas_call x1, Pallas kernels, shards(): call(base_kernel, [jax.ShapeDtypeStruct((rows, columns), F32)] * 2, [SMEM...  4.1 us
    unnamed x20, local copies, waits for them, and re-layouts  3.41 us
    pallas_call x1, Pallas kernels, shards(): call(cache_kernel, [jax.ShapeDtypeStruct(queries.shape, F32)] + [jax.Shap...  1.71 us
    pallas_call x1, Pallas kernels, shards(): call(functools.partial(shrink_far_kernel, cap, pieces), [jax.ShapeDtypeSt...  1.63 us
    pallas_call x1, Pallas kernels, shards(): call(functools.partial(pack_kernel, n, cap, pieces), [jax.ShapeDtypeStruc...  1.37 us
  transfers between devices with their start and end apart: 9, of which 3 were waited for; matrix products, arithmetic and copies ran while one was open for 0% of the time, Pallas kernels for 16%

profile of v9, /device:TPU:0, one launch (start us, length us, event | category | flops | bytes accessed | tf_op | source)
XLA Modules:
  0.0 45.2 jit_solution(16878305846390681295)
XLA Ops:
  0.6 0.0 copy-start
  0.6 0.0 copy-start.1
  0.7 1.1 %copy-done.1 = bf16[48,4096]{1,0:T(8,128)(2,1)S(1)} copy-done((bf16[48,4096]{1,0:T(8,128)(2,1)S(1)}, bf16[48,4096]{1,0:T(8,128)(2,1)}, u32[]{:S(2)}) %copy-start.1) | copy-done | bytes 393240
  1.7 0.0 copy-start.7
  1.7 0.7 %copy-done.7 = s32[48,1]{0,1:T(1,128)S(1)} copy-done((s32[48,1]{0,1:T(1,128)S(1)}, s32[48,1]{0,1:T(1,128)}, u32[]{:S(2)}) %copy-start.7) | copy-done | bytes 216
  2.4 0.0 copy-start.8
  2.4 0.7 %copy-done.8 = s32[8]{0:T(128)S(1)} copy-done((s32[8]{0:T(128)S(1)}, s32[8]{0:T(128)}, u32[]{:S(2)}) %copy-start.8) | copy-done | bytes 56
  3.0 1.4 %shard_map.113 = (s32[1,48]{1,0:T(1,128)S(1)}, s32[1,48]{1,0:T(1,128)S(1)}, bf16[48,1024]{1,0:T(8,128)(2,1)S(1)}, bf16[48,1024]{1,0:T(8,128)(2,1)S(1)}, bf16[48,...) custom-call(s32[1]{0:T(128)} %bitcast.me_ref, ...), custom_call_target="tpu_custom_call" | custom-call | tf_op jit(solution)/shard_map/pallas_call | solution.py:286
  4.4 3.0 %collective-permute-start.4 = (bf16[48,1024]{1,0:T(8,128)(2,1)S(1)}, bf16[48,1024]{1,0:T(8,128)(2,1)S(1)}, u32[]{:S(2)}, u32[]{:S(2)}) collective-permute-start(bf16[48,1024]{1,0:T(8,128)(2,1)S(1)} %get-tuple-element.25), channel_id=1, source_target_pairs={{0,2},{2,0},{4,6},{6,4},{8,10},{10,8},{12,14},{14,12},{1,3},{3,1},... | collective-permute-start | bytes 294920 | tf_op jit(solution)/shard_map/ppermute | solution.py:296
  7.4 1.6 %collective-permute-start.5 = (bf16[48,1024]{1,0:T(8,128)(2,1)S(1)}, bf16[48,1024]{1,0:T(8,128)(2,1)S(1)}, u32[]{:S(2)}, u32[]{:S(2)}) collective-permute-start(bf16[48,1024]{1,0:T(8,128)(2,1)S(1)} %get-tuple-element.26), channel_id=1, source_target_pairs={{0,4},{2,6},{4,0},{6,2},{8,12},{10,14},{12,8},{14,10},{1,5},{3,7},... | collective-permute-start | bytes 294920 | tf_op jit(solution)/shard_map/ppermute | solution.py:296
  9.0 2.6 %collective-permute-start = (bf16[48,1024]{1,0:T(8,128)(2,1)}, bf16[48,1024]{1,0:T(8,128)(2,1)S(1)}, u32[]{:S(2)}, u32[]{:S(2)}) collective-permute-start(bf16[48,1024]{1,0:T(8,128)(2,1)} %get-tuple-element.21), channel_id=1, source_target_pairs={{0,8},{2,10},{4,12},{6,14},{8,0},{10,2},{12,4},{14,6},{1,9},{3,11}... | collective-permute-start | bytes 294920 | tf_op jit(solution)/shard_map/ppermute | solution.py:296
  11.6 0.4 collective-permute-start.6
  11.9 1.3 %collective-permute-start.1 = (bf16[48,1024]{1,0:T(8,128)(2,1)}, bf16[48,1024]{1,0:T(8,128)(2,1)S(1)}, u32[]{:S(2)}, u32[]{:S(2)}) collective-permute-start(bf16[48,1024]{1,0:T(8,128)(2,1)} %get-tuple-element.22), channel_id=1, source_target_pairs={{0,10},{2,8},{4,14},{6,12},{8,2},{10,0},{12,6},{14,4},{1,11},{3,9}... | collective-permute-start | bytes 294920 | tf_op jit(solution)/shard_map/ppermute | solution.py:296
  13.2 0.0 collective-permute-done.4.first_ref.refs_1_
  13.2 3.6 %collective-permute-start.2 = (bf16[48,1024]{1,0:T(8,128)(2,1)}, bf16[48,1024]{1,0:T(8,128)(2,1)}, u32[]{:S(2)}, u32[]{:S(2)}) collective-permute-start(bf16[48,1024]{1,0:T(8,128)(2,1)} %get-tuple-element.23), channel_id=1, source_target_pairs={{0,12},{2,14},{4,8},{6,10},{8,4},{10,6},{12,0},{14,2},{1,13},{3,15... | collective-permute-start | bytes 294920 | tf_op jit(solution)/shard_map/ppermute | solution.py:296
  16.8 0.0 collective-permute-done.5.second_ref.refs_2_
  16.8 1.8 %collective-permute-start.3 = (bf16[48,1024]{1,0:T(8,128)(2,1)}, bf16[48,1024]{1,0:T(8,128)(2,1)}, u32[]{:S(2)}, u32[]{:S(2)}) collective-permute-start(bf16[48,1024]{1,0:T(8,128)(2,1)} %get-tuple-element.24), channel_id=1, source_target_pairs={{0,14},{2,12},{4,10},{6,8},{8,6},{10,4},{12,2},{14,0},{1,15},{3,13... | collective-permute-start | bytes 294920 | tf_op jit(solution)/shard_map/ppermute | solution.py:296
  18.6 0.0 copy-start.2
  18.6 1.0 %copy-done.2 = bf16[48,4096]{1,0:T(8,128)(2,1)S(1)} copy-done((bf16[48,4096]{1,0:T(8,128)(2,1)S(1)}, bf16[48,4096]{1,0:T(8,128)(2,1)}, u32[]{:S(2)}) %copy-start.2) | copy-done | bytes 393240
  19.6 0.0 copy-start.6
  19.6 0.0 copy-start.9
  19.6 0.0 copy-start.3
  19.6 0.0 copy-start.4
  19.6 0.0 copy-start.5
  19.6 4.1 %shard_map.114 = (f32[48,512]{1,0:T(8,128)S(1)}, f32[48,512]{1,0:T(8,128)S(1)}) custom-call(s32[1]{0:T(128)} %bitcast.3.core_ref, bf16[48,4096]{1,0:T(8,128)(2,1)S(1)} %copy-done.2, bf16[4096,1024]{1,0:T(8,128)(2,1)} %weight_hbm.1, bf16[48,1024]{1,0:T(8,128)(2,1)S(1)} %collective-permute-done.4.first_ref.refs_1_, ...), custom_call_target="tpu_custom_call" | custom-call | flops 402653184 | bytes 33554432 | tf_op jit(solution)/shard_map/pallas_call | solution.py:299
  23.7 0.2 shard_map.115
  24.0 0.0 collective-permute-done.6.refs_3_
  24.0 0.0 copy-done
  24.0 0.7 %shard_map.116.refs_6_ = f32[48,128]{1,0:T(8,128)S(1)} custom-call(bf16[48,1024]{1,0:T(8,128)(2,1)S(1)} %get-tuple-element.29.refs_0_, bf16[48,1024]{1,0:T(8,128)(2,1)S(1)} %collective-permute-done.4.first_ref.refs_1_, bf16[48,1024]{1,0:T(8,128)(2,1)S(1)} %collective-permute-done.5.second_ref.refs_2_, bf16[48,1024]{1,0:T(8,128)(2,1)S(1)} %collective-permute-done.6.refs_3_, ...), custom_call_target="tpu_custom_call" | custom-call | tf_op jit(solution)/shard_map/pallas_call | solution.py:321
  24.7 0.0 collective-permute-done.refs_0_
  24.7 0.7 %collective-permute-done.1.refs_1_ = bf16[48,1024]{1,0:T(8,128)(2,1)S(1)} collective-permute-done((bf16[48,1024]{1,0:T(8,128)(2,1)}, bf16[48,1024]{1,0:T(8,128)(2,1)S(1)}, u32[]{:S(2)}, u32[]{:S(2)}) %collective-permute-start.1) | collective-permute-done | bytes 98336 | tf_op jit(solution)/shard_map/ppermute | solution.py:296
  25.4 0.0 collective-permute-done.2.refs_2_
  25.4 0.0 collective-permute-done.3.refs_3_
  25.4 1.6 %shard_map.117.mine_ref = f32[288,128]{1,0:T(8,128)S(1)} custom-call(bf16[48,1024]{1,0:T(8,128)(2,1)S(1)} %collective-permute-done.refs_0_, bf16[48,1024]{1,0:T(8,128)(2,1)S(1)} %collective-permute-done.1.refs_1_, bf16[48,1024]{1,0:T(8,128)(2,1)} %collective-permute-done.2.refs_2_, bf16[48,1024]{1,0:T(8,128)(2,1)} %collective-permute-done.3.refs_3_, ...), custom_call_target="tpu_custom_call" | custom-call | tf_op jit(solution)/shard_map/pallas_call | solution.py:326
  27.1 0.0 collective-permute-start.7
  27.1 1.4 %collective-permute-done.7.other_ref = f32[288,128]{1,0:T(8,128)S(1)} collective-permute-done((f32[288,128]{1,0:T(8,128)S(1)}, f32[288,128]{1,0:T(8,128)S(1)}, u32[]{:S(2)}, u32[]{:S(2)}) %collective-permute-start.7) | collective-permute-done | bytes 147488 | tf_op jit(solution)/shard_map/ppermute | solution.py:331
  28.4 0.0 copy-done.6
  28.4 1.1 %shard_map.118._ = bf16[384,128]{1,0:T(8,128)(2,1)} custom-call(f32[288,128]{1,0:T(8,128)S(1)} %shard_map.117.mine_ref, f32[288,128]{1,0:T(8,128)S(1)} %collective-permute-done.7.other_ref, bf16[1,2,64,256]{3,2,1,0:T(8,128)(2,1)S(1)} %copy-done.6, bf16[384,384]{1,0:T(8,128)(2,1)S(1)} %get-tuple-element.32.table_ref), custom_call_target="tpu_custom_call" | custom-call | tf_op jit(solution)/shard_map/pallas_call | solution.py:332
  29.5 7.3 %all-to-all-start = ((bf16[8,48,128]{2,1,0:T(8,128)(2,1)}), bf16[8,48,128]{2,1,0:T(8,128)(2,1)S(1)}, u32[]{:S(2)}, u32[]{:S(2)}) async-start(bf16[8,48,128]{2,1,0:T(8,128)(2,1)} %bitcast.4), calls=%async_computation | async-start | bytes 196608 | tf_op jit(solution)/shard_map/all_to_all | solution.py:345
  36.8 0.0 copy-done.9
  36.8 0.1 copy.12.length_ref
  36.9 0.0 copy-done.3
  36.9 0.0 copy-done.4
  36.9 0.0 copy-done.5
  36.9 1.7 %shard_map.120 = (f32[48,2048]{1,0:T(8,128)S(1)}, f32[48,128]{1,0:T(8,128)S(1)}, f32[48,128]{1,0:T(8,128)S(1)}) custom-call(bf16[48,2048]{1,0:T(8,128)(2,1)S(1)} %copy-done.5, bf16[48,2,32,128]{3,2,1,0:T(8,128)(2,1)S(1)} %copy-done.3, bf16[48,2,32,128]{3,2,1,0:T(8,128)(2,1)S(1)} %copy-done.4, s32[48,1]{1,0:T(8,128)S(1)} %copy.12.length_ref, ...), custom_call_target="tpu_custom_call" | custom-call | tf_op jit(solution)/shard_map/pallas_call | solution.py:346
  38.6 0.4 shard_map.119
  39.0 4.9 %all-to-all-done = bf16[8,48,128]{2,1,0:T(8,128)(2,1)S(1)} async-done(((bf16[8,48,128]{2,1,0:T(8,128)(2,1)}), bf16[8,48,128]{2,1,0:T(8,128)(2,1)S(1)}, u32[]{:S(2)}, u32[]{:S(2)}) %all-to-all-start) | async-done | bytes 98336 | tf_op jit(solution)/shard_map/all_to_all | solution.py:345
  43.9 1.3 %shard_map.121 = (bf16[48,512]{1,0:T(8,128)(2,1)}, bf16[48,2048]{1,0:T(8,128)(2,1)}) custom-call(bf16[384,128]{1,0:T(8,128)(2,1)S(1)} %bitcast.7, bf16[192,384]{1,0:T(8,128)(2,1)S(1)} %get-tuple-element.35.one_hot_ref, f32[48,512]{1,0:T(8,128)S(1)} %get-tuple-element.36.base_ref, bf16[48,2048]{1,0:T(8,128)(2,1)S(1)} %copy-done.5, ...), custom_call_target="tpu_custom_call" | custom-call | tf_op jit(solution)/shard_map/pallas_call | solution.py:351
Async XLA Ops:
  0.6 23.4 %copy-start = (bf16[1,4096,128]{2,1,0:T(8,128)(2,1)S(1)}, bf16[1,4096,128]{2,1,0:T(8,128)(2,1)}, u32[]{:S(2)}) copy-start(bf16[1,4096,128]{2,1,0:T(8,128)(2,1)} %refs_4_.3) | copy-start | bytes 3145732
  0.6 1.1 %copy-start.1 = (bf16[48,4096]{1,0:T(8,128)(2,1)S(1)}, bf16[48,4096]{1,0:T(8,128)(2,1)}, u32[]{:S(2)}) copy-start(bf16[48,4096]{1,0:T(8,128)(2,1)} %hidden_ref.3) | copy-start | bytes 1179652
  1.7 0.7 %copy-start.7 = (s32[48,1]{0,1:T(1,128)S(1)}, s32[48,1]{0,1:T(1,128)}, u32[]{:S(2)}) copy-start(s32[48,1]{0,1:T(1,128)} %param.17) | copy-start | bytes 580
  2.4 0.7 %copy-start.8 = (s32[8]{0:T(128)S(1)}, s32[8]{0:T(128)}, u32[]{:S(2)}) copy-start(s32[8]{0:T(128)} %param.19) | copy-start | bytes 100
  4.4 8.8 %collective-permute-start.4 = (bf16[48,1024]{1,0:T(8,128)(2,1)S(1)}, bf16[48,1024]{1,0:T(8,128)(2,1)S(1)}, u32[]{:S(2)}, u32[]{:S(2)}) collective-permute-start(bf16[48,1024]{1,0:T(8,128)(2,1)S(1)} %get-tuple-element.25), channel_id=1, source_target_pairs={{0,2},{2,0},{4,6},{6,4},{8,10},{10,8},{12,14},{14,12},{1,3},{3,1},... | collective-permute-start | bytes 294920 | tf_op jit(solution)/shard_map/ppermute | solution.py:296
  7.4 9.5 %collective-permute-start.5 = (bf16[48,1024]{1,0:T(8,128)(2,1)S(1)}, bf16[48,1024]{1,0:T(8,128)(2,1)S(1)}, u32[]{:S(2)}, u32[]{:S(2)}) collective-permute-start(bf16[48,1024]{1,0:T(8,128)(2,1)S(1)} %get-tuple-element.26), channel_id=1, source_target_pairs={{0,4},{2,6},{4,0},{6,2},{8,12},{10,14},{12,8},{14,10},{1,5},{3,7},... | collective-permute-start | bytes 294920 | tf_op jit(solution)/shard_map/ppermute | solution.py:296
  9.0 15.7 %collective-permute-start = (bf16[48,1024]{1,0:T(8,128)(2,1)}, bf16[48,1024]{1,0:T(8,128)(2,1)S(1)}, u32[]{:S(2)}, u32[]{:S(2)}) collective-permute-start(bf16[48,1024]{1,0:T(8,128)(2,1)} %get-tuple-element.21), channel_id=1, source_target_pairs={{0,8},{2,10},{4,12},{6,14},{8,0},{10,2},{12,4},{14,6},{1,9},{3,11}... | collective-permute-start | bytes 294920 | tf_op jit(solution)/shard_map/ppermute | solution.py:296
  11.6 12.4 %collective-permute-start.6 = (bf16[48,1024]{1,0:T(8,128)(2,1)}, bf16[48,1024]{1,0:T(8,128)(2,1)S(1)}, u32[]{:S(2)}, u32[]{:S(2)}) collective-permute-start(bf16[48,1024]{1,0:T(8,128)(2,1)} %get-tuple-element.30), channel_id=1, source_target_pairs={{0,6},{2,4},{4,2},{6,0},{8,14},{10,12},{12,10},{14,8},{1,7},{3,5},... | collective-permute-start | bytes 294920 | tf_op jit(solution)/shard_map/ppermute | solution.py:296
  11.9 13.5 %collective-permute-start.1 = (bf16[48,1024]{1,0:T(8,128)(2,1)}, bf16[48,1024]{1,0:T(8,128)(2,1)S(1)}, u32[]{:S(2)}, u32[]{:S(2)}) collective-permute-start(bf16[48,1024]{1,0:T(8,128)(2,1)} %get-tuple-element.22), channel_id=1, source_target_pairs={{0,10},{2,8},{4,14},{6,12},{8,2},{10,0},{12,6},{14,4},{1,11},{3,9}... | collective-permute-start | bytes 294920 | tf_op jit(solution)/shard_map/ppermute | solution.py:296
  13.2 12.2 %collective-permute-start.2 = (bf16[48,1024]{1,0:T(8,128)(2,1)}, bf16[48,1024]{1,0:T(8,128)(2,1)}, u32[]{:S(2)}, u32[]{:S(2)}) collective-permute-start(bf16[48,1024]{1,0:T(8,128)(2,1)} %get-tuple-element.23), channel_id=1, source_target_pairs={{0,12},{2,14},{4,8},{6,10},{8,4},{10,6},{12,0},{14,2},{1,13},{3,15... | collective-permute-start | bytes 294920 | tf_op jit(solution)/shard_map/ppermute | solution.py:296
  16.8 8.6 %collective-permute-start.3 = (bf16[48,1024]{1,0:T(8,128)(2,1)}, bf16[48,1024]{1,0:T(8,128)(2,1)}, u32[]{:S(2)}, u32[]{:S(2)}) collective-permute-start(bf16[48,1024]{1,0:T(8,128)(2,1)} %get-tuple-element.24), channel_id=1, source_target_pairs={{0,14},{2,12},{4,10},{6,8},{8,6},{10,4},{12,2},{14,0},{1,15},{3,13... | collective-permute-start | bytes 294920 | tf_op jit(solution)/shard_map/ppermute | solution.py:296
  18.6 1.0 %copy-start.2 = (bf16[48,4096]{1,0:T(8,128)(2,1)S(1)}, bf16[48,4096]{1,0:T(8,128)(2,1)}, u32[]{:S(2)}) copy-start(bf16[48,4096]{1,0:T(8,128)(2,1)} %hidden_ref.3) | copy-start | bytes 1179652
  19.6 8.8 %copy-start.6 = (bf16[1,2,64,256]{3,2,1,0:T(8,128)(2,1)S(1)}, bf16[1,2,64,256]{3,2,1,0:T(8,128)(2,1)}, u32[]{:S(2)}) copy-start(bf16[1,2,64,256]{3,2,1,0:T(8,128)(2,1)} %up_ref.1) | copy-start | bytes 196612
  19.6 17.2 %copy-start.9 = (s32[48]{0:T(128)S(1)}, s32[48]{0:T(128)}, u32[]{:S(2)}) copy-start(s32[48]{0:T(128)} %param.18) | copy-start | bytes 580
  19.6 17.3 %copy-start.3 = (bf16[48,2,32,128]{3,2,1,0:T(8,128)(2,1)S(1)}, bf16[48,2,32,128]{3,2,1,0:T(8,128)(2,1)}, u32[]{:S(2)}) copy-start(bf16[48,2,32,128]{3,2,1,0:T(8,128)(2,1)} %key_ref.1) | copy-start | bytes 2359300
  19.6 17.3 %copy-start.4 = (bf16[48,2,32,128]{3,2,1,0:T(8,128)(2,1)S(1)}, bf16[48,2,32,128]{3,2,1,0:T(8,128)(2,1)}, u32[]{:S(2)}) copy-start(bf16[48,2,32,128]{3,2,1,0:T(8,128)(2,1)} %value_ref.1) | copy-start | bytes 2359300
  19.6 17.3 %copy-start.5 = (bf16[48,2048]{1,0:T(8,128)(2,1)S(1)}, bf16[48,2048]{1,0:T(8,128)(2,1)}, u32[]{:S(2)}) copy-start(bf16[48,2048]{1,0:T(8,128)(2,1)} %query_ref.3) | copy-start | bytes 589828
  27.1 1.4 %collective-permute-start.7 = (f32[288,128]{1,0:T(8,128)S(1)}, f32[288,128]{1,0:T(8,128)S(1)}, u32[]{:S(2)}, u32[]{:S(2)}) collective-permute-start(f32[288,128]{1,0:T(8,128)S(1)} %shard_map.117.mine_ref), channel_id=1, source_target_pairs={{0,1},{1,0},{2,3},{3,2},{4,5},{5,4},{6,7},{7,6},{8,9},{9,8},{10,11... | collective-permute-start | bytes 442376 | tf_op jit(solution)/shard_map/ppermute | solution.py:331
  29.5 14.4 %all-to-all-start = ((bf16[8,48,128]{2,1,0:T(8,128)(2,1)}), bf16[8,48,128]{2,1,0:T(8,128)(2,1)S(1)}, u32[]{:S(2)}, u32[]{:S(2)}) async-start(bf16[8,48,128]{2,1,0:T(8,128)(2,1)} %bitcast.4), calls=%async_computation | async-start | bytes 196608 | tf_op jit(solution)/shard_map/all_to_all | solution.py:345

commit v10 on v9

--- a/solution.py
+++ b/solution.py
@@ -10,7 +10,7 @@
 BF16 = jnp.bfloat16
 F32 = jnp.float32
 I32 = jnp.int32
-VMEM_LIMIT = 48 * 1024 * 1024
+VMEM_LIMIT = 20 * 1024 * 1024
 
 
 def iota(shape, dim):
@@ -144,17 +144,22 @@
 def base_kernel(
     core_ref, hidden_ref, weight_hbm, first_ref, second_ref, mine_ref, other_ref, weight_ref, sems
 ):
-    blocks, depth = weight_ref.shape[:2]
-    copies = []
-    for k in range(blocks):
+    slots, depth = weight_ref.shape[:2]
+    blocks = hidden_ref.shape[1] // depth
+
+    def copy(k):
         part = weight_hbm.at[pl.ds(k * depth, depth), :]
-        copies.append(pltpu.make_async_copy(part, weight_ref.at[k], sems.at[k]))
-        copies[k].start()
+        return pltpu.make_async_copy(part, weight_ref.at[k % slots], sems.at[k % slots])
+
+    for k in range(slots):
+        copy(k).start()
     rows, columns = mine_ref.shape
     total = jnp.zeros((rows, 2 * columns), F32)
     for k in range(blocks):
-        copies[k].wait()
-        total = total + dot(hidden_ref[:, k * depth : (k + 1) * depth], weight_ref[k])
+        copy(k).wait()
+        total = total + dot(hidden_ref[:, k * depth : (k + 1) * depth], weight_ref[k % slots])
+        if k + slots < blocks:
+            copy(k + slots).start()
     first, second = total[:, :columns], total[:, columns:]
     mine_ref[...] = jnp.where(core_ref[0] == 0, first, second)
     other_ref[...] = jnp.where(core_ref[0] == 0, second, first)
@@ -295,14 +300,14 @@
     for s in order[1:]:
         arrived[s] = lax.ppermute(packed[s], "pool", [(i, i ^ s) for i in range(n)])
 
-    blocks = 4
+    slots, depth = 4, 512
     base_mine, base_other = call(
         base_kernel,
         [jax.ShapeDtypeStruct((rows, columns), F32)] * 2,
         [SMEM, VMEM, ANY, ANY, ANY],
         [
-            pltpu.VMEM((blocks, width // blocks, 2 * columns), BF16),
-            pltpu.SemaphoreType.DMA((blocks,)),
+            pltpu.VMEM((slots, depth, 2 * columns), BF16),
+            pltpu.SemaphoreType.DMA((slots,)),
         ],
         pl.CostEstimate(
             flops=4 * rows * width * columns, bytes_accessed=16 * width * columns, transcendentals=0

time: 45.5 us -> 43.6 us (0.958)
  Pallas kernels: 12.5 us -> 9.03 us
  local copies, waits for them, and re-layouts: 3.5 us -> 6.79 us
  starting transfers between devices: 21.4 us -> 20.4 us
  waiting for transfers between devices: 7.04 us -> 6.32 us
    unnamed x20 -> x22, local copies, waits for them, and re-layouts: 3.41 us -> 6.7 us
    pallas_call x1, Pallas kernels: 4.1 us -> 2.3 us  [shards(): call(base_kernel, [jax.ShapeDtypeStruct((rows, columns), F32)] * 2, [SMEM...]
    all_to_all x1, starting transfers between devices: 7.26 us -> 6.3 us  [shards(): lax.all_to_all(terms, 'pool', split_axis=0, concat_axis=0, tiled=True)]
    pallas_call x1, Pallas kernels: 1.63 us -> 0.69 us  [shards(): call(functools.partial(shrink_far_kernel, cap, pieces), [jax.ShapeDtypeSt...]
    ppermute x7, waiting for transfers between devices: 0.74 us -> 0.02 us  [shards(): arrived[s] = lax.ppermute(packed[s], 'pool', [(i, i ^ s) for i in range(n)])]
    pallas_call x1, Pallas kernels: 1.37 us -> 0.65 us  [shards(): call(functools.partial(pack_kernel, n, cap, pieces), [jax.ShapeDtypeStruc...]
  transfers between devices with their start and end apart: 9 -> 9, of which waited for: 3 -> 2; matrix products, arithmetic and copies ran while one was open for 0% -> 0% of each run, Pallas kernels for 16% -> 12%
where the time goes in v10:
time: 43.6 us; the launch traced here: 43.3 us
  starting transfers between devices  20.4 us (47%)
  Pallas kernels  9.03 us (21%)
  local copies, waits for them, and re-layouts  6.79 us (16%)
  waiting for transfers between devices  6.32 us (14%)
  between operations  0.76 us (2%)
    ppermute x7, starting transfers between devices, shards(): arrived[s] = lax.ppermute(packed[s], 'pool', [(i, i ^ s) for i in range(n)])  14.1 us
    unnamed x22, local copies, waits for them, and re-layouts  6.7 us
    all_to_all x1, starting transfers between devices, shards(): lax.all_to_all(terms, 'pool', split_axis=0, concat_axis=0, tiled=True)  6.3 us
    all_to_all x1, waiting for transfers between devices, shards(): lax.all_to_all(terms, 'pool', split_axis=0, concat_axis=0, tiled=True)  4.92 us
    pallas_call x1, Pallas kernels, shards(): call(base_kernel, [jax.ShapeDtypeStruct((rows, columns), F32)] * 2, [SMEM...  2.3 us
    pallas_call x1, Pallas kernels, shards(): call(cache_kernel, [jax.ShapeDtypeStruct(queries.shape, F32)] + [jax.Shap...  1.71 us
    ppermute x1, waiting for transfers between devices, shards(): other_sums = swap(sums)  1.38 us
    pallas_call x1, Pallas kernels, shards(): call(combine_kernel, [jax.ShapeDtypeStruct((rows, columns), BF16), jax.Sh...  1.33 us
  transfers between devices with their start and end apart: 9, of which 2 were waited for; matrix products, arithmetic and copies ran while one was open for 0% of the time, Pallas kernels for 12%

profile of v10, /device:TPU:0, one launch (start us, length us, event | category | flops | bytes accessed | tf_op | source)
XLA Modules:
  0.0 43.3 jit_solution(8277533941509425337)
XLA Ops:
  0.6 0.0 copy-start.10
  0.6 0.0 copy-start.2
  0.7 1.0 %copy-done.2 = bf16[48,4096]{1,0:T(8,128)(2,1)S(1)} copy-done((bf16[48,4096]{1,0:T(8,128)(2,1)S(1)}, bf16[48,4096]{1,0:T(8,128)(2,1)}, u32[]{:S(2)}) %copy-start.2) | copy-done | bytes 393240
  1.6 0.0 copy-start.8
  1.6 0.7 %copy-done.8 = s32[48,1]{0,1:T(1,128)S(1)} copy-done((s32[48,1]{0,1:T(1,128)S(1)}, s32[48,1]{0,1:T(1,128)}, u32[]{:S(2)}) %copy-start.8) | copy-done | bytes 216
  2.3 0.0 copy-start.9
  2.3 0.7 %copy-done.9 = s32[8]{0:T(128)S(1)} copy-done((s32[8]{0:T(128)S(1)}, s32[8]{0:T(128)}, u32[]{:S(2)}) %copy-start.9) | copy-done | bytes 56
  3.0 0.0 copy-start.7
  3.0 0.0 copy-start.6
  3.0 0.7 %shard_map.113 = (s32[1,48]{1,0:T(1,128)S(1)}, s32[1,48]{1,0:T(1,128)S(1)}, bf16[48,1024]{1,0:T(8,128)(2,1)S(1)}, bf16[48,1024]{1,0:T(8,128)(2,1)S(1)}, bf16[48,...) custom-call(s32[1]{0:T(128)} %bitcast.me_ref, ...), custom_call_target="tpu_custom_call" | custom-call | tf_op jit(solution)/shard_map/pallas_call | solution.py:291
  3.6 3.0 %collective-permute-start.4 = (bf16[48,1024]{1,0:T(8,128)(2,1)S(1)}, bf16[48,1024]{1,0:T(8,128)(2,1)S(1)}, u32[]{:S(2)}, u32[]{:S(2)}) collective-permute-start(bf16[48,1024]{1,0:T(8,128)(2,1)S(1)} %get-tuple-element.25), channel_id=1, source_target_pairs={{0,2},{2,0},{4,6},{6,4},{8,10},{10,8},{12,14},{14,12},{1,3},{3,1},... | collective-permute-start | bytes 294920 | tf_op jit(solution)/shard_map/ppermute | solution.py:301
  6.7 1.6 %collective-permute-start.5 = (bf16[48,1024]{1,0:T(8,128)(2,1)S(1)}, bf16[48,1024]{1,0:T(8,128)(2,1)S(1)}, u32[]{:S(2)}, u32[]{:S(2)}) collective-permute-start(bf16[48,1024]{1,0:T(8,128)(2,1)S(1)} %get-tuple-element.26), channel_id=1, source_target_pairs={{0,4},{2,6},{4,0},{6,2},{8,12},{10,14},{12,8},{14,10},{1,5},{3,7},... | collective-permute-start | bytes 294920 | tf_op jit(solution)/shard_map/ppermute | solution.py:301
  8.2 2.6 %collective-permute-start = (bf16[48,1024]{1,0:T(8,128)(2,1)S(1)}, bf16[48,1024]{1,0:T(8,128)(2,1)S(1)}, u32[]{:S(2)}, u32[]{:S(2)}) collective-permute-start(bf16[48,1024]{1,0:T(8,128)(2,1)S(1)} %get-tuple-element.21), channel_id=1, source_target_pairs={{0,8},{2,10},{4,12},{6,14},{8,0},{10,2},{12,4},{14,6},{1,9},{3,11}... | collective-permute-start | bytes 294920 | tf_op jit(solution)/shard_map/ppermute | solution.py:301
  10.8 0.4 collective-permute-start.6
  11.2 1.3 %collective-permute-start.1 = (bf16[48,1024]{1,0:T(8,128)(2,1)S(1)}, bf16[48,1024]{1,0:T(8,128)(2,1)S(1)}, u32[]{:S(2)}, u32[]{:S(2)}) collective-permute-start(bf16[48,1024]{1,0:T(8,128)(2,1)S(1)} %get-tuple-element.22), channel_id=1, source_target_pairs={{0,10},{2,8},{4,14},{6,12},{8,2},{10,0},{12,6},{14,4},{1,11},{3,9}... | collective-permute-start | bytes 294920 | tf_op jit(solution)/shard_map/ppermute | solution.py:301
  12.5 0.0 collective-permute-done.4.first_ref.refs_1_
  12.5 3.6 %collective-permute-start.2 = (bf16[48,1024]{1,0:T(8,128)(2,1)S(1)}, bf16[48,1024]{1,0:T(8,128)(2,1)S(1)}, u32[]{:S(2)}, u32[]{:S(2)}) collective-permute-start(bf16[48,1024]{1,0:T(8,128)(2,1)S(1)} %get-tuple-element.23), channel_id=1, source_target_pairs={{0,12},{2,14},{4,8},{6,10},{8,4},{10,6},{12,0},{14,2},{1,13},{3,15... | collective-permute-start | bytes 294920 | tf_op jit(solution)/shard_map/ppermute | solution.py:301
  16.1 0.0 collective-permute-done.5.second_ref.refs_2_
  16.1 1.6 %collective-permute-start.3 = (bf16[48,1024]{1,0:T(8,128)(2,1)S(1)}, bf16[48,1024]{1,0:T(8,128)(2,1)S(1)}, u32[]{:S(2)}, u32[]{:S(2)}) collective-permute-start(bf16[48,1024]{1,0:T(8,128)(2,1)S(1)} %get-tuple-element.24), channel_id=1, source_target_pairs={{0,14},{2,12},{4,10},{6,8},{8,6},{10,4},{12,2},{14,0},{1,15},{3,13... | collective-permute-start | bytes 294920 | tf_op jit(solution)/shard_map/ppermute | solution.py:301
  17.7 0.0 copy-start
  17.7 3.4 %copy-done = bf16[4096,1024]{1,0:T(8,128)(2,1)S(1)} copy-done((bf16[4096,1024]{1,0:T(8,128)(2,1)S(1)}, bf16[4096,1024]{1,0:T(8,128)(2,1)}, u32[]{:S(2)}) %copy-start) | copy-done | bytes 8388632
  21.1 0.0 copy-start.3
  21.1 1.0 %copy-done.3 = bf16[48,4096]{1,0:T(8,128)(2,1)S(1)} copy-done((bf16[48,4096]{1,0:T(8,128)(2,1)S(1)}, bf16[48,4096]{1,0:T(8,128)(2,1)}, u32[]{:S(2)}) %copy-start.3) | copy-done | bytes 393240
  22.1 0.0 copy-start.1
  22.1 2.3 %shard_map.114 = (f32[48,512]{1,0:T(8,128)S(1)}, f32[48,512]{1,0:T(8,128)S(1)}) custom-call(s32[1]{0:T(128)} %bitcast.3.core_ref, bf16[48,4096]{1,0:T(8,128)(2,1)S(1)} %copy-done.3, bf16[4096,1024]{1,0:T(8,128)(2,1)S(1)} %copy-done, bf16[48,1024]{1,0:T(8,128)(2,1)S(1)} %collective-permute-done.4.first_ref.refs_1_, ...), custom_call_target="tpu_custom_call" | custom-call | flops 402653184 | bytes 33554432 | tf_op jit(solution)/shard_map/pallas_call | solution.py:304
  24.4 0.2 shard_map.115
  24.7 0.0 collective-permute-done.6.refs_3_
  24.7 0.0 copy-done.1
  24.7 0.7 %shard_map.116.refs_6_ = f32[48,128]{1,0:T(8,128)S(1)} custom-call(bf16[48,1024]{1,0:T(8,128)(2,1)S(1)} %get-tuple-element.29.refs_0_, bf16[48,1024]{1,0:T(8,128)(2,1)S(1)} %collective-permute-done.4.first_ref.refs_1_, bf16[48,1024]{1,0:T(8,128)(2,1)S(1)} %collective-permute-done.5.second_ref.refs_2_, bf16[48,1024]{1,0:T(8,128)(2,1)S(1)} %collective-permute-done.6.refs_3_, ...), custom_call_target="tpu_custom_call" | custom-call | tf_op jit(solution)/shard_map/pallas_call | solution.py:326
  25.4 0.0 collective-permute-done.refs_0_
  25.4 0.0 collective-permute-done.1.refs_1_
  25.4 0.0 collective-permute-done.2.refs_2_
  25.4 0.0 collective-permute-done.3.refs_3_
  25.4 0.7 %shard_map.117.mine_ref = f32[288,128]{1,0:T(8,128)S(1)} custom-call(bf16[48,1024]{1,0:T(8,128)(2,1)S(1)} %collective-permute-done.refs_0_, bf16[48,1024]{1,0:T(8,128)(2,1)S(1)} %collective-permute-done.1.refs_1_, bf16[48,1024]{1,0:T(8,128)(2,1)S(1)} %collective-permute-done.2.refs_2_, bf16[48,1024]{1,0:T(8,128)(2,1)S(1)} %collective-permute-done.3.refs_3_, ...), custom_call_target="tpu_custom_call" | custom-call | tf_op jit(solution)/shard_map/pallas_call | solution.py:331
  26.1 0.0 collective-permute-start.7
  26.1 1.4 %collective-permute-done.7.other_ref = f32[288,128]{1,0:T(8,128)S(1)} collective-permute-done((f32[288,128]{1,0:T(8,128)S(1)}, f32[288,128]{1,0:T(8,128)S(1)}, u32[]{:S(2)}, u32[]{:S(2)}) %collective-permute-start.7) | collective-permute-done | bytes 147488 | tf_op jit(solution)/shard_map/ppermute | solution.py:336
  27.5 0.0 copy-done.7
  27.5 1.0 %shard_map.118._ = bf16[384,128]{1,0:T(8,128)(2,1)} custom-call(f32[288,128]{1,0:T(8,128)S(1)} %shard_map.117.mine_ref, f32[288,128]{1,0:T(8,128)S(1)} %collective-permute-done.7.other_ref, bf16[1,2,64,256]{3,2,1,0:T(8,128)(2,1)S(1)} %copy-done.7, bf16[384,384]{1,0:T(8,128)(2,1)S(1)} %get-tuple-element.32.table_ref), custom_call_target="tpu_custom_call" | custom-call | tf_op jit(solution)/shard_map/pallas_call | solution.py:337
  28.5 6.3 %all-to-all-start = ((bf16[8,48,128]{2,1,0:T(8,128)(2,1)}), bf16[8,48,128]{2,1,0:T(8,128)(2,1)S(1)}, u32[]{:S(2)}, u32[]{:S(2)}) async-start(bf16[8,48,128]{2,1,0:T(8,128)(2,1)} %bitcast.4), calls=%async_computation | async-start | bytes 196608 | tf_op jit(solution)/shard_map/all_to_all | solution.py:350
  34.8 0.0 copy-done.10
  34.8 0.1 copy.12.length_ref
  34.9 0.0 copy-done.6
  34.9 0.0 copy-done.4
  34.9 0.0 copy-done.5
  35.0 1.7 %shard_map.120 = (f32[48,2048]{1,0:T(8,128)S(1)}, f32[48,128]{1,0:T(8,128)S(1)}, f32[48,128]{1,0:T(8,128)S(1)}) custom-call(bf16[48,2048]{1,0:T(8,128)(2,1)S(1)} %copy-done.6, bf16[48,2,32,128]{3,2,1,0:T(8,128)(2,1)S(1)} %copy-done.4, bf16[48,2,32,128]{3,2,1,0:T(8,128)(2,1)S(1)} %copy-done.5, s32[48,1]{1,0:T(8,128)S(1)} %copy.12.length_ref, ...), custom_call_target="tpu_custom_call" | custom-call | tf_op jit(solution)/shard_map/pallas_call | solution.py:351
  36.7 0.4 shard_map.119
  37.0 4.9 %all-to-all-done = bf16[8,48,128]{2,1,0:T(8,128)(2,1)S(1)} async-done(((bf16[8,48,128]{2,1,0:T(8,128)(2,1)}), bf16[8,48,128]{2,1,0:T(8,128)(2,1)S(1)}, u32[]{:S(2)}, u32[]{:S(2)}) %all-to-all-start) | async-done | bytes 98336 | tf_op jit(solution)/shard_map/all_to_all | solution.py:350
  42.0 1.3 %shard_map.121 = (bf16[48,512]{1,0:T(8,128)(2,1)}, bf16[48,2048]{1,0:T(8,128)(2,1)}) custom-call(bf16[384,128]{1,0:T(8,128)(2,1)S(1)} %bitcast.7, bf16[192,384]{1,0:T(8,128)(2,1)S(1)} %get-tuple-element.35.one_hot_ref, f32[48,512]{1,0:T(8,128)S(1)} %get-tuple-element.36.base_ref, bf16[48,2048]{1,0:T(8,128)(2,1)S(1)} %copy-done.6, ...), custom_call_target="tpu_custom_call" | custom-call | tf_op jit(solution)/shard_map/pallas_call | solution.py:356
  (2 shorter events, 0.0 us)
Async XLA Ops:
  0.6 34.2 %copy-start.10 = (s32[48]{0:T(128)S(1)}, s32[48]{0:T(128)}, u32[]{:S(2)}) copy-start(s32[48]{0:T(128)} %param.18) | copy-start | bytes 580
  0.6 1.0 %copy-start.2 = (bf16[48,4096]{1,0:T(8,128)(2,1)S(1)}, bf16[48,4096]{1,0:T(8,128)(2,1)}, u32[]{:S(2)}) copy-start(bf16[48,4096]{1,0:T(8,128)(2,1)} %hidden_ref.3) | copy-start | bytes 1179652
  1.6 0.7 %copy-start.8 = (s32[48,1]{0,1:T(1,128)S(1)}, s32[48,1]{0,1:T(1,128)}, u32[]{:S(2)}) copy-start(s32[48,1]{0,1:T(1,128)} %param.17) | copy-start | bytes 580
  2.3 0.7 %copy-start.9 = (s32[8]{0:T(128)S(1)}, s32[8]{0:T(128)}, u32[]{:S(2)}) copy-start(s32[8]{0:T(128)} %param.19) | copy-start | bytes 100
  3.0 24.5 %copy-start.7 = (bf16[1,2,64,256]{3,2,1,0:T(8,128)(2,1)S(1)}, bf16[1,2,64,256]{3,2,1,0:T(8,128)(2,1)}, u32[]{:S(2)}) copy-start(bf16[1,2,64,256]{3,2,1,0:T(8,128)(2,1)} %up_ref.1) | copy-start | bytes 196612
  3.0 32.0 %copy-start.6 = (bf16[48,2048]{1,0:T(8,128)(2,1)S(1)}, bf16[48,2048]{1,0:T(8,128)(2,1)}, u32[]{:S(2)}) copy-start(bf16[48,2048]{1,0:T(8,128)(2,1)} %query_ref.3) | copy-start | bytes 589828
  3.6 8.9 %collective-permute-start.4 = (bf16[48,1024]{1,0:T(8,128)(2,1)S(1)}, bf16[48,1024]{1,0:T(8,128)(2,1)S(1)}, u32[]{:S(2)}, u32[]{:S(2)}) collective-permute-start(bf16[48,1024]{1,0:T(8,128)(2,1)S(1)} %get-tuple-element.25), channel_id=1, source_target_pairs={{0,2},{2,0},{4,6},{6,4},{8,10},{10,8},{12,14},{14,12},{1,3},{3,1},... | collective-permute-start | bytes 294920 | tf_op jit(solution)/shard_map/ppermute | solution.py:301
  6.7 9.5 %collective-permute-start.5 = (bf16[48,1024]{1,0:T(8,128)(2,1)S(1)}, bf16[48,1024]{1,0:T(8,128)(2,1)S(1)}, u32[]{:S(2)}, u32[]{:S(2)}) collective-permute-start(bf16[48,1024]{1,0:T(8,128)(2,1)S(1)} %get-tuple-element.26), channel_id=1, source_target_pairs={{0,4},{2,6},{4,0},{6,2},{8,12},{10,14},{12,8},{14,10},{1,5},{3,7},... | collective-permute-start | bytes 294920 | tf_op jit(solution)/shard_map/ppermute | solution.py:301
  8.2 17.2 %collective-permute-start = (bf16[48,1024]{1,0:T(8,128)(2,1)S(1)}, bf16[48,1024]{1,0:T(8,128)(2,1)S(1)}, u32[]{:S(2)}, u32[]{:S(2)}) collective-permute-start(bf16[48,1024]{1,0:T(8,128)(2,1)S(1)} %get-tuple-element.21), channel_id=1, source_target_pairs={{0,8},{2,10},{4,12},{6,14},{8,0},{10,2},{12,4},{14,6},{1,9},{3,11}... | collective-permute-start | bytes 294920 | tf_op jit(solution)/shard_map/ppermute | solution.py:301
  10.8 13.9 %collective-permute-start.6 = (bf16[48,1024]{1,0:T(8,128)(2,1)S(1)}, bf16[48,1024]{1,0:T(8,128)(2,1)S(1)}, u32[]{:S(2)}, u32[]{:S(2)}) collective-permute-start(bf16[48,1024]{1,0:T(8,128)(2,1)S(1)} %get-tuple-element.30), channel_id=1, source_target_pairs={{0,6},{2,4},{4,2},{6,0},{8,14},{10,12},{12,10},{14,8},{1,7},{3,5},... | collective-permute-start | bytes 294920 | tf_op jit(solution)/shard_map/ppermute | solution.py:301
  11.2 14.2 %collective-permute-start.1 = (bf16[48,1024]{1,0:T(8,128)(2,1)S(1)}, bf16[48,1024]{1,0:T(8,128)(2,1)S(1)}, u32[]{:S(2)}, u32[]{:S(2)}) collective-permute-start(bf16[48,1024]{1,0:T(8,128)(2,1)S(1)} %get-tuple-element.22), channel_id=1, source_target_pairs={{0,10},{2,8},{4,14},{6,12},{8,2},{10,0},{12,6},{14,4},{1,11},{3,9}... | collective-permute-start | bytes 294920 | tf_op jit(solution)/shard_map/ppermute | solution.py:301
  12.5 12.9 %collective-permute-start.2 = (bf16[48,1024]{1,0:T(8,128)(2,1)S(1)}, bf16[48,1024]{1,0:T(8,128)(2,1)S(1)}, u32[]{:S(2)}, u32[]{:S(2)}) collective-permute-start(bf16[48,1024]{1,0:T(8,128)(2,1)S(1)} %get-tuple-element.23), channel_id=1, source_target_pairs={{0,12},{2,14},{4,8},{6,10},{8,4},{10,6},{12,0},{14,2},{1,13},{3,15... | collective-permute-start | bytes 294920 | tf_op jit(solution)/shard_map/ppermute | solution.py:301
  16.1 9.3 %collective-permute-start.3 = (bf16[48,1024]{1,0:T(8,128)(2,1)S(1)}, bf16[48,1024]{1,0:T(8,128)(2,1)S(1)}, u32[]{:S(2)}, u32[]{:S(2)}) collective-permute-start(bf16[48,1024]{1,0:T(8,128)(2,1)S(1)} %get-tuple-element.24), channel_id=1, source_target_pairs={{0,14},{2,12},{4,10},{6,8},{8,6},{10,4},{12,2},{14,0},{1,15},{3,13... | collective-permute-start | bytes 294920 | tf_op jit(solution)/shard_map/ppermute | solution.py:301
  17.7 3.4 %copy-start = (bf16[4096,1024]{1,0:T(8,128)(2,1)S(1)}, bf16[4096,1024]{1,0:T(8,128)(2,1)}, u32[]{:S(2)}) copy-start(bf16[4096,1024]{1,0:T(8,128)(2,1)} %weight_hbm.1) | copy-start | bytes 25165828
  21.1 1.0 %copy-start.3 = (bf16[48,4096]{1,0:T(8,128)(2,1)S(1)}, bf16[48,4096]{1,0:T(8,128)(2,1)}, u32[]{:S(2)}) copy-start(bf16[48,4096]{1,0:T(8,128)(2,1)} %hidden_ref.3) | copy-start | bytes 1179652
  22.1 2.6 %copy-start.1 = (bf16[1,4096,128]{2,1,0:T(8,128)(2,1)S(1)}, bf16[1,4096,128]{2,1,0:T(8,128)(2,1)}, u32[]{:S(2)}) copy-start(bf16[1,4096,128]{2,1,0:T(8,128)(2,1)} %refs_4_.3) | copy-start | bytes 3145732
  22.1 12.8 %copy-start.4 = (bf16[48,2,32,128]{3,2,1,0:T(8,128)(2,1)S(1)}, bf16[48,2,32,128]{3,2,1,0:T(8,128)(2,1)}, u32[]{:S(2)}) copy-start(bf16[48,2,32,128]{3,2,1,0:T(8,128)(2,1)} %key_ref.1) | copy-start | bytes 2359300
  22.1 12.8 %copy-start.5 = (bf16[48,2,32,128]{3,2,1,0:T(8,128)(2,1)S(1)}, bf16[48,2,32,128]{3,2,1,0:T(8,128)(2,1)}, u32[]{:S(2)}) copy-start(bf16[48,2,32,128]{3,2,1,0:T(8,128)(2,1)} %value_ref.1) | copy-start | bytes 2359300
  26.1 1.4 %collective-permute-start.7 = (f32[288,128]{1,0:T(8,128)S(1)}, f32[288,128]{1,0:T(8,128)S(1)}, u32[]{:S(2)}, u32[]{:S(2)}) collective-permute-start(f32[288,128]{1,0:T(8,128)S(1)} %shard_map.117.mine_ref), channel_id=1, source_target_pairs={{0,1},{1,0},{2,3},{3,2},{4,5},{5,4},{6,7},{7,6},{8,9},{9,8},{10,11... | collective-permute-start | bytes 442376 | tf_op jit(solution)/shard_map/ppermute | solution.py:336
  28.5 13.4 %all-to-all-start = ((bf16[8,48,128]{2,1,0:T(8,128)(2,1)}), bf16[8,48,128]{2,1,0:T(8,128)(2,1)S(1)}, u32[]{:S(2)}, u32[]{:S(2)}) async-start(bf16[8,48,128]{2,1,0:T(8,128)(2,1)} %bitcast.4), calls=%async_computation | async-start | bytes 196608 | tf_op jit(solution)/shard_map/all_to_all | solution.py:350

commit v11 on v10

--- a/solution.py
+++ b/solution.py
@@ -55,7 +55,12 @@
     )
 
 
-def pack_kernel(n, cap, pieces, me_ref, idx_ref, table_ref, hidden_ref, slot_ref, rank_ref, *out_refs):
+def place_of(slot, me, half):
+    apart = lax.bitwise_xor(slot, me)
+    return jnp.where(apart < half, lax.bitwise_and(slot, half - 1), apart)
+
+
+def pack_kernel(n, cap, pieces, me_ref, idx_ref, table_ref, hidden_ref, slot_ref, rank_ref, near_ref, *far_refs):
     rows = hidden_ref.shape[0]
     named = (iota((n, rows), 0) == idx_ref[...]).astype(F32).astype(BF16)
     table = jnp.broadcast_to(table_ref[...].astype(F32).astype(BF16), (16, n))
@@ -67,11 +72,13 @@
     slot_ref[...] = slot
     rank_ref[...] = rank
     per = pieces * cap
-    apart = lax.bitwise_xor(slot, me_ref[0])
-    one_hot = one_hot_of(codes_of(apart, rank, cap, pieces), 0, n * per)
+    half = n // 2
+    place = place_of(slot, me_ref[0], half)
+    one_hot = one_hot_of(codes_of(place, rank, cap, pieces), 0, n * per)
     packed = dot(one_hot, stack_pieces(hidden_ref[...], pieces)).astype(BF16)
-    for s, out_ref in enumerate(out_refs):
-        out_ref[...] = packed[s * per : (s + 1) * per]
+    near_ref[...] = packed[: half * per]
+    for s, far_ref in enumerate(far_refs, half):
+        far_ref[...] = packed[s * per : (s + 1) * per]
 
 
 def tables_kernel(n, cap, pieces, out_pieces, me_ref, _, shrink_ref, expand_ref):
@@ -81,8 +88,8 @@
     shrink_ref[...] = same.astype(F32).astype(BF16)
     per = out_pieces * cap
     out_row, in_row = iota(expand_ref.shape, 0), iota(expand_ref.shape, 1)
-    apart = lax.bitwise_xor(out_row // per, me_ref[0])
-    source = (out_row // cap % out_pieces) * (n * cap) + apart * cap + out_row % cap
+    place = place_of(out_row // per, me_ref[0], n // 2)
+    source = (out_row // cap % out_pieces) * (n * cap) + place * cap + out_row % cap
     expand_ref[...] = (source == in_row).astype(F32).astype(BF16)
 
 
@@ -99,15 +106,14 @@
     return select_sum(table_ref[...], total)
 
 
-def shrink_near_kernel(cap, pieces, *refs):
+def shrink_far_kernel(cap, pieces, *refs):
     refs[-1][...] = shrink(cap, pieces, refs[:-3], *refs[-3:-1])
 
 
-def shrink_far_kernel(cap, pieces, *refs):
-    near_ref, base_ref, out_ref = refs[-3:]
-    half = near_ref.shape[0]
-    out_ref[:half, :] = near_ref[...]
-    out_ref[half : 2 * half, :] = shrink(cap, pieces, refs[:-5], *refs[-5:-3])
+def shrink_near_kernel(cap, pieces, near_ref, down_ref, table_ref, far_ref, base_ref, out_ref):
+    half = far_ref.shape[0]
+    out_ref[:half, :] = shrink(cap, pieces, [near_ref], down_ref, table_ref)
+    out_ref[half : 2 * half, :] = far_ref[...]
     rows = base_ref.shape[0]
     lanes = out_ref.shape[1]
     for i in range(base_ref.shape[1] // lanes):
@@ -142,7 +148,7 @@
 
 
 def base_kernel(
-    core_ref, hidden_ref, weight_hbm, first_ref, second_ref, mine_ref, other_ref, weight_ref, sems
+    core_ref, hidden_ref, weight_hbm, mine_ref, other_ref, weight_ref, sems
 ):
     slots, depth = weight_ref.shape[:2]
     blocks = hidden_ref.shape[1] // depth
@@ -288,31 +294,40 @@
     swap = functools.partial(lax.ppermute, axis_name="tp", perm=[(0, 1), (1, 0)])
 
     me = lax.axis_index("pool").reshape(1)
-    slot, rank, *packed = call(
+    half = n // 2
+    per = pieces * cap
+    slot, rank, near, *far = call(
         functools.partial(pack_kernel, n, cap, pieces),
         [jax.ShapeDtypeStruct((1, rows), I32)] * 2
-        + [jax.ShapeDtypeStruct((pieces * cap, width // pieces), BF16)] * n,
+        + [jax.ShapeDtypeStruct((half * per, width // pieces), BF16)]
+        + [jax.ShapeDtypeStruct((per, width // pieces), BF16)] * half,
         [SMEM, VMEM, VMEM, VMEM],
     )(me, row_adapter_index.reshape(1, rows), adapter_slot_table.reshape(1, n), hidden)
-    half = n // 2
-    order = [0, 1, 2, *range(half, n), *range(3, half)]
-    arrived = {0: packed[0]}
-    for s in order[1:]:
-        arrived[s] = lax.ppermute(packed[s], "pool", [(i, i ^ s) for i in range(n)])
+    far = [
+        lax.ppermute(chunk, "pool", [(i, i ^ s) for i in range(n)]) for s, chunk in enumerate(far, half)
+    ]
+    near = lax.all_to_all(
+        near,
+        "pool",
+        split_axis=0,
+        concat_axis=0,
+        tiled=True,
+        axis_index_groups=[list(range(half)), list(range(half, n))],
+    )
 
     slots, depth = 4, 512
     base_mine, base_other = call(
         base_kernel,
         [jax.ShapeDtypeStruct((rows, columns), F32)] * 2,
-        [SMEM, VMEM, ANY, ANY, ANY],
+        [SMEM, VMEM, ANY],
         [
             pltpu.VMEM((slots, depth, 2 * columns), BF16),
             pltpu.SemaphoreType.DMA((slots,)),
         ],
         pl.CostEstimate(
-            flops=4 * rows * width * columns, bytes_accessed=16 * width * columns, transcendentals=0
+            flops=4 * rows * width * columns, bytes_accessed=128 * width * columns, transcendentals=0
         ),
-    )(lax.axis_index("tp").reshape(1), hidden, key_value_weight, arrived[1], arrived[2])
+    )(lax.axis_index("tp").reshape(1), hidden, key_value_weight)
 
     size = n * out_pieces * cap
     shrink_table, expand_table = call(
@@ -323,16 +338,16 @@
         ],
         [SMEM, ANY],
     )(me, base_mine)
-    (near_sum,) = call(
-        functools.partial(shrink_near_kernel, cap, pieces),
+    (far_sum,) = call(
+        functools.partial(shrink_far_kernel, cap, pieces),
         [jax.ShapeDtypeStruct((half * cap, rank2), F32)],
         [VMEM] * (half + 2),
-    )(*[arrived[s] for s in range(half)], adapter_down_weight, shrink_table)
+    )(*far, adapter_down_weight, shrink_table)
     (sums,) = call(
-        functools.partial(shrink_far_kernel, cap, pieces),
+        functools.partial(shrink_near_kernel, cap, pieces),
         [jax.ShapeDtypeStruct((n * cap + rows * columns // rank2, rank2), F32)],
-        [VMEM] * (half + 4),
-    )(*[arrived[s] for s in range(half, n)], adapter_down_weight, shrink_table, near_sum, base_other)
+        [VMEM] * 5,
+    )(near, adapter_down_weight, shrink_table, far_sum, base_other)
     other_sums = swap(sums)
     (terms,) = call(
         functools.partial(expand_kernel, n, cap),

time: 43.6 us -> 52.6 us (1.21)
  local copies, waits for them, and re-layouts: 6.79 us -> 13.3 us
  Pallas kernels: 9.03 us -> 10.8 us
  waiting for transfers between devices: 6.32 us -> 7.55 us
  starting transfers between devices: 20.4 us -> 19.6 us
    ppermute x7 -> x4, starting transfers between devices: 14.1 us -> 7.88 us  [shards(): lax.ppermute(chunk, 'pool', [(i, i ^ s) for i in range(n)])]
    unnamed x22 -> x36, local copies, waits for them, and re-layouts: 6.7 us -> 12.6 us
    all_to_all x0 -> x1, starting transfers between devices: none -> 5.25 us  [shards(): lax.all_to_all(near, 'pool', split_axis=0, concat_axis=0, tiled=True, axi...]
    ppermute x7 -> x4, waiting for transfers between devices: 0.02 us -> 3.18 us  [shards(): lax.ppermute(chunk, 'pool', [(i, i ^ s) for i in range(n)])]
    all_to_all x1, waiting for transfers between devices: 4.92 us -> 2.99 us  [shards(): lax.all_to_all(terms, 'pool', split_axis=0, concat_axis=0, tiled=True)]
    pallas_call x1, Pallas kernels: 0.69 us -> 1.62 us  [shards(): call(functools.partial(shrink_far_kernel, cap, pieces), [jax.ShapeDtypeSt...]
    pallas_call x1, Pallas kernels: 0.65 us -> 1.46 us  [shards(): call(functools.partial(pack_kernel, n, cap, pieces), [jax.ShapeDtypeStruc...]
    reshape x1, local copies, waits for them, and re-layouts: 0.09 us -> 0.74 us  [shards(): stored_cache_lengths.reshape(rows, 1)]
  transfers between devices with their start and end apart: 9 -> 7, of which waited for: 2 -> 3; matrix products, arithmetic and copies ran while one was open for 0% -> 1% of each run, Pallas kernels for 12% -> 12%
where the time goes in v11:
time: 52.6 us; the launch traced here: 52 us
  starting transfers between devices  19.6 us (37%)
  local copies, waits for them, and re-layouts  13.3 us (25%)
  Pallas kernels  10.8 us (21%)
  waiting for transfers between devices  7.55 us (14%)
  between operations  0.76 us (1%)
    unnamed x36, local copies, waits for them, and re-layouts  12.6 us
    ppermute x4, starting transfers between devices, shards(): lax.ppermute(chunk, 'pool', [(i, i ^ s) for i in range(n)])  7.88 us
    all_to_all x1, starting transfers between devices, shards(): lax.all_to_all(terms, 'pool', split_axis=0, concat_axis=0, tiled=True)  6.52 us
    all_to_all x1, starting transfers between devices, shards(): lax.all_to_all(near, 'pool', split_axis=0, concat_axis=0, tiled=True, axi...  5.25 us
    ppermute x4, waiting for transfers between devices, shards(): lax.ppermute(chunk, 'pool', [(i, i ^ s) for i in range(n)])  3.18 us
    all_to_all x1, waiting for transfers between devices, shards(): lax.all_to_all(terms, 'pool', split_axis=0, concat_axis=0, tiled=True)  2.99 us
    pallas_call x1, Pallas kernels, shards(): call(base_kernel, [jax.ShapeDtypeStruct((rows, columns), F32)] * 2, [SMEM...  2.3 us
    pallas_call x1, Pallas kernels, shards(): call(cache_kernel, [jax.ShapeDtypeStruct(queries.shape, F32)] + [jax.Shap...  1.71 us
  transfers between devices with their start and end apart: 7, of which 3 were waited for; matrix products, arithmetic and copies ran while one was open for 1% of the time, Pallas kernels for 12%

profile of v11, /device:TPU:0, one launch (start us, length us, event | category | flops | bytes accessed | tf_op | source)
XLA Modules:
  0.0 52.0 jit_solution(2201037106746759755)
XLA Ops:
  0.6 0.0 copy-start.1
  0.6 0.0 copy-start.2
  0.7 1.1 %copy-done.2 = bf16[48,4096]{1,0:T(8,128)(2,1)S(1)} copy-done((bf16[48,4096]{1,0:T(8,128)(2,1)S(1)}, bf16[48,4096]{1,0:T(8,128)(2,1)}, u32[]{:S(2)}) %copy-start.2) | copy-done | bytes 393240
  1.7 0.7 %copy-done.12 = s32[48,1]{0,1:T(1,128)S(1)} copy-done((s32[48,1]{0,1:T(1,128)S(1)}, s32[48,1]{0,1:T(1,128)}, u32[]{:S(2)}) %copy-start.12) | copy-done | bytes 216
  2.4 0.7 %copy-done.13 = s32[8]{0:T(128)S(1)} copy-done((s32[8]{0:T(128)S(1)}, s32[8]{0:T(128)}, u32[]{:S(2)}) %copy-start.13) | copy-done | bytes 56
  3.0 1.5 %shard_map.113 = (s32[1,48]{1,0:T(1,128)S(1)}, s32[1,48]{1,0:T(1,128)S(1)}, bf16[192,1024]{1,0:T(8,128)(2,1)}, bf16[48,1024]{1,0:T(8,128)(2,1)}, bf16[48,1024]{1...) custom-call(s32[1]{0:T(128)} %bitcast.me_ref, s32[1,48]{1,0:T(1,128)S(1)} %bitcast.11, ...), custom_call_target="tpu_custom_call" | custom-call | tf_op jit(solution)/shard_map/pallas_call | solution.py:299
  4.5 0.6 %copy-done.14 = s32[1,48]{1,0:T(1,128)} copy-done((s32[1,48]{1,0:T(1,128)}, s32[1,48]{1,0:T(1,128)S(1)}, u32[]{:S(2)}) %copy-start.14) | copy-done | bytes 216
  5.1 0.5 copy-done.16
  5.6 5.2 %all-to-all-start = ((bf16[4,48,1024]{2,1,0:T(8,128)(2,1)}), bf16[4,48,1024]{2,1,0:T(8,128)(2,1)S(1)}, u32[]{:S(2)}, u32[]{:S(2)}) async-start(bf16[4,48,1024]{2,1,0:T(8,128)(2,1)} %bitcast.3), calls=%async_computation | async-start | bytes 786432 | tf_op jit(solution)/shard_map/all_to_all | solution.py:309
  10.9 2.6 %collective-permute-start = (bf16[48,1024]{1,0:T(8,128)(2,1)}, bf16[48,1024]{1,0:T(8,128)(2,1)S(1)}, u32[]{:S(2)}, u32[]{:S(2)}) collective-permute-start(bf16[48,1024]{1,0:T(8,128)(2,1)} %get-tuple-element.21), channel_id=1, source_target_pairs={{0,8},{2,10},{4,12},{6,14},{8,0},{10,2},{12,4},{14,6},{1,9},{3,11}... | collective-permute-start | bytes 294920 | tf_op jit(solution)/shard_map/ppermute | solution.py:307
  13.5 1.8 %collective-permute-start.1 = (bf16[48,1024]{1,0:T(8,128)(2,1)}, bf16[48,1024]{1,0:T(8,128)(2,1)S(1)}, u32[]{:S(2)}, u32[]{:S(2)}) collective-permute-start(bf16[48,1024]{1,0:T(8,128)(2,1)} %get-tuple-element.22), channel_id=1, source_target_pairs={{0,10},{2,8},{4,14},{6,12},{8,2},{10,0},{12,6},{14,4},{1,11},{3,9}... | collective-permute-start | bytes 294920 | tf_op jit(solution)/shard_map/ppermute | solution.py:307
  15.2 3.5 %collective-permute-start.2 = (bf16[48,1024]{1,0:T(8,128)(2,1)}, bf16[48,1024]{1,0:T(8,128)(2,1)}, u32[]{:S(2)}, u32[]{:S(2)}) collective-permute-start(bf16[48,1024]{1,0:T(8,128)(2,1)} %get-tuple-element.23), channel_id=1, source_target_pairs={{0,12},{2,14},{4,8},{6,10},{8,4},{10,6},{12,0},{14,2},{1,13},{3,15... | collective-permute-start | bytes 294920 | tf_op jit(solution)/shard_map/ppermute | solution.py:307
  18.7 0.0 collective-permute-start.3
  18.7 3.4 %copy-done = bf16[4096,1024]{1,0:T(8,128)(2,1)S(1)} copy-done((bf16[4096,1024]{1,0:T(8,128)(2,1)S(1)}, bf16[4096,1024]{1,0:T(8,128)(2,1)}, u32[]{:S(2)}) %copy-start) | copy-done | bytes 8388632
  22.1 1.0 %copy-done.3 = bf16[48,4096]{1,0:T(8,128)(2,1)S(1)} copy-done((bf16[48,4096]{1,0:T(8,128)(2,1)S(1)}, bf16[48,4096]{1,0:T(8,128)(2,1)}, u32[]{:S(2)}) %copy-start.3) | copy-done | bytes 393240
  23.1 2.3 %shard_map.114 = (f32[48,512]{1,0:T(8,128)S(1)}, f32[48,512]{1,0:T(8,128)S(1)}) custom-call(s32[1]{0:T(128)} %bitcast.5.core_ref, bf16[48,4096]{1,0:T(8,128)(2,1)S(1)} %copy-done.3, bf16[4096,1024]{1,0:T(8,128)(2,1)S(1)} %copy-done), custom_call_target="tpu_custom_call" | custom-call | flops 402653184 | bytes 268435456 | tf_op jit(solution)/shard_map/pallas_call | solution.py:319
  25.4 0.0 copy-start.9
  25.4 0.3 shard_map.115
  25.7 0.0 copy-start.7
  25.7 0.7 %copy-done.7 = bf16[384,384]{1,0:T(8,128)(2,1)} copy-done((bf16[384,384]{1,0:T(8,128)(2,1)}, bf16[384,384]{1,0:T(8,128)(2,1)S(1)}, u32[]{:S(2)}) %copy-start.7) | copy-done | bytes 294936
  26.4 0.0 collective-permute-done.refs_0_
  26.4 3.2 %collective-permute-done.1.refs_1_ = bf16[48,1024]{1,0:T(8,128)(2,1)S(1)} collective-permute-done((bf16[48,1024]{1,0:T(8,128)(2,1)}, bf16[48,1024]{1,0:T(8,128)(2,1)S(1)}, u32[]{:S(2)}, u32[]{:S(2)}) %collective-permute-start.1) | collective-permute-done | bytes 98336 | tf_op jit(solution)/shard_map/ppermute | solution.py:307
  29.6 0.0 collective-permute-done.2.refs_2_
  29.6 0.0 collective-permute-done.3.refs_3_
  29.6 0.0 copy-done.9
  29.6 0.0 copy-done.1
  29.6 1.6 %shard_map.116.far_ref = f32[48,128]{1,0:T(8,128)S(1)} custom-call(bf16[48,1024]{1,0:T(8,128)(2,1)S(1)} %collective-permute-done.refs_0_, bf16[48,1024]{1,0:T(8,128)(2,1)S(1)} %collective-permute-done.1.refs_1_, bf16[48,1024]{1,0:T(8,128)(2,1)} %collective-permute-done.2.refs_2_, bf16[48,1024]{1,0:T(8,128)(2,1)} %collective-permute-done.3.refs_3_, ...), custom_call_target="tpu_custom_call" | custom-call | tf_op jit(solution)/shard_map/pallas_call | solution.py:341
  31.2 0.0 all-to-all-done
  31.3 0.0 copy-start.10
  31.3 0.9 %copy-done.10 = f32[48,512]{1,0:T(8,128)S(1)} copy-done((f32[48,512]{1,0:T(8,128)S(1)}, f32[48,512]{1,0:T(8,128)}, u32[]{:S(2)}) %copy-start.10) | copy-done | bytes 98328
  32.2 0.7 %shard_map.117.mine_ref = f32[288,128]{1,0:T(8,128)S(1)} custom-call(bf16[192,1024]{1,0:T(8,128)(2,1)S(1)} %bitcast.9, bf16[1,4096,128]{2,1,0:T(8,128)(2,1)S(1)} %copy-done.1, bf16[48,192]{1,0:T(8,128)(2,1)S(1)} %get-tuple-element.20.refs_5_.table_ref, f32[48,128]{1,0:T(8,128)S(1)} %shard_map.116.far_ref, f32[48,512]{1,0:T(8,128)S(1)} %copy-done.10), custom_call_target="tpu_custom_call" | custom-call | tf_op jit(solution)/shard_map/pallas_call | solution.py:346
  32.8 0.0 collective-permute-start.4
  32.8 1.4 %collective-permute-done.4.other_ref = f32[288,128]{1,0:T(8,128)S(1)} collective-permute-done((f32[288,128]{1,0:T(8,128)S(1)}, f32[288,128]{1,0:T(8,128)S(1)}, u32[]{:S(2)}, u32[]{:S(2)}) %collective-permute-start.4) | collective-permute-done | bytes 147488 | tf_op jit(solution)/shard_map/ppermute | solution.py:351
  34.2 1.0 %copy-done.8 = bf16[384,384]{1,0:T(8,128)(2,1)S(1)} copy-done((bf16[384,384]{1,0:T(8,128)(2,1)S(1)}, bf16[384,384]{1,0:T(8,128)(2,1)}, u32[]{:S(2)}) %copy-start.8) | copy-done | bytes 294936
  35.2 0.8 %copy-done.11 = bf16[1,2,64,256]{3,2,1,0:T(8,128)(2,1)S(1)} copy-done((bf16[1,2,64,256]{3,2,1,0:T(8,128)(2,1)S(1)}, bf16[1,2,64,256]{3,2,1,0:T(8,128)(2,1)}, u32[]{:S(2)}) %copy-start.11) | copy-done | bytes 65560
  36.0 1.1 %shard_map.118._ = bf16[384,128]{1,0:T(8,128)(2,1)} custom-call(f32[288,128]{1,0:T(8,128)S(1)} %shard_map.117.mine_ref, f32[288,128]{1,0:T(8,128)S(1)} %collective-permute-done.4.other_ref, bf16[1,2,64,256]{3,2,1,0:T(8,128)(2,1)S(1)} %copy-done.11, bf16[384,384]{1,0:T(8,128)(2,1)S(1)} %copy-done.8), custom_call_target="tpu_custom_call" | custom-call | tf_op jit(solution)/shard_map/pallas_call | solution.py:352
  37.1 6.5 %all-to-all-start.1 = ((bf16[8,48,128]{2,1,0:T(8,128)(2,1)}), bf16[8,48,128]{2,1,0:T(8,128)(2,1)S(1)}, u32[]{:S(2)}, u32[]{:S(2)}) async-start(bf16[8,48,128]{2,1,0:T(8,128)(2,1)} %bitcast.6), calls=%async_computation.1 | async-start | bytes 196608 | tf_op jit(solution)/shard_map/all_to_all | solution.py:365
  43.6 0.7 %copy.12.length_ref = s32[48,1]{1,0:T(8,128)S(1)} copy(s32[48,1]{0,1:T(1,128)} %bitcast.13) | data formatting | bytes 384 | tf_op jit(solution)/shard_map/reshape | solution.py:370
  44.3 0.0 copy-done.4
  44.3 0.0 copy-done.5
  44.3 0.0 copy-done.6
  44.3 1.7 %shard_map.120 = (f32[48,2048]{1,0:T(8,128)S(1)}, f32[48,128]{1,0:T(8,128)S(1)}, f32[48,128]{1,0:T(8,128)S(1)}) custom-call(bf16[48,2048]{1,0:T(8,128)(2,1)S(1)} %copy-done.6, bf16[48,2,32,128]{3,2,1,0:T(8,128)(2,1)S(1)} %copy-done.4, bf16[48,2,32,128]{3,2,1,0:T(8,128)(2,1)S(1)} %copy-done.5, s32[48,1]{1,0:T(8,128)S(1)} %copy.12.length_ref, ...), custom_call_target="tpu_custom_call" | custom-call | tf_op jit(solution)/shard_map/pallas_call | solution.py:366
  46.1 0.0 copy-start.15
  46.1 0.7 %copy-done.15 = s32[1,48]{1,0:T(1,128)S(1)} copy-done((s32[1,48]{1,0:T(1,128)S(1)}, s32[1,48]{1,0:T(1,128)}, u32[]{:S(2)}) %copy-start.15) | copy-done | bytes 216
  46.7 0.6 %copy-done.17 = s32[1,48]{1,0:T(1,128)S(1)} copy-done((s32[1,48]{1,0:T(1,128)S(1)}, s32[1,48]{1,0:T(1,128)}, u32[]{:S(2)}) %copy-start.17) | copy-done | bytes 216
  47.3 0.4 shard_map.119
  47.7 3.0 %all-to-all-done.1 = bf16[8,48,128]{2,1,0:T(8,128)(2,1)S(1)} async-done(((bf16[8,48,128]{2,1,0:T(8,128)(2,1)}), bf16[8,48,128]{2,1,0:T(8,128)(2,1)S(1)}, u32[]{:S(2)}, u32[]{:S(2)}) %all-to-all-start.1) | async-done | bytes 98336 | tf_op jit(solution)/shard_map/all_to_all | solution.py:365
  50.7 1.3 %shard_map.121 = (bf16[48,512]{1,0:T(8,128)(2,1)}, bf16[48,2048]{1,0:T(8,128)(2,1)}) custom-call(bf16[384,128]{1,0:T(8,128)(2,1)S(1)} %bitcast.10, bf16[192,384]{1,0:T(8,128)(2,1)S(1)} %get-tuple-element.29.one_hot_ref, f32[48,512]{1,0:T(8,128)S(1)} %get-tuple-element.30.base_ref, bf16[48,2048]{1,0:T(8,128)(2,1)S(1)} %copy-done.6, ...), custom_call_target="tpu_custom_call" | custom-call | tf_op jit(solution)/shard_map/pallas_call | solution.py:371
  (12 shorter events, 0.0 us)
Async XLA Ops:
  0.6 29.0 %copy-start.1 = (bf16[1,4096,128]{2,1,0:T(8,128)(2,1)S(1)}, bf16[1,4096,128]{2,1,0:T(8,128)(2,1)}, u32[]{:S(2)}) copy-start(bf16[1,4096,128]{2,1,0:T(8,128)(2,1)} %down_ref.1) | copy-start | bytes 3145732
  0.6 1.1 %copy-start.2 = (bf16[48,4096]{1,0:T(8,128)(2,1)S(1)}, bf16[48,4096]{1,0:T(8,128)(2,1)}, u32[]{:S(2)}) copy-start(bf16[48,4096]{1,0:T(8,128)(2,1)} %hidden_ref.3) | copy-start | bytes 1179652
  1.7 0.7 %copy-start.12 = (s32[48,1]{0,1:T(1,128)S(1)}, s32[48,1]{0,1:T(1,128)}, u32[]{:S(2)}) copy-start(s32[48,1]{0,1:T(1,128)} %param.17) | copy-start | bytes 580
  2.4 0.7 %copy-start.13 = (s32[8]{0:T(128)S(1)}, s32[8]{0:T(128)}, u32[]{:S(2)}) copy-start(s32[8]{0:T(128)} %param.19) | copy-start | bytes 100
  4.5 0.6 %copy-start.14 = (s32[1,48]{1,0:T(1,128)}, s32[1,48]{1,0:T(1,128)S(1)}, u32[]{:S(2)}) copy-start(s32[1,48]{1,0:T(1,128)S(1)} %get-tuple-element.27.slot_ref) | copy-start | bytes 580
  5.1 0.5 copy-start.16
  5.6 25.6 %all-to-all-start = ((bf16[4,48,1024]{2,1,0:T(8,128)(2,1)}), bf16[4,48,1024]{2,1,0:T(8,128)(2,1)S(1)}, u32[]{:S(2)}, u32[]{:S(2)}) async-start(bf16[4,48,1024]{2,1,0:T(8,128)(2,1)} %bitcast.3), calls=%async_computation | async-start | bytes 786432 | tf_op jit(solution)/shard_map/all_to_all | solution.py:309
  10.9 15.6 %collective-permute-start = (bf16[48,1024]{1,0:T(8,128)(2,1)}, bf16[48,1024]{1,0:T(8,128)(2,1)S(1)}, u32[]{:S(2)}, u32[]{:S(2)}) collective-permute-start(bf16[48,1024]{1,0:T(8,128)(2,1)} %get-tuple-element.21), channel_id=1, source_target_pairs={{0,8},{2,10},{4,12},{6,14},{8,0},{10,2},{12,4},{14,6},{1,9},{3,11}... | collective-permute-start | bytes 294920 | tf_op jit(solution)/shard_map/ppermute | solution.py:307
  13.5 16.1 %collective-permute-start.1 = (bf16[48,1024]{1,0:T(8,128)(2,1)}, bf16[48,1024]{1,0:T(8,128)(2,1)S(1)}, u32[]{:S(2)}, u32[]{:S(2)}) collective-permute-start(bf16[48,1024]{1,0:T(8,128)(2,1)} %get-tuple-element.22), channel_id=1, source_target_pairs={{0,10},{2,8},{4,14},{6,12},{8,2},{10,0},{12,6},{14,4},{1,11},{3,9}... | collective-permute-start | bytes 294920 | tf_op jit(solution)/shard_map/ppermute | solution.py:307
  15.2 14.4 %collective-permute-start.2 = (bf16[48,1024]{1,0:T(8,128)(2,1)}, bf16[48,1024]{1,0:T(8,128)(2,1)}, u32[]{:S(2)}, u32[]{:S(2)}) collective-permute-start(bf16[48,1024]{1,0:T(8,128)(2,1)} %get-tuple-element.23), channel_id=1, source_target_pairs={{0,12},{2,14},{4,8},{6,10},{8,4},{10,6},{12,0},{14,2},{1,13},{3,15... | collective-permute-start | bytes 294920 | tf_op jit(solution)/shard_map/ppermute | solution.py:307
  18.7 10.9 %collective-permute-start.3 = (bf16[48,1024]{1,0:T(8,128)(2,1)}, bf16[48,1024]{1,0:T(8,128)(2,1)}, u32[]{:S(2)}, u32[]{:S(2)}) collective-permute-start(bf16[48,1024]{1,0:T(8,128)(2,1)} %get-tuple-element.24), channel_id=1, source_target_pairs={{0,14},{2,12},{4,10},{6,8},{8,6},{10,4},{12,2},{14,0},{1,15},{3,13... | collective-permute-start | bytes 294920 | tf_op jit(solution)/shard_map/ppermute | solution.py:307
  18.7 3.4 %copy-start = (bf16[4096,1024]{1,0:T(8,128)(2,1)S(1)}, bf16[4096,1024]{1,0:T(8,128)(2,1)}, u32[]{:S(2)}) copy-start(bf16[4096,1024]{1,0:T(8,128)(2,1)} %weight_hbm.1) | copy-start | bytes 25165828
  22.1 1.0 %copy-start.3 = (bf16[48,4096]{1,0:T(8,128)(2,1)S(1)}, bf16[48,4096]{1,0:T(8,128)(2,1)}, u32[]{:S(2)}) copy-start(bf16[48,4096]{1,0:T(8,128)(2,1)} %hidden_ref.3) | copy-start | bytes 1179652
  23.1 21.2 %copy-start.4 = (bf16[48,2,32,128]{3,2,1,0:T(8,128)(2,1)S(1)}, bf16[48,2,32,128]{3,2,1,0:T(8,128)(2,1)}, u32[]{:S(2)}) copy-start(bf16[48,2,32,128]{3,2,1,0:T(8,128)(2,1)} %key_ref.1) | copy-start | bytes 2359300
  23.1 21.2 %copy-start.5 = (bf16[48,2,32,128]{3,2,1,0:T(8,128)(2,1)S(1)}, bf16[48,2,32,128]{3,2,1,0:T(8,128)(2,1)}, u32[]{:S(2)}) copy-start(bf16[48,2,32,128]{3,2,1,0:T(8,128)(2,1)} %value_ref.1) | copy-start | bytes 2359300
  23.1 21.2 %copy-start.6 = (bf16[48,2048]{1,0:T(8,128)(2,1)S(1)}, bf16[48,2048]{1,0:T(8,128)(2,1)}, u32[]{:S(2)}) copy-start(bf16[48,2048]{1,0:T(8,128)(2,1)} %query_ref.3) | copy-start | bytes 589828
  25.4 4.2 %copy-start.9 = (f32[48,512]{1,0:T(8,128)}, f32[48,512]{1,0:T(8,128)S(1)}, u32[]{:S(2)}) copy-start(f32[48,512]{1,0:T(8,128)S(1)} %get-tuple-element.25.base_ref) | copy-start | bytes 294916
  25.7 0.7 %copy-start.7 = (bf16[384,384]{1,0:T(8,128)(2,1)}, bf16[384,384]{1,0:T(8,128)(2,1)S(1)}, u32[]{:S(2)}) copy-start(bf16[384,384]{1,0:T(8,128)(2,1)S(1)} %get-tuple-element.26.table_ref) | copy-start | bytes 884740
  31.3 0.9 %copy-start.10 = (f32[48,512]{1,0:T(8,128)S(1)}, f32[48,512]{1,0:T(8,128)}, u32[]{:S(2)}) copy-start(f32[48,512]{1,0:T(8,128)} %copy-done.9) | copy-start | bytes 294916
  32.8 1.4 %collective-permute-start.4 = (f32[288,128]{1,0:T(8,128)S(1)}, f32[288,128]{1,0:T(8,128)S(1)}, u32[]{:S(2)}, u32[]{:S(2)}) collective-permute-start(f32[288,128]{1,0:T(8,128)S(1)} %shard_map.117.mine_ref), channel_id=1, source_target_pairs={{0,1},{1,0},{2,3},{3,2},{4,5},{5,4},{6,7},{7,6},{8,9},{9,8},{10,11... | collective-permute-start | bytes 442376 | tf_op jit(solution)/shard_map/ppermute | solution.py:351
  34.2 1.0 %copy-start.8 = (bf16[384,384]{1,0:T(8,128)(2,1)S(1)}, bf16[384,384]{1,0:T(8,128)(2,1)}, u32[]{:S(2)}) copy-start(bf16[384,384]{1,0:T(8,128)(2,1)} %copy-done.7) | copy-start | bytes 884740
  35.2 0.8 %copy-start.11 = (bf16[1,2,64,256]{3,2,1,0:T(8,128)(2,1)S(1)}, bf16[1,2,64,256]{3,2,1,0:T(8,128)(2,1)}, u32[]{:S(2)}) copy-start(bf16[1,2,64,256]{3,2,1,0:T(8,128)(2,1)} %up_ref.1) | copy-start | bytes 196612
  37.1 13.6 %all-to-all-start.1 = ((bf16[8,48,128]{2,1,0:T(8,128)(2,1)}), bf16[8,48,128]{2,1,0:T(8,128)(2,1)S(1)}, u32[]{:S(2)}, u32[]{:S(2)}) async-start(bf16[8,48,128]{2,1,0:T(8,128)(2,1)} %bitcast.6), calls=%async_computation.1 | async-start | bytes 196608 | tf_op jit(solution)/shard_map/all_to_all | solution.py:365
  46.1 0.7 %copy-start.15 = (s32[1,48]{1,0:T(1,128)S(1)}, s32[1,48]{1,0:T(1,128)}, u32[]{:S(2)}) copy-start(s32[1,48]{1,0:T(1,128)} %copy-done.14) | copy-start | bytes 580
  46.7 0.6 %copy-start.17 = (s32[1,48]{1,0:T(1,128)S(1)}, s32[1,48]{1,0:T(1,128)}, u32[]{:S(2)}) copy-start(s32[1,48]{1,0:T(1,128)} %copy-done.16) | copy-start | bytes 580

commit v12 on v10

--- a/solution.py
+++ b/solution.py
@@ -104,22 +104,17 @@
 
 
 def shrink_far_kernel(cap, pieces, *refs):
-    near_ref, base_ref, out_ref = refs[-3:]
+    near_ref, out_ref = refs[-2:]
     half = near_ref.shape[0]
     out_ref[:half, :] = near_ref[...]
-    out_ref[half : 2 * half, :] = shrink(cap, pieces, refs[:-5], *refs[-5:-3])
-    rows = base_ref.shape[0]
-    lanes = out_ref.shape[1]
-    for i in range(base_ref.shape[1] // lanes):
-        first = 2 * half + i * rows
-        out_ref[first : first + rows, :] = base_ref[:, i * lanes : (i + 1) * lanes]
-
-
-def expand_kernel(n, cap, mine_ref, other_ref, up_ref, table_ref, out_ref):
+    out_ref[half:, :] = shrink(cap, pieces, refs[:-4], *refs[-4:-2])
+
+
+def expand_kernel(mine_ref, other_ref, up_ref, table_ref, out_ref):
     rank = up_ref.shape[2]
     head = 128
     blocks = up_ref.shape[3] // head
-    reduced = (mine_ref[: n * cap, :] + other_ref[: n * cap, :]).astype(BF16)
+    reduced = (mine_ref[...] + other_ref[...]).astype(BF16)
     terms = []
     for c in range(2):
         kept = reduced[:, c * rank : (c + 1) * rank]
@@ -128,17 +123,70 @@
     out_ref[...] = dot(table_ref[...], jnp.concatenate(terms, axis=0)).astype(BF16)
 
 
-def prepare_kernel(n, cap, slot_ref, rank_ref, mine_ref, other_ref, _, base_ref, one_hot_ref):
+def prepare_kernel(cap, slot_ref, rank_ref, mine_ref, other_ref, base_ref, one_hot_ref):
     pieces = one_hot_ref.shape[0] // slot_ref.shape[1]
     size = one_hot_ref.shape[1]
-    rows = mine_ref.shape[0]
-    width = other_ref.shape[1]
-    for i in range(mine_ref.shape[1] // width):
-        lanes, first = slice(i * width, (i + 1) * width), n * cap + i * rows
-        base_ref[:, lanes] = mine_ref[:, lanes] + other_ref[first : first + rows, :]
+    base_ref[...] = mine_ref[...] + other_ref[...]
     one_hot = one_hot_of(codes_of(slot_ref[...], rank_ref[...], cap, pieces), 0, size)
     same = (iota((size, size), 0) == iota((size, size), 1)).astype(F32).astype(BF16)
     one_hot_ref[...] = dot_first(one_hot, same).astype(BF16)
+
+
+def combine_kernel(
+    delta_ref,
+    one_hot_ref,
+    base_ref,
+    query_ref,
+    max_ref,
+    sum_ref,
+    acc_ref,
+    token_hbm,
+    out_hbm,
+    token_ref,
+    out_ref,
+    sems,
+):
+    rows = base_ref.shape[0]
+    head = 128
+    groups = base_ref.shape[1] // (2 * head)
+    delta = dot(one_hot_ref[...], delta_ref[...])
+    heads = query_ref.shape[1] // head
+    per_group = heads // groups
+    scale = head ** (-0.5)
+    lane = iota((rows, head), 1)
+    copies = []
+    for g in range(groups):
+        made = []
+        for c in range(2):
+            at = (g * 2 + c) * head
+            piece = c * groups + g
+            made.append((base_ref[:, at : at + head] + delta[piece * rows : (piece + 1) * rows]).astype(BF16))
+            token_ref[:, at : at + head] = made[-1]
+        key, value = made[0].astype(F32), made[1].astype(F32)
+        own = jnp.zeros((rows, head), F32)
+        for h in range(g * per_group, (g + 1) * per_group):
+            query = query_ref[:, h * head : (h + 1) * head].astype(F32)
+            own = jnp.where(lane == h, jnp.sum(query * key, axis=1, keepdims=True), own)
+        own = own * scale
+        cache_max = max_ref[...]
+        highest = jnp.maximum(own, cache_max)
+        cache_factor = jnp.exp(cache_max - highest)
+        own_factor = jnp.exp(own - highest)
+        inverse = 1.0 / (sum_ref[...] * cache_factor + own_factor)
+        cache_factor = cache_factor * inverse
+        own_factor = own_factor * inverse
+        for h in range(g * per_group, (g + 1) * per_group):
+            lanes = slice(h * head, (h + 1) * head)
+            out = acc_ref[:, lanes] * cache_factor[:, h : h + 1] + value * own_factor[:, h : h + 1]
+            out_ref[:, lanes] = out.astype(BF16)
+        for i, (source, target, width) in enumerate(
+            [(token_ref, token_hbm, 2 * head), (out_ref, out_hbm, per_group * head)]
+        ):
+            part = pl.ds(g * width, width)
+            copies.append(pltpu.make_async_copy(source.at[:, part], target.at[:, part], sems.at[2 * g + i]))
+            copies[-1].start()
+    for copy in copies:
+        copy.wait()
 
 
 def base_kernel(
@@ -165,7 +213,10 @@
     other_ref[...] = jnp.where(core_ref[0] == 0, second, first)
 
 
-def cache_kernel(query_ref, key_ref, value_ref, length_ref, _, acc_ref, max_ref, sum_ref):
+def cache_kernel(
+    query_ref, key_ref, value_ref, length_ref, base_ref, _, acc_ref, max_ref, sum_ref, handed_ref
+):
+    handed_ref[...] = base_ref[...]
     rows, groups, positions, head = key_ref.shape
     per_group = query_ref.shape[1] // (groups * head)
     tile = 16
@@ -204,46 +255,6 @@
         sum_ref[at, :] = sums
 
 
-def combine_kernel(
-    delta_ref, one_hot_ref, base_ref, query_ref, max_ref, sum_ref, acc_ref, token_ref, out_ref
-):
-    rows = base_ref.shape[0]
-    head = 128
-    groups = base_ref.shape[1] // (2 * head)
-    delta = dot(one_hot_ref[...], delta_ref[...])
-    heads = query_ref.shape[1] // head
-    per_group = heads // groups
-    scale = head ** (-0.5)
-    lane = iota((rows, head), 1)
-    own = jnp.zeros((rows, head), F32)
-    values = []
-    for g in range(groups):
-        made = []
-        for c in range(2):
-            at = (g * 2 + c) * head
-            piece = c * groups + g
-            made.append((base_ref[:, at : at + head] + delta[piece * rows : (piece + 1) * rows]).astype(BF16))
-            token_ref[:, at : at + head] = made[-1]
-        key = made[0].astype(F32)
-        values.append(made[1].astype(F32))
-        for h in range(g * per_group, (g + 1) * per_group):
-            query = query_ref[:, h * head : (h + 1) * head].astype(F32)
-            own = jnp.where(lane == h, jnp.sum(query * key, axis=1, keepdims=True), own)
-    own = own[:, :heads] * scale
-    cache_max = max_ref[:, :heads]
-    highest = jnp.maximum(own, cache_max)
-    cache_factor = jnp.exp(cache_max - highest)
-    own_factor = jnp.exp(own - highest)
-    inverse = 1.0 / (sum_ref[:, :heads] * cache_factor + own_factor)
-    cache_factor = cache_factor * inverse
-    own_factor = own_factor * inverse
-    for h in range(heads):
-        lanes = slice(h * head, (h + 1) * head)
-        out = acc_ref[:, lanes] * cache_factor[:, h : h + 1]
-        out = out + values[h // per_group] * own_factor[:, h : h + 1]
-        out_ref[:, lanes] = out.astype(BF16)
-
-
 VMEM = pl.BlockSpec(memory_space=pltpu.VMEM)
 SMEM = pl.BlockSpec(memory_space=pltpu.SMEM)
 HBM = pl.BlockSpec(memory_space=pltpu.HBM)
@@ -330,33 +341,49 @@
     )(*[arrived[s] for s in range(half)], adapter_down_weight, shrink_table)
     (sums,) = call(
         functools.partial(shrink_far_kernel, cap, pieces),
-        [jax.ShapeDtypeStruct((n * cap + rows * columns // rank2, rank2), F32)],
-        [VMEM] * (half + 4),
-    )(*[arrived[s] for s in range(half, n)], adapter_down_weight, shrink_table, near_sum, base_other)
-    other_sums = swap(sums)
+        [jax.ShapeDtypeStruct((n * cap, rank2), F32)],
+        [VMEM] * (half + 3),
+    )(*[arrived[s] for s in range(half, n)], adapter_down_weight, shrink_table, near_sum)
     (terms,) = call(
-        functools.partial(expand_kernel, n, cap),
+        expand_kernel,
         [jax.ShapeDtypeStruct((size, head), BF16)],
         [VMEM] * 4,
-    )(sums, other_sums, adapter_up_weight, expand_table)
+    )(sums, swap(sums), adapter_up_weight, expand_table)
+    deltas = lax.all_to_all(terms, "pool", split_axis=0, concat_axis=0, tiled=True)
+    attended, cache_max, cache_sum, base_other = call(
+        cache_kernel,
+        [jax.ShapeDtypeStruct(queries.shape, F32)]
+        + [jax.ShapeDtypeStruct((rows, head), F32)] * 2
+        + [jax.ShapeDtypeStruct((rows, columns), F32)],
+        [VMEM] * 5 + [ANY],
+    )(
+        queries,
+        stored_cache_keys,
+        stored_cache_values,
+        stored_cache_lengths.reshape(rows, 1),
+        base_other,
+        terms,
+    )
     base, one_hot = call(
-        functools.partial(prepare_kernel, n, cap),
+        functools.partial(prepare_kernel, cap),
         [
             jax.ShapeDtypeStruct((rows, columns), F32),
             jax.ShapeDtypeStruct((out_pieces * rows, size), BF16),
         ],
-        [VMEM] * 4 + [ANY],
-    )(slot, rank, base_mine, other_sums, terms)
-    deltas = lax.all_to_all(terms, "pool", split_axis=0, concat_axis=0, tiled=True)
-    attended, cache_max, cache_sum = call(
-        cache_kernel,
-        [jax.ShapeDtypeStruct(queries.shape, F32)] + [jax.ShapeDtypeStruct((rows, head), F32)] * 2,
-        [VMEM] * 4 + [ANY],
-    )(queries, stored_cache_keys, stored_cache_values, stored_cache_lengths.reshape(rows, 1), terms)
-    token, out = call(
+        [VMEM] * 4,
+    )(slot, rank, base_mine, swap(base_other))
+    token, out = pl.pallas_call(
         combine_kernel,
-        [jax.ShapeDtypeStruct((rows, columns), BF16), jax.ShapeDtypeStruct(queries.shape, BF16)],
-        [VMEM] * 7,
+        out_shape=[jax.ShapeDtypeStruct((rows, columns), BF16), jax.ShapeDtypeStruct(queries.shape, BF16)],
+        in_specs=[VMEM] * 7,
+        out_specs=[ANY] * 2,
+        scratch_shapes=[
+            pltpu.VMEM((rows, columns), BF16),
+            pltpu.VMEM(queries.shape, BF16),
+            pltpu.SemaphoreType.DMA((2 * groups,)),
+        ],
+        compiler_params=pltpu.CompilerParams(vmem_limit_bytes=VMEM_LIMIT),
+        cost_estimate=NO_COST,
     )(deltas, one_hot, base, queries, cache_max, cache_sum, attended)
     return token, out
 

time: 43.6 us -> 43.4 us (level)
    all_to_all x1, waiting for transfers between devices: 4.92 us -> 3.55 us  [shards(): lax.all_to_all(terms, 'pool', split_axis=0, concat_axis=0, tiled=True)]
    ppermute x1 -> x2, waiting for transfers between devices: 1.38 us -> 2.52 us  [the longest x1 1.29 us: shards(): swap(base_other)]
  transfers between devices with their start and end apart: 9 -> 10, of which waited for: 2 -> 3; matrix products, arithmetic and copies ran while one was open for 0% -> 0% of each run, Pallas kernels for 12% -> 12%
where the time goes in v12:
time: 43.4 us; the launch traced here: 43.1 us
  starting transfers between devices  20.5 us (47%)
  Pallas kernels  8.99 us (21%)
  local copies, waits for them, and re-layouts  6.79 us (16%)
  waiting for transfers between devices  6.1 us (14%)
  between operations  0.77 us (2%)
    ppermute x7, starting transfers between devices, shards(): arrived[s] = lax.ppermute(packed[s], 'pool', [(i, i ^ s) for i in range(n)])  14.1 us
    unnamed x22, local copies, waits for them, and re-layouts  6.7 us
    all_to_all x1, starting transfers between devices, shards(): lax.all_to_all(terms, 'pool', split_axis=0, concat_axis=0, tiled=True)  6.3 us
    all_to_all x1, waiting for transfers between devices, shards(): lax.all_to_all(terms, 'pool', split_axis=0, concat_axis=0, tiled=True)  3.55 us
    pallas_call x1, Pallas kernels, shards(): call(base_kernel, [jax.ShapeDtypeStruct((rows, columns), F32)] * 2, [SMEM...  2.3 us
    pallas_call x1, Pallas kernels, shards(): call(cache_kernel, [jax.ShapeDtypeStruct(queries.shape, F32)] + [jax.Shap...  1.72 us
    ppermute x1, waiting for transfers between devices, shards(): swap(base_other)  1.29 us
    pallas_call x1, Pallas kernels, shards(): pl.pallas_call(combine_kernel, out_shape=[jax.ShapeDtypeStruct((rows, col...  1.28 us
  transfers between devices with their start and end apart: 10, of which 3 were waited for; matrix products, arithmetic and copies ran while one was open for 0% of the time, Pallas kernels for 12%

profile of v12, /device:TPU:0, one launch (start us, length us, event | category | flops | bytes accessed | tf_op | source)
XLA Modules:
  0.0 43.1 jit_solution(8125717301593576756)
XLA Ops:
  0.6 0.0 copy-start.10
  0.6 0.0 copy-start.2
  0.7 1.0 %copy-done.2 = bf16[48,4096]{1,0:T(8,128)(2,1)S(1)} copy-done((bf16[48,4096]{1,0:T(8,128)(2,1)S(1)}, bf16[48,4096]{1,0:T(8,128)(2,1)}, u32[]{:S(2)}) %copy-start.2) | copy-done | bytes 393240
  1.6 0.0 copy-start.8
  1.6 0.7 %copy-done.8 = s32[48,1]{0,1:T(1,128)S(1)} copy-done((s32[48,1]{0,1:T(1,128)S(1)}, s32[48,1]{0,1:T(1,128)}, u32[]{:S(2)}) %copy-start.8) | copy-done | bytes 216
  2.3 0.0 copy-start.9
  2.3 0.7 %copy-done.9 = s32[8]{0:T(128)S(1)} copy-done((s32[8]{0:T(128)S(1)}, s32[8]{0:T(128)}, u32[]{:S(2)}) %copy-start.9) | copy-done | bytes 56
  3.0 0.0 copy-start.7
  3.0 0.0 copy-start.6
  3.0 0.7 %shard_map.113 = (s32[1,48]{1,0:T(1,128)S(1)}, s32[1,48]{1,0:T(1,128)S(1)}, bf16[48,1024]{1,0:T(8,128)(2,1)S(1)}, bf16[48,1024]{1,0:T(8,128)(2,1)S(1)}, bf16[48,...) custom-call(s32[1]{0:T(128)} %bitcast.me_ref, ...), custom_call_target="tpu_custom_call" | custom-call | tf_op jit(solution)/shard_map/pallas_call | solution.py:302
  3.6 3.0 %collective-permute-start.4 = (bf16[48,1024]{1,0:T(8,128)(2,1)S(1)}, bf16[48,1024]{1,0:T(8,128)(2,1)S(1)}, u32[]{:S(2)}, u32[]{:S(2)}) collective-permute-start(bf16[48,1024]{1,0:T(8,128)(2,1)S(1)} %get-tuple-element.26), channel_id=1, source_target_pairs={{0,2},{2,0},{4,6},{6,4},{8,10},{10,8},{12,14},{14,12},{1,3},{3,1},... | collective-permute-start | bytes 294920 | tf_op jit(solution)/shard_map/ppermute | solution.py:312
  6.7 1.6 %collective-permute-start.5 = (bf16[48,1024]{1,0:T(8,128)(2,1)S(1)}, bf16[48,1024]{1,0:T(8,128)(2,1)S(1)}, u32[]{:S(2)}, u32[]{:S(2)}) collective-permute-start(bf16[48,1024]{1,0:T(8,128)(2,1)S(1)} %get-tuple-element.27), channel_id=1, source_target_pairs={{0,4},{2,6},{4,0},{6,2},{8,12},{10,14},{12,8},{14,10},{1,5},{3,7},... | collective-permute-start | bytes 294920 | tf_op jit(solution)/shard_map/ppermute | solution.py:312
  8.2 2.6 %collective-permute-start = (bf16[48,1024]{1,0:T(8,128)(2,1)S(1)}, bf16[48,1024]{1,0:T(8,128)(2,1)S(1)}, u32[]{:S(2)}, u32[]{:S(2)}) collective-permute-start(bf16[48,1024]{1,0:T(8,128)(2,1)S(1)} %get-tuple-element.22), channel_id=1, source_target_pairs={{0,8},{2,10},{4,12},{6,14},{8,0},{10,2},{12,4},{14,6},{1,9},{3,11}... | collective-permute-start | bytes 294920 | tf_op jit(solution)/shard_map/ppermute | solution.py:312
  10.8 0.4 collective-permute-start.6
  11.2 1.3 %collective-permute-start.1 = (bf16[48,1024]{1,0:T(8,128)(2,1)S(1)}, bf16[48,1024]{1,0:T(8,128)(2,1)S(1)}, u32[]{:S(2)}, u32[]{:S(2)}) collective-permute-start(bf16[48,1024]{1,0:T(8,128)(2,1)S(1)} %get-tuple-element.23), channel_id=1, source_target_pairs={{0,10},{2,8},{4,14},{6,12},{8,2},{10,0},{12,6},{14,4},{1,11},{3,9}... | collective-permute-start | bytes 294920 | tf_op jit(solution)/shard_map/ppermute | solution.py:312
  12.5 0.0 collective-permute-done.4.first_ref.refs_1_
  12.5 3.6 %collective-permute-start.2 = (bf16[48,1024]{1,0:T(8,128)(2,1)S(1)}, bf16[48,1024]{1,0:T(8,128)(2,1)S(1)}, u32[]{:S(2)}, u32[]{:S(2)}) collective-permute-start(bf16[48,1024]{1,0:T(8,128)(2,1)S(1)} %get-tuple-element.24), channel_id=1, source_target_pairs={{0,12},{2,14},{4,8},{6,10},{8,4},{10,6},{12,0},{14,2},{1,13},{3,15... | collective-permute-start | bytes 294920 | tf_op jit(solution)/shard_map/ppermute | solution.py:312
  16.1 0.0 collective-permute-done.5.second_ref.refs_2_
  16.1 1.6 %collective-permute-start.3 = (bf16[48,1024]{1,0:T(8,128)(2,1)S(1)}, bf16[48,1024]{1,0:T(8,128)(2,1)S(1)}, u32[]{:S(2)}, u32[]{:S(2)}) collective-permute-start(bf16[48,1024]{1,0:T(8,128)(2,1)S(1)} %get-tuple-element.25), channel_id=1, source_target_pairs={{0,14},{2,12},{4,10},{6,8},{8,6},{10,4},{12,2},{14,0},{1,15},{3,13... | collective-permute-start | bytes 294920 | tf_op jit(solution)/shard_map/ppermute | solution.py:312
  17.7 0.0 copy-start
  17.7 3.4 %copy-done = bf16[4096,1024]{1,0:T(8,128)(2,1)S(1)} copy-done((bf16[4096,1024]{1,0:T(8,128)(2,1)S(1)}, bf16[4096,1024]{1,0:T(8,128)(2,1)}, u32[]{:S(2)}) %copy-start) | copy-done | bytes 8388632
  21.1 1.0 %copy-done.3 = bf16[48,4096]{1,0:T(8,128)(2,1)S(1)} copy-done((bf16[48,4096]{1,0:T(8,128)(2,1)S(1)}, bf16[48,4096]{1,0:T(8,128)(2,1)}, u32[]{:S(2)}) %copy-start.3) | copy-done | bytes 393240
  22.1 2.3 %shard_map.114 = (f32[48,512]{1,0:T(8,128)S(1)}, f32[48,512]{1,0:T(8,128)S(1)}) custom-call(s32[1]{0:T(128)} %bitcast.3.core_ref, bf16[48,4096]{1,0:T(8,128)(2,1)S(1)} %copy-done.3, bf16[4096,1024]{1,0:T(8,128)(2,1)S(1)} %copy-done, bf16[48,1024]{1,0:T(8,128)(2,1)S(1)} %collective-permute-done.4.first_ref.refs_1_, ...), custom_call_target="tpu_custom_call" | custom-call | flops 402653184 | bytes 33554432 | tf_op jit(solution)/shard_map/pallas_call | solution.py:315
  24.4 0.2 shard_map.115
  24.7 0.0 collective-permute-done.6.refs_3_
  24.7 0.0 copy-done.1
  24.7 0.7 %shard_map.116.refs_6_ = f32[48,128]{1,0:T(8,128)S(1)} custom-call(bf16[48,1024]{1,0:T(8,128)(2,1)S(1)} %get-tuple-element.30.refs_0_, bf16[48,1024]{1,0:T(8,128)(2,1)S(1)} %collective-permute-done.4.first_ref.refs_1_, bf16[48,1024]{1,0:T(8,128)(2,1)S(1)} %collective-permute-done.5.second_ref.refs_2_, bf16[48,1024]{1,0:T(8,128)(2,1)S(1)} %collective-permute-done.6.refs_3_, ...), custom_call_target="tpu_custom_call" | custom-call | tf_op jit(solution)/shard_map/pallas_call | solution.py:337
  25.4 0.0 collective-permute-done.refs_0_
  25.4 0.0 collective-permute-done.1.refs_1_
  25.4 0.0 collective-permute-done.2.refs_2_
  25.4 0.0 collective-permute-done.3.refs_3_
  25.4 0.7 %shard_map.117.mine_ref = f32[96,128]{1,0:T(8,128)S(1)} custom-call(bf16[48,1024]{1,0:T(8,128)(2,1)S(1)} %collective-permute-done.refs_0_, bf16[48,1024]{1,0:T(8,128)(2,1)S(1)} %collective-permute-done.1.refs_1_, bf16[48,1024]{1,0:T(8,128)(2,1)S(1)} %collective-permute-done.2.refs_2_, bf16[48,1024]{1,0:T(8,128)(2,1)S(1)} %collective-permute-done.3.refs_3_, ...), custom_call_target="tpu_custom_call" | custom-call | tf_op jit(solution)/shard_map/pallas_call | solution.py:342
  26.1 0.0 collective-permute-start.7
  26.1 1.2 %collective-permute-done.7.other_ref = f32[96,128]{1,0:T(8,128)S(1)} collective-permute-done((f32[96,128]{1,0:T(8,128)S(1)}, f32[96,128]{1,0:T(8,128)S(1)}, u32[]{:S(2)}, u32[]{:S(2)}) %collective-permute-start.7) | collective-permute-done | bytes 49184 | tf_op jit(solution)/shard_map/ppermute | solution.py:351
  27.4 0.0 copy-done.7
  27.4 1.1 %shard_map.118._ = bf16[384,128]{1,0:T(8,128)(2,1)} custom-call(f32[96,128]{1,0:T(8,128)S(1)} %shard_map.117.mine_ref, f32[96,128]{1,0:T(8,128)S(1)} %collective-permute-done.7.other_ref, bf16[1,2,64,256]{3,2,1,0:T(8,128)(2,1)S(1)} %copy-done.7, bf16[384,384]{1,0:T(8,128)(2,1)S(1)} %get-tuple-element.32.table_ref), custom_call_target="tpu_custom_call" | custom-call | tf_op jit(solution)/shard_map/pallas_call | solution.py:347
  28.4 6.3 %all-to-all-start = ((bf16[8,48,128]{2,1,0:T(8,128)(2,1)}), bf16[8,48,128]{2,1,0:T(8,128)(2,1)S(1)}, u32[]{:S(2)}, u32[]{:S(2)}) async-start(bf16[8,48,128]{2,1,0:T(8,128)(2,1)} %bitcast.4), calls=%async_computation | async-start | bytes 196608 | tf_op jit(solution)/shard_map/all_to_all | solution.py:352
  34.7 0.0 copy-done.10
  34.7 0.1 copy.12.length_ref
  34.8 0.0 copy-done.6
  34.8 0.0 copy-done.4
  34.8 0.0 copy-done.5
  34.8 1.7 %shard_map.119 = (f32[48,2048]{1,0:T(8,128)S(1)}, f32[48,128]{1,0:T(8,128)S(1)}, f32[48,128]{1,0:T(8,128)S(1)}, f32[48,512]{1,0:T(8,128)S(1)}) custom-call(bf16[48,2048]{1,0:T(8,128)(2,1)S(1)} %copy-done.6, bf16[48,2,32,128]{3,2,1,0:T(8,128)(2,1)S(1)} %copy-done.4, bf16[48,2,32,128]{3,2,1,0:T(8,128)(2,1)S(1)} %copy-done.5, s32[48,1]{1,0:T(8,128)S(1)} %copy.12.length_ref, ...), custom_call_target="tpu_custom_call" | custom-call | tf_op jit(solution)/shard_map/pallas_call | solution.py:353
  36.5 0.1 collective-permute-start.8
  36.6 1.3 %collective-permute-done.8.other_ref = f32[48,512]{1,0:T(8,128)S(1)} collective-permute-done((f32[48,512]{1,0:T(8,128)S(1)}, f32[48,512]{1,0:T(8,128)S(1)}, u32[]{:S(2)}, u32[]{:S(2)}) %collective-permute-start.8) | collective-permute-done | bytes 98336 | tf_op jit(solution)/shard_map/ppermute | solution.py:374
  37.9 0.4 shard_map.120
  38.3 3.6 %all-to-all-done = bf16[8,48,128]{2,1,0:T(8,128)(2,1)S(1)} async-done(((bf16[8,48,128]{2,1,0:T(8,128)(2,1)}), bf16[8,48,128]{2,1,0:T(8,128)(2,1)S(1)}, u32[]{:S(2)}, u32[]{:S(2)}) %all-to-all-start) | async-done | bytes 98336 | tf_op jit(solution)/shard_map/all_to_all | solution.py:352
  41.8 1.3 %shard_map.121 = (bf16[48,512]{1,0:T(8,128)(2,1)}, bf16[48,2048]{1,0:T(8,128)(2,1)}) custom-call(bf16[384,128]{1,0:T(8,128)(2,1)S(1)} %bitcast.7, bf16[192,384]{1,0:T(8,128)(2,1)S(1)} %get-tuple-element.37.one_hot_ref, f32[48,512]{1,0:T(8,128)S(1)} %get-tuple-element.38.base_ref, bf16[48,2048]{1,0:T(8,128)(2,1)S(1)} %copy-done.6, ...), custom_call_target="tpu_custom_call" | custom-call | tf_op jit(solution)/shard_map/pallas_call | solution.py:375
  (4 shorter events, 0.0 us)
Async XLA Ops:
  0.6 34.1 %copy-start.10 = (s32[48]{0:T(128)S(1)}, s32[48]{0:T(128)}, u32[]{:S(2)}) copy-start(s32[48]{0:T(128)} %param.18) | copy-start | bytes 580
  0.6 1.0 %copy-start.2 = (bf16[48,4096]{1,0:T(8,128)(2,1)S(1)}, bf16[48,4096]{1,0:T(8,128)(2,1)}, u32[]{:S(2)}) copy-start(bf16[48,4096]{1,0:T(8,128)(2,1)} %hidden_ref.3) | copy-start | bytes 1179652
  1.6 0.7 %copy-start.8 = (s32[48,1]{0,1:T(1,128)S(1)}, s32[48,1]{0,1:T(1,128)}, u32[]{:S(2)}) copy-start(s32[48,1]{0,1:T(1,128)} %param.17) | copy-start | bytes 580
  2.3 0.7 %copy-start.9 = (s32[8]{0:T(128)S(1)}, s32[8]{0:T(128)}, u32[]{:S(2)}) copy-start(s32[8]{0:T(128)} %param.19) | copy-start | bytes 100
  3.0 24.4 %copy-start.7 = (bf16[1,2,64,256]{3,2,1,0:T(8,128)(2,1)S(1)}, bf16[1,2,64,256]{3,2,1,0:T(8,128)(2,1)}, u32[]{:S(2)}) copy-start(bf16[1,2,64,256]{3,2,1,0:T(8,128)(2,1)} %up_ref.1) | copy-start | bytes 196612
  3.0 31.8 %copy-start.6 = (bf16[48,2048]{1,0:T(8,128)(2,1)S(1)}, bf16[48,2048]{1,0:T(8,128)(2,1)}, u32[]{:S(2)}) copy-start(bf16[48,2048]{1,0:T(8,128)(2,1)} %query_ref.3) | copy-start | bytes 589828
  3.6 8.9 %collective-permute-start.4 = (bf16[48,1024]{1,0:T(8,128)(2,1)S(1)}, bf16[48,1024]{1,0:T(8,128)(2,1)S(1)}, u32[]{:S(2)}, u32[]{:S(2)}) collective-permute-start(bf16[48,1024]{1,0:T(8,128)(2,1)S(1)} %get-tuple-element.26), channel_id=1, source_target_pairs={{0,2},{2,0},{4,6},{6,4},{8,10},{10,8},{12,14},{14,12},{1,3},{3,1},... | collective-permute-start | bytes 294920 | tf_op jit(solution)/shard_map/ppermute | solution.py:312
  6.7 9.5 %collective-permute-start.5 = (bf16[48,1024]{1,0:T(8,128)(2,1)S(1)}, bf16[48,1024]{1,0:T(8,128)(2,1)S(1)}, u32[]{:S(2)}, u32[]{:S(2)}) collective-permute-start(bf16[48,1024]{1,0:T(8,128)(2,1)S(1)} %get-tuple-element.27), channel_id=1, source_target_pairs={{0,4},{2,6},{4,0},{6,2},{8,12},{10,14},{12,8},{14,10},{1,5},{3,7},... | collective-permute-start | bytes 294920 | tf_op jit(solution)/shard_map/ppermute | solution.py:312
  8.2 17.2 %collective-permute-start = (bf16[48,1024]{1,0:T(8,128)(2,1)S(1)}, bf16[48,1024]{1,0:T(8,128)(2,1)S(1)}, u32[]{:S(2)}, u32[]{:S(2)}) collective-permute-start(bf16[48,1024]{1,0:T(8,128)(2,1)S(1)} %get-tuple-element.22), channel_id=1, source_target_pairs={{0,8},{2,10},{4,12},{6,14},{8,0},{10,2},{12,4},{14,6},{1,9},{3,11}... | collective-permute-start | bytes 294920 | tf_op jit(solution)/shard_map/ppermute | solution.py:312
  10.8 13.9 %collective-permute-start.6 = (bf16[48,1024]{1,0:T(8,128)(2,1)S(1)}, bf16[48,1024]{1,0:T(8,128)(2,1)S(1)}, u32[]{:S(2)}, u32[]{:S(2)}) collective-permute-start(bf16[48,1024]{1,0:T(8,128)(2,1)S(1)} %get-tuple-element.31), channel_id=1, source_target_pairs={{0,6},{2,4},{4,2},{6,0},{8,14},{10,12},{12,10},{14,8},{1,7},{3,5},... | collective-permute-start | bytes 294920 | tf_op jit(solution)/shard_map/ppermute | solution.py:312
  11.2 14.2 %collective-permute-start.1 = (bf16[48,1024]{1,0:T(8,128)(2,1)S(1)}, bf16[48,1024]{1,0:T(8,128)(2,1)S(1)}, u32[]{:S(2)}, u32[]{:S(2)}) collective-permute-start(bf16[48,1024]{1,0:T(8,128)(2,1)S(1)} %get-tuple-element.23), channel_id=1, source_target_pairs={{0,10},{2,8},{4,14},{6,12},{8,2},{10,0},{12,6},{14,4},{1,11},{3,9}... | collective-permute-start | bytes 294920 | tf_op jit(solution)/shard_map/ppermute | solution.py:312
  12.5 12.9 %collective-permute-start.2 = (bf16[48,1024]{1,0:T(8,128)(2,1)S(1)}, bf16[48,1024]{1,0:T(8,128)(2,1)S(1)}, u32[]{:S(2)}, u32[]{:S(2)}) collective-permute-start(bf16[48,1024]{1,0:T(8,128)(2,1)S(1)} %get-tuple-element.24), channel_id=1, source_target_pairs={{0,12},{2,14},{4,8},{6,10},{8,4},{10,6},{12,0},{14,2},{1,13},{3,15... | collective-permute-start | bytes 294920 | tf_op jit(solution)/shard_map/ppermute | solution.py:312
  16.1 9.3 %collective-permute-start.3 = (bf16[48,1024]{1,0:T(8,128)(2,1)S(1)}, bf16[48,1024]{1,0:T(8,128)(2,1)S(1)}, u32[]{:S(2)}, u32[]{:S(2)}) collective-permute-start(bf16[48,1024]{1,0:T(8,128)(2,1)S(1)} %get-tuple-element.25), channel_id=1, source_target_pairs={{0,14},{2,12},{4,10},{6,8},{8,6},{10,4},{12,2},{14,0},{1,15},{3,13... | collective-permute-start | bytes 294920 | tf_op jit(solution)/shard_map/ppermute | solution.py:312
  17.7 3.4 %copy-start = (bf16[4096,1024]{1,0:T(8,128)(2,1)S(1)}, bf16[4096,1024]{1,0:T(8,128)(2,1)}, u32[]{:S(2)}) copy-start(bf16[4096,1024]{1,0:T(8,128)(2,1)} %weight_hbm.1) | copy-start | bytes 25165828
  21.1 1.0 %copy-start.3 = (bf16[48,4096]{1,0:T(8,128)(2,1)S(1)}, bf16[48,4096]{1,0:T(8,128)(2,1)}, u32[]{:S(2)}) copy-start(bf16[48,4096]{1,0:T(8,128)(2,1)} %hidden_ref.3) | copy-start | bytes 1179652
  22.1 2.6 %copy-start.1 = (bf16[1,4096,128]{2,1,0:T(8,128)(2,1)S(1)}, bf16[1,4096,128]{2,1,0:T(8,128)(2,1)}, u32[]{:S(2)}) copy-start(bf16[1,4096,128]{2,1,0:T(8,128)(2,1)} %refs_4_.3) | copy-start | bytes 3145732
  22.1 12.7 %copy-start.4 = (bf16[48,2,32,128]{3,2,1,0:T(8,128)(2,1)S(1)}, bf16[48,2,32,128]{3,2,1,0:T(8,128)(2,1)}, u32[]{:S(2)}) copy-start(bf16[48,2,32,128]{3,2,1,0:T(8,128)(2,1)} %key_ref.1) | copy-start | bytes 2359300
  22.1 12.7 %copy-start.5 = (bf16[48,2,32,128]{3,2,1,0:T(8,128)(2,1)S(1)}, bf16[48,2,32,128]{3,2,1,0:T(8,128)(2,1)}, u32[]{:S(2)}) copy-start(bf16[48,2,32,128]{3,2,1,0:T(8,128)(2,1)} %value_ref.1) | copy-start | bytes 2359300
  26.1 1.2 %collective-permute-start.7 = (f32[96,128]{1,0:T(8,128)S(1)}, f32[96,128]{1,0:T(8,128)S(1)}, u32[]{:S(2)}, u32[]{:S(2)}) collective-permute-start(f32[96,128]{1,0:T(8,128)S(1)} %shard_map.117.mine_ref), channel_id=1, source_target_pairs={{0,1},{1,0},{2,3},{3,2},{4,5},{5,4},{6,7},{7,6},{8,9},{9,8},{10,11... | collective-permute-start | bytes 147464 | tf_op jit(solution)/shard_map/ppermute | solution.py:351
  28.4 13.4 %all-to-all-start = ((bf16[8,48,128]{2,1,0:T(8,128)(2,1)}), bf16[8,48,128]{2,1,0:T(8,128)(2,1)S(1)}, u32[]{:S(2)}, u32[]{:S(2)}) async-start(bf16[8,48,128]{2,1,0:T(8,128)(2,1)} %bitcast.4), calls=%async_computation | async-start | bytes 196608 | tf_op jit(solution)/shard_map/all_to_all | solution.py:352
  36.5 1.4 %collective-permute-start.8 = (f32[48,512]{1,0:T(8,128)S(1)}, f32[48,512]{1,0:T(8,128)S(1)}, u32[]{:S(2)}, u32[]{:S(2)}) collective-permute-start(f32[48,512]{1,0:T(8,128)S(1)} %get-tuple-element.36), channel_id=1, source_target_pairs={{0,1},{1,0},{2,3},{3,2},{4,5},{5,4},{6,7},{7,6},{8,9},{9,8},{10,11... | collective-permute-start | bytes 294920 | tf_op jit(solution)/shard_map/ppermute | solution.py:374

commit v13 on v10

--- a/solution.py
+++ b/solution.py
@@ -55,10 +55,10 @@
     )
 
 
-def pack_kernel(n, cap, pieces, me_ref, idx_ref, table_ref, hidden_ref, slot_ref, rank_ref, *out_refs):
+def pack_kernel(n, cap, pieces, me_ref, small_ref, hidden_ref, slot_ref, rank_ref, *out_refs):
     rows = hidden_ref.shape[0]
-    named = (iota((n, rows), 0) == idx_ref[...]).astype(F32).astype(BF16)
-    table = jnp.broadcast_to(table_ref[...].astype(F32).astype(BF16), (16, n))
+    named = (iota((n, rows), 0) == small_ref[:, :rows]).astype(F32).astype(BF16)
+    table = jnp.broadcast_to(small_ref[:, rows:].astype(F32).astype(BF16), (16, n))
     slot = dot(table, named)[0:1, :].astype(I32)
     member = (iota((n, rows), 0) == slot).astype(F32)
     before = (iota((rows, rows), 0) < iota((rows, rows), 1)).astype(F32).astype(BF16)
@@ -288,12 +288,13 @@
     swap = functools.partial(lax.ppermute, axis_name="tp", perm=[(0, 1), (1, 0)])
 
     me = lax.axis_index("pool").reshape(1)
+    small = jnp.concatenate([row_adapter_index.reshape(1, rows), adapter_slot_table.reshape(1, n)], axis=1)
     slot, rank, *packed = call(
         functools.partial(pack_kernel, n, cap, pieces),
         [jax.ShapeDtypeStruct((1, rows), I32)] * 2
         + [jax.ShapeDtypeStruct((pieces * cap, width // pieces), BF16)] * n,
-        [SMEM, VMEM, VMEM, VMEM],
-    )(me, row_adapter_index.reshape(1, rows), adapter_slot_table.reshape(1, n), hidden)
+        [SMEM, VMEM, VMEM],
+    )(me, small, hidden)
     half = n // 2
     order = [0, 1, 2, *range(half, n), *range(3, half)]
     arrived = {0: packed[0]}

time: 43.6 us -> 43.1 us (0.989)
  local copies, waits for them, and re-layouts: 6.79 us -> 5.49 us
  other arithmetic: 0 us -> 0.75 us
    unnamed x22 -> x18, local copies, waits for them, and re-layouts: 6.7 us -> 5.39 us
    concatenate x0 -> x1, other arithmetic: none -> 0.75 us  [shards(): jnp.concatenate([row_adapter_index.reshape(1, rows), adapter_slot_table.r...]
where the time goes in v13:
time: 43.1 us; the launch traced here: 42.8 us
  starting transfers between devices  20.4 us (47%)
  Pallas kernels  9.1 us (21%)
  waiting for transfers between devices  6.32 us (15%)
  local copies, waits for them, and re-layouts  5.49 us (13%)
  other arithmetic  0.75 us (2%)
  between operations  0.75 us (2%)
    ppermute x7, starting transfers between devices, shards(): arrived[s] = lax.ppermute(packed[s], 'pool', [(i, i ^ s) for i in range(n)])  14.1 us
    all_to_all x1, starting transfers between devices, shards(): lax.all_to_all(terms, 'pool', split_axis=0, concat_axis=0, tiled=True)  6.3 us
    unnamed x18, local copies, waits for them, and re-layouts  5.39 us
    all_to_all x1, waiting for transfers between devices, shards(): lax.all_to_all(terms, 'pool', split_axis=0, concat_axis=0, tiled=True)  4.92 us
    pallas_call x1, Pallas kernels, shards(): call(base_kernel, [jax.ShapeDtypeStruct((rows, columns), F32)] * 2, [SMEM...  2.3 us
    pallas_call x1, Pallas kernels, shards(): call(cache_kernel, [jax.ShapeDtypeStruct(queries.shape, F32)] + [jax.Shap...  1.71 us
    ppermute x1, waiting for transfers between devices, shards(): other_sums = swap(sums)  1.38 us
    pallas_call x1, Pallas kernels, shards(): call(combine_kernel, [jax.ShapeDtypeStruct((rows, columns), BF16), jax.Sh...  1.33 us
  transfers between devices with their start and end apart: 9, of which 2 were waited for; matrix products, arithmetic and copies ran while one was open for 0% of the time, Pallas kernels for 12%

profile of v13, /device:TPU:0, one launch (start us, length us, event | category | flops | bytes accessed | tf_op | source)
XLA Modules:
  0.0 42.8 jit_solution(12961523687435228449)
XLA Ops:
  0.6 0.0 copy-start.8
  0.6 0.7 %pad_add_fusion.small_ref = s32[1,56]{1,0:T(1,128)S(1)} fusion(s32[1,8]{1,0:T(1,128)} %bitcast.9, s32[1,48]{1,0:T(1,128)} %bitcast.10), kind=kLoop, calls=%fused_computation | loop fusion | flops 56 | bytes 448 | tf_op jit(solution)/shard_map/concatenate | solution.py:291
  1.4 0.0 copy-start.2
  1.4 1.0 %copy-done.2 = bf16[48,4096]{1,0:T(8,128)(2,1)S(1)} copy-done((bf16[48,4096]{1,0:T(8,128)(2,1)S(1)}, bf16[48,4096]{1,0:T(8,128)(2,1)}, u32[]{:S(2)}) %copy-start.2) | copy-done | bytes 393240
  2.4 0.0 copy-start.7
  2.4 0.0 copy-start.6
  2.4 0.7 %shard_map.113 = (s32[1,48]{1,0:T(1,128)S(1)}, s32[1,48]{1,0:T(1,128)S(1)}, bf16[48,1024]{1,0:T(8,128)(2,1)S(1)}, bf16[48,1024]{1,0:T(8,128)(2,1)S(1)}, bf16[48,...) custom-call(s32[1]{0:T(128)} %bitcast.me_ref, ...), custom_call_target="tpu_custom_call" | custom-call | tf_op jit(solution)/shard_map/pallas_call | solution.py:292
  3.1 3.0 %collective-permute-start.4 = (bf16[48,1024]{1,0:T(8,128)(2,1)S(1)}, bf16[48,1024]{1,0:T(8,128)(2,1)S(1)}, u32[]{:S(2)}, u32[]{:S(2)}) collective-permute-start(bf16[48,1024]{1,0:T(8,128)(2,1)S(1)} %get-tuple-element.25), channel_id=1, source_target_pairs={{0,2},{2,0},{4,6},{6,4},{8,10},{10,8},{12,14},{14,12},{1,3},{3,1},... | collective-permute-start | bytes 294920 | tf_op jit(solution)/shard_map/ppermute | solution.py:302
  6.1 1.6 %collective-permute-start.5 = (bf16[48,1024]{1,0:T(8,128)(2,1)S(1)}, bf16[48,1024]{1,0:T(8,128)(2,1)S(1)}, u32[]{:S(2)}, u32[]{:S(2)}) collective-permute-start(bf16[48,1024]{1,0:T(8,128)(2,1)S(1)} %get-tuple-element.26), channel_id=1, source_target_pairs={{0,4},{2,6},{4,0},{6,2},{8,12},{10,14},{12,8},{14,10},{1,5},{3,7},... | collective-permute-start | bytes 294920 | tf_op jit(solution)/shard_map/ppermute | solution.py:302
  7.7 2.6 %collective-permute-start = (bf16[48,1024]{1,0:T(8,128)(2,1)S(1)}, bf16[48,1024]{1,0:T(8,128)(2,1)S(1)}, u32[]{:S(2)}, u32[]{:S(2)}) collective-permute-start(bf16[48,1024]{1,0:T(8,128)(2,1)S(1)} %get-tuple-element.21), channel_id=1, source_target_pairs={{0,8},{2,10},{4,12},{6,14},{8,0},{10,2},{12,4},{14,6},{1,9},{3,11}... | collective-permute-start | bytes 294920 | tf_op jit(solution)/shard_map/ppermute | solution.py:302
  10.3 0.4 collective-permute-start.6
  10.7 1.3 %collective-permute-start.1 = (bf16[48,1024]{1,0:T(8,128)(2,1)S(1)}, bf16[48,1024]{1,0:T(8,128)(2,1)S(1)}, u32[]{:S(2)}, u32[]{:S(2)}) collective-permute-start(bf16[48,1024]{1,0:T(8,128)(2,1)S(1)} %get-tuple-element.22), channel_id=1, source_target_pairs={{0,10},{2,8},{4,14},{6,12},{8,2},{10,0},{12,6},{14,4},{1,11},{3,9}... | collective-permute-start | bytes 294920 | tf_op jit(solution)/shard_map/ppermute | solution.py:302
  12.0 0.0 collective-permute-done.4.first_ref.refs_1_
  12.0 3.6 %collective-permute-start.2 = (bf16[48,1024]{1,0:T(8,128)(2,1)S(1)}, bf16[48,1024]{1,0:T(8,128)(2,1)S(1)}, u32[]{:S(2)}, u32[]{:S(2)}) collective-permute-start(bf16[48,1024]{1,0:T(8,128)(2,1)S(1)} %get-tuple-element.23), channel_id=1, source_target_pairs={{0,12},{2,14},{4,8},{6,10},{8,4},{10,6},{12,0},{14,2},{1,13},{3,15... | collective-permute-start | bytes 294920 | tf_op jit(solution)/shard_map/ppermute | solution.py:302
  15.6 0.0 collective-permute-done.5.second_ref.refs_2_
  15.6 1.6 %collective-permute-start.3 = (bf16[48,1024]{1,0:T(8,128)(2,1)S(1)}, bf16[48,1024]{1,0:T(8,128)(2,1)S(1)}, u32[]{:S(2)}, u32[]{:S(2)}) collective-permute-start(bf16[48,1024]{1,0:T(8,128)(2,1)S(1)} %get-tuple-element.24), channel_id=1, source_target_pairs={{0,14},{2,12},{4,10},{6,8},{8,6},{10,4},{12,2},{14,0},{1,15},{3,13... | collective-permute-start | bytes 294920 | tf_op jit(solution)/shard_map/ppermute | solution.py:302
  17.2 0.0 copy-start
  17.2 3.4 %copy-done = bf16[4096,1024]{1,0:T(8,128)(2,1)S(1)} copy-done((bf16[4096,1024]{1,0:T(8,128)(2,1)S(1)}, bf16[4096,1024]{1,0:T(8,128)(2,1)}, u32[]{:S(2)}) %copy-start) | copy-done | bytes 8388632
  20.6 0.0 copy-start.3
  20.6 1.0 %copy-done.3 = bf16[48,4096]{1,0:T(8,128)(2,1)S(1)} copy-done((bf16[48,4096]{1,0:T(8,128)(2,1)S(1)}, bf16[48,4096]{1,0:T(8,128)(2,1)}, u32[]{:S(2)}) %copy-start.3) | copy-done | bytes 393240
  21.6 0.0 copy-start.1
  21.6 0.0 copy-start.4
  21.6 0.0 copy-start.5
  21.6 2.3 %shard_map.114 = (f32[48,512]{1,0:T(8,128)S(1)}, f32[48,512]{1,0:T(8,128)S(1)}) custom-call(s32[1]{0:T(128)} %bitcast.3.core_ref, bf16[48,4096]{1,0:T(8,128)(2,1)S(1)} %copy-done.3, bf16[4096,1024]{1,0:T(8,128)(2,1)S(1)} %copy-done, bf16[48,1024]{1,0:T(8,128)(2,1)S(1)} %collective-permute-done.4.first_ref.refs_1_, ...), custom_call_target="tpu_custom_call" | custom-call | flops 402653184 | bytes 33554432 | tf_op jit(solution)/shard_map/pallas_call | solution.py:305
  23.9 0.2 shard_map.115
  24.2 0.0 collective-permute-done.6.refs_3_
  24.2 0.0 copy-done.1
  24.2 0.7 %shard_map.116.refs_6_ = f32[48,128]{1,0:T(8,128)S(1)} custom-call(bf16[48,1024]{1,0:T(8,128)(2,1)S(1)} %get-tuple-element.29.refs_0_, bf16[48,1024]{1,0:T(8,128)(2,1)S(1)} %collective-permute-done.4.first_ref.refs_1_, bf16[48,1024]{1,0:T(8,128)(2,1)S(1)} %collective-permute-done.5.second_ref.refs_2_, bf16[48,1024]{1,0:T(8,128)(2,1)S(1)} %collective-permute-done.6.refs_3_, ...), custom_call_target="tpu_custom_call" | custom-call | tf_op jit(solution)/shard_map/pallas_call | solution.py:327
  24.9 0.0 collective-permute-done.refs_0_
  24.9 0.0 collective-permute-done.1.refs_1_
  24.9 0.0 collective-permute-done.2.refs_2_
  24.9 0.0 collective-permute-done.3.refs_3_
  24.9 0.7 %shard_map.117.mine_ref = f32[288,128]{1,0:T(8,128)S(1)} custom-call(bf16[48,1024]{1,0:T(8,128)(2,1)S(1)} %collective-permute-done.refs_0_, bf16[48,1024]{1,0:T(8,128)(2,1)S(1)} %collective-permute-done.1.refs_1_, bf16[48,1024]{1,0:T(8,128)(2,1)S(1)} %collective-permute-done.2.refs_2_, bf16[48,1024]{1,0:T(8,128)(2,1)S(1)} %collective-permute-done.3.refs_3_, ...), custom_call_target="tpu_custom_call" | custom-call | tf_op jit(solution)/shard_map/pallas_call | solution.py:332
  25.6 0.0 collective-permute-start.7
  25.6 1.4 %collective-permute-done.7.other_ref = f32[288,128]{1,0:T(8,128)S(1)} collective-permute-done((f32[288,128]{1,0:T(8,128)S(1)}, f32[288,128]{1,0:T(8,128)S(1)}, u32[]{:S(2)}, u32[]{:S(2)}) %collective-permute-start.7) | collective-permute-done | bytes 147488 | tf_op jit(solution)/shard_map/ppermute | solution.py:337
  27.0 0.0 copy-done.7
  27.0 1.0 %shard_map.118._ = bf16[384,128]{1,0:T(8,128)(2,1)} custom-call(f32[288,128]{1,0:T(8,128)S(1)} %shard_map.117.mine_ref, f32[288,128]{1,0:T(8,128)S(1)} %collective-permute-done.7.other_ref, bf16[1,2,64,256]{3,2,1,0:T(8,128)(2,1)S(1)} %copy-done.7, bf16[384,384]{1,0:T(8,128)(2,1)S(1)} %get-tuple-element.32.table_ref), custom_call_target="tpu_custom_call" | custom-call | tf_op jit(solution)/shard_map/pallas_call | solution.py:338
  28.1 6.3 %all-to-all-start = ((bf16[8,48,128]{2,1,0:T(8,128)(2,1)}), bf16[8,48,128]{2,1,0:T(8,128)(2,1)S(1)}, u32[]{:S(2)}, u32[]{:S(2)}) async-start(bf16[8,48,128]{2,1,0:T(8,128)(2,1)} %bitcast.4), calls=%async_computation | async-start | bytes 196608 | tf_op jit(solution)/shard_map/all_to_all | solution.py:351
  34.3 0.0 copy-done.8
  34.4 0.1 copy.12.length_ref
  34.4 0.0 copy-done.6
  34.4 0.0 copy-done.4
  34.4 0.0 copy-done.5
  34.5 1.7 %shard_map.120 = (f32[48,2048]{1,0:T(8,128)S(1)}, f32[48,128]{1,0:T(8,128)S(1)}, f32[48,128]{1,0:T(8,128)S(1)}) custom-call(bf16[48,2048]{1,0:T(8,128)(2,1)S(1)} %copy-done.6, bf16[48,2,32,128]{3,2,1,0:T(8,128)(2,1)S(1)} %copy-done.4, bf16[48,2,32,128]{3,2,1,0:T(8,128)(2,1)S(1)} %copy-done.5, s32[48,1]{1,0:T(8,128)S(1)} %copy.12.length_ref, ...), custom_call_target="tpu_custom_call" | custom-call | tf_op jit(solution)/shard_map/pallas_call | solution.py:352
  36.2 0.4 shard_map.119
  36.5 4.9 %all-to-all-done = bf16[8,48,128]{2,1,0:T(8,128)(2,1)S(1)} async-done(((bf16[8,48,128]{2,1,0:T(8,128)(2,1)}), bf16[8,48,128]{2,1,0:T(8,128)(2,1)S(1)}, u32[]{:S(2)}, u32[]{:S(2)}) %all-to-all-start) | async-done | bytes 98336 | tf_op jit(solution)/shard_map/all_to_all | solution.py:351
  41.5 1.3 %shard_map.121 = (bf16[48,512]{1,0:T(8,128)(2,1)}, bf16[48,2048]{1,0:T(8,128)(2,1)}) custom-call(bf16[384,128]{1,0:T(8,128)(2,1)S(1)} %bitcast.7, bf16[192,384]{1,0:T(8,128)(2,1)S(1)} %get-tuple-element.35.one_hot_ref, f32[48,512]{1,0:T(8,128)S(1)} %get-tuple-element.36.base_ref, bf16[48,2048]{1,0:T(8,128)(2,1)S(1)} %copy-done.6, ...), custom_call_target="tpu_custom_call" | custom-call | tf_op jit(solution)/shard_map/pallas_call | solution.py:357
Async XLA Ops:
  0.6 33.7 %copy-start.8 = (s32[48]{0:T(128)S(1)}, s32[48]{0:T(128)}, u32[]{:S(2)}) copy-start(s32[48]{0:T(128)} %param.18) | copy-start | bytes 580
  1.4 1.0 %copy-start.2 = (bf16[48,4096]{1,0:T(8,128)(2,1)S(1)}, bf16[48,4096]{1,0:T(8,128)(2,1)}, u32[]{:S(2)}) copy-start(bf16[48,4096]{1,0:T(8,128)(2,1)} %hidden_ref.3) | copy-start | bytes 1179652
  2.4 24.6 %copy-start.7 = (bf16[1,2,64,256]{3,2,1,0:T(8,128)(2,1)S(1)}, bf16[1,2,64,256]{3,2,1,0:T(8,128)(2,1)}, u32[]{:S(2)}) copy-start(bf16[1,2,64,256]{3,2,1,0:T(8,128)(2,1)} %up_ref.1) | copy-start | bytes 196612
  2.4 32.1 %copy-start.6 = (bf16[48,2048]{1,0:T(8,128)(2,1)S(1)}, bf16[48,2048]{1,0:T(8,128)(2,1)}, u32[]{:S(2)}) copy-start(bf16[48,2048]{1,0:T(8,128)(2,1)} %query_ref.3) | copy-start | bytes 589828
  3.1 8.9 %collective-permute-start.4 = (bf16[48,1024]{1,0:T(8,128)(2,1)S(1)}, bf16[48,1024]{1,0:T(8,128)(2,1)S(1)}, u32[]{:S(2)}, u32[]{:S(2)}) collective-permute-start(bf16[48,1024]{1,0:T(8,128)(2,1)S(1)} %get-tuple-element.25), channel_id=1, source_target_pairs={{0,2},{2,0},{4,6},{6,4},{8,10},{10,8},{12,14},{14,12},{1,3},{3,1},... | collective-permute-start | bytes 294920 | tf_op jit(solution)/shard_map/ppermute | solution.py:302
  6.1 9.5 %collective-permute-start.5 = (bf16[48,1024]{1,0:T(8,128)(2,1)S(1)}, bf16[48,1024]{1,0:T(8,128)(2,1)S(1)}, u32[]{:S(2)}, u32[]{:S(2)}) collective-permute-start(bf16[48,1024]{1,0:T(8,128)(2,1)S(1)} %get-tuple-element.26), channel_id=1, source_target_pairs={{0,4},{2,6},{4,0},{6,2},{8,12},{10,14},{12,8},{14,10},{1,5},{3,7},... | collective-permute-start | bytes 294920 | tf_op jit(solution)/shard_map/ppermute | solution.py:302
  7.7 17.2 %collective-permute-start = (bf16[48,1024]{1,0:T(8,128)(2,1)S(1)}, bf16[48,1024]{1,0:T(8,128)(2,1)S(1)}, u32[]{:S(2)}, u32[]{:S(2)}) collective-permute-start(bf16[48,1024]{1,0:T(8,128)(2,1)S(1)} %get-tuple-element.21), channel_id=1, source_target_pairs={{0,8},{2,10},{4,12},{6,14},{8,0},{10,2},{12,4},{14,6},{1,9},{3,11}... | collective-permute-start | bytes 294920 | tf_op jit(solution)/shard_map/ppermute | solution.py:302
  10.3 13.9 %collective-permute-start.6 = (bf16[48,1024]{1,0:T(8,128)(2,1)S(1)}, bf16[48,1024]{1,0:T(8,128)(2,1)S(1)}, u32[]{:S(2)}, u32[]{:S(2)}) collective-permute-start(bf16[48,1024]{1,0:T(8,128)(2,1)S(1)} %get-tuple-element.30), channel_id=1, source_target_pairs={{0,6},{2,4},{4,2},{6,0},{8,14},{10,12},{12,10},{14,8},{1,7},{3,5},... | collective-permute-start | bytes 294920 | tf_op jit(solution)/shard_map/ppermute | solution.py:302
  10.7 14.2 %collective-permute-start.1 = (bf16[48,1024]{1,0:T(8,128)(2,1)S(1)}, bf16[48,1024]{1,0:T(8,128)(2,1)S(1)}, u32[]{:S(2)}, u32[]{:S(2)}) collective-permute-start(bf16[48,1024]{1,0:T(8,128)(2,1)S(1)} %get-tuple-element.22), channel_id=1, source_target_pairs={{0,10},{2,8},{4,14},{6,12},{8,2},{10,0},{12,6},{14,4},{1,11},{3,9}... | collective-permute-start | bytes 294920 | tf_op jit(solution)/shard_map/ppermute | solution.py:302
  12.0 12.9 %collective-permute-start.2 = (bf16[48,1024]{1,0:T(8,128)(2,1)S(1)}, bf16[48,1024]{1,0:T(8,128)(2,1)S(1)}, u32[]{:S(2)}, u32[]{:S(2)}) collective-permute-start(bf16[48,1024]{1,0:T(8,128)(2,1)S(1)} %get-tuple-element.23), channel_id=1, source_target_pairs={{0,12},{2,14},{4,8},{6,10},{8,4},{10,6},{12,0},{14,2},{1,13},{3,15... | collective-permute-start | bytes 294920 | tf_op jit(solution)/shard_map/ppermute | solution.py:302
  15.6 9.3 %collective-permute-start.3 = (bf16[48,1024]{1,0:T(8,128)(2,1)S(1)}, bf16[48,1024]{1,0:T(8,128)(2,1)S(1)}, u32[]{:S(2)}, u32[]{:S(2)}) collective-permute-start(bf16[48,1024]{1,0:T(8,128)(2,1)S(1)} %get-tuple-element.24), channel_id=1, source_target_pairs={{0,14},{2,12},{4,10},{6,8},{8,6},{10,4},{12,2},{14,0},{1,15},{3,13... | collective-permute-start | bytes 294920 | tf_op jit(solution)/shard_map/ppermute | solution.py:302
  17.2 3.4 %copy-start = (bf16[4096,1024]{1,0:T(8,128)(2,1)S(1)}, bf16[4096,1024]{1,0:T(8,128)(2,1)}, u32[]{:S(2)}) copy-start(bf16[4096,1024]{1,0:T(8,128)(2,1)} %weight_hbm.1) | copy-start | bytes 25165828
  20.6 1.0 %copy-start.3 = (bf16[48,4096]{1,0:T(8,128)(2,1)S(1)}, bf16[48,4096]{1,0:T(8,128)(2,1)}, u32[]{:S(2)}) copy-start(bf16[48,4096]{1,0:T(8,128)(2,1)} %hidden_ref.3) | copy-start | bytes 1179652
  21.6 2.6 %copy-start.1 = (bf16[1,4096,128]{2,1,0:T(8,128)(2,1)S(1)}, bf16[1,4096,128]{2,1,0:T(8,128)(2,1)}, u32[]{:S(2)}) copy-start(bf16[1,4096,128]{2,1,0:T(8,128)(2,1)} %refs_4_.3) | copy-start | bytes 3145732
  21.6 12.8 %copy-start.4 = (bf16[48,2,32,128]{3,2,1,0:T(8,128)(2,1)S(1)}, bf16[48,2,32,128]{3,2,1,0:T(8,128)(2,1)}, u32[]{:S(2)}) copy-start(bf16[48,2,32,128]{3,2,1,0:T(8,128)(2,1)} %key_ref.1) | copy-start | bytes 2359300
  21.6 12.8 %copy-start.5 = (bf16[48,2,32,128]{3,2,1,0:T(8,128)(2,1)S(1)}, bf16[48,2,32,128]{3,2,1,0:T(8,128)(2,1)}, u32[]{:S(2)}) copy-start(bf16[48,2,32,128]{3,2,1,0:T(8,128)(2,1)} %value_ref.1) | copy-start | bytes 2359300
  25.6 1.4 %collective-permute-start.7 = (f32[288,128]{1,0:T(8,128)S(1)}, f32[288,128]{1,0:T(8,128)S(1)}, u32[]{:S(2)}, u32[]{:S(2)}) collective-permute-start(f32[288,128]{1,0:T(8,128)S(1)} %shard_map.117.mine_ref), channel_id=1, source_target_pairs={{0,1},{1,0},{2,3},{3,2},{4,5},{5,4},{6,7},{7,6},{8,9},{9,8},{10,11... | collective-permute-start | bytes 442376 | tf_op jit(solution)/shard_map/ppermute | solution.py:337
  28.1 13.4 %all-to-all-start = ((bf16[8,48,128]{2,1,0:T(8,128)(2,1)}), bf16[8,48,128]{2,1,0:T(8,128)(2,1)S(1)}, u32[]{:S(2)}, u32[]{:S(2)}) async-start(bf16[8,48,128]{2,1,0:T(8,128)(2,1)} %bitcast.4), calls=%async_computation | async-start | bytes 196608 | tf_op jit(solution)/shard_map/all_to_all | solution.py:351

commit v14 on v12

--- a/solution.py
+++ b/solution.py
@@ -55,10 +55,10 @@
     )
 
 
-def pack_kernel(n, cap, pieces, me_ref, idx_ref, table_ref, hidden_ref, slot_ref, rank_ref, *out_refs):
+def pack_kernel(n, cap, pieces, me_ref, small_ref, hidden_ref, slot_ref, rank_ref, *out_refs):
     rows = hidden_ref.shape[0]
-    named = (iota((n, rows), 0) == idx_ref[...]).astype(F32).astype(BF16)
-    table = jnp.broadcast_to(table_ref[...].astype(F32).astype(BF16), (16, n))
+    named = (iota((n, rows), 0) == small_ref[:, :rows]).astype(F32).astype(BF16)
+    table = jnp.broadcast_to(small_ref[:, rows:].astype(F32).astype(BF16), (16, n))
     slot = dot(table, named)[0:1, :].astype(I32)
     member = (iota((n, rows), 0) == slot).astype(F32)
     before = (iota((rows, rows), 0) < iota((rows, rows), 1)).astype(F32).astype(BF16)
@@ -299,12 +299,13 @@
     swap = functools.partial(lax.ppermute, axis_name="tp", perm=[(0, 1), (1, 0)])
 
     me = lax.axis_index("pool").reshape(1)
+    small = jnp.concatenate([row_adapter_index.reshape(1, rows), adapter_slot_table.reshape(1, n)], axis=1)
     slot, rank, *packed = call(
         functools.partial(pack_kernel, n, cap, pieces),
         [jax.ShapeDtypeStruct((1, rows), I32)] * 2
         + [jax.ShapeDtypeStruct((pieces * cap, width // pieces), BF16)] * n,
-        [SMEM, VMEM, VMEM, VMEM],
-    )(me, row_adapter_index.reshape(1, rows), adapter_slot_table.reshape(1, n), hidden)
+        [SMEM, VMEM, VMEM],
+    )(me, small, hidden)
     half = n // 2
     order = [0, 1, 2, *range(half, n), *range(3, half)]
     arrived = {0: packed[0]}

time: 43.4 us -> 42.9 us (0.988)
  local copies, waits for them, and re-layouts: 6.79 us -> 5.49 us
  other arithmetic: 0 us -> 0.75 us
    unnamed x22 -> x18, local copies, waits for them, and re-layouts: 6.7 us -> 5.39 us
    concatenate x0 -> x1, other arithmetic: none -> 0.75 us  [shards(): jnp.concatenate([row_adapter_index.reshape(1, rows), adapter_slot_table.r...]
  transfers between devices with their start and end apart: 10 -> 10, of which waited for: 3 -> 3; matrix products, arithmetic and copies ran while one was open for 0% -> 0% of each run, Pallas kernels for 12% -> 13%
where the time goes in v14:
time: 42.9 us; the launch traced here: 42.6 us
  starting transfers between devices  20.5 us (48%)
  Pallas kernels  9.06 us (21%)
  waiting for transfers between devices  6.09 us (14%)
  local copies, waits for them, and re-layouts  5.49 us (13%)
  between operations  0.76 us (2%)
  other arithmetic  0.75 us (2%)
    ppermute x7, starting transfers between devices, shards(): arrived[s] = lax.ppermute(packed[s], 'pool', [(i, i ^ s) for i in range(n)])  14.1 us
    all_to_all x1, starting transfers between devices, shards(): lax.all_to_all(terms, 'pool', split_axis=0, concat_axis=0, tiled=True)  6.29 us
    unnamed x18, local copies, waits for them, and re-layouts  5.39 us
    all_to_all x1, waiting for transfers between devices, shards(): lax.all_to_all(terms, 'pool', split_axis=0, concat_axis=0, tiled=True)  3.55 us
    pallas_call x1, Pallas kernels, shards(): call(base_kernel, [jax.ShapeDtypeStruct((rows, columns), F32)] * 2, [SMEM...  2.3 us
    pallas_call x1, Pallas kernels, shards(): call(cache_kernel, [jax.ShapeDtypeStruct(queries.shape, F32)] + [jax.Shap...  1.72 us
    ppermute x1, waiting for transfers between devices, shards(): swap(base_other)  1.29 us
    pallas_call x1, Pallas kernels, shards(): pl.pallas_call(combine_kernel, out_shape=[jax.ShapeDtypeStruct((rows, col...  1.28 us
  transfers between devices with their start and end apart: 10, of which 3 were waited for; matrix products, arithmetic and copies ran while one was open for 0% of the time, Pallas kernels for 13%

profile of v14, /device:TPU:0, one launch (start us, length us, event | category | flops | bytes accessed | tf_op | source)
XLA Modules:
  0.0 42.6 jit_solution(7656094952068596642)
XLA Ops:
  0.6 0.0 copy-start.8
  0.6 0.7 %pad_add_fusion.small_ref = s32[1,56]{1,0:T(1,128)S(1)} fusion(s32[1,8]{1,0:T(1,128)} %bitcast.9, s32[1,48]{1,0:T(1,128)} %bitcast.10), kind=kLoop, calls=%fused_computation | loop fusion | flops 56 | bytes 448 | tf_op jit(solution)/shard_map/concatenate | solution.py:302
  1.4 0.0 copy-start.2
  1.4 1.0 %copy-done.2 = bf16[48,4096]{1,0:T(8,128)(2,1)S(1)} copy-done((bf16[48,4096]{1,0:T(8,128)(2,1)S(1)}, bf16[48,4096]{1,0:T(8,128)(2,1)}, u32[]{:S(2)}) %copy-start.2) | copy-done | bytes 393240
  2.4 0.0 copy-start.7
  2.4 0.0 copy-start.6
  2.4 0.7 %shard_map.113 = (s32[1,48]{1,0:T(1,128)S(1)}, s32[1,48]{1,0:T(1,128)S(1)}, bf16[48,1024]{1,0:T(8,128)(2,1)S(1)}, bf16[48,1024]{1,0:T(8,128)(2,1)S(1)}, bf16[48,...) custom-call(s32[1]{0:T(128)} %bitcast.me_ref, ...), custom_call_target="tpu_custom_call" | custom-call | tf_op jit(solution)/shard_map/pallas_call | solution.py:303
  3.1 3.0 %collective-permute-start.4 = (bf16[48,1024]{1,0:T(8,128)(2,1)S(1)}, bf16[48,1024]{1,0:T(8,128)(2,1)S(1)}, u32[]{:S(2)}, u32[]{:S(2)}) collective-permute-start(bf16[48,1024]{1,0:T(8,128)(2,1)S(1)} %get-tuple-element.26), channel_id=1, source_target_pairs={{0,2},{2,0},{4,6},{6,4},{8,10},{10,8},{12,14},{14,12},{1,3},{3,1},... | collective-permute-start | bytes 294920 | tf_op jit(solution)/shard_map/ppermute | solution.py:313
  6.1 1.6 %collective-permute-start.5 = (bf16[48,1024]{1,0:T(8,128)(2,1)S(1)}, bf16[48,1024]{1,0:T(8,128)(2,1)S(1)}, u32[]{:S(2)}, u32[]{:S(2)}) collective-permute-start(bf16[48,1024]{1,0:T(8,128)(2,1)S(1)} %get-tuple-element.27), channel_id=1, source_target_pairs={{0,4},{2,6},{4,0},{6,2},{8,12},{10,14},{12,8},{14,10},{1,5},{3,7},... | collective-permute-start | bytes 294920 | tf_op jit(solution)/shard_map/ppermute | solution.py:313
  7.7 2.6 %collective-permute-start = (bf16[48,1024]{1,0:T(8,128)(2,1)S(1)}, bf16[48,1024]{1,0:T(8,128)(2,1)S(1)}, u32[]{:S(2)}, u32[]{:S(2)}) collective-permute-start(bf16[48,1024]{1,0:T(8,128)(2,1)S(1)} %get-tuple-element.22), channel_id=1, source_target_pairs={{0,8},{2,10},{4,12},{6,14},{8,0},{10,2},{12,4},{14,6},{1,9},{3,11}... | collective-permute-start | bytes 294920 | tf_op jit(solution)/shard_map/ppermute | solution.py:313
  10.3 0.4 collective-permute-start.6
  10.7 1.3 %collective-permute-start.1 = (bf16[48,1024]{1,0:T(8,128)(2,1)S(1)}, bf16[48,1024]{1,0:T(8,128)(2,1)S(1)}, u32[]{:S(2)}, u32[]{:S(2)}) collective-permute-start(bf16[48,1024]{1,0:T(8,128)(2,1)S(1)} %get-tuple-element.23), channel_id=1, source_target_pairs={{0,10},{2,8},{4,14},{6,12},{8,2},{10,0},{12,6},{14,4},{1,11},{3,9}... | collective-permute-start | bytes 294920 | tf_op jit(solution)/shard_map/ppermute | solution.py:313
  12.0 0.0 collective-permute-done.4.first_ref.refs_1_
  12.0 3.6 %collective-permute-start.2 = (bf16[48,1024]{1,0:T(8,128)(2,1)S(1)}, bf16[48,1024]{1,0:T(8,128)(2,1)S(1)}, u32[]{:S(2)}, u32[]{:S(2)}) collective-permute-start(bf16[48,1024]{1,0:T(8,128)(2,1)S(1)} %get-tuple-element.24), channel_id=1, source_target_pairs={{0,12},{2,14},{4,8},{6,10},{8,4},{10,6},{12,0},{14,2},{1,13},{3,15... | collective-permute-start | bytes 294920 | tf_op jit(solution)/shard_map/ppermute | solution.py:313
  15.6 0.0 collective-permute-done.5.second_ref.refs_2_
  15.6 1.6 %collective-permute-start.3 = (bf16[48,1024]{1,0:T(8,128)(2,1)S(1)}, bf16[48,1024]{1,0:T(8,128)(2,1)S(1)}, u32[]{:S(2)}, u32[]{:S(2)}) collective-permute-start(bf16[48,1024]{1,0:T(8,128)(2,1)S(1)} %get-tuple-element.25), channel_id=1, source_target_pairs={{0,14},{2,12},{4,10},{6,8},{8,6},{10,4},{12,2},{14,0},{1,15},{3,13... | collective-permute-start | bytes 294920 | tf_op jit(solution)/shard_map/ppermute | solution.py:313
  17.2 0.0 copy-start
  17.2 3.4 %copy-done = bf16[4096,1024]{1,0:T(8,128)(2,1)S(1)} copy-done((bf16[4096,1024]{1,0:T(8,128)(2,1)S(1)}, bf16[4096,1024]{1,0:T(8,128)(2,1)}, u32[]{:S(2)}) %copy-start) | copy-done | bytes 8388632
  20.6 1.0 %copy-done.3 = bf16[48,4096]{1,0:T(8,128)(2,1)S(1)} copy-done((bf16[48,4096]{1,0:T(8,128)(2,1)S(1)}, bf16[48,4096]{1,0:T(8,128)(2,1)}, u32[]{:S(2)}) %copy-start.3) | copy-done | bytes 393240
  21.6 0.0 copy-start.1
  21.6 0.0 copy-start.4
  21.6 0.0 copy-start.5
  21.6 2.3 %shard_map.114 = (f32[48,512]{1,0:T(8,128)S(1)}, f32[48,512]{1,0:T(8,128)S(1)}) custom-call(s32[1]{0:T(128)} %bitcast.3.core_ref, bf16[48,4096]{1,0:T(8,128)(2,1)S(1)} %copy-done.3, bf16[4096,1024]{1,0:T(8,128)(2,1)S(1)} %copy-done, bf16[48,1024]{1,0:T(8,128)(2,1)S(1)} %collective-permute-done.4.first_ref.refs_1_, ...), custom_call_target="tpu_custom_call" | custom-call | flops 402653184 | bytes 33554432 | tf_op jit(solution)/shard_map/pallas_call | solution.py:316
  23.9 0.2 shard_map.115
  24.2 0.0 collective-permute-done.6.refs_3_
  24.2 0.0 copy-done.1
  24.2 0.7 %shard_map.116.refs_6_ = f32[48,128]{1,0:T(8,128)S(1)} custom-call(bf16[48,1024]{1,0:T(8,128)(2,1)S(1)} %get-tuple-element.30.refs_0_, bf16[48,1024]{1,0:T(8,128)(2,1)S(1)} %collective-permute-done.4.first_ref.refs_1_, bf16[48,1024]{1,0:T(8,128)(2,1)S(1)} %collective-permute-done.5.second_ref.refs_2_, bf16[48,1024]{1,0:T(8,128)(2,1)S(1)} %collective-permute-done.6.refs_3_, ...), custom_call_target="tpu_custom_call" | custom-call | tf_op jit(solution)/shard_map/pallas_call | solution.py:338
  24.9 0.0 collective-permute-done.refs_0_
  24.9 0.0 collective-permute-done.1.refs_1_
  24.9 0.0 collective-permute-done.2.refs_2_
  24.9 0.0 collective-permute-done.3.refs_3_
  24.9 0.7 %shard_map.117.mine_ref = f32[96,128]{1,0:T(8,128)S(1)} custom-call(bf16[48,1024]{1,0:T(8,128)(2,1)S(1)} %collective-permute-done.refs_0_, bf16[48,1024]{1,0:T(8,128)(2,1)S(1)} %collective-permute-done.1.refs_1_, bf16[48,1024]{1,0:T(8,128)(2,1)S(1)} %collective-permute-done.2.refs_2_, bf16[48,1024]{1,0:T(8,128)(2,1)S(1)} %collective-permute-done.3.refs_3_, ...), custom_call_target="tpu_custom_call" | custom-call | tf_op jit(solution)/shard_map/pallas_call | solution.py:343
  25.6 0.0 collective-permute-start.7
  25.6 1.2 %collective-permute-done.7.other_ref = f32[96,128]{1,0:T(8,128)S(1)} collective-permute-done((f32[96,128]{1,0:T(8,128)S(1)}, f32[96,128]{1,0:T(8,128)S(1)}, u32[]{:S(2)}, u32[]{:S(2)}) %collective-permute-start.7) | collective-permute-done | bytes 49184 | tf_op jit(solution)/shard_map/ppermute | solution.py:352
  26.9 0.0 copy-done.7
  26.9 1.1 %shard_map.118._ = bf16[384,128]{1,0:T(8,128)(2,1)} custom-call(f32[96,128]{1,0:T(8,128)S(1)} %shard_map.117.mine_ref, f32[96,128]{1,0:T(8,128)S(1)} %collective-permute-done.7.other_ref, bf16[1,2,64,256]{3,2,1,0:T(8,128)(2,1)S(1)} %copy-done.7, bf16[384,384]{1,0:T(8,128)(2,1)S(1)} %get-tuple-element.32.table_ref), custom_call_target="tpu_custom_call" | custom-call | tf_op jit(solution)/shard_map/pallas_call | solution.py:348
  27.9 6.3 %all-to-all-start = ((bf16[8,48,128]{2,1,0:T(8,128)(2,1)}), bf16[8,48,128]{2,1,0:T(8,128)(2,1)S(1)}, u32[]{:S(2)}, u32[]{:S(2)}) async-start(bf16[8,48,128]{2,1,0:T(8,128)(2,1)} %bitcast.4), calls=%async_computation | async-start | bytes 196608 | tf_op jit(solution)/shard_map/all_to_all | solution.py:353
  34.2 0.0 copy-done.8
  34.2 0.1 copy.12.length_ref
  34.3 0.0 copy-done.6
  34.3 0.0 copy-done.4
  34.3 0.0 copy-done.5
  34.3 1.7 %shard_map.119 = (f32[48,2048]{1,0:T(8,128)S(1)}, f32[48,128]{1,0:T(8,128)S(1)}, f32[48,128]{1,0:T(8,128)S(1)}, f32[48,512]{1,0:T(8,128)S(1)}) custom-call(bf16[48,2048]{1,0:T(8,128)(2,1)S(1)} %copy-done.6, bf16[48,2,32,128]{3,2,1,0:T(8,128)(2,1)S(1)} %copy-done.4, bf16[48,2,32,128]{3,2,1,0:T(8,128)(2,1)S(1)} %copy-done.5, s32[48,1]{1,0:T(8,128)S(1)} %copy.12.length_ref, ...), custom_call_target="tpu_custom_call" | custom-call | tf_op jit(solution)/shard_map/pallas_call | solution.py:354
  36.0 0.1 collective-permute-start.8
  36.1 1.3 %collective-permute-done.8.other_ref = f32[48,512]{1,0:T(8,128)S(1)} collective-permute-done((f32[48,512]{1,0:T(8,128)S(1)}, f32[48,512]{1,0:T(8,128)S(1)}, u32[]{:S(2)}, u32[]{:S(2)}) %collective-permute-start.8) | collective-permute-done | bytes 98336 | tf_op jit(solution)/shard_map/ppermute | solution.py:375
  37.4 0.4 shard_map.120
  37.8 3.5 %all-to-all-done = bf16[8,48,128]{2,1,0:T(8,128)(2,1)S(1)} async-done(((bf16[8,48,128]{2,1,0:T(8,128)(2,1)}), bf16[8,48,128]{2,1,0:T(8,128)(2,1)S(1)}, u32[]{:S(2)}, u32[]{:S(2)}) %all-to-all-start) | async-done | bytes 98336 | tf_op jit(solution)/shard_map/all_to_all | solution.py:353
  41.3 1.3 %shard_map.121 = (bf16[48,512]{1,0:T(8,128)(2,1)}, bf16[48,2048]{1,0:T(8,128)(2,1)}) custom-call(bf16[384,128]{1,0:T(8,128)(2,1)S(1)} %bitcast.7, bf16[192,384]{1,0:T(8,128)(2,1)S(1)} %get-tuple-element.37.one_hot_ref, f32[48,512]{1,0:T(8,128)S(1)} %get-tuple-element.38.base_ref, bf16[48,2048]{1,0:T(8,128)(2,1)S(1)} %copy-done.6, ...), custom_call_target="tpu_custom_call" | custom-call | tf_op jit(solution)/shard_map/pallas_call | solution.py:376
  (1 shorter events, 0.0 us)
Async XLA Ops:
  0.6 33.6 %copy-start.8 = (s32[48]{0:T(128)S(1)}, s32[48]{0:T(128)}, u32[]{:S(2)}) copy-start(s32[48]{0:T(128)} %param.18) | copy-start | bytes 580
  1.4 1.0 %copy-start.2 = (bf16[48,4096]{1,0:T(8,128)(2,1)S(1)}, bf16[48,4096]{1,0:T(8,128)(2,1)}, u32[]{:S(2)}) copy-start(bf16[48,4096]{1,0:T(8,128)(2,1)} %hidden_ref.3) | copy-start | bytes 1179652
  2.4 24.5 %copy-start.7 = (bf16[1,2,64,256]{3,2,1,0:T(8,128)(2,1)S(1)}, bf16[1,2,64,256]{3,2,1,0:T(8,128)(2,1)}, u32[]{:S(2)}) copy-start(bf16[1,2,64,256]{3,2,1,0:T(8,128)(2,1)} %up_ref.1) | copy-start | bytes 196612
  2.4 31.9 %copy-start.6 = (bf16[48,2048]{1,0:T(8,128)(2,1)S(1)}, bf16[48,2048]{1,0:T(8,128)(2,1)}, u32[]{:S(2)}) copy-start(bf16[48,2048]{1,0:T(8,128)(2,1)} %query_ref.3) | copy-start | bytes 589828
  3.1 8.9 %collective-permute-start.4 = (bf16[48,1024]{1,0:T(8,128)(2,1)S(1)}, bf16[48,1024]{1,0:T(8,128)(2,1)S(1)}, u32[]{:S(2)}, u32[]{:S(2)}) collective-permute-start(bf16[48,1024]{1,0:T(8,128)(2,1)S(1)} %get-tuple-element.26), channel_id=1, source_target_pairs={{0,2},{2,0},{4,6},{6,4},{8,10},{10,8},{12,14},{14,12},{1,3},{3,1},... | collective-permute-start | bytes 294920 | tf_op jit(solution)/shard_map/ppermute | solution.py:313
  6.1 9.5 %collective-permute-start.5 = (bf16[48,1024]{1,0:T(8,128)(2,1)S(1)}, bf16[48,1024]{1,0:T(8,128)(2,1)S(1)}, u32[]{:S(2)}, u32[]{:S(2)}) collective-permute-start(bf16[48,1024]{1,0:T(8,128)(2,1)S(1)} %get-tuple-element.27), channel_id=1, source_target_pairs={{0,4},{2,6},{4,0},{6,2},{8,12},{10,14},{12,8},{14,10},{1,5},{3,7},... | collective-permute-start | bytes 294920 | tf_op jit(solution)/shard_map/ppermute | solution.py:313
  7.7 17.2 %collective-permute-start = (bf16[48,1024]{1,0:T(8,128)(2,1)S(1)}, bf16[48,1024]{1,0:T(8,128)(2,1)S(1)}, u32[]{:S(2)}, u32[]{:S(2)}) collective-permute-start(bf16[48,1024]{1,0:T(8,128)(2,1)S(1)} %get-tuple-element.22), channel_id=1, source_target_pairs={{0,8},{2,10},{4,12},{6,14},{8,0},{10,2},{12,4},{14,6},{1,9},{3,11}... | collective-permute-start | bytes 294920 | tf_op jit(solution)/shard_map/ppermute | solution.py:313
  10.3 13.9 %collective-permute-start.6 = (bf16[48,1024]{1,0:T(8,128)(2,1)S(1)}, bf16[48,1024]{1,0:T(8,128)(2,1)S(1)}, u32[]{:S(2)}, u32[]{:S(2)}) collective-permute-start(bf16[48,1024]{1,0:T(8,128)(2,1)S(1)} %get-tuple-element.31), channel_id=1, source_target_pairs={{0,6},{2,4},{4,2},{6,0},{8,14},{10,12},{12,10},{14,8},{1,7},{3,5},... | collective-permute-start | bytes 294920 | tf_op jit(solution)/shard_map/ppermute | solution.py:313
  10.7 14.2 %collective-permute-start.1 = (bf16[48,1024]{1,0:T(8,128)(2,1)S(1)}, bf16[48,1024]{1,0:T(8,128)(2,1)S(1)}, u32[]{:S(2)}, u32[]{:S(2)}) collective-permute-start(bf16[48,1024]{1,0:T(8,128)(2,1)S(1)} %get-tuple-element.23), channel_id=1, source_target_pairs={{0,10},{2,8},{4,14},{6,12},{8,2},{10,0},{12,6},{14,4},{1,11},{3,9}... | collective-permute-start | bytes 294920 | tf_op jit(solution)/shard_map/ppermute | solution.py:313
  12.0 12.9 %collective-permute-start.2 = (bf16[48,1024]{1,0:T(8,128)(2,1)S(1)}, bf16[48,1024]{1,0:T(8,128)(2,1)S(1)}, u32[]{:S(2)}, u32[]{:S(2)}) collective-permute-start(bf16[48,1024]{1,0:T(8,128)(2,1)S(1)} %get-tuple-element.24), channel_id=1, source_target_pairs={{0,12},{2,14},{4,8},{6,10},{8,4},{10,6},{12,0},{14,2},{1,13},{3,15... | collective-permute-start | bytes 294920 | tf_op jit(solution)/shard_map/ppermute | solution.py:313
  15.6 9.3 %collective-permute-start.3 = (bf16[48,1024]{1,0:T(8,128)(2,1)S(1)}, bf16[48,1024]{1,0:T(8,128)(2,1)S(1)}, u32[]{:S(2)}, u32[]{:S(2)}) collective-permute-start(bf16[48,1024]{1,0:T(8,128)(2,1)S(1)} %get-tuple-element.25), channel_id=1, source_target_pairs={{0,14},{2,12},{4,10},{6,8},{8,6},{10,4},{12,2},{14,0},{1,15},{3,13... | collective-permute-start | bytes 294920 | tf_op jit(solution)/shard_map/ppermute | solution.py:313
  17.2 3.4 %copy-start = (bf16[4096,1024]{1,0:T(8,128)(2,1)S(1)}, bf16[4096,1024]{1,0:T(8,128)(2,1)}, u32[]{:S(2)}) copy-start(bf16[4096,1024]{1,0:T(8,128)(2,1)} %weight_hbm.1) | copy-start | bytes 25165828
  20.6 1.0 %copy-start.3 = (bf16[48,4096]{1,0:T(8,128)(2,1)S(1)}, bf16[48,4096]{1,0:T(8,128)(2,1)}, u32[]{:S(2)}) copy-start(bf16[48,4096]{1,0:T(8,128)(2,1)} %hidden_ref.3) | copy-start | bytes 1179652
  21.6 2.6 %copy-start.1 = (bf16[1,4096,128]{2,1,0:T(8,128)(2,1)S(1)}, bf16[1,4096,128]{2,1,0:T(8,128)(2,1)}, u32[]{:S(2)}) copy-start(bf16[1,4096,128]{2,1,0:T(8,128)(2,1)} %refs_4_.3) | copy-start | bytes 3145732
  21.6 12.7 %copy-start.4 = (bf16[48,2,32,128]{3,2,1,0:T(8,128)(2,1)S(1)}, bf16[48,2,32,128]{3,2,1,0:T(8,128)(2,1)}, u32[]{:S(2)}) copy-start(bf16[48,2,32,128]{3,2,1,0:T(8,128)(2,1)} %key_ref.1) | copy-start | bytes 2359300
  21.6 12.7 %copy-start.5 = (bf16[48,2,32,128]{3,2,1,0:T(8,128)(2,1)S(1)}, bf16[48,2,32,128]{3,2,1,0:T(8,128)(2,1)}, u32[]{:S(2)}) copy-start(bf16[48,2,32,128]{3,2,1,0:T(8,128)(2,1)} %value_ref.1) | copy-start | bytes 2359300
  25.6 1.2 %collective-permute-start.7 = (f32[96,128]{1,0:T(8,128)S(1)}, f32[96,128]{1,0:T(8,128)S(1)}, u32[]{:S(2)}, u32[]{:S(2)}) collective-permute-start(f32[96,128]{1,0:T(8,128)S(1)} %shard_map.117.mine_ref), channel_id=1, source_target_pairs={{0,1},{1,0},{2,3},{3,2},{4,5},{5,4},{6,7},{7,6},{8,9},{9,8},{10,11... | collective-permute-start | bytes 147464 | tf_op jit(solution)/shard_map/ppermute | solution.py:352
  27.9 13.4 %all-to-all-start = ((bf16[8,48,128]{2,1,0:T(8,128)(2,1)}), bf16[8,48,128]{2,1,0:T(8,128)(2,1)S(1)}, u32[]{:S(2)}, u32[]{:S(2)}) async-start(bf16[8,48,128]{2,1,0:T(8,128)(2,1)} %bitcast.4), calls=%async_computation | async-start | bytes 196608 | tf_op jit(solution)/shard_map/all_to_all | solution.py:353
  36.0 1.4 %collective-permute-start.8 = (f32[48,512]{1,0:T(8,128)S(1)}, f32[48,512]{1,0:T(8,128)S(1)}, u32[]{:S(2)}, u32[]{:S(2)}) collective-permute-start(f32[48,512]{1,0:T(8,128)S(1)} %get-tuple-element.36), channel_id=1, source_target_pairs={{0,1},{1,0},{2,3},{3,2},{4,5},{5,4},{6,7},{7,6},{8,9},{9,8},{10,11... | collective-permute-start | bytes 294920 | tf_op jit(solution)/shard_map/ppermute | solution.py:375

commit v15 on v14

--- a/solution.py
+++ b/solution.py
@@ -74,11 +74,12 @@
         out_ref[...] = packed[s * per : (s + 1) * per]
 
 
-def tables_kernel(n, cap, pieces, out_pieces, me_ref, _, shrink_ref, expand_ref):
+def tables_kernel(n, cap, pieces, out_pieces, me_ref, _, shrink_ref, part_ref, expand_ref):
     per = pieces * cap
-    out_row, in_row = iota(shrink_ref.shape, 0), iota(shrink_ref.shape, 1)
-    same = (out_row // cap == in_row // per) & (out_row % cap == in_row % cap)
-    shrink_ref[...] = same.astype(F32).astype(BF16)
+    for ref in (shrink_ref, part_ref):
+        out_row, in_row = iota(ref.shape, 0), iota(ref.shape, 1)
+        same = (out_row // cap == in_row // per) & (out_row % cap == in_row % cap)
+        ref[...] = same.astype(F32).astype(BF16)
     per = out_pieces * cap
     out_row, in_row = iota(expand_ref.shape, 0), iota(expand_ref.shape, 1)
     apart = lax.bitwise_xor(out_row // per, me_ref[0])
@@ -99,15 +100,17 @@
     return select_sum(table_ref[...], total)
 
 
-def shrink_near_kernel(cap, pieces, *refs):
-    refs[-1][...] = shrink(cap, pieces, refs[:-3], *refs[-3:-1])
+def shrink_near_kernel(cap, pieces, count, *refs):
+    refs[-1][...] = shrink(cap, pieces, refs[:count], *refs[count : count + 2])
 
 
 def shrink_far_kernel(cap, pieces, *refs):
-    near_ref, out_ref = refs[-2:]
+    near_ref, part_ref, out_ref = refs[-3:]
     half = near_ref.shape[0]
+    done = half + part_ref.shape[0]
     out_ref[:half, :] = near_ref[...]
-    out_ref[half:, :] = shrink(cap, pieces, refs[:-4], *refs[-4:-2])
+    out_ref[half:done, :] = part_ref[...]
+    out_ref[done:, :] = shrink(cap, pieces, refs[:-5], *refs[-5:-3])
 
 
 def expand_kernel(mine_ref, other_ref, up_ref, table_ref, out_ref):
@@ -327,24 +330,31 @@
     )(lax.axis_index("tp").reshape(1), hidden, key_value_weight, arrived[1], arrived[2])
 
     size = n * out_pieces * cap
-    shrink_table, expand_table = call(
+    shrink_table, part_table, expand_table = call(
         functools.partial(tables_kernel, n, cap, pieces, out_pieces),
         [
             jax.ShapeDtypeStruct((half * cap, half * pieces * cap), BF16),
+            jax.ShapeDtypeStruct((half // 2 * cap, half // 2 * pieces * cap), BF16),
             jax.ShapeDtypeStruct((size, size), BF16),
         ],
         [SMEM, ANY],
     )(me, base_mine)
     (near_sum,) = call(
-        functools.partial(shrink_near_kernel, cap, pieces),
+        functools.partial(shrink_near_kernel, cap, pieces, half),
         [jax.ShapeDtypeStruct((half * cap, rank2), F32)],
         [VMEM] * (half + 2),
     )(*[arrived[s] for s in range(half)], adapter_down_weight, shrink_table)
+    middle = half + half // 2
+    (part_sum,) = call(
+        functools.partial(shrink_near_kernel, cap, pieces, half // 2),
+        [jax.ShapeDtypeStruct((half // 2 * cap, rank2), F32)],
+        [VMEM] * (half // 2 + 2) + [ANY],
+    )(*[arrived[s] for s in range(half, middle)], adapter_down_weight, part_table, near_sum)
     (sums,) = call(
         functools.partial(shrink_far_kernel, cap, pieces),
         [jax.ShapeDtypeStruct((n * cap, rank2), F32)],
-        [VMEM] * (half + 3),
-    )(*[arrived[s] for s in range(half, n)], adapter_down_weight, shrink_table, near_sum)
+        [VMEM] * (half // 2 + 4),
+    )(*[arrived[s] for s in range(middle, n)], adapter_down_weight, part_table, near_sum, part_sum)
     (terms,) = call(
         expand_kernel,
         [jax.ShapeDtypeStruct((size, head), BF16)],

time: 42.9 us -> 45.9 us (1.070)
  Pallas kernels: 9.06 us -> 11.9 us
  starting transfers between devices: 20.5 us -> 18.4 us
  waiting for transfers between devices: 6.09 us -> 8.14 us
    ppermute x7, waiting for transfers between devices: 0.02 us -> 2.06 us  [shards(): arrived[s] = lax.ppermute(packed[s], 'pool', [(i, i ^ s) for i in range(n)])]
    ppermute x7, starting transfers between devices: 14.1 us -> 12.4 us  [shards(): arrived[s] = lax.ppermute(packed[s], 'pool', [(i, i ^ s) for i in range(n)])]
    pallas_call x1 -> x2, Pallas kernels: 0.69 us -> 2.06 us  [the longest x1 1.58 us: shards(): call(functools.partial(shrink_near_kernel, cap, pieces, half), [jax.Shape...]
    pallas_call x1, Pallas kernels: 0.69 us -> 1.43 us  [shards(): call(functools.partial(shrink_far_kernel, cap, pieces), [jax.ShapeDtypeSt...]
    pallas_call x1, Pallas kernels: 0.71 us -> 1.44 us  [shards(): call(functools.partial(pack_kernel, n, cap, pieces), [jax.ShapeDtypeStruc...]
  transfers between devices with their start and end apart: 10 -> 10, of which waited for: 3 -> 4; matrix products, arithmetic and copies ran while one was open for 0% -> 0% of each run, Pallas kernels for 13% -> 15%
where the time goes in v15:
time: 45.9 us; the launch traced here: 45.5 us
  starting transfers between devices  18.4 us (40%)
  Pallas kernels  11.9 us (26%)
  waiting for transfers between devices  8.14 us (18%)
  local copies, waits for them, and re-layouts  5.49 us (12%)
  other arithmetic  0.83 us (2%)
  between operations  0.74 us (2%)
    ppermute x7, starting transfers between devices, shards(): arrived[s] = lax.ppermute(packed[s], 'pool', [(i, i ^ s) for i in range(n)])  12.4 us
    all_to_all x1, starting transfers between devices, shards(): lax.all_to_all(terms, 'pool', split_axis=0, concat_axis=0, tiled=True)  5.93 us
    unnamed x18, local copies, waits for them, and re-layouts  5.4 us
    all_to_all x1, waiting for transfers between devices, shards(): lax.all_to_all(terms, 'pool', split_axis=0, concat_axis=0, tiled=True)  3.55 us
    pallas_call x1, Pallas kernels, shards(): call(base_kernel, [jax.ShapeDtypeStruct((rows, columns), F32)] * 2, [SMEM...  2.31 us
    ppermute x7, waiting for transfers between devices, shards(): arrived[s] = lax.ppermute(packed[s], 'pool', [(i, i ^ s) for i in range(n)])  2.06 us
    pallas_call x1, Pallas kernels, shards(): call(cache_kernel, [jax.ShapeDtypeStruct(queries.shape, F32)] + [jax.Shap...  1.72 us
    pallas_call x1, Pallas kernels, shards(): call(functools.partial(shrink_near_kernel, cap, pieces, half), [jax.Shape...  1.58 us
  transfers between devices with their start and end apart: 10, of which 4 were waited for; matrix products, arithmetic and copies ran while one was open for 0% of the time, Pallas kernels for 15%

profile of v15, /device:TPU:0, one launch (start us, length us, event | category | flops | bytes accessed | tf_op | source)
XLA Modules:
  0.0 45.5 jit_solution(12242607508858465869)
XLA Ops:
  0.6 0.0 copy-start
  0.6 0.8 %pad_add_fusion.small_ref = s32[1,56]{1,0:T(1,128)S(1)} fusion(s32[1,8]{1,0:T(1,128)} %bitcast.9, s32[1,48]{1,0:T(1,128)} %bitcast.10), kind=kLoop, calls=%fused_computation | loop fusion | flops 56 | bytes 448 | tf_op jit(solution)/shard_map/concatenate | solution.py:305
  1.5 0.0 copy-start.2
  1.5 1.0 %copy-done.2 = bf16[48,4096]{1,0:T(8,128)(2,1)S(1)} copy-done((bf16[48,4096]{1,0:T(8,128)(2,1)S(1)}, bf16[48,4096]{1,0:T(8,128)(2,1)}, u32[]{:S(2)}) %copy-start.2) | copy-done | bytes 393240
  2.5 1.4 %shard_map.113 = (s32[1,48]{1,0:T(1,128)S(1)}, s32[1,48]{1,0:T(1,128)S(1)}, bf16[48,1024]{1,0:T(8,128)(2,1)S(1)}, bf16[48,1024]{1,0:T(8,128)(2,1)S(1)}, bf16[48,...) custom-call(s32[1]{0:T(128)} %bitcast.me_ref, ...), custom_call_target="tpu_custom_call" | custom-call | tf_op jit(solution)/shard_map/pallas_call | solution.py:306
  3.9 3.0 %collective-permute-start.2 = (bf16[48,1024]{1,0:T(8,128)(2,1)S(1)}, bf16[48,1024]{1,0:T(8,128)(2,1)S(1)}, u32[]{:S(2)}, u32[]{:S(2)}) collective-permute-start(bf16[48,1024]{1,0:T(8,128)(2,1)S(1)} %get-tuple-element.25), channel_id=1, source_target_pairs={{0,2},{2,0},{4,6},{6,4},{8,10},{10,8},{12,14},{14,12},{1,3},{3,1},... | collective-permute-start | bytes 294920 | tf_op jit(solution)/shard_map/ppermute | solution.py:316
  6.9 1.6 %collective-permute-start.3 = (bf16[48,1024]{1,0:T(8,128)(2,1)S(1)}, bf16[48,1024]{1,0:T(8,128)(2,1)S(1)}, u32[]{:S(2)}, u32[]{:S(2)}) collective-permute-start(bf16[48,1024]{1,0:T(8,128)(2,1)S(1)} %get-tuple-element.26), channel_id=1, source_target_pairs={{0,4},{2,6},{4,0},{6,2},{8,12},{10,14},{12,8},{14,10},{1,5},{3,7},... | collective-permute-start | bytes 294920 | tf_op jit(solution)/shard_map/ppermute | solution.py:316
  8.5 0.0 collective-permute-start.4
  8.5 3.0 %collective-permute-start.5 = (bf16[48,1024]{1,0:T(8,128)(2,1)}, bf16[48,1024]{1,0:T(8,128)(2,1)S(1)}, u32[]{:S(2)}, u32[]{:S(2)}) collective-permute-start(bf16[48,1024]{1,0:T(8,128)(2,1)} %get-tuple-element.32), channel_id=1, source_target_pairs={{0,8},{2,10},{4,12},{6,14},{8,0},{10,2},{12,4},{14,6},{1,9},{3,11}... | collective-permute-start | bytes 294920 | tf_op jit(solution)/shard_map/ppermute | solution.py:316
  11.4 1.3 %collective-permute-start.6 = (bf16[48,1024]{1,0:T(8,128)(2,1)}, bf16[48,1024]{1,0:T(8,128)(2,1)S(1)}, u32[]{:S(2)}, u32[]{:S(2)}) collective-permute-start(bf16[48,1024]{1,0:T(8,128)(2,1)} %get-tuple-element.33), channel_id=1, source_target_pairs={{0,10},{2,8},{4,14},{6,12},{8,2},{10,0},{12,6},{14,4},{1,11},{3,9}... | collective-permute-start | bytes 294920 | tf_op jit(solution)/shard_map/ppermute | solution.py:316
  12.7 0.0 collective-permute-done.2.first_ref.refs_1_
  12.7 3.6 %collective-permute-start = (bf16[48,1024]{1,0:T(8,128)(2,1)}, bf16[48,1024]{1,0:T(8,128)(2,1)}, u32[]{:S(2)}, u32[]{:S(2)}) collective-permute-start(bf16[48,1024]{1,0:T(8,128)(2,1)} %get-tuple-element.23), channel_id=1, source_target_pairs={{0,12},{2,14},{4,8},{6,10},{8,4},{10,6},{12,0},{14,2},{1,13},{3,15... | collective-permute-start | bytes 294920 | tf_op jit(solution)/shard_map/ppermute | solution.py:316
  16.3 0.0 collective-permute-done.3.second_ref.refs_2_
  16.3 0.0 collective-permute-start.1
  16.4 0.0 copy-start.1
  16.4 3.4 %copy-done.1 = bf16[4096,1024]{1,0:T(8,128)(2,1)S(1)} copy-done((bf16[4096,1024]{1,0:T(8,128)(2,1)S(1)}, bf16[4096,1024]{1,0:T(8,128)(2,1)}, u32[]{:S(2)}) %copy-start.1) | copy-done | bytes 8388632
  19.7 0.0 copy-start.3
  19.7 1.0 %copy-done.3 = bf16[48,4096]{1,0:T(8,128)(2,1)S(1)} copy-done((bf16[48,4096]{1,0:T(8,128)(2,1)S(1)}, bf16[48,4096]{1,0:T(8,128)(2,1)}, u32[]{:S(2)}) %copy-start.3) | copy-done | bytes 393240
  20.7 0.0 copy-start.7
  20.7 0.0 copy-start.8
  20.7 0.0 copy-start.6
  20.8 2.3 %shard_map.114 = (f32[48,512]{1,0:T(8,128)S(1)}, f32[48,512]{1,0:T(8,128)S(1)}) custom-call(s32[1]{0:T(128)} %bitcast.3.core_ref, bf16[48,4096]{1,0:T(8,128)(2,1)S(1)} %copy-done.3, bf16[4096,1024]{1,0:T(8,128)(2,1)S(1)} %copy-done.1, bf16[48,1024]{1,0:T(8,128)(2,1)S(1)} %collective-permute-done.2.first_ref.refs_1_, ...), custom_call_target="tpu_custom_call" | custom-call | flops 402653184 | bytes 33554432 | tf_op jit(solution)/shard_map/pallas_call | solution.py:319
  23.1 0.3 shard_map.115
  23.3 0.0 collective-permute-done.4.refs_3_
  23.3 0.0 copy-done
  23.3 1.6 %shard_map.116.refs_4_ = f32[48,128]{1,0:T(8,128)S(1)} custom-call(bf16[48,1024]{1,0:T(8,128)(2,1)S(1)} %get-tuple-element.29.refs_0_, bf16[48,1024]{1,0:T(8,128)(2,1)S(1)} %collective-permute-done.2.first_ref.refs_1_, bf16[48,1024]{1,0:T(8,128)(2,1)S(1)} %collective-permute-done.3.second_ref.refs_2_, bf16[48,1024]{1,0:T(8,128)(2,1)} %collective-permute-done.4.refs_3_, ...), custom_call_target="tpu_custom_call" | custom-call | tf_op jit(solution)/shard_map/pallas_call | solution.py:342
  24.9 0.0 collective-permute-done.5.refs_0_
  24.9 2.0 %collective-permute-done.6.refs_1_ = bf16[48,1024]{1,0:T(8,128)(2,1)S(1)} collective-permute-done((bf16[48,1024]{1,0:T(8,128)(2,1)}, bf16[48,1024]{1,0:T(8,128)(2,1)S(1)}, u32[]{:S(2)}, u32[]{:S(2)}) %collective-permute-start.6) | collective-permute-done | bytes 98336 | tf_op jit(solution)/shard_map/ppermute | solution.py:316
  27.0 0.5 %shard_map.117.refs_5_ = f32[24,128]{1,0:T(8,128)S(1)} custom-call(bf16[48,1024]{1,0:T(8,128)(2,1)S(1)} %collective-permute-done.5.refs_0_, bf16[48,1024]{1,0:T(8,128)(2,1)S(1)} %collective-permute-done.6.refs_1_, bf16[1,4096,128]{2,1,0:T(8,128)(2,1)S(1)} %copy-done, bf16[24,96]{1,0:T(8,128)(2,1)S(1)} %get-tuple-element.28.refs_3_, ...), custom_call_target="tpu_custom_call" | custom-call | tf_op jit(solution)/shard_map/pallas_call | solution.py:348
  27.5 0.0 collective-permute-done.refs_0_
  27.5 0.0 collective-permute-done.1.refs_1_
  27.5 1.4 %shard_map.118.mine_ref = f32[96,128]{1,0:T(8,128)S(1)} custom-call(bf16[48,1024]{1,0:T(8,128)(2,1)} %collective-permute-done.refs_0_, bf16[48,1024]{1,0:T(8,128)(2,1)} %collective-permute-done.1.refs_1_, bf16[1,4096,128]{2,1,0:T(8,128)(2,1)S(1)} %copy-done, bf16[24,96]{1,0:T(8,128)(2,1)S(1)} %get-tuple-element.28.refs_3_, ...), custom_call_target="tpu_custom_call" | custom-call | tf_op jit(solution)/shard_map/pallas_call | solution.py:353
  28.9 0.0 collective-permute-start.7
  28.9 1.2 %collective-permute-done.7.other_ref = f32[96,128]{1,0:T(8,128)S(1)} collective-permute-done((f32[96,128]{1,0:T(8,128)S(1)}, f32[96,128]{1,0:T(8,128)S(1)}, u32[]{:S(2)}, u32[]{:S(2)}) %collective-permute-start.7) | collective-permute-done | bytes 49184 | tf_op jit(solution)/shard_map/ppermute | solution.py:362
  30.1 0.0 copy-done.7
  30.1 1.0 %shard_map.119._ = bf16[384,128]{1,0:T(8,128)(2,1)} custom-call(f32[96,128]{1,0:T(8,128)S(1)} %shard_map.118.mine_ref, f32[96,128]{1,0:T(8,128)S(1)} %collective-permute-done.7.other_ref, bf16[1,2,64,256]{3,2,1,0:T(8,128)(2,1)S(1)} %copy-done.7, bf16[384,384]{1,0:T(8,128)(2,1)S(1)} %get-tuple-element.34.table_ref), custom_call_target="tpu_custom_call" | custom-call | tf_op jit(solution)/shard_map/pallas_call | solution.py:358
  31.2 5.9 %all-to-all-start = ((bf16[8,48,128]{2,1,0:T(8,128)(2,1)}), bf16[8,48,128]{2,1,0:T(8,128)(2,1)S(1)}, u32[]{:S(2)}, u32[]{:S(2)}) async-start(bf16[8,48,128]{2,1,0:T(8,128)(2,1)} %bitcast.4), calls=%async_computation | async-start | bytes 196608 | tf_op jit(solution)/shard_map/all_to_all | solution.py:363
  37.1 0.0 copy-done.8
  37.1 0.1 copy.12.length_ref
  37.2 0.0 copy-done.4
  37.2 0.0 copy-done.5
  37.2 0.0 copy-done.6
  37.2 1.7 %shard_map.120 = (f32[48,2048]{1,0:T(8,128)S(1)}, f32[48,128]{1,0:T(8,128)S(1)}, f32[48,128]{1,0:T(8,128)S(1)}, f32[48,512]{1,0:T(8,128)S(1)}) custom-call(bf16[48,2048]{1,0:T(8,128)(2,1)S(1)} %copy-done.6, bf16[48,2,32,128]{3,2,1,0:T(8,128)(2,1)S(1)} %copy-done.4, bf16[48,2,32,128]{3,2,1,0:T(8,128)(2,1)S(1)} %copy-done.5, s32[48,1]{1,0:T(8,128)S(1)} %copy.12.length_ref, ...), custom_call_target="tpu_custom_call" | custom-call | tf_op jit(solution)/shard_map/pallas_call | solution.py:364
  39.0 0.1 collective-permute-start.8
  39.0 1.3 %collective-permute-done.8.other_ref = f32[48,512]{1,0:T(8,128)S(1)} collective-permute-done((f32[48,512]{1,0:T(8,128)S(1)}, f32[48,512]{1,0:T(8,128)S(1)}, u32[]{:S(2)}, u32[]{:S(2)}) %collective-permute-start.8) | collective-permute-done | bytes 98336 | tf_op jit(solution)/shard_map/ppermute | solution.py:385
  40.3 0.4 shard_map.121
  40.7 3.6 %all-to-all-done = bf16[8,48,128]{2,1,0:T(8,128)(2,1)S(1)} async-done(((bf16[8,48,128]{2,1,0:T(8,128)(2,1)}), bf16[8,48,128]{2,1,0:T(8,128)(2,1)S(1)}, u32[]{:S(2)}, u32[]{:S(2)}) %all-to-all-start) | async-done | bytes 98336 | tf_op jit(solution)/shard_map/all_to_all | solution.py:363
  44.3 1.3 %shard_map.122 = (bf16[48,512]{1,0:T(8,128)(2,1)}, bf16[48,2048]{1,0:T(8,128)(2,1)}) custom-call(bf16[384,128]{1,0:T(8,128)(2,1)S(1)} %bitcast.7, bf16[192,384]{1,0:T(8,128)(2,1)S(1)} %get-tuple-element.39.one_hot_ref, f32[48,512]{1,0:T(8,128)S(1)} %get-tuple-element.40.base_ref, bf16[48,2048]{1,0:T(8,128)(2,1)S(1)} %copy-done.6, ...), custom_call_target="tpu_custom_call" | custom-call | tf_op jit(solution)/shard_map/pallas_call | solution.py:386
  (2 shorter events, 0.0 us)
Async XLA Ops:
  0.6 22.7 %copy-start = (bf16[1,4096,128]{2,1,0:T(8,128)(2,1)S(1)}, bf16[1,4096,128]{2,1,0:T(8,128)(2,1)}, u32[]{:S(2)}) copy-start(bf16[1,4096,128]{2,1,0:T(8,128)(2,1)} %refs_2_.3) | copy-start | bytes 3145732
  1.5 1.0 %copy-start.2 = (bf16[48,4096]{1,0:T(8,128)(2,1)S(1)}, bf16[48,4096]{1,0:T(8,128)(2,1)}, u32[]{:S(2)}) copy-start(bf16[48,4096]{1,0:T(8,128)(2,1)} %hidden_ref.3) | copy-start | bytes 1179652
  3.9 8.8 %collective-permute-start.2 = (bf16[48,1024]{1,0:T(8,128)(2,1)S(1)}, bf16[48,1024]{1,0:T(8,128)(2,1)S(1)}, u32[]{:S(2)}, u32[]{:S(2)}) collective-permute-start(bf16[48,1024]{1,0:T(8,128)(2,1)S(1)} %get-tuple-element.25), channel_id=1, source_target_pairs={{0,2},{2,0},{4,6},{6,4},{8,10},{10,8},{12,14},{14,12},{1,3},{3,1},... | collective-permute-start | bytes 294920 | tf_op jit(solution)/shard_map/ppermute | solution.py:316
  6.9 9.5 %collective-permute-start.3 = (bf16[48,1024]{1,0:T(8,128)(2,1)S(1)}, bf16[48,1024]{1,0:T(8,128)(2,1)S(1)}, u32[]{:S(2)}, u32[]{:S(2)}) collective-permute-start(bf16[48,1024]{1,0:T(8,128)(2,1)S(1)} %get-tuple-element.26), channel_id=1, source_target_pairs={{0,4},{2,6},{4,0},{6,2},{8,12},{10,14},{12,8},{14,10},{1,5},{3,7},... | collective-permute-start | bytes 294920 | tf_op jit(solution)/shard_map/ppermute | solution.py:316
  8.5 14.9 %collective-permute-start.4 = (bf16[48,1024]{1,0:T(8,128)(2,1)}, bf16[48,1024]{1,0:T(8,128)(2,1)}, u32[]{:S(2)}, u32[]{:S(2)}) collective-permute-start(bf16[48,1024]{1,0:T(8,128)(2,1)} %get-tuple-element.30), channel_id=1, source_target_pairs={{0,6},{2,4},{4,2},{6,0},{8,14},{10,12},{12,10},{14,8},{1,7},{3,5},... | collective-permute-start | bytes 294920 | tf_op jit(solution)/shard_map/ppermute | solution.py:316
  8.5 16.5 %collective-permute-start.5 = (bf16[48,1024]{1,0:T(8,128)(2,1)}, bf16[48,1024]{1,0:T(8,128)(2,1)S(1)}, u32[]{:S(2)}, u32[]{:S(2)}) collective-permute-start(bf16[48,1024]{1,0:T(8,128)(2,1)} %get-tuple-element.32), channel_id=1, source_target_pairs={{0,8},{2,10},{4,12},{6,14},{8,0},{10,2},{12,4},{14,6},{1,9},{3,11}... | collective-permute-start | bytes 294920 | tf_op jit(solution)/shard_map/ppermute | solution.py:316
  11.4 15.5 %collective-permute-start.6 = (bf16[48,1024]{1,0:T(8,128)(2,1)}, bf16[48,1024]{1,0:T(8,128)(2,1)S(1)}, u32[]{:S(2)}, u32[]{:S(2)}) collective-permute-start(bf16[48,1024]{1,0:T(8,128)(2,1)} %get-tuple-element.33), channel_id=1, source_target_pairs={{0,10},{2,8},{4,14},{6,12},{8,2},{10,0},{12,6},{14,4},{1,11},{3,9}... | collective-permute-start | bytes 294920 | tf_op jit(solution)/shard_map/ppermute | solution.py:316
  12.7 14.7 %collective-permute-start = (bf16[48,1024]{1,0:T(8,128)(2,1)}, bf16[48,1024]{1,0:T(8,128)(2,1)}, u32[]{:S(2)}, u32[]{:S(2)}) collective-permute-start(bf16[48,1024]{1,0:T(8,128)(2,1)} %get-tuple-element.23), channel_id=1, source_target_pairs={{0,12},{2,14},{4,8},{6,10},{8,4},{10,6},{12,0},{14,2},{1,13},{3,15... | collective-permute-start | bytes 294920 | tf_op jit(solution)/shard_map/ppermute | solution.py:316
  16.3 11.1 %collective-permute-start.1 = (bf16[48,1024]{1,0:T(8,128)(2,1)}, bf16[48,1024]{1,0:T(8,128)(2,1)}, u32[]{:S(2)}, u32[]{:S(2)}) collective-permute-start(bf16[48,1024]{1,0:T(8,128)(2,1)} %get-tuple-element.24), channel_id=1, source_target_pairs={{0,14},{2,12},{4,10},{6,8},{8,6},{10,4},{12,2},{14,0},{1,15},{3,13... | collective-permute-start | bytes 294920 | tf_op jit(solution)/shard_map/ppermute | solution.py:316
  16.4 3.4 %copy-start.1 = (bf16[4096,1024]{1,0:T(8,128)(2,1)S(1)}, bf16[4096,1024]{1,0:T(8,128)(2,1)}, u32[]{:S(2)}) copy-start(bf16[4096,1024]{1,0:T(8,128)(2,1)} %weight_hbm.1) | copy-start | bytes 25165828
  19.7 1.0 %copy-start.3 = (bf16[48,4096]{1,0:T(8,128)(2,1)S(1)}, bf16[48,4096]{1,0:T(8,128)(2,1)}, u32[]{:S(2)}) copy-start(bf16[48,4096]{1,0:T(8,128)(2,1)} %hidden_ref.3) | copy-start | bytes 1179652
  20.7 9.4 %copy-start.7 = (bf16[1,2,64,256]{3,2,1,0:T(8,128)(2,1)S(1)}, bf16[1,2,64,256]{3,2,1,0:T(8,128)(2,1)}, u32[]{:S(2)}) copy-start(bf16[1,2,64,256]{3,2,1,0:T(8,128)(2,1)} %up_ref.1) | copy-start | bytes 196612
  20.7 16.4 %copy-start.8 = (s32[48]{0:T(128)S(1)}, s32[48]{0:T(128)}, u32[]{:S(2)}) copy-start(s32[48]{0:T(128)} %param.18) | copy-start | bytes 580
  20.7 16.5 %copy-start.4 = (bf16[48,2,32,128]{3,2,1,0:T(8,128)(2,1)S(1)}, bf16[48,2,32,128]{3,2,1,0:T(8,128)(2,1)}, u32[]{:S(2)}) copy-start(bf16[48,2,32,128]{3,2,1,0:T(8,128)(2,1)} %key_ref.1) | copy-start | bytes 2359300
  20.7 16.5 %copy-start.5 = (bf16[48,2,32,128]{3,2,1,0:T(8,128)(2,1)S(1)}, bf16[48,2,32,128]{3,2,1,0:T(8,128)(2,1)}, u32[]{:S(2)}) copy-start(bf16[48,2,32,128]{3,2,1,0:T(8,128)(2,1)} %value_ref.1) | copy-start | bytes 2359300
  20.7 16.5 %copy-start.6 = (bf16[48,2048]{1,0:T(8,128)(2,1)S(1)}, bf16[48,2048]{1,0:T(8,128)(2,1)}, u32[]{:S(2)}) copy-start(bf16[48,2048]{1,0:T(8,128)(2,1)} %query_ref.3) | copy-start | bytes 589828
  28.9 1.2 %collective-permute-start.7 = (f32[96,128]{1,0:T(8,128)S(1)}, f32[96,128]{1,0:T(8,128)S(1)}, u32[]{:S(2)}, u32[]{:S(2)}) collective-permute-start(f32[96,128]{1,0:T(8,128)S(1)} %shard_map.118.mine_ref), channel_id=1, source_target_pairs={{0,1},{1,0},{2,3},{3,2},{4,5},{5,4},{6,7},{7,6},{8,9},{9,8},{10,11... | collective-permute-start | bytes 147464 | tf_op jit(solution)/shard_map/ppermute | solution.py:362
  31.2 13.1 %all-to-all-start = ((bf16[8,48,128]{2,1,0:T(8,128)(2,1)}), bf16[8,48,128]{2,1,0:T(8,128)(2,1)S(1)}, u32[]{:S(2)}, u32[]{:S(2)}) async-start(bf16[8,48,128]{2,1,0:T(8,128)(2,1)} %bitcast.4), calls=%async_computation | async-start | bytes 196608 | tf_op jit(solution)/shard_map/all_to_all | solution.py:363
  39.0 1.4 %collective-permute-start.8 = (f32[48,512]{1,0:T(8,128)S(1)}, f32[48,512]{1,0:T(8,128)S(1)}, u32[]{:S(2)}, u32[]{:S(2)}) collective-permute-start(f32[48,512]{1,0:T(8,128)S(1)} %get-tuple-element.38), channel_id=1, source_target_pairs={{0,1},{1,0},{2,3},{3,2},{4,5},{5,4},{6,7},{7,6},{8,9},{9,8},{10,11... | collective-permute-start | bytes 294920 | tf_op jit(solution)/shard_map/ppermute | solution.py:385

commit v16 on v14

--- a/solution.py
+++ b/solution.py
@@ -107,7 +107,9 @@
     near_ref, out_ref = refs[-2:]
     half = near_ref.shape[0]
     out_ref[:half, :] = near_ref[...]
-    out_ref[half:, :] = shrink(cap, pieces, refs[:-4], *refs[-4:-2])
+    count = len(refs) - 4
+    received_refs = refs[count // 2 : count] + refs[: count // 2]
+    out_ref[half:, :] = shrink(cap, pieces, received_refs, *refs[-4:-2])
 
 
 def expand_kernel(mine_ref, other_ref, up_ref, table_ref, out_ref):
@@ -307,7 +309,8 @@
         [SMEM, VMEM, VMEM],
     )(me, small, hidden)
     half = n // 2
-    order = [0, 1, 2, *range(half, n), *range(3, half)]
+    far = [*range(half + half // 2, n), *range(half, half + half // 2)]
+    order = [0, 1, 2, *far, *range(3, half)]
     arrived = {0: packed[0]}
     for s in order[1:]:
         arrived[s] = lax.ppermute(packed[s], "pool", [(i, i ^ s) for i in range(n)])
@@ -344,7 +347,7 @@
         functools.partial(shrink_far_kernel, cap, pieces),
         [jax.ShapeDtypeStruct((n * cap, rank2), F32)],
         [VMEM] * (half + 3),
-    )(*[arrived[s] for s in range(half, n)], adapter_down_weight, shrink_table, near_sum)
+    )(*[arrived[s] for s in far], adapter_down_weight, shrink_table, near_sum)
     (terms,) = call(
         expand_kernel,
         [jax.ShapeDtypeStruct((size, head), BF16)],

time: 42.9 us -> 43.8 us (1.021)
  waiting for transfers between devices: 6.09 us -> 10.3 us
  starting transfers between devices: 20.5 us -> 17.2 us
    ppermute x7, waiting for transfers between devices: 0.02 us -> 4.23 us  [shards(): arrived[s] = lax.ppermute(packed[s], 'pool', [(i, i ^ s) for i in range(n)])]
    ppermute x7, starting transfers between devices: 14.1 us -> 12.4 us  [shards(): arrived[s] = lax.ppermute(packed[s], 'pool', [(i, i ^ s) for i in range(n)])]
    all_to_all x1, starting transfers between devices: 6.29 us -> 4.67 us  [shards(): lax.all_to_all(terms, 'pool', split_axis=0, concat_axis=0, tiled=True)]
  transfers between devices with their start and end apart: 10 -> 10, of which waited for: 3 -> 5; matrix products, arithmetic and copies ran while one was open for 0% -> 0% of each run, Pallas kernels for 13% -> 12%
where the time goes in v16:
time: 43.8 us; the launch traced here: 43.5 us
  starting transfers between devices  17.2 us (39%)
  waiting for transfers between devices  10.3 us (24%)
  Pallas kernels  9.05 us (21%)
  local copies, waits for them, and re-layouts  5.49 us (13%)
  other arithmetic  0.75 us (2%)
  between operations  0.74 us (2%)
    ppermute x7, starting transfers between devices, shards(): arrived[s] = lax.ppermute(packed[s], 'pool', [(i, i ^ s) for i in range(n)])  12.4 us
    unnamed x18, local copies, waits for them, and re-layouts  5.39 us
    all_to_all x1, starting transfers between devices, shards(): lax.all_to_all(terms, 'pool', split_axis=0, concat_axis=0, tiled=True)  4.67 us
    ppermute x7, waiting for transfers between devices, shards(): arrived[s] = lax.ppermute(packed[s], 'pool', [(i, i ^ s) for i in range(n)])  4.23 us
    all_to_all x1, waiting for transfers between devices, shards(): lax.all_to_all(terms, 'pool', split_axis=0, concat_axis=0, tiled=True)  3.55 us
    pallas_call x1, Pallas kernels, shards(): call(base_kernel, [jax.ShapeDtypeStruct((rows, columns), F32)] * 2, [SMEM...  2.3 us
    pallas_call x1, Pallas kernels, shards(): call(cache_kernel, [jax.ShapeDtypeStruct(queries.shape, F32)] + [jax.Shap...  1.72 us
    ppermute x1, waiting for transfers between devices, shards(): swap(base_other)  1.29 us
  transfers between devices with their start and end apart: 10, of which 5 were waited for; matrix products, arithmetic and copies ran while one was open for 0% of the time, Pallas kernels for 12%

profile of v16, /device:TPU:0, one launch (start us, length us, event | category | flops | bytes accessed | tf_op | source)
XLA Modules:
  0.0 43.5 jit_solution(3448061239438251132)
XLA Ops:
  0.6 0.0 copy-start.8
  0.6 0.7 %pad_add_fusion.small_ref = s32[1,56]{1,0:T(1,128)S(1)} fusion(s32[1,8]{1,0:T(1,128)} %bitcast.9, s32[1,48]{1,0:T(1,128)} %bitcast.10), kind=kLoop, calls=%fused_computation | loop fusion | flops 56 | bytes 448 | tf_op jit(solution)/shard_map/concatenate | solution.py:304
  1.4 0.0 copy-start.2
  1.4 1.0 %copy-done.2 = bf16[48,4096]{1,0:T(8,128)(2,1)S(1)} copy-done((bf16[48,4096]{1,0:T(8,128)(2,1)S(1)}, bf16[48,4096]{1,0:T(8,128)(2,1)}, u32[]{:S(2)}) %copy-start.2) | copy-done | bytes 393240
  2.4 0.0 copy-start.7
  2.4 0.0 copy-start.6
  2.4 0.7 %shard_map.113 = (s32[1,48]{1,0:T(1,128)S(1)}, s32[1,48]{1,0:T(1,128)S(1)}, bf16[48,1024]{1,0:T(8,128)(2,1)S(1)}, bf16[48,1024]{1,0:T(8,128)(2,1)S(1)}, bf16[48,...) custom-call(s32[1]{0:T(128)} %bitcast.me_ref, ...), custom_call_target="tpu_custom_call" | custom-call | tf_op jit(solution)/shard_map/pallas_call | solution.py:305
  3.1 3.0 %collective-permute-start.4 = (bf16[48,1024]{1,0:T(8,128)(2,1)S(1)}, bf16[48,1024]{1,0:T(8,128)(2,1)S(1)}, u32[]{:S(2)}, u32[]{:S(2)}) collective-permute-start(bf16[48,1024]{1,0:T(8,128)(2,1)S(1)} %get-tuple-element.26), channel_id=1, source_target_pairs={{0,2},{2,0},{4,6},{6,4},{8,10},{10,8},{12,14},{14,12},{1,3},{3,1},... | collective-permute-start | bytes 294920 | tf_op jit(solution)/shard_map/ppermute | solution.py:316
  6.1 1.6 %collective-permute-start.5 = (bf16[48,1024]{1,0:T(8,128)(2,1)S(1)}, bf16[48,1024]{1,0:T(8,128)(2,1)S(1)}, u32[]{:S(2)}, u32[]{:S(2)}) collective-permute-start(bf16[48,1024]{1,0:T(8,128)(2,1)S(1)} %get-tuple-element.27), channel_id=1, source_target_pairs={{0,4},{2,6},{4,0},{6,2},{8,12},{10,14},{12,8},{14,10},{1,5},{3,7},... | collective-permute-start | bytes 294920 | tf_op jit(solution)/shard_map/ppermute | solution.py:316
  7.7 2.5 %collective-permute-start = (bf16[48,1024]{1,0:T(8,128)(2,1)S(1)}, bf16[48,1024]{1,0:T(8,128)(2,1)S(1)}, u32[]{:S(2)}, u32[]{:S(2)}) collective-permute-start(bf16[48,1024]{1,0:T(8,128)(2,1)S(1)} %get-tuple-element.22), channel_id=1, source_target_pairs={{0,12},{2,14},{4,8},{6,10},{8,4},{10,6},{12,0},{14,2},{1,13},{3,15... | collective-permute-start | bytes 294920 | tf_op jit(solution)/shard_map/ppermute | solution.py:316
  10.2 0.6 %collective-permute-start.6 = (bf16[48,1024]{1,0:T(8,128)(2,1)S(1)}, bf16[48,1024]{1,0:T(8,128)(2,1)S(1)}, u32[]{:S(2)}, u32[]{:S(2)}) collective-permute-start(bf16[48,1024]{1,0:T(8,128)(2,1)S(1)} %get-tuple-element.31), channel_id=1, source_target_pairs={{0,6},{2,4},{4,2},{6,0},{8,14},{10,12},{12,10},{14,8},{1,7},{3,5},... | collective-permute-start | bytes 294920 | tf_op jit(solution)/shard_map/ppermute | solution.py:316
  10.8 1.9 %collective-permute-start.1 = (bf16[48,1024]{1,0:T(8,128)(2,1)S(1)}, bf16[48,1024]{1,0:T(8,128)(2,1)S(1)}, u32[]{:S(2)}, u32[]{:S(2)}) collective-permute-start(bf16[48,1024]{1,0:T(8,128)(2,1)S(1)} %get-tuple-element.23), channel_id=1, source_target_pairs={{0,14},{2,12},{4,10},{6,8},{8,6},{10,4},{12,2},{14,0},{1,15},{3,13... | collective-permute-start | bytes 294920 | tf_op jit(solution)/shard_map/ppermute | solution.py:316
  12.7 0.0 collective-permute-done.4.first_ref.refs_1_
  12.7 1.9 %collective-permute-start.2 = (bf16[48,1024]{1,0:T(8,128)(2,1)S(1)}, bf16[48,1024]{1,0:T(8,128)(2,1)S(1)}, u32[]{:S(2)}, u32[]{:S(2)}) collective-permute-start(bf16[48,1024]{1,0:T(8,128)(2,1)S(1)} %get-tuple-element.24), channel_id=1, source_target_pairs={{0,8},{2,10},{4,12},{6,14},{8,0},{10,2},{12,4},{14,6},{1,9},{3,11}... | collective-permute-start | bytes 294920 | tf_op jit(solution)/shard_map/ppermute | solution.py:316
  14.6 0.0 collective-permute-done.5.second_ref.refs_2_
  14.6 1.0 %collective-permute-start.3 = (bf16[48,1024]{1,0:T(8,128)(2,1)S(1)}, bf16[48,1024]{1,0:T(8,128)(2,1)S(1)}, u32[]{:S(2)}, u32[]{:S(2)}) collective-permute-start(bf16[48,1024]{1,0:T(8,128)(2,1)S(1)} %get-tuple-element.25), channel_id=1, source_target_pairs={{0,10},{2,8},{4,14},{6,12},{8,2},{10,0},{12,6},{14,4},{1,11},{3,9}... | collective-permute-start | bytes 294920 | tf_op jit(solution)/shard_map/ppermute | solution.py:316
  15.6 0.0 copy-start
  15.6 3.4 %copy-done = bf16[4096,1024]{1,0:T(8,128)(2,1)S(1)} copy-done((bf16[4096,1024]{1,0:T(8,128)(2,1)S(1)}, bf16[4096,1024]{1,0:T(8,128)(2,1)}, u32[]{:S(2)}) %copy-start) | copy-done | bytes 8388632
  18.9 0.0 copy-start.3
  18.9 1.0 %copy-done.3 = bf16[48,4096]{1,0:T(8,128)(2,1)S(1)} copy-done((bf16[48,4096]{1,0:T(8,128)(2,1)S(1)}, bf16[48,4096]{1,0:T(8,128)(2,1)}, u32[]{:S(2)}) %copy-start.3) | copy-done | bytes 393240
  19.9 0.0 copy-start.1
  19.9 0.0 copy-start.4
  19.9 2.3 %shard_map.114 = (f32[48,512]{1,0:T(8,128)S(1)}, f32[48,512]{1,0:T(8,128)S(1)}) custom-call(s32[1]{0:T(128)} %bitcast.3.core_ref, bf16[48,4096]{1,0:T(8,128)(2,1)S(1)} %copy-done.3, bf16[4096,1024]{1,0:T(8,128)(2,1)S(1)} %copy-done, bf16[48,1024]{1,0:T(8,128)(2,1)S(1)} %collective-permute-done.4.first_ref.refs_1_, ...), custom_call_target="tpu_custom_call" | custom-call | flops 402653184 | bytes 33554432 | tf_op jit(solution)/shard_map/pallas_call | solution.py:319
  22.3 0.2 shard_map.115
  22.5 0.0 collective-permute-done.6.refs_3_
  22.5 0.0 copy-done.1
  22.5 0.7 %shard_map.116.refs_6_ = f32[48,128]{1,0:T(8,128)S(1)} custom-call(bf16[48,1024]{1,0:T(8,128)(2,1)S(1)} %get-tuple-element.30.refs_0_, bf16[48,1024]{1,0:T(8,128)(2,1)S(1)} %collective-permute-done.4.first_ref.refs_1_, bf16[48,1024]{1,0:T(8,128)(2,1)S(1)} %collective-permute-done.5.second_ref.refs_2_, bf16[48,1024]{1,0:T(8,128)(2,1)S(1)} %collective-permute-done.6.refs_3_, ...), custom_call_target="tpu_custom_call" | custom-call | tf_op jit(solution)/shard_map/pallas_call | solution.py:341
  23.2 0.0 collective-permute-done.refs_0_
  23.2 0.0 collective-permute-done.1.refs_1_
  23.2 3.1 %collective-permute-done.2.refs_2_ = bf16[48,1024]{1,0:T(8,128)(2,1)S(1)} collective-permute-done((bf16[48,1024]{1,0:T(8,128)(2,1)S(1)}, bf16[48,1024]{1,0:T(8,128)(2,1)S(1)}, u32[]{:S(2)}, u32[]{:S(2)}) %collective-permute-start.2) | collective-permute-done | bytes 98336 | tf_op jit(solution)/shard_map/ppermute | solution.py:316
  26.3 1.1 %collective-permute-done.3.refs_3_ = bf16[48,1024]{1,0:T(8,128)(2,1)S(1)} collective-permute-done((bf16[48,1024]{1,0:T(8,128)(2,1)S(1)}, bf16[48,1024]{1,0:T(8,128)(2,1)S(1)}, u32[]{:S(2)}, u32[]{:S(2)}) %collective-permute-start.3) | collective-permute-done | bytes 98336 | tf_op jit(solution)/shard_map/ppermute | solution.py:316
  27.5 0.7 %shard_map.117.mine_ref = f32[96,128]{1,0:T(8,128)S(1)} custom-call(bf16[48,1024]{1,0:T(8,128)(2,1)S(1)} %collective-permute-done.refs_0_, bf16[48,1024]{1,0:T(8,128)(2,1)S(1)} %collective-permute-done.1.refs_1_, bf16[48,1024]{1,0:T(8,128)(2,1)S(1)} %collective-permute-done.2.refs_2_, bf16[48,1024]{1,0:T(8,128)(2,1)S(1)} %collective-permute-done.3.refs_3_, ...), custom_call_target="tpu_custom_call" | custom-call | tf_op jit(solution)/shard_map/pallas_call | solution.py:346
  28.1 0.0 collective-permute-start.7
  28.1 1.2 %collective-permute-done.7.other_ref = f32[96,128]{1,0:T(8,128)S(1)} collective-permute-done((f32[96,128]{1,0:T(8,128)S(1)}, f32[96,128]{1,0:T(8,128)S(1)}, u32[]{:S(2)}, u32[]{:S(2)}) %collective-permute-start.7) | collective-permute-done | bytes 49184 | tf_op jit(solution)/shard_map/ppermute | solution.py:355
  29.4 0.0 copy-done.7
  29.4 1.0 %shard_map.118._ = bf16[384,128]{1,0:T(8,128)(2,1)} custom-call(f32[96,128]{1,0:T(8,128)S(1)} %shard_map.117.mine_ref, f32[96,128]{1,0:T(8,128)S(1)} %collective-permute-done.7.other_ref, bf16[1,2,64,256]{3,2,1,0:T(8,128)(2,1)S(1)} %copy-done.7, bf16[384,384]{1,0:T(8,128)(2,1)S(1)} %get-tuple-element.32.table_ref), custom_call_target="tpu_custom_call" | custom-call | tf_op jit(solution)/shard_map/pallas_call | solution.py:351
  30.4 4.7 %all-to-all-start = ((bf16[8,48,128]{2,1,0:T(8,128)(2,1)}), bf16[8,48,128]{2,1,0:T(8,128)(2,1)S(1)}, u32[]{:S(2)}, u32[]{:S(2)}) async-start(bf16[8,48,128]{2,1,0:T(8,128)(2,1)} %bitcast.4), calls=%async_computation | async-start | bytes 196608 | tf_op jit(solution)/shard_map/all_to_all | solution.py:356
  35.1 0.0 copy-done.8
  35.1 0.1 copy.12.length_ref
  35.2 0.0 copy-done.6
  35.2 0.0 copy-done.4
  35.2 0.0 copy-done.5
  35.2 1.7 %shard_map.119 = (f32[48,2048]{1,0:T(8,128)S(1)}, f32[48,128]{1,0:T(8,128)S(1)}, f32[48,128]{1,0:T(8,128)S(1)}, f32[48,512]{1,0:T(8,128)S(1)}) custom-call(bf16[48,2048]{1,0:T(8,128)(2,1)S(1)} %copy-done.6, bf16[48,2,32,128]{3,2,1,0:T(8,128)(2,1)S(1)} %copy-done.4, bf16[48,2,32,128]{3,2,1,0:T(8,128)(2,1)S(1)} %copy-done.5, s32[48,1]{1,0:T(8,128)S(1)} %copy.12.length_ref, ...), custom_call_target="tpu_custom_call" | custom-call | tf_op jit(solution)/shard_map/pallas_call | solution.py:357
  36.9 0.1 collective-permute-start.8
  37.0 1.3 %collective-permute-done.8.other_ref = f32[48,512]{1,0:T(8,128)S(1)} collective-permute-done((f32[48,512]{1,0:T(8,128)S(1)}, f32[48,512]{1,0:T(8,128)S(1)}, u32[]{:S(2)}, u32[]{:S(2)}) %collective-permute-start.8) | collective-permute-done | bytes 98336 | tf_op jit(solution)/shard_map/ppermute | solution.py:378
  38.3 0.4 shard_map.120
  38.7 3.6 %all-to-all-done = bf16[8,48,128]{2,1,0:T(8,128)(2,1)S(1)} async-done(((bf16[8,48,128]{2,1,0:T(8,128)(2,1)}), bf16[8,48,128]{2,1,0:T(8,128)(2,1)S(1)}, u32[]{:S(2)}, u32[]{:S(2)}) %all-to-all-start) | async-done | bytes 98336 | tf_op jit(solution)/shard_map/all_to_all | solution.py:356
  42.2 1.3 %shard_map.121 = (bf16[48,512]{1,0:T(8,128)(2,1)}, bf16[48,2048]{1,0:T(8,128)(2,1)}) custom-call(bf16[384,128]{1,0:T(8,128)(2,1)S(1)} %bitcast.7, bf16[192,384]{1,0:T(8,128)(2,1)S(1)} %get-tuple-element.37.one_hot_ref, f32[48,512]{1,0:T(8,128)S(1)} %get-tuple-element.38.base_ref, bf16[48,2048]{1,0:T(8,128)(2,1)S(1)} %copy-done.6, ...), custom_call_target="tpu_custom_call" | custom-call | tf_op jit(solution)/shard_map/pallas_call | solution.py:379
  (1 shorter events, 0.0 us)
Async XLA Ops:
  0.6 34.5 %copy-start.8 = (s32[48]{0:T(128)S(1)}, s32[48]{0:T(128)}, u32[]{:S(2)}) copy-start(s32[48]{0:T(128)} %param.18) | copy-start | bytes 580
  1.4 1.0 %copy-start.2 = (bf16[48,4096]{1,0:T(8,128)(2,1)S(1)}, bf16[48,4096]{1,0:T(8,128)(2,1)}, u32[]{:S(2)}) copy-start(bf16[48,4096]{1,0:T(8,128)(2,1)} %hidden_ref.3) | copy-start | bytes 1179652
  2.4 27.0 %copy-start.7 = (bf16[1,2,64,256]{3,2,1,0:T(8,128)(2,1)S(1)}, bf16[1,2,64,256]{3,2,1,0:T(8,128)(2,1)}, u32[]{:S(2)}) copy-start(bf16[1,2,64,256]{3,2,1,0:T(8,128)(2,1)} %up_ref.1) | copy-start | bytes 196612
  2.4 32.8 %copy-start.6 = (bf16[48,2048]{1,0:T(8,128)(2,1)S(1)}, bf16[48,2048]{1,0:T(8,128)(2,1)}, u32[]{:S(2)}) copy-start(bf16[48,2048]{1,0:T(8,128)(2,1)} %query_ref.3) | copy-start | bytes 589828
  3.1 9.6 %collective-permute-start.4 = (bf16[48,1024]{1,0:T(8,128)(2,1)S(1)}, bf16[48,1024]{1,0:T(8,128)(2,1)S(1)}, u32[]{:S(2)}, u32[]{:S(2)}) collective-permute-start(bf16[48,1024]{1,0:T(8,128)(2,1)S(1)} %get-tuple-element.26), channel_id=1, source_target_pairs={{0,2},{2,0},{4,6},{6,4},{8,10},{10,8},{12,14},{14,12},{1,3},{3,1},... | collective-permute-start | bytes 294920 | tf_op jit(solution)/shard_map/ppermute | solution.py:316
  6.1 8.4 %collective-permute-start.5 = (bf16[48,1024]{1,0:T(8,128)(2,1)S(1)}, bf16[48,1024]{1,0:T(8,128)(2,1)S(1)}, u32[]{:S(2)}, u32[]{:S(2)}) collective-permute-start(bf16[48,1024]{1,0:T(8,128)(2,1)S(1)} %get-tuple-element.27), channel_id=1, source_target_pairs={{0,4},{2,6},{4,0},{6,2},{8,12},{10,14},{12,8},{14,10},{1,5},{3,7},... | collective-permute-start | bytes 294920 | tf_op jit(solution)/shard_map/ppermute | solution.py:316
  7.7 15.5 %collective-permute-start = (bf16[48,1024]{1,0:T(8,128)(2,1)S(1)}, bf16[48,1024]{1,0:T(8,128)(2,1)S(1)}, u32[]{:S(2)}, u32[]{:S(2)}) collective-permute-start(bf16[48,1024]{1,0:T(8,128)(2,1)S(1)} %get-tuple-element.22), channel_id=1, source_target_pairs={{0,12},{2,14},{4,8},{6,10},{8,4},{10,6},{12,0},{14,2},{1,13},{3,15... | collective-permute-start | bytes 294920 | tf_op jit(solution)/shard_map/ppermute | solution.py:316
  10.2 12.3 %collective-permute-start.6 = (bf16[48,1024]{1,0:T(8,128)(2,1)S(1)}, bf16[48,1024]{1,0:T(8,128)(2,1)S(1)}, u32[]{:S(2)}, u32[]{:S(2)}) collective-permute-start(bf16[48,1024]{1,0:T(8,128)(2,1)S(1)} %get-tuple-element.31), channel_id=1, source_target_pairs={{0,6},{2,4},{4,2},{6,0},{8,14},{10,12},{12,10},{14,8},{1,7},{3,5},... | collective-permute-start | bytes 294920 | tf_op jit(solution)/shard_map/ppermute | solution.py:316
  10.8 12.4 %collective-permute-start.1 = (bf16[48,1024]{1,0:T(8,128)(2,1)S(1)}, bf16[48,1024]{1,0:T(8,128)(2,1)S(1)}, u32[]{:S(2)}, u32[]{:S(2)}) collective-permute-start(bf16[48,1024]{1,0:T(8,128)(2,1)S(1)} %get-tuple-element.23), channel_id=1, source_target_pairs={{0,14},{2,12},{4,10},{6,8},{8,6},{10,4},{12,2},{14,0},{1,15},{3,13... | collective-permute-start | bytes 294920 | tf_op jit(solution)/shard_map/ppermute | solution.py:316
  12.7 13.6 %collective-permute-start.2 = (bf16[48,1024]{1,0:T(8,128)(2,1)S(1)}, bf16[48,1024]{1,0:T(8,128)(2,1)S(1)}, u32[]{:S(2)}, u32[]{:S(2)}) collective-permute-start(bf16[48,1024]{1,0:T(8,128)(2,1)S(1)} %get-tuple-element.24), channel_id=1, source_target_pairs={{0,8},{2,10},{4,12},{6,14},{8,0},{10,2},{12,4},{14,6},{1,9},{3,11}... | collective-permute-start | bytes 294920 | tf_op jit(solution)/shard_map/ppermute | solution.py:316
  14.6 12.9 %collective-permute-start.3 = (bf16[48,1024]{1,0:T(8,128)(2,1)S(1)}, bf16[48,1024]{1,0:T(8,128)(2,1)S(1)}, u32[]{:S(2)}, u32[]{:S(2)}) collective-permute-start(bf16[48,1024]{1,0:T(8,128)(2,1)S(1)} %get-tuple-element.25), channel_id=1, source_target_pairs={{0,10},{2,8},{4,14},{6,12},{8,2},{10,0},{12,6},{14,4},{1,11},{3,9}... | collective-permute-start | bytes 294920 | tf_op jit(solution)/shard_map/ppermute | solution.py:316
  15.6 3.4 %copy-start = (bf16[4096,1024]{1,0:T(8,128)(2,1)S(1)}, bf16[4096,1024]{1,0:T(8,128)(2,1)}, u32[]{:S(2)}) copy-start(bf16[4096,1024]{1,0:T(8,128)(2,1)} %weight_hbm.1) | copy-start | bytes 25165828
  18.9 1.0 %copy-start.3 = (bf16[48,4096]{1,0:T(8,128)(2,1)S(1)}, bf16[48,4096]{1,0:T(8,128)(2,1)}, u32[]{:S(2)}) copy-start(bf16[48,4096]{1,0:T(8,128)(2,1)} %hidden_ref.3) | copy-start | bytes 1179652
  19.9 2.6 %copy-start.1 = (bf16[1,4096,128]{2,1,0:T(8,128)(2,1)S(1)}, bf16[1,4096,128]{2,1,0:T(8,128)(2,1)}, u32[]{:S(2)}) copy-start(bf16[1,4096,128]{2,1,0:T(8,128)(2,1)} %refs_4_.3) | copy-start | bytes 3145732
  19.9 15.3 %copy-start.4 = (bf16[48,2,32,128]{3,2,1,0:T(8,128)(2,1)S(1)}, bf16[48,2,32,128]{3,2,1,0:T(8,128)(2,1)}, u32[]{:S(2)}) copy-start(bf16[48,2,32,128]{3,2,1,0:T(8,128)(2,1)} %key_ref.1) | copy-start | bytes 2359300
  19.9 15.3 %copy-start.5 = (bf16[48,2,32,128]{3,2,1,0:T(8,128)(2,1)S(1)}, bf16[48,2,32,128]{3,2,1,0:T(8,128)(2,1)}, u32[]{:S(2)}) copy-start(bf16[48,2,32,128]{3,2,1,0:T(8,128)(2,1)} %value_ref.1) | copy-start | bytes 2359300
  28.1 1.2 %collective-permute-start.7 = (f32[96,128]{1,0:T(8,128)S(1)}, f32[96,128]{1,0:T(8,128)S(1)}, u32[]{:S(2)}, u32[]{:S(2)}) collective-permute-start(f32[96,128]{1,0:T(8,128)S(1)} %shard_map.117.mine_ref), channel_id=1, source_target_pairs={{0,1},{1,0},{2,3},{3,2},{4,5},{5,4},{6,7},{7,6},{8,9},{9,8},{10,11... | collective-permute-start | bytes 147464 | tf_op jit(solution)/shard_map/ppermute | solution.py:355
  30.4 11.8 %all-to-all-start = ((bf16[8,48,128]{2,1,0:T(8,128)(2,1)}), bf16[8,48,128]{2,1,0:T(8,128)(2,1)S(1)}, u32[]{:S(2)}, u32[]{:S(2)}) async-start(bf16[8,48,128]{2,1,0:T(8,128)(2,1)} %bitcast.4), calls=%async_computation | async-start | bytes 196608 | tf_op jit(solution)/shard_map/all_to_all | solution.py:356
  36.9 1.4 %collective-permute-start.8 = (f32[48,512]{1,0:T(8,128)S(1)}, f32[48,512]{1,0:T(8,128)S(1)}, u32[]{:S(2)}, u32[]{:S(2)}) collective-permute-start(f32[48,512]{1,0:T(8,128)S(1)} %get-tuple-element.36), channel_id=1, source_target_pairs={{0,1},{1,0},{2,3},{3,2},{4,5},{5,4},{6,7},{7,6},{8,9},{9,8},{10,11... | collective-permute-start | bytes 294920 | tf_op jit(solution)/shard_map/ppermute | solution.py:378

commit v17 on v16

--- a/solution.py
+++ b/solution.py
@@ -108,7 +108,7 @@
     half = near_ref.shape[0]
     out_ref[:half, :] = near_ref[...]
     count = len(refs) - 4
-    received_refs = refs[count // 2 : count] + refs[: count // 2]
+    received_refs = refs[0:count:2] + refs[1:count:2]
     out_ref[half:, :] = shrink(cap, pieces, received_refs, *refs[-4:-2])
 
 
@@ -309,7 +309,7 @@
         [SMEM, VMEM, VMEM],
     )(me, small, hidden)
     half = n // 2
-    far = [*range(half + half // 2, n), *range(half, half + half // 2)]
+    far = [s for i in range(half // 2) for s in (half + i, half + half // 2 + i)]
     order = [0, 1, 2, *far, *range(3, half)]
     arrived = {0: packed[0]}
     for s in order[1:]:

time: 43.8 us -> 42.9 us (0.979)
  waiting for transfers between devices: 10.3 us -> 8.09 us
  starting transfers between devices: 17.2 us -> 18.4 us
    ppermute x7, waiting for transfers between devices: 4.23 us -> 2.01 us  [shards(): arrived[s] = lax.ppermute(packed[s], 'pool', [(i, i ^ s) for i in range(n)])]
    ppermute x7, starting transfers between devices: 12.4 us -> 13.5 us  [shards(): arrived[s] = lax.ppermute(packed[s], 'pool', [(i, i ^ s) for i in range(n)])]
  transfers between devices with their start and end apart: 10 -> 10, of which waited for: 5 -> 4; matrix products, arithmetic and copies ran while one was open for 0% -> 0% of each run, Pallas kernels for 12% -> 13%
where the time goes in v17:
time: 42.9 us; the launch traced here: 42.5 us
  starting transfers between devices  18.4 us (43%)
  Pallas kernels  9.06 us (21%)
  waiting for transfers between devices  8.09 us (19%)
  local copies, waits for them, and re-layouts  5.49 us (13%)
  other arithmetic  0.75 us (2%)
  between operations  0.74 us (2%)
    ppermute x7, starting transfers between devices, shards(): arrived[s] = lax.ppermute(packed[s], 'pool', [(i, i ^ s) for i in range(n)])  13.5 us
    unnamed x18, local copies, waits for them, and re-layouts  5.39 us
    all_to_all x1, starting transfers between devices, shards(): lax.all_to_all(terms, 'pool', split_axis=0, concat_axis=0, tiled=True)  4.88 us
    all_to_all x1, waiting for transfers between devices, shards(): lax.all_to_all(terms, 'pool', split_axis=0, concat_axis=0, tiled=True)  3.55 us
    pallas_call x1, Pallas kernels, shards(): call(base_kernel, [jax.ShapeDtypeStruct((rows, columns), F32)] * 2, [SMEM...  2.3 us
    ppermute x7, waiting for transfers between devices, shards(): arrived[s] = lax.ppermute(packed[s], 'pool', [(i, i ^ s) for i in range(n)])  2.01 us
    pallas_call x1, Pallas kernels, shards(): call(cache_kernel, [jax.ShapeDtypeStruct(queries.shape, F32)] + [jax.Shap...  1.72 us
    ppermute x1, waiting for transfers between devices, shards(): swap(base_other)  1.29 us
  transfers between devices with their start and end apart: 10, of which 4 were waited for; matrix products, arithmetic and copies ran while one was open for 0% of the time, Pallas kernels for 13%

profile of v17, /device:TPU:0, one launch (start us, length us, event | category | flops | bytes accessed | tf_op | source)
XLA Modules:
  0.0 42.5 jit_solution(8437832850967423232)
XLA Ops:
  0.6 0.0 copy-start.8
  0.6 0.7 %pad_add_fusion.small_ref = s32[1,56]{1,0:T(1,128)S(1)} fusion(s32[1,8]{1,0:T(1,128)} %bitcast.9, s32[1,48]{1,0:T(1,128)} %bitcast.10), kind=kLoop, calls=%fused_computation | loop fusion | flops 56 | bytes 448 | tf_op jit(solution)/shard_map/concatenate | solution.py:304
  1.4 0.0 copy-start.2
  1.4 1.0 %copy-done.2 = bf16[48,4096]{1,0:T(8,128)(2,1)S(1)} copy-done((bf16[48,4096]{1,0:T(8,128)(2,1)S(1)}, bf16[48,4096]{1,0:T(8,128)(2,1)}, u32[]{:S(2)}) %copy-start.2) | copy-done | bytes 393240
  2.4 0.0 copy-start.7
  2.4 0.0 copy-start.6
  2.4 0.7 %shard_map.113 = (s32[1,48]{1,0:T(1,128)S(1)}, s32[1,48]{1,0:T(1,128)S(1)}, bf16[48,1024]{1,0:T(8,128)(2,1)S(1)}, bf16[48,1024]{1,0:T(8,128)(2,1)S(1)}, bf16[48,...) custom-call(s32[1]{0:T(128)} %bitcast.me_ref, ...), custom_call_target="tpu_custom_call" | custom-call | tf_op jit(solution)/shard_map/pallas_call | solution.py:305
  3.1 3.0 %collective-permute-start.4 = (bf16[48,1024]{1,0:T(8,128)(2,1)S(1)}, bf16[48,1024]{1,0:T(8,128)(2,1)S(1)}, u32[]{:S(2)}, u32[]{:S(2)}) collective-permute-start(bf16[48,1024]{1,0:T(8,128)(2,1)S(1)} %get-tuple-element.26), channel_id=1, source_target_pairs={{0,2},{2,0},{4,6},{6,4},{8,10},{10,8},{12,14},{14,12},{1,3},{3,1},... | collective-permute-start | bytes 294920 | tf_op jit(solution)/shard_map/ppermute | solution.py:316
  6.1 1.6 %collective-permute-start.5 = (bf16[48,1024]{1,0:T(8,128)(2,1)S(1)}, bf16[48,1024]{1,0:T(8,128)(2,1)S(1)}, u32[]{:S(2)}, u32[]{:S(2)}) collective-permute-start(bf16[48,1024]{1,0:T(8,128)(2,1)S(1)} %get-tuple-element.27), channel_id=1, source_target_pairs={{0,4},{2,6},{4,0},{6,2},{8,12},{10,14},{12,8},{14,10},{1,5},{3,7},... | collective-permute-start | bytes 294920 | tf_op jit(solution)/shard_map/ppermute | solution.py:316
  7.7 2.6 %collective-permute-start = (bf16[48,1024]{1,0:T(8,128)(2,1)S(1)}, bf16[48,1024]{1,0:T(8,128)(2,1)S(1)}, u32[]{:S(2)}, u32[]{:S(2)}) collective-permute-start(bf16[48,1024]{1,0:T(8,128)(2,1)S(1)} %get-tuple-element.22), channel_id=1, source_target_pairs={{0,8},{2,10},{4,12},{6,14},{8,0},{10,2},{12,4},{14,6},{1,9},{3,11}... | collective-permute-start | bytes 294920 | tf_op jit(solution)/shard_map/ppermute | solution.py:316
  10.3 0.4 collective-permute-start.6
  10.7 1.3 %collective-permute-start.1 = (bf16[48,1024]{1,0:T(8,128)(2,1)S(1)}, bf16[48,1024]{1,0:T(8,128)(2,1)S(1)}, u32[]{:S(2)}, u32[]{:S(2)}) collective-permute-start(bf16[48,1024]{1,0:T(8,128)(2,1)S(1)} %get-tuple-element.23), channel_id=1, source_target_pairs={{0,12},{2,14},{4,8},{6,10},{8,4},{10,6},{12,0},{14,2},{1,13},{3,15... | collective-permute-start | bytes 294920 | tf_op jit(solution)/shard_map/ppermute | solution.py:316
  12.1 0.0 collective-permute-done.4.first_ref.refs_1_
  12.1 2.7 %collective-permute-start.2 = (bf16[48,1024]{1,0:T(8,128)(2,1)S(1)}, bf16[48,1024]{1,0:T(8,128)(2,1)S(1)}, u32[]{:S(2)}, u32[]{:S(2)}) collective-permute-start(bf16[48,1024]{1,0:T(8,128)(2,1)S(1)} %get-tuple-element.24), channel_id=1, source_target_pairs={{0,10},{2,8},{4,14},{6,12},{8,2},{10,0},{12,6},{14,4},{1,11},{3,9}... | collective-permute-start | bytes 294920 | tf_op jit(solution)/shard_map/ppermute | solution.py:316
  14.7 0.0 collective-permute-done.5.second_ref.refs_2_
  14.7 1.9 %collective-permute-start.3 = (bf16[48,1024]{1,0:T(8,128)(2,1)S(1)}, bf16[48,1024]{1,0:T(8,128)(2,1)S(1)}, u32[]{:S(2)}, u32[]{:S(2)}) collective-permute-start(bf16[48,1024]{1,0:T(8,128)(2,1)S(1)} %get-tuple-element.25), channel_id=1, source_target_pairs={{0,14},{2,12},{4,10},{6,8},{8,6},{10,4},{12,2},{14,0},{1,15},{3,13... | collective-permute-start | bytes 294920 | tf_op jit(solution)/shard_map/ppermute | solution.py:316
  16.6 0.0 copy-start
  16.6 3.4 %copy-done = bf16[4096,1024]{1,0:T(8,128)(2,1)S(1)} copy-done((bf16[4096,1024]{1,0:T(8,128)(2,1)S(1)}, bf16[4096,1024]{1,0:T(8,128)(2,1)}, u32[]{:S(2)}) %copy-start) | copy-done | bytes 8388632
  20.0 0.0 copy-start.3
  20.0 1.0 %copy-done.3 = bf16[48,4096]{1,0:T(8,128)(2,1)S(1)} copy-done((bf16[48,4096]{1,0:T(8,128)(2,1)S(1)}, bf16[48,4096]{1,0:T(8,128)(2,1)}, u32[]{:S(2)}) %copy-start.3) | copy-done | bytes 393240
  21.0 0.0 copy-start.1
  21.0 0.0 copy-start.4
  21.0 2.3 %shard_map.114 = (f32[48,512]{1,0:T(8,128)S(1)}, f32[48,512]{1,0:T(8,128)S(1)}) custom-call(s32[1]{0:T(128)} %bitcast.3.core_ref, bf16[48,4096]{1,0:T(8,128)(2,1)S(1)} %copy-done.3, bf16[4096,1024]{1,0:T(8,128)(2,1)S(1)} %copy-done, bf16[48,1024]{1,0:T(8,128)(2,1)S(1)} %collective-permute-done.4.first_ref.refs_1_, ...), custom_call_target="tpu_custom_call" | custom-call | flops 402653184 | bytes 33554432 | tf_op jit(solution)/shard_map/pallas_call | solution.py:319
  23.3 0.2 shard_map.115
  23.5 0.0 collective-permute-done.6.refs_3_
  23.6 0.0 copy-done.1
  23.6 0.7 %shard_map.116.refs_6_ = f32[48,128]{1,0:T(8,128)S(1)} custom-call(bf16[48,1024]{1,0:T(8,128)(2,1)S(1)} %get-tuple-element.30.refs_0_, bf16[48,1024]{1,0:T(8,128)(2,1)S(1)} %collective-permute-done.4.first_ref.refs_1_, bf16[48,1024]{1,0:T(8,128)(2,1)S(1)} %collective-permute-done.5.second_ref.refs_2_, bf16[48,1024]{1,0:T(8,128)(2,1)S(1)} %collective-permute-done.6.refs_3_, ...), custom_call_target="tpu_custom_call" | custom-call | tf_op jit(solution)/shard_map/pallas_call | solution.py:341
  24.3 0.0 collective-permute-done.refs_0_
  24.3 0.0 collective-permute-done.1.refs_1_
  24.3 2.0 %collective-permute-done.2.refs_2_ = bf16[48,1024]{1,0:T(8,128)(2,1)S(1)} collective-permute-done((bf16[48,1024]{1,0:T(8,128)(2,1)S(1)}, bf16[48,1024]{1,0:T(8,128)(2,1)S(1)}, u32[]{:S(2)}, u32[]{:S(2)}) %collective-permute-start.2) | collective-permute-done | bytes 98336 | tf_op jit(solution)/shard_map/ppermute | solution.py:316
  26.3 0.0 collective-permute-done.3.refs_3_
  26.3 0.7 %shard_map.117.mine_ref = f32[96,128]{1,0:T(8,128)S(1)} custom-call(bf16[48,1024]{1,0:T(8,128)(2,1)S(1)} %collective-permute-done.refs_0_, bf16[48,1024]{1,0:T(8,128)(2,1)S(1)} %collective-permute-done.1.refs_1_, bf16[48,1024]{1,0:T(8,128)(2,1)S(1)} %collective-permute-done.2.refs_2_, bf16[48,1024]{1,0:T(8,128)(2,1)S(1)} %collective-permute-done.3.refs_3_, ...), custom_call_target="tpu_custom_call" | custom-call | tf_op jit(solution)/shard_map/pallas_call | solution.py:346
  27.0 0.0 collective-permute-start.7
  27.0 1.2 %collective-permute-done.7.other_ref = f32[96,128]{1,0:T(8,128)S(1)} collective-permute-done((f32[96,128]{1,0:T(8,128)S(1)}, f32[96,128]{1,0:T(8,128)S(1)}, u32[]{:S(2)}, u32[]{:S(2)}) %collective-permute-start.7) | collective-permute-done | bytes 49184 | tf_op jit(solution)/shard_map/ppermute | solution.py:355
  28.2 0.0 copy-done.7
  28.2 1.1 %shard_map.118._ = bf16[384,128]{1,0:T(8,128)(2,1)} custom-call(f32[96,128]{1,0:T(8,128)S(1)} %shard_map.117.mine_ref, f32[96,128]{1,0:T(8,128)S(1)} %collective-permute-done.7.other_ref, bf16[1,2,64,256]{3,2,1,0:T(8,128)(2,1)S(1)} %copy-done.7, bf16[384,384]{1,0:T(8,128)(2,1)S(1)} %get-tuple-element.32.table_ref), custom_call_target="tpu_custom_call" | custom-call | tf_op jit(solution)/shard_map/pallas_call | solution.py:351
  29.3 4.9 %all-to-all-start = ((bf16[8,48,128]{2,1,0:T(8,128)(2,1)}), bf16[8,48,128]{2,1,0:T(8,128)(2,1)S(1)}, u32[]{:S(2)}, u32[]{:S(2)}) async-start(bf16[8,48,128]{2,1,0:T(8,128)(2,1)} %bitcast.4), calls=%async_computation | async-start | bytes 196608 | tf_op jit(solution)/shard_map/all_to_all | solution.py:356
  34.1 0.0 copy-done.8
  34.1 0.1 copy.12.length_ref
  34.2 0.0 copy-done.6
  34.2 0.0 copy-done.4
  34.2 0.0 copy-done.5
  34.3 1.7 %shard_map.119 = (f32[48,2048]{1,0:T(8,128)S(1)}, f32[48,128]{1,0:T(8,128)S(1)}, f32[48,128]{1,0:T(8,128)S(1)}, f32[48,512]{1,0:T(8,128)S(1)}) custom-call(bf16[48,2048]{1,0:T(8,128)(2,1)S(1)} %copy-done.6, bf16[48,2,32,128]{3,2,1,0:T(8,128)(2,1)S(1)} %copy-done.4, bf16[48,2,32,128]{3,2,1,0:T(8,128)(2,1)S(1)} %copy-done.5, s32[48,1]{1,0:T(8,128)S(1)} %copy.12.length_ref, ...), custom_call_target="tpu_custom_call" | custom-call | tf_op jit(solution)/shard_map/pallas_call | solution.py:357
  36.0 0.1 collective-permute-start.8
  36.1 1.3 %collective-permute-done.8.other_ref = f32[48,512]{1,0:T(8,128)S(1)} collective-permute-done((f32[48,512]{1,0:T(8,128)S(1)}, f32[48,512]{1,0:T(8,128)S(1)}, u32[]{:S(2)}, u32[]{:S(2)}) %collective-permute-start.8) | collective-permute-done | bytes 98336 | tf_op jit(solution)/shard_map/ppermute | solution.py:378
  37.4 0.4 shard_map.120
  37.7 3.5 %all-to-all-done = bf16[8,48,128]{2,1,0:T(8,128)(2,1)S(1)} async-done(((bf16[8,48,128]{2,1,0:T(8,128)(2,1)}), bf16[8,48,128]{2,1,0:T(8,128)(2,1)S(1)}, u32[]{:S(2)}, u32[]{:S(2)}) %all-to-all-start) | async-done | bytes 98336 | tf_op jit(solution)/shard_map/all_to_all | solution.py:356
  41.3 1.3 %shard_map.121 = (bf16[48,512]{1,0:T(8,128)(2,1)}, bf16[48,2048]{1,0:T(8,128)(2,1)}) custom-call(bf16[384,128]{1,0:T(8,128)(2,1)S(1)} %bitcast.7, bf16[192,384]{1,0:T(8,128)(2,1)S(1)} %get-tuple-element.37.one_hot_ref, f32[48,512]{1,0:T(8,128)S(1)} %get-tuple-element.38.base_ref, bf16[48,2048]{1,0:T(8,128)(2,1)S(1)} %copy-done.6, ...), custom_call_target="tpu_custom_call" | custom-call | tf_op jit(solution)/shard_map/pallas_call | solution.py:379
  (1 shorter events, 0.0 us)
Async XLA Ops:
  0.6 33.5 %copy-start.8 = (s32[48]{0:T(128)S(1)}, s32[48]{0:T(128)}, u32[]{:S(2)}) copy-start(s32[48]{0:T(128)} %param.18) | copy-start | bytes 580
  1.4 1.0 %copy-start.2 = (bf16[48,4096]{1,0:T(8,128)(2,1)S(1)}, bf16[48,4096]{1,0:T(8,128)(2,1)}, u32[]{:S(2)}) copy-start(bf16[48,4096]{1,0:T(8,128)(2,1)} %hidden_ref.3) | copy-start | bytes 1179652
  2.4 25.8 %copy-start.7 = (bf16[1,2,64,256]{3,2,1,0:T(8,128)(2,1)S(1)}, bf16[1,2,64,256]{3,2,1,0:T(8,128)(2,1)}, u32[]{:S(2)}) copy-start(bf16[1,2,64,256]{3,2,1,0:T(8,128)(2,1)} %up_ref.1) | copy-start | bytes 196612
  2.4 31.9 %copy-start.6 = (bf16[48,2048]{1,0:T(8,128)(2,1)S(1)}, bf16[48,2048]{1,0:T(8,128)(2,1)}, u32[]{:S(2)}) copy-start(bf16[48,2048]{1,0:T(8,128)(2,1)} %query_ref.3) | copy-start | bytes 589828
  3.1 8.9 %collective-permute-start.4 = (bf16[48,1024]{1,0:T(8,128)(2,1)S(1)}, bf16[48,1024]{1,0:T(8,128)(2,1)S(1)}, u32[]{:S(2)}, u32[]{:S(2)}) collective-permute-start(bf16[48,1024]{1,0:T(8,128)(2,1)S(1)} %get-tuple-element.26), channel_id=1, source_target_pairs={{0,2},{2,0},{4,6},{6,4},{8,10},{10,8},{12,14},{14,12},{1,3},{3,1},... | collective-permute-start | bytes 294920 | tf_op jit(solution)/shard_map/ppermute | solution.py:316
  6.1 8.6 %collective-permute-start.5 = (bf16[48,1024]{1,0:T(8,128)(2,1)S(1)}, bf16[48,1024]{1,0:T(8,128)(2,1)S(1)}, u32[]{:S(2)}, u32[]{:S(2)}) collective-permute-start(bf16[48,1024]{1,0:T(8,128)(2,1)S(1)} %get-tuple-element.27), channel_id=1, source_target_pairs={{0,4},{2,6},{4,0},{6,2},{8,12},{10,14},{12,8},{14,10},{1,5},{3,7},... | collective-permute-start | bytes 294920 | tf_op jit(solution)/shard_map/ppermute | solution.py:316
  7.7 16.5 %collective-permute-start = (bf16[48,1024]{1,0:T(8,128)(2,1)S(1)}, bf16[48,1024]{1,0:T(8,128)(2,1)S(1)}, u32[]{:S(2)}, u32[]{:S(2)}) collective-permute-start(bf16[48,1024]{1,0:T(8,128)(2,1)S(1)} %get-tuple-element.22), channel_id=1, source_target_pairs={{0,8},{2,10},{4,12},{6,14},{8,0},{10,2},{12,4},{14,6},{1,9},{3,11}... | collective-permute-start | bytes 294920 | tf_op jit(solution)/shard_map/ppermute | solution.py:316
  10.3 13.2 %collective-permute-start.6 = (bf16[48,1024]{1,0:T(8,128)(2,1)S(1)}, bf16[48,1024]{1,0:T(8,128)(2,1)S(1)}, u32[]{:S(2)}, u32[]{:S(2)}) collective-permute-start(bf16[48,1024]{1,0:T(8,128)(2,1)S(1)} %get-tuple-element.31), channel_id=1, source_target_pairs={{0,6},{2,4},{4,2},{6,0},{8,14},{10,12},{12,10},{14,8},{1,7},{3,5},... | collective-permute-start | bytes 294920 | tf_op jit(solution)/shard_map/ppermute | solution.py:316
  10.7 13.6 %collective-permute-start.1 = (bf16[48,1024]{1,0:T(8,128)(2,1)S(1)}, bf16[48,1024]{1,0:T(8,128)(2,1)S(1)}, u32[]{:S(2)}, u32[]{:S(2)}) collective-permute-start(bf16[48,1024]{1,0:T(8,128)(2,1)S(1)} %get-tuple-element.23), channel_id=1, source_target_pairs={{0,12},{2,14},{4,8},{6,10},{8,4},{10,6},{12,0},{14,2},{1,13},{3,15... | collective-permute-start | bytes 294920 | tf_op jit(solution)/shard_map/ppermute | solution.py:316
  12.1 14.2 %collective-permute-start.2 = (bf16[48,1024]{1,0:T(8,128)(2,1)S(1)}, bf16[48,1024]{1,0:T(8,128)(2,1)S(1)}, u32[]{:S(2)}, u32[]{:S(2)}) collective-permute-start(bf16[48,1024]{1,0:T(8,128)(2,1)S(1)} %get-tuple-element.24), channel_id=1, source_target_pairs={{0,10},{2,8},{4,14},{6,12},{8,2},{10,0},{12,6},{14,4},{1,11},{3,9}... | collective-permute-start | bytes 294920 | tf_op jit(solution)/shard_map/ppermute | solution.py:316
  14.7 11.6 %collective-permute-start.3 = (bf16[48,1024]{1,0:T(8,128)(2,1)S(1)}, bf16[48,1024]{1,0:T(8,128)(2,1)S(1)}, u32[]{:S(2)}, u32[]{:S(2)}) collective-permute-start(bf16[48,1024]{1,0:T(8,128)(2,1)S(1)} %get-tuple-element.25), channel_id=1, source_target_pairs={{0,14},{2,12},{4,10},{6,8},{8,6},{10,4},{12,2},{14,0},{1,15},{3,13... | collective-permute-start | bytes 294920 | tf_op jit(solution)/shard_map/ppermute | solution.py:316
  16.6 3.4 %copy-start = (bf16[4096,1024]{1,0:T(8,128)(2,1)S(1)}, bf16[4096,1024]{1,0:T(8,128)(2,1)}, u32[]{:S(2)}) copy-start(bf16[4096,1024]{1,0:T(8,128)(2,1)} %weight_hbm.1) | copy-start | bytes 25165828
  20.0 1.0 %copy-start.3 = (bf16[48,4096]{1,0:T(8,128)(2,1)S(1)}, bf16[48,4096]{1,0:T(8,128)(2,1)}, u32[]{:S(2)}) copy-start(bf16[48,4096]{1,0:T(8,128)(2,1)} %hidden_ref.3) | copy-start | bytes 1179652
  21.0 2.6 %copy-start.1 = (bf16[1,4096,128]{2,1,0:T(8,128)(2,1)S(1)}, bf16[1,4096,128]{2,1,0:T(8,128)(2,1)}, u32[]{:S(2)}) copy-start(bf16[1,4096,128]{2,1,0:T(8,128)(2,1)} %refs_4_.3) | copy-start | bytes 3145732
  21.0 13.3 %copy-start.4 = (bf16[48,2,32,128]{3,2,1,0:T(8,128)(2,1)S(1)}, bf16[48,2,32,128]{3,2,1,0:T(8,128)(2,1)}, u32[]{:S(2)}) copy-start(bf16[48,2,32,128]{3,2,1,0:T(8,128)(2,1)} %key_ref.1) | copy-start | bytes 2359300
  21.0 13.3 %copy-start.5 = (bf16[48,2,32,128]{3,2,1,0:T(8,128)(2,1)S(1)}, bf16[48,2,32,128]{3,2,1,0:T(8,128)(2,1)}, u32[]{:S(2)}) copy-start(bf16[48,2,32,128]{3,2,1,0:T(8,128)(2,1)} %value_ref.1) | copy-start | bytes 2359300
  27.0 1.2 %collective-permute-start.7 = (f32[96,128]{1,0:T(8,128)S(1)}, f32[96,128]{1,0:T(8,128)S(1)}, u32[]{:S(2)}, u32[]{:S(2)}) collective-permute-start(f32[96,128]{1,0:T(8,128)S(1)} %shard_map.117.mine_ref), channel_id=1, source_target_pairs={{0,1},{1,0},{2,3},{3,2},{4,5},{5,4},{6,7},{7,6},{8,9},{9,8},{10,11... | collective-permute-start | bytes 147464 | tf_op jit(solution)/shard_map/ppermute | solution.py:355
  29.3 12.0 %all-to-all-start = ((bf16[8,48,128]{2,1,0:T(8,128)(2,1)}), bf16[8,48,128]{2,1,0:T(8,128)(2,1)S(1)}, u32[]{:S(2)}, u32[]{:S(2)}) async-start(bf16[8,48,128]{2,1,0:T(8,128)(2,1)} %bitcast.4), calls=%async_computation | async-start | bytes 196608 | tf_op jit(solution)/shard_map/all_to_all | solution.py:356
  36.0 1.4 %collective-permute-start.8 = (f32[48,512]{1,0:T(8,128)S(1)}, f32[48,512]{1,0:T(8,128)S(1)}, u32[]{:S(2)}, u32[]{:S(2)}) collective-permute-start(f32[48,512]{1,0:T(8,128)S(1)} %get-tuple-element.36), channel_id=1, source_target_pairs={{0,1},{1,0},{2,3},{3,2},{4,5},{5,4},{6,7},{7,6},{8,9},{9,8},{10,11... | collective-permute-start | bytes 294920 | tf_op jit(solution)/shard_map/ppermute | solution.py:378
